TPU v7x, 256 devices: a whole 4x4x8 slice. The times are simulated.
256 devices in a mesh: group: 2 (over z_hi), dp: 32 (over y, x, core), tensor: 4 (over z_lo).
Axes of the slice: x: 4, y: 4, z: 8 (z_hi: 2, z_lo: 4; z = z_hi * 4 + z_lo), core: 2. Of those that a mesh axis runs over, the one named last changes fastest.
Arguments:
- hidden: bfloat16 [14336, 4096], P('dp', ('group', 'tensor')), may hold values from -42 to 42
- cotangent: bfloat16 [14336, 4096], P('dp', ('group', 'tensor')), may hold values from -6 to 6
- query_weight: bfloat16 [4096, 2048], P(None, ('group', 'tensor')), may hold values from -0.09375 to 0.09375
- out_weight: bfloat16 [2048, 4096], P(('group', 'tensor')), may hold values from -0.125 to 0.125
- condition_weight: bfloat16 [4096, 1792], P(None, ('group', 'tensor')), may hold values from -0.09375 to 0.09375
- key_value_weight: bfloat16 [2, 896, 2048], P(None, None, ('group', 'tensor')), may hold values from -0.1875 to 0.1875
- encoder_query: bfloat16 [896, 896], replicated, may hold values from -0.1875 to 0.1875
- encoder_out: bfloat16 [896, 896], replicated, may hold values from -0.1875 to 0.1875
- database: bfloat16 [512, 128, 896], P('dp', ('group', 'tensor')), may hold values from -36 to 36
- neighbours: int32 [224, 2], P('dp'), may hold values from 0 to 15
- owners: int32 [224, 1], P('dp'), may hold values from 0 to 31; in each aligned block of 7 rows (0 to 6, 7 to 13, ...) no two rows name the same one
Outputs:
- branch_grad: bfloat16 [14336, 4096], P('dp', ('group', 'tensor'))
Inputs may be any that keep to these rules, and one draw needn't show every extreme that they name: `owners`: within the 7 segments of one index of dp no owner is named more than 1 times, a bound that some block reaches.
All inputs are finite; a program needn't handle non-finite values.
Results may differ from a plain program's by a relative error of at most 0.025.
Values may be sent and summed in bfloat16 or wider, within the bound.
No kernel may reach another device: no remote copies, remote signals or barrier semaphores. Data moves between devices by JAX's collectives and lax.ppermute only.
A program may use at most 128 MiB of HBM per device.

v0:
```python
import functools

import jax
import jax.numpy as jnp
from jax import lax
from jax.experimental import pallas as pl
from jax.experimental.pallas import tpu as pltpu
from jax.sharding import PartitionSpec as P

D = 4096
HEAD = 128
DE = 896
EHEADS = 7
SEG = 64
NLEN = 128
NEIGH = 2
KEYS = NLEN * NEIGH
NZ = 8
NDP = 32
SEGS = 7
FEAT = D // NZ
TOK = SEGS * SEG
HALF = 8 * HEAD
SCALE = HEAD**-0.5
epsilon = 1e-05
Z = ("group", "tensor")
BF = jnp.bfloat16
F32 = jnp.float32
PARAMS = pltpu.CompilerParams(vmem_limit_bytes=40 * 1024 * 1024)
VMEM = pl.BlockSpec(memory_space=pltpu.VMEM)
SMEM = pl.BlockSpec(memory_space=pltpu.SMEM)
ANY = pl.BlockSpec(memory_space=pl.ANY)
NT = (((1,), (1,)), ((), ()))


def dot(a, b):
    return jnp.dot(a, b, preferred_element_type=F32)


def dot_nt(a, b):
    return lax.dot_general(a, b, NT, preferred_element_type=F32)


def shift(x, by):
    return lax.ppermute(x, Z, [(i, (i + by) % NZ) for i in range(NZ)])


def tie(*arrays):
    return lax.optimization_barrier(arrays)


def ring(x):
    rows = x.shape[0] // 2
    chunks = [(x, 0)]
    right = left = x
    for step in range(1, 4):
        right, left = shift(right, 1), shift(left, -1)
        chunks += [(right, -step), (left, step)]
    far = (shift(right[:rows], 1), shift(left[rows:], -1))
    return chunks, far


def exchange(x, axis):
    return lax.all_to_all(x, axis, split_axis=0, concat_axis=0, tiled=True)


def start(pairs, sem):
    copies = [pltpu.make_async_copy(a, b, sem.at[i]) for i, (a, b) in enumerate(pairs)]
    for copy in copies:
        copy.start()
    return copies


def wait(copies):
    for copy in copies:
        copy.wait()


def cost(flops, size):
    return pl.CostEstimate(flops=flops, bytes_accessed=size, transcendentals=0)


def like(x):
    return pltpu.VMEM(x.shape, x.dtype)


def encoder_queries(fetched_hbm, weight_hbm, out_ref, fetched_ref, weight_ref, sem):
    copies = start([(fetched_hbm, fetched_ref), (weight_hbm, weight_ref)], sem)
    copies[0].wait()
    rows = fetched_ref[...].astype(F32)
    inverse = lax.rsqrt(jnp.mean(rows * rows, axis=-1, keepdims=True) + epsilon)
    normed = (rows * inverse).astype(BF)
    copies[1].wait()
    out_ref[...] = dot(normed, weight_ref[...]).astype(BF)


def project(count, index_ref, *refs):
    chunks_hbm, refs = refs[:count], refs[count:]
    query_hbm, cond_hbm, out_hbm, acc_ref, squares_ref = refs[:5]
    chunk_ref, query_ref, cond_ref, out_weight_ref, sem = refs[5:]
    copies = []
    for k in range(count):
        at = pl.ds(pl.multiple_of(index_ref[k] * FEAT, FEAT), FEAT)
        copies.append(
            start(
                [
                    (chunks_hbm[k], chunk_ref.at[k]), (query_hbm.at[at], query_ref.at[k]),
                    (cond_hbm.at[at], cond_ref.at[k]), (out_hbm.at[:, at], out_weight_ref.at[k]),
                ], sem.at[k],
            )
        )
    for k in range(count):
        wait(copies[k])
        chunk = chunk_ref[k, :TOK]
        squares = jnp.sum(jnp.square(chunk.astype(F32)), axis=-1, keepdims=True)
        parts = (
            dot(chunk, query_ref[k]),
            dot_nt(chunk_ref[k, TOK:], out_weight_ref[k]),
            dot(chunk, cond_ref[k]),
        )
        for columns, part in zip((slice(0, 256), slice(256, 512), slice(512, 736)), parts):
            acc_ref[:, columns] = part if k == 0 else acc_ref[:, columns] + part
        squares_ref[...] = squares if k == 0 else squares_ref[...] + squares


def project_last(
    index_ref, hidden_hbm, cot_hbm, acc_hbm, squares_hbm, query_hbm, cond_hbm, out_hbm,
    sent_ref, inverse_ref,
    hidden_ref, cot_ref, acc_ref, squares_ref, query_ref, cond_ref, out_weight_ref, sem,
):
    at = pl.ds(pl.multiple_of(index_ref[0] * FEAT, FEAT), FEAT)
    copies = start(
        [
            (hidden_hbm, hidden_ref), (squares_hbm, squares_ref), (acc_hbm, acc_ref),
            (query_hbm.at[at], query_ref), (cond_hbm.at[at], cond_ref),
            (cot_hbm, cot_ref), (out_hbm.at[:, at], out_weight_ref),
        ], sem,
    )
    wait(copies)
    chunk = hidden_ref[...]
    squares = squares_ref[...] + jnp.sum(
        jnp.square(chunk.astype(F32)), axis=-1, keepdims=True
    )
    inverse = lax.rsqrt(squares / D + epsilon)
    inverse_ref[...] = inverse
    queries = (acc_ref[:, :256] + dot(chunk, query_ref[...])) * inverse
    grads = acc_ref[:, 256:512] + dot_nt(cot_ref[...], out_weight_ref[...])
    condition = (acc_ref[:, 512:736] + dot(chunk, cond_ref[...])) * inverse
    for columns, part in (
        (slice(0, 256), queries), (slice(256, 512), grads), (slice(512, 736), condition)
    ):
        sent_ref[:SEGS, :, columns] = part.astype(BF).reshape(SEGS, SEG, -1)
    sent_ref[:, :, 736:] = jnp.zeros((NZ, SEG, 32), BF)
    sent_ref[SEGS, :, :736] = jnp.zeros((SEG, 736), BF)


def attention(
    fetched_hbm, enc_q_hbm, got_hbm, enc_out_hbm, weights_hbm, out_ref,
    fetched_ref, enc_q_ref, got_ref, enc_out_ref, kv_ref, key_ref, value_ref, mixed_ref, sem,
):
    small = start(
        [
            (got_hbm, got_ref), (enc_q_hbm, enc_q_ref),
            (fetched_hbm, fetched_ref), (enc_out_hbm, enc_out_ref),
        ], sem,
    )
    large = [
        pltpu.make_async_copy(
            weights_hbm.at[:, j, pl.ds(0, 112), :], kv_ref.at[j], sem.at[4 + j]
        )
        for j in range(2)
    ]
    for copy in large:
        copy.start()
    wait(small)
    cond_keys, cond_values = (
        jnp.concatenate([got_ref[z, :, 512:736] for z in range(n, n + 4)], axis=1)
        for n in (0, 4)
    )
    for h in range(EHEADS):
        columns = slice(h * HEAD, (h + 1) * HEAD)
        exponent = jnp.exp(dot_nt(enc_q_ref[:, columns], cond_keys[:, columns]) * SCALE)
        weights = (exponent / jnp.sum(exponent, axis=-1, keepdims=True)).astype(BF)
        mixed_ref[:, columns] = dot(weights, cond_values[:, columns]).astype(BF)
    encoded = (fetched_ref[...].astype(F32) + dot(mixed_ref[...], enc_out_ref[...])).astype(BF)
    total = jnp.zeros((SEG, HEAD), F32)
    for j in range(2):
        large[j].wait()
        key_ref[j] = dot(encoded, kv_ref[j, 0:8].reshape(DE, HALF)).astype(BF)
        value_ref[j] = dot(encoded, kv_ref[j, 8:16].reshape(DE, HALF)).astype(BF)
        for z in range(NZ):
            columns = slice(z * HEAD, (z + 1) * HEAD)
            query = got_ref[z, :, j * HEAD : (j + 1) * HEAD]
            grad_att = got_ref[z, :, (2 + j) * HEAD : (3 + j) * HEAD]
            key, value = key_ref[j, :, columns], value_ref[j, :, columns]
            exponent = jnp.exp(dot_nt(query, key) * SCALE)
            probs = exponent / jnp.sum(exponent, axis=-1, keepdims=True)
            attended = dot(probs.astype(BF), value).astype(BF)
            delta = jnp.sum(
                grad_att.astype(F32) * attended.astype(F32), axis=-1, keepdims=True
            )
            grad_probs = dot_nt(grad_att, value)
            grad_scores = (probs * (grad_probs - delta) * SCALE).astype(BF)
            grad_query = dot(grad_scores, key).astype(BF)
            out_ref[:, j * HALF + z * HEAD : j * HALF + (z + 1) * HEAD] = grad_query
            total = total + grad_query.astype(F32) * query.astype(F32)
    stat = jnp.sum(total, axis=-1, keepdims=True) / D
    high = stat.astype(BF)
    low = (stat - high.astype(F32)).astype(BF)
    lane = lax.broadcasted_iota(jnp.int32, (SEG, HEAD), 1)
    out_ref[:, 2 * HALF :] = jnp.where(
        lane == 0, high.astype(F32), jnp.where(lane == 1, low.astype(F32), 0.0)
    ).astype(BF)


def finish(starts, first, *refs):
    count = len(starts)
    source_ref, refs = refs[0], refs[1:]
    chunks_hbm, refs = refs[:count], refs[count:]
    hidden_hbm, inverse_hbm, weights_hbm = refs[:3]
    refs = refs[3 if first else 4 :]
    out_hbm, refs = refs[0], refs[1:]
    chunk_refs, refs = refs[:count], refs[count:]
    hidden_refs, refs = refs[:count], refs[count:]
    out_refs, refs = refs[:count], refs[count:]
    inverse_ref, weight_ref, sem, out_sem = refs
    places = []
    for k in range(count):
        source = source_ref[k]
        rows = chunk_refs[k].shape[0]
        at = jnp.where(source < SEGS, source, 0) * SEG + starts[k]
        places.append((source < SEGS, pl.ds(pl.multiple_of(at, 32), rows)))
    loads = [(inverse_hbm, inverse_ref)]
    loads += [
        (weights_hbm.at[:, pl.ds(112 + 16 * j, 16), :], weight_ref.at[j]) for j in range(2)
    ]
    for k in range(count):
        loads.append((chunks_hbm[k], chunk_refs[k]))
        loads.append((hidden_hbm.at[places[k][1]], hidden_refs[k]))
    wait(start(loads, sem))
    rows = [c.shape[0] for c in chunk_refs]
    chunks = jnp.concatenate([c[...] for c in chunk_refs], axis=0)
    grads = sum(
        dot_nt(chunks[:, j * HALF : (j + 1) * HALF], weight_ref[j].reshape(FEAT, HALF))
        for j in range(2)
    )
    for k in range(count):
        grad = grads[sum(rows[:k]) : sum(rows[: k + 1])]
        tail = chunk_refs[k][:, 2 * HALF :].astype(F32)
        stat = tail[:, 0:1] + tail[:, 1:2]
        inverse = inverse_ref[places[k][1], :]
        out_refs[k][...] = (
            inverse * grad - hidden_refs[k][...].astype(F32) * (inverse * inverse * stat)
        ).astype(BF)

        @pl.when(places[k][0])
        def _(k=k):
            pltpu.make_async_copy(
                out_refs[k], out_hbm.at[places[k][1]], out_sem.at[k]
            ).start()

    for k in range(count):

        @pl.when(places[k][0])
        def _(k=k):
            pltpu.make_async_copy(
                out_refs[k], out_hbm.at[places[k][1]], out_sem.at[k]
            ).wait()


def finish_call(chunks, starts, sources, hidden, inverse, weights, previous):
    first = previous is None
    operands = [sources, *chunks, hidden, inverse, weights] + ([] if first else [previous])
    rows = [c.shape[0] for c in chunks]
    return pl.pallas_call(
        functools.partial(finish, starts, first),
        out_shape=jax.ShapeDtypeStruct((TOK, FEAT), BF),
        in_specs=[SMEM] + [ANY] * (len(operands) - 1),
        out_specs=ANY,
        scratch_shapes=[like(c) for c in chunks]
        + [pltpu.VMEM((r, FEAT), BF) for r in rows] * 2
        + [
            like(inverse),
            pltpu.VMEM((2, NDP, 16, HALF), BF),
            pltpu.SemaphoreType.DMA((3 + 2 * len(chunks),)),
            pltpu.SemaphoreType.DMA((len(chunks),)),
        ],
        input_output_aliases={} if first else {len(operands) - 1: 0},
        compiler_params=PARAMS,
        cost_estimate=cost(2 * sum(rows) * FEAT * 2048, 4_000_000),
        name="finish",
    )(*operands)


def shards(
    hidden,
    cotangent,
    query_weight,
    out_weight,
    condition_weight,
    key_value_weight,
    encoder_query,
    encoder_out,
    database,
    neighbours,
    owners,
):
    me = lax.axis_index(Z)
    mine = lax.axis_index("dp")

    owner = owners[:, 0]
    selector = owner[None, :] == jnp.arange(NDP, dtype=jnp.int32)[:, None]
    wanted = jnp.sum(selector.astype(jnp.int32)[:, :, None] * neighbours[None, :, :], axis=1)
    kv_part = lax.dynamic_slice(
        key_value_weight.reshape(2 * DE, 2 * HEAD),
        (mine // 2 * 112, mine % 2 * HEAD),
        (112, HEAD),
    )
    q_part = lax.dynamic_slice(
        query_weight.reshape(NZ, FEAT, 2 * HEAD), (0, mine * 16, 0), (NZ, 16, 2 * HEAD)
    )
    q_part = q_part.reshape(NZ, 16, 2, HEAD).transpose(0, 2, 1, 3).reshape(NZ, 32, HEAD)
    part = jnp.concatenate([jnp.broadcast_to(kv_part, (NZ, 112, HEAD)), q_part], axis=1)
    both = jnp.concatenate([hidden, cotangent], axis=0)

    wanted, part, both = tie(wanted, part, both)
    asked = exchange(wanted, "dp")
    part = exchange(part, Z).transpose(1, 0, 2).reshape(144, HALF)
    weights = lax.all_gather(part, "dp", axis=0, tiled=True).reshape(16, 2, 144, HALF)
    returned = exchange(database[asked].reshape(NDP, NEIGH * NLEN // NZ, DE), "dp")
    fetched = exchange(returned[jnp.concatenate([owner, owner[:1]])], Z).reshape(KEYS, DE)
    enc_q = pl.pallas_call(
        encoder_queries,
        out_shape=jax.ShapeDtypeStruct((KEYS, DE), BF),
        in_specs=[ANY, ANY],
        out_specs=VMEM,
        scratch_shapes=[like(fetched), like(encoder_query), pltpu.SemaphoreType.DMA((2,))],
        compiler_params=PARAMS,
        cost_estimate=cost(2 * KEYS * DE * DE, 3_000_000),
        name="encoder_queries",
    )(fetched, encoder_query)

    chunks, far = ring(both)
    index = jnp.stack([(me + offset) % NZ for _, offset in chunks])
    chunks = [c for c, _ in chunks]
    count = len(chunks)
    acc, squares = pl.pallas_call(
        functools.partial(project, count),
        out_shape=(
            jax.ShapeDtypeStruct((TOK, 768), F32),
            jax.ShapeDtypeStruct((TOK, 1), F32),
        ),
        in_specs=[SMEM] + [ANY] * (count + 3),
        out_specs=(VMEM, VMEM),
        scratch_shapes=[
            pltpu.VMEM((count, 2 * TOK, FEAT), BF),
            pltpu.VMEM((count, FEAT, 256), BF),
            pltpu.VMEM((count, FEAT, 224), BF),
            pltpu.VMEM((count, 256, FEAT), BF),
            pltpu.SemaphoreType.DMA((count, 4)),
        ],
        compiler_params=PARAMS,
        cost_estimate=cost(2 * count * TOK * FEAT * 736, 16_000_000),
        name="project",
    )(index, *chunks, query_weight, condition_weight, out_weight)
    sent, inverse = pl.pallas_call(
        project_last,
        out_shape=(
            jax.ShapeDtypeStruct((NZ, SEG, 768), BF),
            jax.ShapeDtypeStruct((TOK, 1), F32),
        ),
        in_specs=[SMEM] + [ANY] * 7,
        out_specs=(VMEM, VMEM),
        scratch_shapes=[
            pltpu.VMEM((TOK, FEAT), BF),
            pltpu.VMEM((TOK, FEAT), BF),
            like(acc),
            like(squares),
            pltpu.VMEM((FEAT, 256), BF),
            pltpu.VMEM((FEAT, 224), BF),
            pltpu.VMEM((256, FEAT), BF),
            pltpu.SemaphoreType.DMA((7,)),
        ],
        compiler_params=PARAMS,
        cost_estimate=cost(2 * TOK * FEAT * 736, 4_000_000),
        name="project_last",
    )(
        jnp.stack([(me + 4) % NZ]), far[0], far[1], acc, squares,
        query_weight, condition_weight, out_weight,
    )
    got = exchange(sent, Z)
    operands = (fetched, enc_q, got, encoder_out)
    grad_query = pl.pallas_call(
        attention,
        out_shape=jax.ShapeDtypeStruct((SEG, 2 * HALF + HEAD), BF),
        in_specs=[ANY] * 5,
        out_specs=VMEM,
        scratch_shapes=[like(x) for x in operands]
        + [
            pltpu.VMEM((2, 16, 112, HALF), BF),
            pltpu.VMEM((2, KEYS, HALF), BF),
            pltpu.VMEM((2, KEYS, HALF), BF),
            pltpu.VMEM((KEYS, DE), BF),
            pltpu.SemaphoreType.DMA((6,)),
        ],
        compiler_params=PARAMS,
        cost_estimate=cost(4_000_000_000, 12_000_000),
        name="attention",
    )(*operands, weights)

    chunks, far = ring(grad_query)
    out = None
    for group in (chunks[:5], chunks[5:7], [(far[0], 4), (far[1], 4)]):
        sources = jnp.stack([(me + offset) % NZ for _, offset in group])
        group = [c for c, _ in group]
        starts = (0, SEG // 2) if group[0].shape[0] < SEG else (0,) * len(group)
        out = finish_call(
            group, starts, sources, hidden, inverse, weights.reshape(NDP, 144, HALF), out
        )
    return out


def solution(mesh):
    return jax.shard_map(
        shards,
        mesh=mesh,
        in_specs=(
            P("dp", Z),
            P("dp", Z),
            P(None, Z),
            P(Z, None),
            P(None, Z),
            P(None, None, Z),
            P(),
            P(),
            P("dp", Z, None),
            P("dp", None),
            P("dp", None),
        ),
        out_specs=P("dp", Z),
        check_vma=False,
    )
```

profile of v0, /device:TPU:2, one launch (start us, length us, event | category | flops | bytes accessed | tf_op | source)
XLA Modules:
  0.0 228.3 jit_solution(16459282005441239514)
XLA Ops:
  6.5 0.9 constant_dynamic-slice_fusion
  7.5 0.8 copy.43
  8.3 0.7 fusion
  9.0 0.8 dynamic_slice.6
  9.8 1.2 pad_maximum_fusion.refs_0_
  11.1 20.8 %all_to_all.32 = bf16[8,144,128]{2,1,0:T(8,128)(2,1)S(1)} all-to-all(bf16[8,144,128]{2,1,0:T(8,128)(2,1)S(1)} %pad_maximum_fusion.1), channel_id=1, replica_groups=mesh['group'=2,'dp'=32,'tensor'=4] {'group','tensor'}, dimensions={0} | all-to-all | bytes 589824 | tf_op jit(solution)/shard_map/all_to_all | solution.py:64
  31.9 0.8 copy_bitcast_fusion
  32.7 0.6 collective-permute-start
  33.4 2.7 %collective-permute-start.4 = (bf16[896,512]{1,0:T(8,128)(2,1)S(1)}, bf16[896,512]{1,0:T(8,128)(2,1)S(1)}, u32[]{:S(2)}, u32[]{:S(2)}) collective-permute-start(bf16[896,512]{1,0:T(8,128)(2,1)S(1)} %pad_maximum_fusion.refs_0_), channel_id=1, source_target_pairs={{0,131},{1,0},{2,1},{3,2},{128,3},{129,128},{130,129},{131,130},{4... | collective-permute-start | bytes 2752520 | tf_op jit(solution)/shard_map/ppermute | solution.py:45
  36.0 0.1 copy.45
  36.1 13.6 %all_to_all.33 = s32[32,1,2]{2,1,0:T(1,128)S(1)} all-to-all(s32[32,1,2]{2,1,0:T(1,128)S(1)} %copy.45), channel_id=1, replica_groups=mesh['group'=2,'dp'=32,'tensor'=4] {'dp'}, dimensions={0} | all-to-all | bytes 512 | tf_op jit(solution)/shard_map/all_to_all | solution.py:64
  49.8 0.1 copy.47
  49.9 0.1 reshape.154
  50.0 2.1 gather_fusion
  52.1 5.9 %all-to-all-start.1 = ((bf16[32,32,896]{2,1,0:T(8,128)(2,1)}), bf16[32,32,896]{2,1,0:T(8,128)(2,1)}, u32[]{:S(2)}, u32[]{:S(2)}) async-start(bf16[32,32,896]{2,1,0:T(8,128)(2,1)} %bitcast.36), calls=%async_computation.1 | async-start | bytes 3670016 | tf_op jit(solution)/shard_map/all_to_all | solution.py:64
  58.1 0.9 copy-done.13
  59.1 3.2 %collective-permute-start.5 = (bf16[896,512]{1,0:T(8,128)(2,1)S(1)}, bf16[896,512]{1,0:T(8,128)(2,1)}, u32[]{:S(2)}, u32[]{:S(2)}) collective-permute-start(bf16[896,512]{1,0:T(8,128)(2,1)S(1)} %collective-permute-done.4.refs_2_), channel_id=1, source_target_pairs={{0,131},{1,0},{2,1},{3,2},{128,3},{129,128},{130,129},{131,130},{4... | collective-permute-start | bytes 2752520 | tf_op jit(solution)/shard_map/ppermute | solution.py:45
  62.3 0.9 copy-done.15
  63.2 18.6 %collective-permute-done.1.refs_3_ = bf16[896,512]{1,0:T(8,128)(2,1)} collective-permute-done((bf16[896,512]{1,0:T(8,128)(2,1)S(1)}, bf16[896,512]{1,0:T(8,128)(2,1)}, u32[]{:S(2)}, u32[]{:S(2)}) %collective-permute-start.1) | collective-permute-done | bytes 917536 | tf_op jit(solution)/shard_map/ppermute | solution.py:45
  81.8 0.1 collective-permute-done.5.refs_4_
  81.9 3.8 %collective-permute-start.6 = (bf16[896,512]{1,0:T(8,128)(2,1)}, bf16[896,512]{1,0:T(8,128)(2,1)S(1)}, u32[]{:S(2)}, u32[]{:S(2)}) collective-permute-start(bf16[896,512]{1,0:T(8,128)(2,1)} %collective-permute-done.5.refs_4_), channel_id=1, source_target_pairs={{0,131},{1,0},{2,1},{3,2},{128,3},{129,128},{130,129},{131,130},{4... | collective-permute-start | bytes 2752520 | tf_op jit(solution)/shard_map/ppermute | solution.py:45
  85.7 0.1 fusion.1
  85.8 9.6 %all-to-all-done.1 = bf16[32,32,896]{2,1,0:T(8,128)(2,1)} async-done(((bf16[32,32,896]{2,1,0:T(8,128)(2,1)}), bf16[32,32,896]{2,1,0:T(8,128)(2,1)}, u32[]{:S(2)}, u32[]{:S(2)}) %all-to-all-start.1) | async-done | bytes 1835040 | tf_op jit(solution)/shard_map/all_to_all | solution.py:64
  95.5 2.9 %gather_fusion.1 = bf16[8,32,896]{2,1,0:T(8,128)(2,1)} fusion(bf16[32,32,896]{2,1,0:T(8,128)(2,1)} %all-to-all-done.1, s32[1024]{0:T(1024)S(1)} %pad_clamp_fusion), kind=kCustom, calls=%fused_computation.1 | custom fusion | bytes 917536 | tf_op jit(solution)/shard_map/gather | solution.py:331
  98.3 4.1 %all-to-all-start.2 = ((bf16[8,32,896]{2,1,0:T(8,128)(2,1)}), bf16[8,32,896]{2,1,0:T(8,128)(2,1)}, u32[]{:S(2)}, u32[]{:S(2)}) async-start(bf16[8,32,896]{2,1,0:T(8,128)(2,1)} %gather_fusion.1), calls=%async_computation.2 | async-start | bytes 917504 | tf_op jit(solution)/shard_map/all_to_all | solution.py:64
  102.5 2.3 %collective-permute-done.2.refs_5_ = bf16[896,512]{1,0:T(8,128)(2,1)S(1)} collective-permute-done((bf16[896,512]{1,0:T(8,128)(2,1)}, bf16[896,512]{1,0:T(8,128)(2,1)S(1)}, u32[]{:S(2)}, u32[]{:S(2)}) %collective-permute-start.2) | collective-permute-done | bytes 917536 | tf_op jit(solution)/shard_map/ppermute | solution.py:45
  104.8 0.9 slice.25
  105.7 1.2 collective-permute-done.6.refs_6_
  106.9 0.8 slice.26
  107.7 4.7 %collective-permute-start.7 = (bf16[448,512]{1,0:T(8,128)(2,1)}, bf16[448,512]{1,0:T(8,128)(2,1)}, u32[]{:S(2)}, u32[]{:S(2)}) collective-permute-start(bf16[448,512]{1,0:T(8,128)(2,1)} %slice.26), channel_id=1, source_target_pairs={{0,131},{1,0},{2,1},{3,2},{128,3},{129,128},{130,129},{131,130},{4... | collective-permute-start | bytes 1376264 | tf_op jit(solution)/shard_map/ppermute | solution.py:45
  112.5 3.2 %copy.48.refs_8_.cond_hbm = bf16[4096,224]{1,0:T(8,128)(2,1)S(1)} copy(bf16[4096,224]{0,1:T(8,128)(2,1)} %param.15) | data formatting | bytes 3670016 | tf_op args[4]
  115.8 0.1 stack.54.index_ref
  115.9 1.6 copy-done.3
  117.5 1.6 copy-done.5
  119.1 1.2 copy-done.9
  120.2 1.2 copy-done.11
  121.4 1.2 copy-done.14
  122.6 1.2 copy-done.16
  123.8 6.7 %project.1 = (f32[448,768]{1,0:T(8,128)S(1)}, f32[448,1]{1,0:T(8,128)S(1)}) custom-call(s32[7]{0:T(128)S(1)} %stack.54.index_ref, bf16[896,512]{1,0:T(8,128)(2,1)S(1)} %pad_maximum_fusion.refs_0_, bf16[896,512]{1,0:T(8,128)(2,1)S(1)} %copy-done.14, bf16[896,512]{1,0:T(8,128)(2,1)S(1)} %copy-done.16, bf16[896,512]{1,0:T(8,128)(2,1)} %collective-permute-done.1.refs_3_, ...), custom_call_target="tpu_custom_call" | custom-call | flops 2363490304 | bytes 16000000 | tf_op jit(solution)/shard_map/project/pallas_call | solution.py:347
  130.5 2.2 project_last.1
  132.7 0.9 copy-done.17
  133.6 3.5 %all-to-all-start.3 = ((bf16[8,64,768]{2,1,0:T(8,128)(2,1)}), bf16[8,64,768]{2,1,0:T(8,128)(2,1)S(1)}, u32[]{:S(2)}, u32[]{:S(2)}) async-start(bf16[8,64,768]{2,1,0:T(8,128)(2,1)} %copy-done.17), calls=%async_computation.3 | async-start | bytes 1572864 | tf_op jit(solution)/shard_map/all_to_all | solution.py:64
  137.2 1.4 copy-done.12
  138.6 1.9 encoder_queries.1.enc_q_hbm
  140.5 17.8 %all-to-all-done.3.got_hbm = bf16[8,64,768]{2,1,0:T(8,128)(2,1)S(1)} async-done(((bf16[8,64,768]{2,1,0:T(8,128)(2,1)}), bf16[8,64,768]{2,1,0:T(8,128)(2,1)S(1)}, u32[]{:S(2)}, u32[]{:S(2)}) %all-to-all-start.3) | async-done | bytes 786464 | tf_op jit(solution)/shard_map/all_to_all | solution.py:64
  158.3 3.7 %copy-done.1 = bf16[4608,1024]{1,0:T(8,128)(2,1)S(1)} copy-done((bf16[4608,1024]{1,0:T(8,128)(2,1)S(1)}, bf16[4608,1024]{1,0:T(8,128)(2,1)}, u32[]{:S(2)}) %copy-start.1) | copy-done | bytes 9437208
  162.0 1.4 copy-done.20
  163.4 12.2 %attention.1.refs_1_ = bf16[64,2176]{1,0:T(8,128)(2,1)S(1)} custom-call(bf16[256,896]{1,0:T(8,128)(2,1)} %bitcast.10.fetched_hbm, bf16[256,896]{1,0:T(8,128)(2,1)S(1)} %encoder_queries.1.enc_q_hbm, bf16[8,64,768]{2,1,0:T(8,128)(2,1)S(1)} %all-to-all-done.3.got_hbm, bf16[896,896]{1,0:T(8,128)(2,1)S(1)} %copy-done.20, bf16[16,2,144,1024]{3,2,1,0:T(8,128)(2,1)S(1)} %bitcast.31), custom_call_target="tpu_custom_call" | custom-call | flops 4000000000 | bytes 12000000 | tf_op jit(solution)/shard_map/attention/pallas_call | solution.py:393
  175.6 0.8 collective-permute-start.8
  176.4 2.7 %collective-permute-start.12 = (bf16[64,2176]{1,0:T(8,128)(2,1)S(1)}, bf16[64,2176]{1,0:T(8,128)(2,1)S(1)}, u32[]{:S(2)}, u32[]{:S(2)}) collective-permute-start(bf16[64,2176]{1,0:T(8,128)(2,1)S(1)} %attention.1.refs_1_), channel_id=1, source_target_pairs={{0,131},{1,0},{2,1},{3,2},{128,3},{129,128},{130,129},{131,130},{4... | collective-permute-start | bytes 835592 | tf_op jit(solution)/shard_map/ppermute | solution.py:45
  179.1 4.6 %collective-permute-done.8.refs_2_ = bf16[64,2176]{1,0:T(8,128)(2,1)S(1)} collective-permute-done((bf16[64,2176]{1,0:T(8,128)(2,1)S(1)}, bf16[64,2176]{1,0:T(8,128)(2,1)S(1)}, u32[]{:S(2)}, u32[]{:S(2)}) %collective-permute-start.8) | collective-permute-done | bytes 278560 | tf_op jit(solution)/shard_map/ppermute | solution.py:45
  183.7 3.5 %collective-permute-start.13 = (bf16[64,2176]{1,0:T(8,128)(2,1)S(1)}, bf16[64,2176]{1,0:T(8,128)(2,1)S(1)}, u32[]{:S(2)}, u32[]{:S(2)}) collective-permute-start(bf16[64,2176]{1,0:T(8,128)(2,1)S(1)} %collective-permute-done.12.refs_3_), channel_id=1, source_target_pairs={{0,131},{1,0},{2,1},{3,2},{128,3},{129,128},{130,129},{131,130},{4... | collective-permute-start | bytes 835592 | tf_op jit(solution)/shard_map/ppermute | solution.py:45
  187.2 5.4 %collective-permute-done.9.refs_4_ = bf16[64,2176]{1,0:T(8,128)(2,1)S(1)} collective-permute-done((bf16[64,2176]{1,0:T(8,128)(2,1)S(1)}, bf16[64,2176]{1,0:T(8,128)(2,1)S(1)}, u32[]{:S(2)}, u32[]{:S(2)}) %collective-permute-start.9) | collective-permute-done | bytes 278560 | tf_op jit(solution)/shard_map/ppermute | solution.py:45
  192.6 0.1 collective-permute-done.13.refs_5_
  192.7 3.7 %collective-permute-start.14 = (bf16[64,2176]{1,0:T(8,128)(2,1)S(1)}, bf16[64,2176]{1,0:T(8,128)(2,1)S(1)}, u32[]{:S(2)}, u32[]{:S(2)}) collective-permute-start(bf16[64,2176]{1,0:T(8,128)(2,1)S(1)} %collective-permute-done.13.refs_5_), channel_id=1, source_target_pairs={{0,131},{1,0},{2,1},{3,2},{128,3},{129,128},{130,129},{131,130},{4... | collective-permute-start | bytes 835592 | tf_op jit(solution)/shard_map/ppermute | solution.py:45
  196.5 5.4 %collective-permute-done.10.refs_1_ = bf16[64,2176]{1,0:T(8,128)(2,1)S(1)} collective-permute-done((bf16[64,2176]{1,0:T(8,128)(2,1)S(1)}, bf16[64,2176]{1,0:T(8,128)(2,1)S(1)}, u32[]{:S(2)}, u32[]{:S(2)}) %collective-permute-start.10) | collective-permute-done | bytes 278560 | tf_op jit(solution)/shard_map/ppermute | solution.py:45
  202.0 0.7 slice.28
  202.6 3.7 %collective-permute-start.15 = (bf16[32,2176]{1,0:T(8,128)(2,1)}, bf16[32,2176]{1,0:T(8,128)(2,1)}, u32[]{:S(2)}, u32[]{:S(2)}) collective-permute-start(bf16[32,2176]{1,0:T(8,128)(2,1)} %slice.28), channel_id=1, source_target_pairs={{0,131},{1,0},{2,1},{3,2},{128,3},{129,128},{130,129},{131,130},{4... | collective-permute-start | bytes 417800 | tf_op jit(solution)/shard_map/ppermute | solution.py:45
  206.5 3.7 %copy-done.2 = bf16[4608,1024]{1,0:T(8,128)(2,1)S(1)} copy-done((bf16[4608,1024]{1,0:T(8,128)(2,1)S(1)}, bf16[4608,1024]{1,0:T(8,128)(2,1)}, u32[]{:S(2)}) %copy-start.2) | copy-done | bytes 9437208
  210.1 3.3 %finish.3.refs_6_ = bf16[448,512]{1,0:T(8,128)(2,1)} custom-call(s32[5]{0:T(128)S(1)} %stack.56.refs_0_, bf16[64,2176]{1,0:T(8,128)(2,1)S(1)} %attention.1.refs_1_, bf16[64,2176]{1,0:T(8,128)(2,1)S(1)} %collective-permute-done.8.refs_2_, bf16[64,2176]{1,0:T(8,128)(2,1)S(1)} %collective-permute-done.12.refs_3_, ...), custom_call_target="tpu_custom_call" | custom-call | flops 671088640 | bytes 4000000 | tf_op jit(solution)/shard_map/finish/pallas_call | solution.py:275
  213.4 2.9 %finish.4.refs_6_ = bf16[448,512]{1,0:T(8,128)(2,1)} custom-call(s32[2]{0:T(128)S(1)} %pad_add_fusion.1.refs_0_, bf16[64,2176]{1,0:T(8,128)(2,1)S(1)} %collective-permute-done.10.refs_1_, bf16[64,2176]{1,0:T(8,128)(2,1)S(1)} %collective-permute-done.14.refs_2_, bf16[448,512]{1,0:T(8,128)(2,1)S(1)} %copy-done.7, ...), custom_call_target="tpu_custom_call", output_to_operand_aliasing={{}: (6, {})} | custom-call | flops 268435456 | bytes 4000000 | tf_op jit(solution)/shard_map/finish/pallas_call | solution.py:275
  216.3 0.6 copy-done.18
  217.0 0.9 copy-done.19
  217.9 3.6 %finish.5 = bf16[448,512]{1,0:T(8,128)(2,1)} custom-call(s32[2]{0:T(128)S(1)} %pad_add_fusion.refs_0_, bf16[32,2176]{1,0:T(8,128)(2,1)S(1)} %copy-done.19, bf16[32,2176]{1,0:T(8,128)(2,1)} %collective-permute-done.15.refs_2_, bf16[448,512]{1,0:T(8,128)(2,1)S(1)} %copy-done.7, ...), custom_call_target="tpu_custom_call", output_to_operand_aliasing={{}: (6, {})} | custom-call | flops 134217728 | bytes 4000000 | tf_op jit(solution)/shard_map/finish/pallas_call | solution.py:275
  (60 shorter events, 0.8 us)
Async XLA Ops:
  6.5 43.5 %copy-start = (bf16[16,16,896]{2,1,0:T(8,128)(2,1)S(1)}, bf16[16,16,896]{2,1,0:T(8,128)(2,1)}, u32[]{:S(2)}) copy-start(bf16[16,16,896]{2,1,0:T(8,128)(2,1)} %param.19) | copy-start | bytes 1376260
  6.5 151.7 %all-gather.2.cloned.1.call-start = ((), (), s32[]{:S(2)}) async-start(), calls=%async_computation.5 | async-start | bytes 9732096 | tf_op jit(solution)/shard_map/all_gather | solution.py:329
  32.7 25.3 %collective-permute-start = (bf16[896,512]{1,0:T(8,128)(2,1)S(1)}, bf16[896,512]{1,0:T(8,128)(2,1)S(1)}, u32[]{:S(2)}, u32[]{:S(2)}) collective-permute-start(bf16[896,512]{1,0:T(8,128)(2,1)S(1)} %pad_maximum_fusion.refs_0_), channel_id=1, source_target_pairs={{0,1},{1,2},{2,3},{3,128},{128,129},{129,130},{130,131},{131,0},{4... | collective-permute-start | bytes 2752520 | tf_op jit(solution)/shard_map/ppermute | solution.py:45
  33.4 25.7 %collective-permute-start.4 = (bf16[896,512]{1,0:T(8,128)(2,1)S(1)}, bf16[896,512]{1,0:T(8,128)(2,1)S(1)}, u32[]{:S(2)}, u32[]{:S(2)}) collective-permute-start(bf16[896,512]{1,0:T(8,128)(2,1)S(1)} %pad_maximum_fusion.refs_0_), channel_id=1, source_target_pairs={{0,131},{1,0},{2,1},{3,2},{128,3},{129,128},{130,129},{131,130},{4... | collective-permute-start | bytes 2752520 | tf_op jit(solution)/shard_map/ppermute | solution.py:45
  52.1 33.6 %copy-start.21 = (s32[7,1]{0,1:T(1,128)S(1)}, s32[7,1]{0,1:T(1,128)}, u32[]{:S(2)}) copy-start(s32[7,1]{0,1:T(1,128)} %param.21) | copy-start | bytes 88
  52.1 43.4 %all-to-all-start.1 = ((bf16[32,32,896]{2,1,0:T(8,128)(2,1)}), bf16[32,32,896]{2,1,0:T(8,128)(2,1)}, u32[]{:S(2)}, u32[]{:S(2)}) async-start(bf16[32,32,896]{2,1,0:T(8,128)(2,1)} %bitcast.36), calls=%async_computation.1 | async-start | bytes 3670016 | tf_op jit(solution)/shard_map/all_to_all | solution.py:64
  58.0 23.8 %collective-permute-start.1 = (bf16[896,512]{1,0:T(8,128)(2,1)S(1)}, bf16[896,512]{1,0:T(8,128)(2,1)}, u32[]{:S(2)}, u32[]{:S(2)}) collective-permute-start(bf16[896,512]{1,0:T(8,128)(2,1)S(1)} %collective-permute-done.refs_1_), channel_id=1, source_target_pairs={{0,1},{1,2},{2,3},{3,128},{128,129},{129,130},{130,131},{131,0},{4... | collective-permute-start | bytes 2752520 | tf_op jit(solution)/shard_map/ppermute | solution.py:45
  58.1 0.9 copy-start.13
  59.1 22.9 %collective-permute-start.5 = (bf16[896,512]{1,0:T(8,128)(2,1)S(1)}, bf16[896,512]{1,0:T(8,128)(2,1)}, u32[]{:S(2)}, u32[]{:S(2)}) collective-permute-start(bf16[896,512]{1,0:T(8,128)(2,1)S(1)} %collective-permute-done.4.refs_2_), channel_id=1, source_target_pairs={{0,131},{1,0},{2,1},{3,2},{128,3},{129,128},{130,129},{131,130},{4... | collective-permute-start | bytes 2752520 | tf_op jit(solution)/shard_map/ppermute | solution.py:45
  62.3 0.9 copy-start.15
  81.8 23.0 %collective-permute-start.2 = (bf16[896,512]{1,0:T(8,128)(2,1)}, bf16[896,512]{1,0:T(8,128)(2,1)S(1)}, u32[]{:S(2)}, u32[]{:S(2)}) collective-permute-start(bf16[896,512]{1,0:T(8,128)(2,1)} %collective-permute-done.1.refs_3_), channel_id=1, source_target_pairs={{0,1},{1,2},{2,3},{3,128},{128,129},{129,130},{130,131},{131,0},{4... | collective-permute-start | bytes 2752520 | tf_op jit(solution)/shard_map/ppermute | solution.py:45
  81.9 25.0 %collective-permute-start.6 = (bf16[896,512]{1,0:T(8,128)(2,1)}, bf16[896,512]{1,0:T(8,128)(2,1)S(1)}, u32[]{:S(2)}, u32[]{:S(2)}) collective-permute-start(bf16[896,512]{1,0:T(8,128)(2,1)} %collective-permute-done.5.refs_4_), channel_id=1, source_target_pairs={{0,131},{1,0},{2,1},{3,2},{128,3},{129,128},{130,129},{131,130},{4... | collective-permute-start | bytes 2752520 | tf_op jit(solution)/shard_map/ppermute | solution.py:45
  98.3 35.2 %all-to-all-start.2 = ((bf16[8,32,896]{2,1,0:T(8,128)(2,1)}), bf16[8,32,896]{2,1,0:T(8,128)(2,1)}, u32[]{:S(2)}, u32[]{:S(2)}) async-start(bf16[8,32,896]{2,1,0:T(8,128)(2,1)} %gather_fusion.1), calls=%async_computation.2 | async-start | bytes 917504 | tf_op jit(solution)/shard_map/all_to_all | solution.py:64
  104.8 7.7 %copy-start.8 = (bf16[896,512]{1,0:T(8,128)(2,1)}, bf16[896,512]{1,0:T(8,128)(2,1)S(1)}, u32[]{:S(2)}) copy-start(bf16[896,512]{1,0:T(8,128)(2,1)S(1)} %collective-permute-done.2.refs_5_) | copy-start | bytes 2752516
  105.7 24.7 %collective-permute-start.3 = (bf16[448,512]{1,0:T(8,128)(2,1)}, bf16[448,512]{1,0:T(8,128)(2,1)}, u32[]{:S(2)}, u32[]{:S(2)}) collective-permute-start(bf16[448,512]{1,0:T(8,128)(2,1)} %slice.25), channel_id=1, source_target_pairs={{0,1},{1,2},{2,3},{3,128},{128,129},{129,130},{130,131},{131,0},{4... | collective-permute-start | bytes 1376264 | tf_op jit(solution)/shard_map/ppermute | solution.py:45
  106.9 5.6 %copy-start.10 = (bf16[896,512]{1,0:T(8,128)(2,1)}, bf16[896,512]{1,0:T(8,128)(2,1)S(1)}, u32[]{:S(2)}) copy-start(bf16[896,512]{1,0:T(8,128)(2,1)S(1)} %collective-permute-done.6.refs_6_) | copy-start | bytes 2752516
  107.7 22.7 %collective-permute-start.7 = (bf16[448,512]{1,0:T(8,128)(2,1)}, bf16[448,512]{1,0:T(8,128)(2,1)}, u32[]{:S(2)}, u32[]{:S(2)}) collective-permute-start(bf16[448,512]{1,0:T(8,128)(2,1)} %slice.26), channel_id=1, source_target_pairs={{0,131},{1,0},{2,1},{3,2},{128,3},{129,128},{130,129},{131,130},{4... | collective-permute-start | bytes 1376264 | tf_op jit(solution)/shard_map/ppermute | solution.py:45
  115.9 1.6 copy-start.3
  117.5 1.6 copy-start.5
  119.0 1.2 copy-start.9
  120.2 1.2 copy-start.11
  121.4 1.2 copy-start.14
  122.6 1.2 copy-start.16
  123.8 6.7 %copy-start.4 = (bf16[4096,256]{1,0:T(8,128)(2,1)S(1)}, bf16[4096,256]{1,0:T(8,128)(2,1)}, u32[]{:S(2)}) copy-start(bf16[4096,256]{1,0:T(8,128)(2,1)} %query_hbm.1) | copy-start | bytes 6291460
  123.8 6.7 %copy-start.6 = (bf16[256,4096]{1,0:T(8,128)(2,1)S(1)}, bf16[256,4096]{1,0:T(8,128)(2,1)}, u32[]{:S(2)}) copy-start(bf16[256,4096]{1,0:T(8,128)(2,1)} %out_hbm.1) | copy-start | bytes 6291460
  132.7 0.9 copy-start.17
  133.6 24.7 %all-to-all-start.3 = ((bf16[8,64,768]{2,1,0:T(8,128)(2,1)}), bf16[8,64,768]{2,1,0:T(8,128)(2,1)S(1)}, u32[]{:S(2)}, u32[]{:S(2)}) async-start(bf16[8,64,768]{2,1,0:T(8,128)(2,1)} %copy-done.17), calls=%async_computation.3 | async-start | bytes 1572864 | tf_op jit(solution)/shard_map/all_to_all | solution.py:64
  137.2 1.4 copy-start.12
  158.3 3.7 %copy-start.1 = (bf16[4608,1024]{1,0:T(8,128)(2,1)S(1)}, bf16[4608,1024]{1,0:T(8,128)(2,1)}, u32[]{:S(2)}) copy-start(bf16[4608,1024]{1,0:T(8,128)(2,1)} %all-gather.2.cloned.1.call-done) | copy-start | bytes 28311556
  162.0 1.4 copy-start.20
  163.4 43.1 %copy-start.7 = (bf16[448,512]{1,0:T(8,128)(2,1)S(1)}, bf16[448,512]{1,0:T(8,128)(2,1)}, u32[]{:S(2)}) copy-start(bf16[448,512]{1,0:T(8,128)(2,1)} %refs_3_.3) | copy-start | bytes 1376260
  175.6 8.1 %collective-permute-start.8 = (bf16[64,2176]{1,0:T(8,128)(2,1)S(1)}, bf16[64,2176]{1,0:T(8,128)(2,1)S(1)}, u32[]{:S(2)}, u32[]{:S(2)}) collective-permute-start(bf16[64,2176]{1,0:T(8,128)(2,1)S(1)} %attention.1.refs_1_), channel_id=1, source_target_pairs={{0,1},{1,2},{2,3},{3,128},{128,129},{129,130},{130,131},{131,0},{4... | collective-permute-start | bytes 835592 | tf_op jit(solution)/shard_map/ppermute | solution.py:45
  176.4 7.3 %collective-permute-start.12 = (bf16[64,2176]{1,0:T(8,128)(2,1)S(1)}, bf16[64,2176]{1,0:T(8,128)(2,1)S(1)}, u32[]{:S(2)}, u32[]{:S(2)}) collective-permute-start(bf16[64,2176]{1,0:T(8,128)(2,1)S(1)} %attention.1.refs_1_), channel_id=1, source_target_pairs={{0,131},{1,0},{2,1},{3,2},{128,3},{129,128},{130,129},{131,130},{4... | collective-permute-start | bytes 835592 | tf_op jit(solution)/shard_map/ppermute | solution.py:45
  183.7 8.9 %collective-permute-start.9 = (bf16[64,2176]{1,0:T(8,128)(2,1)S(1)}, bf16[64,2176]{1,0:T(8,128)(2,1)S(1)}, u32[]{:S(2)}, u32[]{:S(2)}) collective-permute-start(bf16[64,2176]{1,0:T(8,128)(2,1)S(1)} %collective-permute-done.8.refs_2_), channel_id=1, source_target_pairs={{0,1},{1,2},{2,3},{3,128},{128,129},{129,130},{130,131},{131,0},{4... | collective-permute-start | bytes 835592 | tf_op jit(solution)/shard_map/ppermute | solution.py:45
  183.7 9.0 %collective-permute-start.13 = (bf16[64,2176]{1,0:T(8,128)(2,1)S(1)}, bf16[64,2176]{1,0:T(8,128)(2,1)S(1)}, u32[]{:S(2)}, u32[]{:S(2)}) collective-permute-start(bf16[64,2176]{1,0:T(8,128)(2,1)S(1)} %collective-permute-done.12.refs_3_), channel_id=1, source_target_pairs={{0,131},{1,0},{2,1},{3,2},{128,3},{129,128},{130,129},{131,130},{4... | collective-permute-start | bytes 835592 | tf_op jit(solution)/shard_map/ppermute | solution.py:45
  192.6 9.3 %collective-permute-start.10 = (bf16[64,2176]{1,0:T(8,128)(2,1)S(1)}, bf16[64,2176]{1,0:T(8,128)(2,1)S(1)}, u32[]{:S(2)}, u32[]{:S(2)}) collective-permute-start(bf16[64,2176]{1,0:T(8,128)(2,1)S(1)} %collective-permute-done.9.refs_4_), channel_id=1, source_target_pairs={{0,1},{1,2},{2,3},{3,128},{128,129},{129,130},{130,131},{131,0},{4... | collective-permute-start | bytes 835592 | tf_op jit(solution)/shard_map/ppermute | solution.py:45
  192.7 9.3 %collective-permute-start.14 = (bf16[64,2176]{1,0:T(8,128)(2,1)S(1)}, bf16[64,2176]{1,0:T(8,128)(2,1)S(1)}, u32[]{:S(2)}, u32[]{:S(2)}) collective-permute-start(bf16[64,2176]{1,0:T(8,128)(2,1)S(1)} %collective-permute-done.13.refs_5_), channel_id=1, source_target_pairs={{0,131},{1,0},{2,1},{3,2},{128,3},{129,128},{130,129},{131,130},{4... | collective-permute-start | bytes 835592 | tf_op jit(solution)/shard_map/ppermute | solution.py:45
  201.9 14.5 %collective-permute-start.11 = (bf16[32,2176]{1,0:T(8,128)(2,1)S(1)}, bf16[32,2176]{1,0:T(8,128)(2,1)S(1)}, u32[]{:S(2)}, u32[]{:S(2)}) collective-permute-start(bf16[32,2176]{1,0:T(8,128)(2,1)S(1)} %slice.27), channel_id=1, source_target_pairs={{0,1},{1,2},{2,3},{3,128},{128,129},{129,130},{130,131},{131,0},{4... | collective-permute-start | bytes 417800 | tf_op jit(solution)/shard_map/ppermute | solution.py:45
  202.6 14.4 %collective-permute-start.15 = (bf16[32,2176]{1,0:T(8,128)(2,1)}, bf16[32,2176]{1,0:T(8,128)(2,1)}, u32[]{:S(2)}, u32[]{:S(2)}) collective-permute-start(bf16[32,2176]{1,0:T(8,128)(2,1)} %slice.28), channel_id=1, source_target_pairs={{0,131},{1,0},{2,1},{3,2},{128,3},{129,128},{130,129},{131,130},{4... | collective-permute-start | bytes 417800 | tf_op jit(solution)/shard_map/ppermute | solution.py:45
  206.5 3.7 %copy-start.2 = (bf16[4608,1024]{1,0:T(8,128)(2,1)S(1)}, bf16[4608,1024]{1,0:T(8,128)(2,1)}, u32[]{:S(2)}) copy-start(bf16[4608,1024]{1,0:T(8,128)(2,1)} %all-gather.2.cloned.1.call-done) | copy-start | bytes 28311556
  216.3 0.7 copy-start.18
  217.0 0.9 copy-start.19
Sparse Core Ops, SparseCore 0:
  32.8 69.5 all-gather.1
where the time goes:
time: 232 us; the launch traced here: 228 us
  waiting for transfers between devices  65.1 us (28%)
  starting transfers between devices  43.3 us (19%)
  local copies, waits for them, and re-layouts  36.8 us (16%)
  blocking collectives  34.4 us (15%)
  Pallas kernels  32.7 us (14%)
  between operations  13.8 us (6%)
  other arithmetic  2.33 us (1%)
    ppermute x16, waiting for transfers between devices, shift(): return lax.ppermute(x, Z, [(i, (i + by) % NZ) for i in range(NZ)])  37.7 us
    all_to_all x2, blocking collectives, exchange(): return lax.all_to_all(x, axis, split_axis=0, concat_axis=0, tiled=True)  34.4 us
    ppermute x16, starting transfers between devices, shift(): return lax.ppermute(x, Z, [(i, (i + by) % NZ) for i in range(NZ)])  29.7 us
    all_to_all x3, waiting for transfers between devices, exchange(): return lax.all_to_all(x, axis, split_axis=0, concat_axis=0, tiled=True)  27.4 us
    unnamed x46, local copies, waits for them, and re-layouts  26.4 us
    all_to_all x3, starting transfers between devices, exchange(): return lax.all_to_all(x, axis, split_axis=0, concat_axis=0, tiled=True)  13.6 us
    pallas_call x1, Pallas kernels, shards(): pl.pallas_call(attention, out_shape=jax.ShapeDtypeStruct((SEG, 2 * HALF +...  12.2 us
    pallas_call x3, Pallas kernels, finish_call(): pl.pallas_call(functools.partial(finish, starts, first), out_shape=jax.Sh...  9.72 us
  transfers between devices with their start and end apart: 20, of which 10 were waited for; matrix products, arithmetic and copies ran while one was open for 5% of the time, Pallas kernels for 7%

commit v1 on v0

--- a/solution.py
+++ b/solution.py
@@ -26,7 +26,9 @@
 Z = ("group", "tensor")
 BF = jnp.bfloat16
 F32 = jnp.float32
-PARAMS = pltpu.CompilerParams(vmem_limit_bytes=40 * 1024 * 1024)
+MIB = 1024 * 1024
+PARAMS = pltpu.CompilerParams(vmem_limit_bytes=20 * MIB)
+HBM = pl.BlockSpec(memory_space=pltpu.HBM)
 VMEM = pl.BlockSpec(memory_space=pltpu.VMEM)
 SMEM = pl.BlockSpec(memory_space=pltpu.SMEM)
 ANY = pl.BlockSpec(memory_space=pl.ANY)
@@ -47,17 +49,6 @@
 
 def tie(*arrays):
     return lax.optimization_barrier(arrays)
-
-
-def ring(x):
-    rows = x.shape[0] // 2
-    chunks = [(x, 0)]
-    right = left = x
-    for step in range(1, 4):
-        right, left = shift(right, 1), shift(left, -1)
-        chunks += [(right, -step), (left, step)]
-    far = (shift(right[:rows], 1), shift(left[rows:], -1))
-    return chunks, far
 
 
 def exchange(x, axis):
@@ -94,45 +85,81 @@
     out_ref[...] = dot(normed, weight_ref[...]).astype(BF)
 
 
-def project(count, index_ref, *refs):
-    chunks_hbm, refs = refs[:count], refs[count:]
-    query_hbm, cond_hbm, out_hbm, acc_ref, squares_ref = refs[:5]
-    chunk_ref, query_ref, cond_ref, out_weight_ref, sem = refs[5:]
+def project(count, first, index_ref, *refs):
+    hiddens_hbm, cots_hbm, refs = refs[:count], refs[count : 2 * count], refs[2 * count :]
+    query_hbm, cond_hbm, out_hbm = refs[:3]
+    if not first:
+        old_acc_ref, old_squares_ref = refs[3:5]
+    acc_ref, squares_ref = refs[3 if first else 5 :][:2]
+    hidden_ref, cot_ref, query_ref, cond_ref, out_weight_ref, sem = refs[-6:]
     copies = []
     for k in range(count):
         at = pl.ds(pl.multiple_of(index_ref[k] * FEAT, FEAT), FEAT)
         copies.append(
             start(
                 [
-                    (chunks_hbm[k], chunk_ref.at[k]), (query_hbm.at[at], query_ref.at[k]),
-                    (cond_hbm.at[at], cond_ref.at[k]), (out_hbm.at[:, at], out_weight_ref.at[k]),
+                    (hiddens_hbm[k], hidden_ref.at[k]), (query_hbm.at[at], query_ref.at[k]),
+                    (cond_hbm.at[:, at], cond_ref.at[k]), (cots_hbm[k], cot_ref.at[k]),
+                    (out_hbm.at[:, at], out_weight_ref.at[k]),
                 ], sem.at[k],
             )
         )
     for k in range(count):
         wait(copies[k])
-        chunk = chunk_ref[k, :TOK]
+        chunk = hidden_ref[k]
         squares = jnp.sum(jnp.square(chunk.astype(F32)), axis=-1, keepdims=True)
         parts = (
             dot(chunk, query_ref[k]),
-            dot_nt(chunk_ref[k, TOK:], out_weight_ref[k]),
-            dot(chunk, cond_ref[k]),
+            dot_nt(cot_ref[k], out_weight_ref[k]),
+            dot_nt(chunk, cond_ref[k]),
         )
+        source, source_squares = acc_ref, squares_ref
+        if k == 0 and not first:
+            source, source_squares = old_acc_ref, old_squares_ref
+        fresh = first and k == 0
         for columns, part in zip((slice(0, 256), slice(256, 512), slice(512, 736)), parts):
-            acc_ref[:, columns] = part if k == 0 else acc_ref[:, columns] + part
-        squares_ref[...] = squares if k == 0 else squares_ref[...] + squares
+            acc_ref[:, columns] = part if fresh else source[:, columns] + part
+        squares_ref[...] = squares if fresh else source_squares[...] + squares
+
+
+def project_call(hiddens, cots, index, weights, before):
+    count, first = len(hiddens), before is None
+    before = () if first else before
+    results = (
+        jax.ShapeDtypeStruct((TOK, 768), F32),
+        jax.ShapeDtypeStruct((TOK, 1), F32),
+    )
+    at = 1 + 2 * count + 3
+    return pl.pallas_call(
+        functools.partial(project, count, first),
+        out_shape=results,
+        in_specs=[SMEM] + [ANY] * (2 * count) + [HBM] * 3 + [VMEM] * len(before),
+        out_specs=(VMEM, VMEM),
+        scratch_shapes=[
+            pltpu.VMEM((count, TOK, FEAT), BF),
+            pltpu.VMEM((count, TOK, FEAT), BF),
+            pltpu.VMEM((count, FEAT, 256), BF),
+            pltpu.VMEM((count, 224, FEAT), BF),
+            pltpu.VMEM((count, 256, FEAT), BF),
+            pltpu.SemaphoreType.DMA((count, 5)),
+        ],
+        input_output_aliases={} if first else {at: 0, at + 1: 1},
+        compiler_params=PARAMS,
+        cost_estimate=cost(2 * count * TOK * FEAT * 736, 6_000_000),
+        name="project",
+    )(jnp.stack(index), *hiddens, *cots, *weights, *before)
 
 
 def project_last(
-    index_ref, hidden_hbm, cot_hbm, acc_hbm, squares_hbm, query_hbm, cond_hbm, out_hbm,
+    index_ref, hidden_hbm, cot_hbm, acc_ref, squares_ref, query_hbm, cond_hbm, out_hbm,
     sent_ref, inverse_ref,
-    hidden_ref, cot_ref, acc_ref, squares_ref, query_ref, cond_ref, out_weight_ref, sem,
+    hidden_ref, cot_ref, query_ref, cond_ref, out_weight_ref, sem,
 ):
     at = pl.ds(pl.multiple_of(index_ref[0] * FEAT, FEAT), FEAT)
     copies = start(
         [
-            (hidden_hbm, hidden_ref), (squares_hbm, squares_ref), (acc_hbm, acc_ref),
-            (query_hbm.at[at], query_ref), (cond_hbm.at[at], cond_ref),
+            (hidden_hbm, hidden_ref),
+            (query_hbm.at[at], query_ref), (cond_hbm.at[:, at], cond_ref),
             (cot_hbm, cot_ref), (out_hbm.at[:, at], out_weight_ref),
         ], sem,
     )
@@ -145,7 +172,7 @@
     inverse_ref[...] = inverse
     queries = (acc_ref[:, :256] + dot(chunk, query_ref[...])) * inverse
     grads = acc_ref[:, 256:512] + dot_nt(cot_ref[...], out_weight_ref[...])
-    condition = (acc_ref[:, 512:736] + dot(chunk, cond_ref[...])) * inverse
+    condition = (acc_ref[:, 512:736] + dot_nt(chunk, cond_ref[...])) * inverse
     for columns, part in (
         (slice(0, 256), queries), (slice(256, 512), grads), (slice(512, 736), condition)
     ):
@@ -166,7 +193,7 @@
     )
     large = [
         pltpu.make_async_copy(
-            weights_hbm.at[:, j, pl.ds(0, 112), :], kv_ref.at[j], sem.at[4 + j]
+            weights_hbm.at[:, j], kv_ref.at[j], sem.at[4 + j]
         )
         for j in range(2)
     ]
@@ -232,7 +259,7 @@
         places.append((source < SEGS, pl.ds(pl.multiple_of(at, 32), rows)))
     loads = [(inverse_hbm, inverse_ref)]
     loads += [
-        (weights_hbm.at[:, pl.ds(112 + 16 * j, 16), :], weight_ref.at[j]) for j in range(2)
+        (weights_hbm.at[:, j], weight_ref.at[j]) for j in range(2)
     ]
     for k in range(count):
         loads.append((chunks_hbm[k], chunk_refs[k]))
@@ -275,8 +302,8 @@
     return pl.pallas_call(
         functools.partial(finish, starts, first),
         out_shape=jax.ShapeDtypeStruct((TOK, FEAT), BF),
-        in_specs=[SMEM] + [ANY] * (len(operands) - 1),
-        out_specs=ANY,
+        in_specs=[SMEM] + [ANY] * (len(chunks) + 2) + [HBM] * (1 if first else 2),
+        out_specs=HBM,
         scratch_shapes=[like(c) for c in chunks]
         + [pltpu.VMEM((r, FEAT), BF) for r in rows] * 2
         + [
@@ -321,18 +348,35 @@
     )
     q_part = q_part.reshape(NZ, 16, 2, HEAD).transpose(0, 2, 1, 3).reshape(NZ, 32, HEAD)
     part = jnp.concatenate([jnp.broadcast_to(kv_part, (NZ, 112, HEAD)), q_part], axis=1)
-    both = jnp.concatenate([hidden, cotangent], axis=0)
-
-    wanted, part, both = tie(wanted, part, both)
+
+    projections = (query_weight, condition_weight.T, out_weight)
+    right = left = hidden
+    grad_right = grad_left = cotangent
+    acc = project_call([hidden], [cotangent], [me], projections, None)
+    for step in range(1, 4):
+        right, left = shift(right, 1), shift(left, -1)
+        if step == 1:
+            wanted, part, right, left = tie(wanted, part, right, left)
+        else:
+            right, left, _, _ = tie(right, left, grad_right, grad_left)
+        grad_right, grad_left = shift(grad_right, 1), shift(grad_left, -1)
+        grad_right, grad_left, right, left, *acc = tie(grad_right, grad_left, right, left, *acc)
+        index = [(me - step) % NZ, (me + step) % NZ]
+        acc = project_call([right, left], [grad_right, grad_left], index, projections, acc)
+    far = (shift(right, 1), shift(grad_left, -1))
+    acc, squares = acc
+
     asked = exchange(wanted, "dp")
     part = exchange(part, Z).transpose(1, 0, 2).reshape(144, HALF)
-    weights = lax.all_gather(part, "dp", axis=0, tiled=True).reshape(16, 2, 144, HALF)
+    kv_weights = lax.all_gather(part[:112], "dp", axis=0, tiled=True).reshape(16, 2, 112, HALF)
+    q_rows, _ = tie(part[112:], right)
+    q_weights = lax.all_gather(q_rows, "dp", axis=0, tiled=True).reshape(NDP, 2, 16, HALF)
     returned = exchange(database[asked].reshape(NDP, NEIGH * NLEN // NZ, DE), "dp")
     fetched = exchange(returned[jnp.concatenate([owner, owner[:1]])], Z).reshape(KEYS, DE)
     enc_q = pl.pallas_call(
         encoder_queries,
         out_shape=jax.ShapeDtypeStruct((KEYS, DE), BF),
-        in_specs=[ANY, ANY],
+        in_specs=[HBM, HBM],
         out_specs=VMEM,
         scratch_shapes=[like(fetched), like(encoder_query), pltpu.SemaphoreType.DMA((2,))],
         compiler_params=PARAMS,
@@ -340,64 +384,38 @@
         name="encoder_queries",
     )(fetched, encoder_query)
 
-    chunks, far = ring(both)
-    index = jnp.stack([(me + offset) % NZ for _, offset in chunks])
-    chunks = [c for c, _ in chunks]
-    count = len(chunks)
-    acc, squares = pl.pallas_call(
-        functools.partial(project, count),
-        out_shape=(
-            jax.ShapeDtypeStruct((TOK, 768), F32),
-            jax.ShapeDtypeStruct((TOK, 1), F32),
-        ),
-        in_specs=[SMEM] + [ANY] * (count + 3),
-        out_specs=(VMEM, VMEM),
-        scratch_shapes=[
-            pltpu.VMEM((count, 2 * TOK, FEAT), BF),
-            pltpu.VMEM((count, FEAT, 256), BF),
-            pltpu.VMEM((count, FEAT, 224), BF),
-            pltpu.VMEM((count, 256, FEAT), BF),
-            pltpu.SemaphoreType.DMA((count, 4)),
-        ],
-        compiler_params=PARAMS,
-        cost_estimate=cost(2 * count * TOK * FEAT * 736, 16_000_000),
-        name="project",
-    )(index, *chunks, query_weight, condition_weight, out_weight)
     sent, inverse = pl.pallas_call(
         project_last,
         out_shape=(
             jax.ShapeDtypeStruct((NZ, SEG, 768), BF),
             jax.ShapeDtypeStruct((TOK, 1), F32),
         ),
-        in_specs=[SMEM] + [ANY] * 7,
+        in_specs=[SMEM] + [ANY] * 2 + [VMEM] * 2 + [HBM] * 3,
         out_specs=(VMEM, VMEM),
         scratch_shapes=[
             pltpu.VMEM((TOK, FEAT), BF),
             pltpu.VMEM((TOK, FEAT), BF),
-            like(acc),
-            like(squares),
             pltpu.VMEM((FEAT, 256), BF),
-            pltpu.VMEM((FEAT, 224), BF),
+            pltpu.VMEM((224, FEAT), BF),
             pltpu.VMEM((256, FEAT), BF),
-            pltpu.SemaphoreType.DMA((7,)),
+            pltpu.SemaphoreType.DMA((5,)),
         ],
         compiler_params=PARAMS,
         cost_estimate=cost(2 * TOK * FEAT * 736, 4_000_000),
         name="project_last",
     )(
-        jnp.stack([(me + 4) % NZ]), far[0], far[1], acc, squares,
-        query_weight, condition_weight, out_weight,
+        jnp.stack([(me + 4) % NZ]), far[0], far[1], acc, squares, *projections
     )
     got = exchange(sent, Z)
     operands = (fetched, enc_q, got, encoder_out)
     grad_query = pl.pallas_call(
         attention,
         out_shape=jax.ShapeDtypeStruct((SEG, 2 * HALF + HEAD), BF),
-        in_specs=[ANY] * 5,
+        in_specs=[HBM, ANY, HBM, HBM, HBM],
         out_specs=VMEM,
         scratch_shapes=[like(x) for x in operands]
         + [
-            pltpu.VMEM((2, 16, 112, HALF), BF),
+            like(kv_weights.transpose(1, 0, 2, 3)),
             pltpu.VMEM((2, KEYS, HALF), BF),
             pltpu.VMEM((2, KEYS, HALF), BF),
             pltpu.VMEM((KEYS, DE), BF),
@@ -406,18 +424,23 @@
         compiler_params=PARAMS,
         cost_estimate=cost(4_000_000_000, 12_000_000),
         name="attention",
-    )(*operands, weights)
-
-    chunks, far = ring(grad_query)
-    out = None
-    for group in (chunks[:5], chunks[5:7], [(far[0], 4), (far[1], 4)]):
-        sources = jnp.stack([(me + offset) % NZ for _, offset in group])
-        group = [c for c, _ in group]
+    )(*operands, kv_weights)
+
+    def finished(group, offsets, out):
+        sources = jnp.stack([(me + offset) % NZ for offset in offsets])
         starts = (0, SEG // 2) if group[0].shape[0] < SEG else (0,) * len(group)
-        out = finish_call(
-            group, starts, sources, hidden, inverse, weights.reshape(NDP, 144, HALF), out
-        )
-    return out
+        return finish_call(group, starts, sources, hidden, inverse, q_weights, out)
+
+    right = left = grad_query
+    group, offsets, out = [grad_query], [0], None
+    for step in range(1, 4):
+        right, left = shift(right, 1), shift(left, -1)
+        out = finished(group, offsets, out)
+        group, offsets = [right, left], [-step, step]
+        right, left, out = tie(right, left, out)
+    far = [shift(right[: SEG // 2], 1), shift(left[SEG // 2 :], -1)]
+    out = finished(group, offsets, out)
+    return finished(far, (4, 4), out)
 
 
 def solution(mesh):

time: 232 us -> 239 us (1.030)
  starting transfers between devices: 43.3 us -> 65.6 us
  blocking collectives: 34.4 us -> 17.1 us
  waiting for transfers between devices: 65.1 us -> 52.5 us
  Pallas kernels: 32.7 us -> 42.5 us
  local copies, waits for them, and re-layouts: 36.8 us -> 44.9 us
    all_to_all x2 -> x1, blocking collectives: 34.4 us -> 17.1 us  [exchange(): return lax.all_to_all(x, axis, split_axis=0, concat_axis=0, tiled=True)]
    all_to_all x3 -> x4, starting transfers between devices: 13.6 us -> 26.7 us  [exchange(): return lax.all_to_all(x, axis, split_axis=0, concat_axis=0, tiled=True)]
    ppermute x16 -> x22, starting transfers between devices: 29.7 us -> 38.9 us  [shift(): return lax.ppermute(x, Z, [(i, (i + by) % NZ) for i in range(NZ)])]
    unnamed x46 -> x61, local copies, waits for them, and re-layouts: 26.4 us -> 33.8 us
    all_to_all x3 -> x4, waiting for transfers between devices: 27.4 us -> 20.5 us  [exchange(): return lax.all_to_all(x, axis, split_axis=0, concat_axis=0, tiled=True)]
    ppermute x16 -> x22, waiting for transfers between devices: 37.7 us -> 31.9 us  [shift(): return lax.ppermute(x, Z, [(i, (i + by) % NZ) for i in range(NZ)])]
    pallas_call x3 -> x5, Pallas kernels: 9.72 us -> 15.3 us  [finish_call(): pl.pallas_call(functools.partial(finish, starts, first), out_shape=jax.Sh...]
    pallas_call x1 -> x4, Pallas kernels: 6.68 us -> 10.7 us  [project_call(): pl.pallas_call(functools.partial(project, count, first), out_shape=result...]
  transfers between devices with their start and end apart: 20 -> 28, of which waited for: 10 -> 9; matrix products, arithmetic and copies ran while one was open for 5% -> 5% of each run, Pallas kernels for 7% -> 17%
where the time goes in v1:
time: 239 us; the launch traced here: 238 us
  starting transfers between devices  65.6 us (27%)
  waiting for transfers between devices  52.5 us (22%)
  local copies, waits for them, and re-layouts  44.9 us (19%)
  Pallas kernels  42.5 us (18%)
  blocking collectives  17.1 us (7%)
  between operations  13.7 us (6%)
    ppermute x22, starting transfers between devices, shift(): return lax.ppermute(x, Z, [(i, (i + by) % NZ) for i in range(NZ)])  38.9 us
    unnamed x61, local copies, waits for them, and re-layouts  33.8 us
    ppermute x22, waiting for transfers between devices, shift(): return lax.ppermute(x, Z, [(i, (i + by) % NZ) for i in range(NZ)])  31.9 us
    all_to_all x4, starting transfers between devices, exchange(): return lax.all_to_all(x, axis, split_axis=0, concat_axis=0, tiled=True)  26.7 us
    all_to_all x4, waiting for transfers between devices, exchange(): return lax.all_to_all(x, axis, split_axis=0, concat_axis=0, tiled=True)  20.5 us
    all_to_all x1, blocking collectives, exchange(): return lax.all_to_all(x, axis, split_axis=0, concat_axis=0, tiled=True)  17.1 us
    pallas_call x5, Pallas kernels, finish_call(): pl.pallas_call(functools.partial(finish, starts, first), out_shape=jax.Sh...  15.3 us
    pallas_call x1, Pallas kernels, shards(): pl.pallas_call(attention, out_shape=jax.ShapeDtypeStruct((SEG, 2 * HALF +...  12.9 us
  transfers between devices with their start and end apart: 28, of which 9 were waited for; matrix products, arithmetic and copies ran while one was open for 5% of the time, Pallas kernels for 17%

profile of v1, /device:TPU:2, one launch (start us, length us, event | category | flops | bytes accessed | tf_op | source)
XLA Modules:
  0.0 237.5 jit_solution(13051295997501764927)
XLA Ops:
  6.5 2.0 collective-permute-start
  8.5 4.0 %collective-permute-start.1 = (bf16[448,512]{1,0:T(8,128)(2,1)}, bf16[448,512]{1,0:T(8,128)(2,1)S(1)}, u32[]{:S(2)}, u32[]{:S(2)}) collective-permute-start(bf16[448,512]{1,0:T(8,128)(2,1)} %refs_3_.7), channel_id=1, source_target_pairs={{0,131},{1,0},{2,1},{3,2},{128,3},{129,128},{130,129},{131,130},{4... | collective-permute-start | bytes 1376264 | tf_op jit(solution)/shard_map/ppermute | solution.py:47
  17.3 6.0 %collective-permute-done.refs_0_ = bf16[448,512]{1,0:T(8,128)(2,1)} collective-permute-done((bf16[448,512]{1,0:T(8,128)(2,1)}, bf16[448,512]{1,0:T(8,128)(2,1)}, u32[]{:S(2)}, u32[]{:S(2)}) %collective-permute-start) | collective-permute-done | bytes 458784 | tf_op jit(solution)/shard_map/ppermute | solution.py:47
  23.3 17.1 %all_to_all.32 = bf16[8,144,128]{2,1,0:T(8,128)(2,1)S(1)} all-to-all(bf16[8,144,128]{2,1,0:T(8,128)(2,1)S(1)} %pad_maximum_fusion), channel_id=1, replica_groups=mesh['group'=2,'dp'=32,'tensor'=4] {'group','tensor'}, dimensions={0} | all-to-all | bytes 589824 | tf_op jit(solution)/shard_map/all_to_all | solution.py:55
  42.5 2.7 %collective-permute-start.3 = (bf16[448,512]{1,0:T(8,128)(2,1)}, bf16[448,512]{1,0:T(8,128)(2,1)}, u32[]{:S(2)}, u32[]{:S(2)}) collective-permute-start(bf16[448,512]{1,0:T(8,128)(2,1)} %refs_1_.1), channel_id=1, source_target_pairs={{0,131},{1,0},{2,1},{3,2},{128,3},{129,128},{130,129},{131,130},{4... | collective-permute-start | bytes 1376264 | tf_op jit(solution)/shard_map/ppermute | solution.py:47
  45.2 1.6 copy-done.2
  46.8 1.5 copy-done.8
  48.3 1.0 copy-done.23
  49.3 1.2 project.4
  50.5 1.1 copy-done.12
  51.6 1.0 collective-permute-done.2.refs_2_
  53.3 7.6 %all-to-all-start = ((s32[32,1,2]{2,1,0:T(1,128)}), s32[32,1,2]{2,1,0:T(1,128)S(1)}, u32[]{:S(2)}, u32[]{:S(2)}) async-start(s32[32,1,2]{2,1,0:T(1,128)} %copy.44), calls=%async_computation | async-start | bytes 32768 | tf_op jit(solution)/shard_map/all_to_all | solution.py:55
  60.9 3.3 %collective-permute-start.7 = (bf16[448,512]{1,0:T(8,128)(2,1)}, bf16[448,512]{1,0:T(8,128)(2,1)}, u32[]{:S(2)}, u32[]{:S(2)}) collective-permute-start(bf16[448,512]{1,0:T(8,128)(2,1)} %copy-done.24), channel_id=1, source_target_pairs={{0,131},{1,0},{2,1},{3,2},{128,3},{129,128},{130,129},{131,130},{4... | collective-permute-start | bytes 1376264 | tf_op jit(solution)/shard_map/ppermute | solution.py:47
  64.2 3.2 %collective-permute-start.5 = (bf16[448,512]{1,0:T(8,128)(2,1)}, bf16[448,512]{1,0:T(8,128)(2,1)}, u32[]{:S(2)}, u32[]{:S(2)}) collective-permute-start(bf16[448,512]{1,0:T(8,128)(2,1)} %collective-permute-done.3.refs_3_), channel_id=1, source_target_pairs={{0,131},{1,0},{2,1},{3,2},{128,3},{129,128},{130,129},{131,130},{4... | collective-permute-start | bytes 1376264 | tf_op jit(solution)/shard_map/ppermute | solution.py:47
  67.8 2.0 gather_fusion
  69.8 7.4 %all-to-all-start.1 = ((bf16[32,32,896]{2,1,0:T(8,128)(2,1)}), bf16[32,32,896]{2,1,0:T(8,128)(2,1)}, u32[]{:S(2)}, u32[]{:S(2)}) async-start(bf16[32,32,896]{2,1,0:T(8,128)(2,1)} %bitcast.50), calls=%async_computation.1 | async-start | bytes 3670016 | tf_op jit(solution)/shard_map/all_to_all | solution.py:55
  77.4 1.6 copy-done.3
  79.0 1.6 copy-done.9
  80.6 1.4 copy-done.13
  82.0 1.0 copy-done.25
  83.0 3.2 %project.5 = (f32[448,768]{1,0:T(8,128)S(1)}, f32[448,1]{1,0:T(8,128)S(1)}) custom-call(s32[2]{0:T(128)S(1)} %pad_add_fusion.1.index_ref.refs_0_, bf16[448,512]{1,0:T(8,128)(2,1)} %collective-permute-done.refs_0_, bf16[448,512]{1,0:T(8,128)(2,1)S(1)} %copy-done.25, ...), custom_call_target="tpu_custom_call", output_to_operand_aliasing={{0}: (8, {}), {1}: (9, {})} | custom-call | flops 675282944 | bytes 6000000 | tf_op jit(solution)/shard_map/project/pallas_call | solution.py:133
  86.2 1.1 copy-done.14
  87.4 3.2 %collective-permute-start.11 = (bf16[448,512]{1,0:T(8,128)(2,1)}, bf16[448,512]{1,0:T(8,128)(2,1)}, u32[]{:S(2)}, u32[]{:S(2)}) collective-permute-start(bf16[448,512]{1,0:T(8,128)(2,1)} %collective-permute-done.7.refs_1_), channel_id=1, source_target_pairs={{0,131},{1,0},{2,1},{3,2},{128,3},{129,128},{130,129},{131,130},{4... | collective-permute-start | bytes 1376264 | tf_op jit(solution)/shard_map/ppermute | solution.py:47
  90.6 3.2 %collective-permute-start.9 = (bf16[448,512]{1,0:T(8,128)(2,1)}, bf16[448,512]{1,0:T(8,128)(2,1)}, u32[]{:S(2)}, u32[]{:S(2)}) collective-permute-start(bf16[448,512]{1,0:T(8,128)(2,1)} %collective-permute-done.5.refs_3_), channel_id=1, source_target_pairs={{0,131},{1,0},{2,1},{3,2},{128,3},{129,128},{130,129},{131,130},{4... | collective-permute-start | bytes 1376264 | tf_op jit(solution)/shard_map/ppermute | solution.py:47
  93.9 1.7 copy-done.4
  95.7 1.5 copy-done.10
  97.2 1.3 copy-done.15
  98.5 3.2 %project.6 = (f32[448,768]{1,0:T(8,128)S(1)}, f32[448,1]{1,0:T(8,128)S(1)}) custom-call(s32[2]{0:T(128)S(1)} %pad_add_fusion.2.index_ref.refs_0_, bf16[448,512]{1,0:T(8,128)(2,1)} %collective-permute-done.6.refs_0_, bf16[448,512]{1,0:T(8,128)(2,1)} %collective-permute-done.7.refs_1_, ...), custom_call_target="tpu_custom_call", output_to_operand_aliasing={{0}: (8, {}), {1}: (9, {})} | custom-call | flops 675282944 | bytes 6000000 | tf_op jit(solution)/shard_map/project/pallas_call | solution.py:133
  101.7 1.1 copy-done.16
  102.8 1.5 copy_bitcast_fusion.1
  104.3 6.9 %collective-permute-done.8.refs_2_ = bf16[448,512]{1,0:T(8,128)(2,1)} collective-permute-done((bf16[448,512]{1,0:T(8,128)(2,1)}, bf16[448,512]{1,0:T(8,128)(2,1)}, u32[]{:S(2)}, u32[]{:S(2)}) %collective-permute-start.8) | collective-permute-done | bytes 458784 | tf_op jit(solution)/shard_map/ppermute | solution.py:47
  111.4 1.8 all-to-all-done.1
  113.2 2.9 %gather_fusion.1 = bf16[8,32,896]{2,1,0:T(8,128)(2,1)} fusion(bf16[32,32,896]{2,1,0:T(8,128)(2,1)} %all-to-all-done.1, s32[1024]{0:T(1024)S(1)} %pad_clamp_fusion), kind=kCustom, calls=%fused_computation.1 | custom fusion | bytes 917536 | tf_op jit(solution)/shard_map/gather | solution.py:375
  116.0 7.1 %all-to-all-start.2 = ((bf16[8,32,896]{2,1,0:T(8,128)(2,1)}), bf16[8,32,896]{2,1,0:T(8,128)(2,1)}, u32[]{:S(2)}, u32[]{:S(2)}) async-start(bf16[8,32,896]{2,1,0:T(8,128)(2,1)} %gather_fusion.1), calls=%async_computation.2 | async-start | bytes 917504 | tf_op jit(solution)/shard_map/all_to_all | solution.py:55
  123.1 2.0 collective-permute-start.12
  125.1 1.2 collective-permute-start.13
  126.5 1.6 copy-done.5
  128.1 1.5 copy-done.11
  129.6 1.3 copy-done.17
  130.9 3.2 %project.7 = (f32[448,768]{1,0:T(8,128)S(1)}, f32[448,1]{1,0:T(8,128)S(1)}) custom-call(s32[2]{0:T(128)S(1)} %pad_add_fusion.3.index_ref.refs_0_, bf16[448,512]{1,0:T(8,128)(2,1)} %collective-permute-done.10.refs_0_, bf16[448,512]{1,0:T(8,128)(2,1)} %collective-permute-done.11.refs_1_, ...), custom_call_target="tpu_custom_call", output_to_operand_aliasing={{0}: (8, {}), {1}: (9, {})} | custom-call | flops 675282944 | bytes 6000000 | tf_op jit(solution)/shard_map/project/pallas_call | solution.py:133
  134.1 11.5 %collective-permute-done.12.hidden_hbm = bf16[448,512]{1,0:T(8,128)(2,1)} collective-permute-done((bf16[448,512]{1,0:T(8,128)(2,1)}, bf16[448,512]{1,0:T(8,128)(2,1)}, u32[]{:S(2)}, u32[]{:S(2)}) %collective-permute-start.12) | collective-permute-done | bytes 458784 | tf_op jit(solution)/shard_map/ppermute | solution.py:47
  145.6 1.8 project_last.1
  147.4 0.9 copy-done.20
  148.3 4.5 %all-to-all-start.3 = ((bf16[8,64,768]{2,1,0:T(8,128)(2,1)}), bf16[8,64,768]{2,1,0:T(8,128)(2,1)}, u32[]{:S(2)}, u32[]{:S(2)}) async-start(bf16[8,64,768]{2,1,0:T(8,128)(2,1)} %copy-done.20), calls=%async_computation.3 | async-start | bytes 1572864 | tf_op jit(solution)/shard_map/all_to_all | solution.py:55
  152.8 1.4 copy-done.19
  154.2 1.9 encoder_queries.1.enc_q_hbm
  156.9 18.7 %all-to-all-done.3.got_hbm = bf16[8,64,768]{2,1,0:T(8,128)(2,1)} async-done(((bf16[8,64,768]{2,1,0:T(8,128)(2,1)}), bf16[8,64,768]{2,1,0:T(8,128)(2,1)}, u32[]{:S(2)}, u32[]{:S(2)}) %all-to-all-start.3) | async-done | bytes 786464 | tf_op jit(solution)/shard_map/all_to_all | solution.py:55
  175.6 1.0 copy-done.22
  176.6 3.1 %copy-done.26 = bf16[3584,1024]{1,0:T(8,128)(2,1)S(1)} copy-done((bf16[3584,1024]{1,0:T(8,128)(2,1)S(1)}, bf16[3584,1024]{1,0:T(8,128)(2,1)}, u32[]{:S(2)}) %copy-start.26) | copy-done | bytes 7340056
  179.7 1.4 copy-done.27
  181.1 12.9 %attention.1.refs_1_ = bf16[64,2176]{1,0:T(8,128)(2,1)} custom-call(bf16[256,896]{1,0:T(8,128)(2,1)} %bitcast.10.fetched_hbm, bf16[256,896]{1,0:T(8,128)(2,1)S(1)} %copy-done.22, bf16[8,64,768]{2,1,0:T(8,128)(2,1)} %all-to-all-done.3.got_hbm, bf16[896,896]{1,0:T(8,128)(2,1)S(1)} %copy-done.27, bf16[16,2,112,1024]{3,2,1,0:T(8,128)(2,1)S(1)} %bitcast.49), custom_call_target="tpu_custom_call" | custom-call | flops 4000000000 | bytes 12000000 | tf_op jit(solution)/shard_map/attention/pallas_call | solution.py:411
  194.7 2.7 %collective-permute-start.15 = (bf16[64,2176]{1,0:T(8,128)(2,1)}, bf16[64,2176]{1,0:T(8,128)(2,1)}, u32[]{:S(2)}, u32[]{:S(2)}) collective-permute-start(bf16[64,2176]{1,0:T(8,128)(2,1)} %attention.1.refs_1_), channel_id=1, source_target_pairs={{0,131},{1,0},{2,1},{3,2},{128,3},{129,128},{130,129},{131,130},{4... | collective-permute-start | bytes 835592 | tf_op jit(solution)/shard_map/ppermute | solution.py:47
  197.4 1.6 copy-done.6
  199.0 3.0 %finish.5.refs_6_ = bf16[448,512]{1,0:T(8,128)(2,1)} custom-call(s32[1]{0:T(128)} %bitcast.21.refs_0_, bf16[64,2176]{1,0:T(8,128)(2,1)} %attention.1.refs_1_, bf16[448,512]{1,0:T(8,128)(2,1)S(1)} %copy-done.18, f32[448,1]{1,0:T(8,128)S(1)} %get-tuple-element.86.refs_3_.refs_4_, bf16[32,2,16,1024]{3,2,1,0:T(8,128)(2,1)S(1)} %bitcast.39), custom_call_target="tpu_custom_call" | custom-call | flops 134217728 | bytes 4000000 | tf_op jit(solution)/shard_map/finish/pallas_call | solution.py:302
  202.0 2.3 collective-permute-done.14.refs_1_
  204.2 3.2 %collective-permute-start.17 = (bf16[64,2176]{1,0:T(8,128)(2,1)}, bf16[64,2176]{1,0:T(8,128)(2,1)S(1)}, u32[]{:S(2)}, u32[]{:S(2)}) collective-permute-start(bf16[64,2176]{1,0:T(8,128)(2,1)} %collective-permute-done.15.refs_2_), channel_id=1, source_target_pairs={{0,131},{1,0},{2,1},{3,2},{128,3},{129,128},{130,129},{131,130},{4... | collective-permute-start | bytes 835592 | tf_op jit(solution)/shard_map/ppermute | solution.py:47
  207.5 3.7 %finish.6.refs_6_ = bf16[448,512]{1,0:T(8,128)(2,1)} custom-call(s32[2]{0:T(128)S(1)} %pad_add_fusion.1.index_ref.refs_0_, bf16[64,2176]{1,0:T(8,128)(2,1)} %collective-permute-done.14.refs_1_, bf16[64,2176]{1,0:T(8,128)(2,1)} %collective-permute-done.15.refs_2_, bf16[448,512]{1,0:T(8,128)(2,1)S(1)} %copy-done.18, ...), custom_call_target="tpu_custom_call", output_to_operand_aliasing={{}: (6, {})} | custom-call | flops 268435456 | bytes 4000000 | tf_op jit(solution)/shard_map/finish/pallas_call | solution.py:302
  211.1 2.3 collective-permute-done.16.refs_1_
  213.4 3.2 %collective-permute-start.19 = (bf16[64,2176]{1,0:T(8,128)(2,1)S(1)}, bf16[64,2176]{1,0:T(8,128)(2,1)S(1)}, u32[]{:S(2)}, u32[]{:S(2)}) collective-permute-start(bf16[64,2176]{1,0:T(8,128)(2,1)S(1)} %collective-permute-done.17.refs_2_), channel_id=1, source_target_pairs={{0,131},{1,0},{2,1},{3,2},{128,3},{129,128},{130,129},{131,130},{4... | collective-permute-start | bytes 835592 | tf_op jit(solution)/shard_map/ppermute | solution.py:47
  216.6 2.8 %finish.7.refs_6_ = bf16[448,512]{1,0:T(8,128)(2,1)} custom-call(s32[2]{0:T(128)S(1)} %pad_add_fusion.2.index_ref.refs_0_, bf16[64,2176]{1,0:T(8,128)(2,1)S(1)} %collective-permute-done.16.refs_1_, bf16[64,2176]{1,0:T(8,128)(2,1)S(1)} %collective-permute-done.17.refs_2_, bf16[448,512]{1,0:T(8,128)(2,1)S(1)} %copy-done.18, ...), custom_call_target="tpu_custom_call", output_to_operand_aliasing={{}: (6, {})} | custom-call | flops 268435456 | bytes 4000000 | tf_op jit(solution)/shard_map/finish/pallas_call | solution.py:302
  219.5 1.9 collective-permute-done.18.refs_1_
  221.5 3.3 %collective-permute-start.21 = (bf16[32,2176]{1,0:T(8,128)(2,1)S(1)}, bf16[32,2176]{1,0:T(8,128)(2,1)S(1)}, u32[]{:S(2)}, u32[]{:S(2)}) collective-permute-start(bf16[32,2176]{1,0:T(8,128)(2,1)S(1)} %slice.28), channel_id=1, source_target_pairs={{0,131},{1,0},{2,1},{3,2},{128,3},{129,128},{130,129},{131,130},{4... | collective-permute-start | bytes 417800 | tf_op jit(solution)/shard_map/ppermute | solution.py:47
  224.9 2.9 %finish.8.refs_6_ = bf16[448,512]{1,0:T(8,128)(2,1)} custom-call(s32[2]{0:T(128)S(1)} %pad_add_fusion.3.index_ref.refs_0_, bf16[64,2176]{1,0:T(8,128)(2,1)S(1)} %collective-permute-done.18.refs_1_, bf16[64,2176]{1,0:T(8,128)(2,1)S(1)} %collective-permute-done.19.refs_2_, bf16[448,512]{1,0:T(8,128)(2,1)S(1)} %copy-done.18, ...), custom_call_target="tpu_custom_call", output_to_operand_aliasing={{}: (6, {})} | custom-call | flops 268435456 | bytes 4000000 | tf_op jit(solution)/shard_map/finish/pallas_call | solution.py:302
  227.8 2.9 %finish.9 = bf16[448,512]{1,0:T(8,128)(2,1)} custom-call(s32[2]{0:T(128)S(1)} %pad_add_fusion.refs_0_, bf16[32,2176]{1,0:T(8,128)(2,1)S(1)} %collective-permute-done.20.refs_1_, bf16[32,2176]{1,0:T(8,128)(2,1)S(1)} %collective-permute-done.21.refs_2_, bf16[448,512]{1,0:T(8,128)(2,1)S(1)} %copy-done.18, ...), custom_call_target="tpu_custom_call", output_to_operand_aliasing={{}: (6, {})} | custom-call | flops 134217728 | bytes 4000000 | tf_op jit(solution)/shard_map/finish/pallas_call | solution.py:302
  (94 shorter events, 10.0 us)
Async XLA Ops:
  6.5 61.3 %copy-start = (bf16[16,16,896]{2,1,0:T(8,128)(2,1)S(1)}, bf16[16,16,896]{2,1,0:T(8,128)(2,1)}, u32[]{:S(2)}) copy-start(bf16[16,16,896]{2,1,0:T(8,128)(2,1)} %param.19) | copy-start | bytes 1376260
  6.5 38.6 %copy-start.18 = (bf16[448,512]{1,0:T(8,128)(2,1)S(1)}, bf16[448,512]{1,0:T(8,128)(2,1)}, u32[]{:S(2)}) copy-start(bf16[448,512]{1,0:T(8,128)(2,1)} %refs_3_.7) | copy-start | bytes 1376260
  6.5 38.6 %copy-start.1 = (bf16[4096,256]{1,0:T(8,128)(2,1)S(1)}, bf16[4096,256]{1,0:T(8,128)(2,1)}, u32[]{:S(2)}) copy-start(bf16[4096,256]{1,0:T(8,128)(2,1)} %query_hbm.1) | copy-start | bytes 6291460
  6.5 169.1 %all-gather.3.cloned.1.call-start = ((), (), s32[]{:S(2)}) async-start(), calls=%async_computation.5 | async-start | bytes 7569408 | tf_op jit(solution)/shard_map/all_gather | solution.py:371
  6.5 16.8 %collective-permute-start = (bf16[448,512]{1,0:T(8,128)(2,1)}, bf16[448,512]{1,0:T(8,128)(2,1)}, u32[]{:S(2)}, u32[]{:S(2)}) collective-permute-start(bf16[448,512]{1,0:T(8,128)(2,1)} %refs_3_.7), channel_id=1, source_target_pairs={{0,1},{1,2},{2,3},{3,128},{128,129},{129,130},{130,131},{131,0},{4... | collective-permute-start | bytes 1376264 | tf_op jit(solution)/shard_map/ppermute | solution.py:47
  8.5 14.8 %collective-permute-start.1 = (bf16[448,512]{1,0:T(8,128)(2,1)}, bf16[448,512]{1,0:T(8,128)(2,1)S(1)}, u32[]{:S(2)}, u32[]{:S(2)}) collective-permute-start(bf16[448,512]{1,0:T(8,128)(2,1)} %refs_3_.7), channel_id=1, source_target_pairs={{0,131},{1,0},{2,1},{3,2},{128,3},{129,128},{130,129},{131,130},{4... | collective-permute-start | bytes 1376264 | tf_op jit(solution)/shard_map/ppermute | solution.py:47
  23.3 21.9 %copy-start.24 = (bf16[448,512]{1,0:T(8,128)(2,1)}, bf16[448,512]{1,0:T(8,128)(2,1)S(1)}, u32[]{:S(2)}) copy-start(bf16[448,512]{1,0:T(8,128)(2,1)S(1)} %collective-permute-done.1.refs_1_) | copy-start | bytes 1376260
  40.4 0.7 copy-start.28
  41.9 10.8 %collective-permute-start.2 = (bf16[448,512]{1,0:T(8,128)(2,1)}, bf16[448,512]{1,0:T(8,128)(2,1)}, u32[]{:S(2)}, u32[]{:S(2)}) collective-permute-start(bf16[448,512]{1,0:T(8,128)(2,1)} %refs_1_.1), channel_id=1, source_target_pairs={{0,1},{1,2},{2,3},{3,128},{128,129},{129,130},{130,131},{131,0},{4... | collective-permute-start | bytes 1376264 | tf_op jit(solution)/shard_map/ppermute | solution.py:47
  42.5 10.1 %collective-permute-start.3 = (bf16[448,512]{1,0:T(8,128)(2,1)}, bf16[448,512]{1,0:T(8,128)(2,1)}, u32[]{:S(2)}, u32[]{:S(2)}) collective-permute-start(bf16[448,512]{1,0:T(8,128)(2,1)} %refs_1_.1), channel_id=1, source_target_pairs={{0,131},{1,0},{2,1},{3,2},{128,3},{129,128},{130,129},{131,130},{4... | collective-permute-start | bytes 1376264 | tf_op jit(solution)/shard_map/ppermute | solution.py:47
  45.2 1.6 copy-start.2
  46.8 1.5 copy-start.8
  48.3 1.0 copy-start.23
  50.5 1.1 copy-start.12
  52.6 34.7 %collective-permute-start.6 = (bf16[448,512]{1,0:T(8,128)(2,1)}, bf16[448,512]{1,0:T(8,128)(2,1)}, u32[]{:S(2)}, u32[]{:S(2)}) collective-permute-start(bf16[448,512]{1,0:T(8,128)(2,1)} %collective-permute-done.refs_0_), channel_id=1, source_target_pairs={{0,1},{1,2},{2,3},{3,128},{128,129},{129,130},{130,131},{131,0},{4... | collective-permute-start | bytes 1376264 | tf_op jit(solution)/shard_map/ppermute | solution.py:47
  53.3 14.2 %all-to-all-start = ((s32[32,1,2]{2,1,0:T(1,128)}), s32[32,1,2]{2,1,0:T(1,128)S(1)}, u32[]{:S(2)}, u32[]{:S(2)}) async-start(s32[32,1,2]{2,1,0:T(1,128)} %copy.44), calls=%async_computation | async-start | bytes 32768 | tf_op jit(solution)/shard_map/all_to_all | solution.py:55
  60.9 26.4 %collective-permute-start.7 = (bf16[448,512]{1,0:T(8,128)(2,1)}, bf16[448,512]{1,0:T(8,128)(2,1)}, u32[]{:S(2)}, u32[]{:S(2)}) collective-permute-start(bf16[448,512]{1,0:T(8,128)(2,1)} %copy-done.24), channel_id=1, source_target_pairs={{0,131},{1,0},{2,1},{3,2},{128,3},{129,128},{130,129},{131,130},{4... | collective-permute-start | bytes 1376264 | tf_op jit(solution)/shard_map/ppermute | solution.py:47
  64.2 23.1 %collective-permute-start.4 = (bf16[448,512]{1,0:T(8,128)(2,1)}, bf16[448,512]{1,0:T(8,128)(2,1)}, u32[]{:S(2)}, u32[]{:S(2)}) collective-permute-start(bf16[448,512]{1,0:T(8,128)(2,1)} %collective-permute-done.2.refs_2_), channel_id=1, source_target_pairs={{0,1},{1,2},{2,3},{3,128},{128,129},{129,130},{130,131},{131,0},{4... | collective-permute-start | bytes 1376264 | tf_op jit(solution)/shard_map/ppermute | solution.py:47
  64.2 23.1 %collective-permute-start.5 = (bf16[448,512]{1,0:T(8,128)(2,1)}, bf16[448,512]{1,0:T(8,128)(2,1)}, u32[]{:S(2)}, u32[]{:S(2)}) collective-permute-start(bf16[448,512]{1,0:T(8,128)(2,1)} %collective-permute-done.3.refs_3_), channel_id=1, source_target_pairs={{0,131},{1,0},{2,1},{3,2},{128,3},{129,128},{130,129},{131,130},{4... | collective-permute-start | bytes 1376264 | tf_op jit(solution)/shard_map/ppermute | solution.py:47
  69.8 43.4 %all-to-all-start.1 = ((bf16[32,32,896]{2,1,0:T(8,128)(2,1)}), bf16[32,32,896]{2,1,0:T(8,128)(2,1)}, u32[]{:S(2)}, u32[]{:S(2)}) async-start(bf16[32,32,896]{2,1,0:T(8,128)(2,1)} %bitcast.50), calls=%async_computation.1 | async-start | bytes 3670016 | tf_op jit(solution)/shard_map/all_to_all | solution.py:55
  77.2 120.1 %all-gather.5.cloned.1.call-start = ((), (), s32[]{:S(2)}) async-start(), calls=%async_computation.6 | async-start | bytes 2162688 | tf_op jit(solution)/shard_map/all_gather | solution.py:373
  77.4 1.6 copy-start.3
  79.0 1.6 copy-start.9
  80.6 1.4 copy-start.13
  82.0 1.0 copy-start.25
  86.2 1.1 copy-start.14
  87.3 16.9 %collective-permute-start.10 = (bf16[448,512]{1,0:T(8,128)(2,1)}, bf16[448,512]{1,0:T(8,128)(2,1)}, u32[]{:S(2)}, u32[]{:S(2)}) collective-permute-start(bf16[448,512]{1,0:T(8,128)(2,1)} %collective-permute-done.6.refs_0_), channel_id=1, source_target_pairs={{0,1},{1,2},{2,3},{3,128},{128,129},{129,130},{130,131},{131,0},{4... | collective-permute-start | bytes 1376264 | tf_op jit(solution)/shard_map/ppermute | solution.py:47
  87.4 16.8 %collective-permute-start.11 = (bf16[448,512]{1,0:T(8,128)(2,1)}, bf16[448,512]{1,0:T(8,128)(2,1)}, u32[]{:S(2)}, u32[]{:S(2)}) collective-permute-start(bf16[448,512]{1,0:T(8,128)(2,1)} %collective-permute-done.7.refs_1_), channel_id=1, source_target_pairs={{0,131},{1,0},{2,1},{3,2},{128,3},{129,128},{130,129},{131,130},{4... | collective-permute-start | bytes 1376264 | tf_op jit(solution)/shard_map/ppermute | solution.py:47
  90.6 20.6 %collective-permute-start.8 = (bf16[448,512]{1,0:T(8,128)(2,1)}, bf16[448,512]{1,0:T(8,128)(2,1)}, u32[]{:S(2)}, u32[]{:S(2)}) collective-permute-start(bf16[448,512]{1,0:T(8,128)(2,1)} %collective-permute-done.4.refs_2_), channel_id=1, source_target_pairs={{0,1},{1,2},{2,3},{3,128},{128,129},{129,130},{130,131},{131,0},{4... | collective-permute-start | bytes 1376264 | tf_op jit(solution)/shard_map/ppermute | solution.py:47
  90.6 20.6 %collective-permute-start.9 = (bf16[448,512]{1,0:T(8,128)(2,1)}, bf16[448,512]{1,0:T(8,128)(2,1)}, u32[]{:S(2)}, u32[]{:S(2)}) collective-permute-start(bf16[448,512]{1,0:T(8,128)(2,1)} %collective-permute-done.5.refs_3_), channel_id=1, source_target_pairs={{0,131},{1,0},{2,1},{3,2},{128,3},{129,128},{130,129},{131,130},{4... | collective-permute-start | bytes 1376264 | tf_op jit(solution)/shard_map/ppermute | solution.py:47
  93.9 1.7 copy-start.4
  95.7 1.5 copy-start.10
  97.2 1.3 copy-start.15
  98.5 12.7 %copy-start.29 = (s32[7,1]{0,1:T(1,128)S(1)}, s32[7,1]{0,1:T(1,128)}, u32[]{:S(2)}) copy-start(s32[7,1]{0,1:T(1,128)} %param.21) | copy-start | bytes 88
  101.7 1.1 copy-start.16
  116.0 32.3 %all-to-all-start.2 = ((bf16[8,32,896]{2,1,0:T(8,128)(2,1)}), bf16[8,32,896]{2,1,0:T(8,128)(2,1)}, u32[]{:S(2)}, u32[]{:S(2)}) async-start(bf16[8,32,896]{2,1,0:T(8,128)(2,1)} %gather_fusion.1), calls=%async_computation.2 | async-start | bytes 917504 | tf_op jit(solution)/shard_map/all_to_all | solution.py:55
  123.1 22.5 %collective-permute-start.12 = (bf16[448,512]{1,0:T(8,128)(2,1)}, bf16[448,512]{1,0:T(8,128)(2,1)}, u32[]{:S(2)}, u32[]{:S(2)}) collective-permute-start(bf16[448,512]{1,0:T(8,128)(2,1)} %collective-permute-done.10.refs_0_), channel_id=1, source_target_pairs={{0,1},{1,2},{2,3},{3,128},{128,129},{129,130},{130,131},{131,0},{4... | collective-permute-start | bytes 1376264 | tf_op jit(solution)/shard_map/ppermute | solution.py:47
  125.1 20.5 %collective-permute-start.13 = (bf16[448,512]{1,0:T(8,128)(2,1)}, bf16[448,512]{1,0:T(8,128)(2,1)}, u32[]{:S(2)}, u32[]{:S(2)}) collective-permute-start(bf16[448,512]{1,0:T(8,128)(2,1)} %collective-permute-done.9.refs_3_), channel_id=1, source_target_pairs={{0,131},{1,0},{2,1},{3,2},{128,3},{129,128},{130,129},{131,130},{4... | collective-permute-start | bytes 1376264 | tf_op jit(solution)/shard_map/ppermute | solution.py:47
  126.4 1.6 copy-start.5
  128.1 1.5 copy-start.11
  129.6 1.3 copy-start.17
  147.4 0.9 copy-start.20
  148.3 27.3 %all-to-all-start.3 = ((bf16[8,64,768]{2,1,0:T(8,128)(2,1)}), bf16[8,64,768]{2,1,0:T(8,128)(2,1)}, u32[]{:S(2)}, u32[]{:S(2)}) async-start(bf16[8,64,768]{2,1,0:T(8,128)(2,1)} %copy-done.20), calls=%async_computation.3 | async-start | bytes 1572864 | tf_op jit(solution)/shard_map/all_to_all | solution.py:55
  152.8 1.4 copy-start.19
  156.2 0.8 copy-start.21
  175.6 1.0 copy-start.22
  176.6 3.1 %copy-start.26 = (bf16[3584,1024]{1,0:T(8,128)(2,1)S(1)}, bf16[3584,1024]{1,0:T(8,128)(2,1)}, u32[]{:S(2)}) copy-start(bf16[3584,1024]{1,0:T(8,128)(2,1)} %all-gather.3.cloned.1.call-done) | copy-start | bytes 22020100
  179.7 1.4 copy-start.27
  194.0 10.2 %collective-permute-start.14 = (bf16[64,2176]{1,0:T(8,128)(2,1)}, bf16[64,2176]{1,0:T(8,128)(2,1)}, u32[]{:S(2)}, u32[]{:S(2)}) collective-permute-start(bf16[64,2176]{1,0:T(8,128)(2,1)} %attention.1.refs_1_), channel_id=1, source_target_pairs={{0,1},{1,2},{2,3},{3,128},{128,129},{129,130},{130,131},{131,0},{4... | collective-permute-start | bytes 835592 | tf_op jit(solution)/shard_map/ppermute | solution.py:47
  194.7 9.5 %collective-permute-start.15 = (bf16[64,2176]{1,0:T(8,128)(2,1)}, bf16[64,2176]{1,0:T(8,128)(2,1)}, u32[]{:S(2)}, u32[]{:S(2)}) collective-permute-start(bf16[64,2176]{1,0:T(8,128)(2,1)} %attention.1.refs_1_), channel_id=1, source_target_pairs={{0,131},{1,0},{2,1},{3,2},{128,3},{129,128},{130,129},{131,130},{4... | collective-permute-start | bytes 835592 | tf_op jit(solution)/shard_map/ppermute | solution.py:47
  197.4 1.6 copy-start.6
  198.9 8.5 %copy-start.7 = (bf16[1024,1024]{1,0:T(8,128)(2,1)S(1)}, bf16[1024,1024]{1,0:T(8,128)(2,1)}, u32[]{:S(2)}) copy-start(bf16[1024,1024]{1,0:T(8,128)(2,1)} %all-gather.5.cloned.1.call-done) | copy-start | bytes 6291460
  204.2 9.2 %collective-permute-start.16 = (bf16[64,2176]{1,0:T(8,128)(2,1)}, bf16[64,2176]{1,0:T(8,128)(2,1)S(1)}, u32[]{:S(2)}, u32[]{:S(2)}) collective-permute-start(bf16[64,2176]{1,0:T(8,128)(2,1)} %collective-permute-done.14.refs_1_), channel_id=1, source_target_pairs={{0,1},{1,2},{2,3},{3,128},{128,129},{129,130},{130,131},{131,0},{4... | collective-permute-start | bytes 835592 | tf_op jit(solution)/shard_map/ppermute | solution.py:47
  204.2 9.2 %collective-permute-start.17 = (bf16[64,2176]{1,0:T(8,128)(2,1)}, bf16[64,2176]{1,0:T(8,128)(2,1)S(1)}, u32[]{:S(2)}, u32[]{:S(2)}) collective-permute-start(bf16[64,2176]{1,0:T(8,128)(2,1)} %collective-permute-done.15.refs_2_), channel_id=1, source_target_pairs={{0,131},{1,0},{2,1},{3,2},{128,3},{129,128},{130,129},{131,130},{4... | collective-permute-start | bytes 835592 | tf_op jit(solution)/shard_map/ppermute | solution.py:47
  213.4 8.0 %collective-permute-start.18 = (bf16[64,2176]{1,0:T(8,128)(2,1)S(1)}, bf16[64,2176]{1,0:T(8,128)(2,1)S(1)}, u32[]{:S(2)}, u32[]{:S(2)}) collective-permute-start(bf16[64,2176]{1,0:T(8,128)(2,1)S(1)} %collective-permute-done.16.refs_1_), channel_id=1, source_target_pairs={{0,1},{1,2},{2,3},{3,128},{128,129},{129,130},{130,131},{131,0},{4... | collective-permute-start | bytes 835592 | tf_op jit(solution)/shard_map/ppermute | solution.py:47
  213.4 8.0 %collective-permute-start.19 = (bf16[64,2176]{1,0:T(8,128)(2,1)S(1)}, bf16[64,2176]{1,0:T(8,128)(2,1)S(1)}, u32[]{:S(2)}, u32[]{:S(2)}) collective-permute-start(bf16[64,2176]{1,0:T(8,128)(2,1)S(1)} %collective-permute-done.17.refs_2_), channel_id=1, source_target_pairs={{0,131},{1,0},{2,1},{3,2},{128,3},{129,128},{130,129},{131,130},{4... | collective-permute-start | bytes 835592 | tf_op jit(solution)/shard_map/ppermute | solution.py:47
  221.4 6.3 %collective-permute-start.20 = (bf16[32,2176]{1,0:T(8,128)(2,1)S(1)}, bf16[32,2176]{1,0:T(8,128)(2,1)S(1)}, u32[]{:S(2)}, u32[]{:S(2)}) collective-permute-start(bf16[32,2176]{1,0:T(8,128)(2,1)S(1)} %slice.27), channel_id=1, source_target_pairs={{0,1},{1,2},{2,3},{3,128},{128,129},{129,130},{130,131},{131,0},{4... | collective-permute-start | bytes 417800 | tf_op jit(solution)/shard_map/ppermute | solution.py:47
  221.5 6.2 %collective-permute-start.21 = (bf16[32,2176]{1,0:T(8,128)(2,1)S(1)}, bf16[32,2176]{1,0:T(8,128)(2,1)S(1)}, u32[]{:S(2)}, u32[]{:S(2)}) collective-permute-start(bf16[32,2176]{1,0:T(8,128)(2,1)S(1)} %slice.28), channel_id=1, source_target_pairs={{0,131},{1,0},{2,1},{3,2},{128,3},{129,128},{130,129},{131,130},{4... | collective-permute-start | bytes 417800 | tf_op jit(solution)/shard_map/ppermute | solution.py:47
Sparse Core Ops, SparseCore 0:
  42.0 70.2 all-gather.2
  114.8 49.3 all-gather.4

commit v2 on v1

--- a/solution.py
+++ b/solution.py
@@ -27,8 +27,9 @@
 BF = jnp.bfloat16
 F32 = jnp.float32
 MIB = 1024 * 1024
-PARAMS = pltpu.CompilerParams(vmem_limit_bytes=20 * MIB)
-HBM = pl.BlockSpec(memory_space=pltpu.HBM)
+KNOB = 20_000_000_000
+PARAMS = pltpu.CompilerParams(vmem_limit_bytes=59 * MIB)
+ROOM = pltpu.CompilerParams(vmem_limit_bytes=53 * MIB + MIB // 2)
 VMEM = pl.BlockSpec(memory_space=pltpu.VMEM)
 SMEM = pl.BlockSpec(memory_space=pltpu.SMEM)
 ANY = pl.BlockSpec(memory_space=pl.ANY)
@@ -75,7 +76,7 @@
     return pltpu.VMEM(x.shape, x.dtype)
 
 
-def encoder_queries(fetched_hbm, weight_hbm, out_ref, fetched_ref, weight_ref, sem):
+def encoder_queries(fetched_hbm, weight_hbm, out_hbm, fetched_ref, weight_ref, out_ref, sem):
     copies = start([(fetched_hbm, fetched_ref), (weight_hbm, weight_ref)], sem)
     copies[0].wait()
     rows = fetched_ref[...].astype(F32)
@@ -83,15 +84,14 @@
     normed = (rows * inverse).astype(BF)
     copies[1].wait()
     out_ref[...] = dot(normed, weight_ref[...]).astype(BF)
-
-
-def project(count, first, index_ref, *refs):
+    wait(start([(out_ref, out_hbm)], sem.at[pl.ds(2, 1)]))
+
+
+def project(count, index_ref, *refs):
     hiddens_hbm, cots_hbm, refs = refs[:count], refs[count : 2 * count], refs[2 * count :]
-    query_hbm, cond_hbm, out_hbm = refs[:3]
-    if not first:
-        old_acc_ref, old_squares_ref = refs[3:5]
-    acc_ref, squares_ref = refs[3 if first else 5 :][:2]
-    hidden_ref, cot_ref, query_ref, cond_ref, out_weight_ref, sem = refs[-6:]
+    query_hbm, cond_hbm, out_hbm, acc_hbm, squares_hbm = refs[:5]
+    hidden_ref, cot_ref, query_ref, cond_ref, out_weight_ref = refs[5:10]
+    acc_ref, squares_ref, sem, out_sem = refs[10:]
     copies = []
     for k in range(count):
         at = pl.ds(pl.multiple_of(index_ref[k] * FEAT, FEAT), FEAT)
@@ -113,52 +113,22 @@
             dot_nt(cot_ref[k], out_weight_ref[k]),
             dot_nt(chunk, cond_ref[k]),
         )
-        source, source_squares = acc_ref, squares_ref
-        if k == 0 and not first:
-            source, source_squares = old_acc_ref, old_squares_ref
-        fresh = first and k == 0
         for columns, part in zip((slice(0, 256), slice(256, 512), slice(512, 736)), parts):
-            acc_ref[:, columns] = part if fresh else source[:, columns] + part
-        squares_ref[...] = squares if fresh else source_squares[...] + squares
-
-
-def project_call(hiddens, cots, index, weights, before):
-    count, first = len(hiddens), before is None
-    before = () if first else before
-    results = (
-        jax.ShapeDtypeStruct((TOK, 768), F32),
-        jax.ShapeDtypeStruct((TOK, 1), F32),
-    )
-    at = 1 + 2 * count + 3
-    return pl.pallas_call(
-        functools.partial(project, count, first),
-        out_shape=results,
-        in_specs=[SMEM] + [ANY] * (2 * count) + [HBM] * 3 + [VMEM] * len(before),
-        out_specs=(VMEM, VMEM),
-        scratch_shapes=[
-            pltpu.VMEM((count, TOK, FEAT), BF),
-            pltpu.VMEM((count, TOK, FEAT), BF),
-            pltpu.VMEM((count, FEAT, 256), BF),
-            pltpu.VMEM((count, 224, FEAT), BF),
-            pltpu.VMEM((count, 256, FEAT), BF),
-            pltpu.SemaphoreType.DMA((count, 5)),
-        ],
-        input_output_aliases={} if first else {at: 0, at + 1: 1},
-        compiler_params=PARAMS,
-        cost_estimate=cost(2 * count * TOK * FEAT * 736, 6_000_000),
-        name="project",
-    )(jnp.stack(index), *hiddens, *cots, *weights, *before)
+            acc_ref[:, columns] = part if k == 0 else acc_ref[:, columns] + part
+        squares_ref[...] = squares if k == 0 else squares_ref[...] + squares
+    wait(start([(acc_ref, acc_hbm), (squares_ref, squares_hbm)], out_sem))
 
 
 def project_last(
-    index_ref, hidden_hbm, cot_hbm, acc_ref, squares_ref, query_hbm, cond_hbm, out_hbm,
-    sent_ref, inverse_ref,
-    hidden_ref, cot_ref, query_ref, cond_ref, out_weight_ref, sem,
+    index_ref, hidden_hbm, cot_hbm, acc_hbm, squares_hbm, query_hbm, cond_hbm, out_hbm,
+    sent_hbm, inverse_hbm,
+    hidden_ref, cot_ref, acc_ref, squares_ref, query_ref, cond_ref, out_weight_ref,
+    sent_ref, inverse_ref, sem, out_sem,
 ):
     at = pl.ds(pl.multiple_of(index_ref[0] * FEAT, FEAT), FEAT)
     copies = start(
         [
-            (hidden_hbm, hidden_ref),
+            (hidden_hbm, hidden_ref), (squares_hbm, squares_ref), (acc_hbm, acc_ref),
             (query_hbm.at[at], query_ref), (cond_hbm.at[:, at], cond_ref),
             (cot_hbm, cot_ref), (out_hbm.at[:, at], out_weight_ref),
         ], sem,
@@ -179,6 +149,7 @@
         sent_ref[:SEGS, :, columns] = part.astype(BF).reshape(SEGS, SEG, -1)
     sent_ref[:, :, 736:] = jnp.zeros((NZ, SEG, 32), BF)
     sent_ref[SEGS, :, :736] = jnp.zeros((SEG, 736), BF)
+    wait(start([(sent_ref, sent_hbm), (inverse_ref, inverse_hbm)], out_sem))
 
 
 def attention(
@@ -193,7 +164,7 @@
     )
     large = [
         pltpu.make_async_copy(
-            weights_hbm.at[:, j], kv_ref.at[j], sem.at[4 + j]
+            weights_hbm.at[:, j, pl.ds(0, 112), :], kv_ref.at[j], sem.at[4 + j]
         )
         for j in range(2)
     ]
@@ -259,7 +230,7 @@
         places.append((source < SEGS, pl.ds(pl.multiple_of(at, 32), rows)))
     loads = [(inverse_hbm, inverse_ref)]
     loads += [
-        (weights_hbm.at[:, j], weight_ref.at[j]) for j in range(2)
+        (weights_hbm.at[:, pl.ds(112 + 16 * j, 16), :], weight_ref.at[j]) for j in range(2)
     ]
     for k in range(count):
         loads.append((chunks_hbm[k], chunk_refs[k]))
@@ -302,8 +273,8 @@
     return pl.pallas_call(
         functools.partial(finish, starts, first),
         out_shape=jax.ShapeDtypeStruct((TOK, FEAT), BF),
-        in_specs=[SMEM] + [ANY] * (len(chunks) + 2) + [HBM] * (1 if first else 2),
-        out_specs=HBM,
+        in_specs=[SMEM] + [ANY] * (len(operands) - 1),
+        out_specs=ANY,
         scratch_shapes=[like(c) for c in chunks]
         + [pltpu.VMEM((r, FEAT), BF) for r in rows] * 2
         + [
@@ -313,7 +284,7 @@
             pltpu.SemaphoreType.DMA((len(chunks),)),
         ],
         input_output_aliases={} if first else {len(operands) - 1: 0},
-        compiler_params=PARAMS,
+        compiler_params=ROOM,
         cost_estimate=cost(2 * sum(rows) * FEAT * 2048, 4_000_000),
         name="finish",
     )(*operands)
@@ -352,33 +323,52 @@
     projections = (query_weight, condition_weight.T, out_weight)
     right = left = hidden
     grad_right = grad_left = cotangent
-    acc = project_call([hidden], [cotangent], [me], projections, None)
+    index, chunks, grad_chunks = [me], [hidden], [cotangent]
     for step in range(1, 4):
         right, left = shift(right, 1), shift(left, -1)
-        if step == 1:
-            wanted, part, right, left = tie(wanted, part, right, left)
-        else:
-            right, left, _, _ = tie(right, left, grad_right, grad_left)
         grad_right, grad_left = shift(grad_right, 1), shift(grad_left, -1)
-        grad_right, grad_left, right, left, *acc = tie(grad_right, grad_left, right, left, *acc)
-        index = [(me - step) % NZ, (me + step) % NZ]
-        acc = project_call([right, left], [grad_right, grad_left], index, projections, acc)
+        index += [(me - step) % NZ, (me + step) % NZ]
+        chunks += [right, left]
+        grad_chunks += [grad_right, grad_left]
     far = (shift(right, 1), shift(grad_left, -1))
-    acc, squares = acc
+    count = len(chunks)
+    acc, squares = pl.pallas_call(
+        functools.partial(project, count),
+        out_shape=(
+            jax.ShapeDtypeStruct((TOK, 768), F32),
+            jax.ShapeDtypeStruct((TOK, 1), F32),
+        ),
+        in_specs=[SMEM] + [ANY] * (2 * count + 3),
+        out_specs=(ANY, ANY),
+        scratch_shapes=[
+            pltpu.VMEM((count, TOK, FEAT), BF),
+            pltpu.VMEM((count, TOK, FEAT), BF),
+            pltpu.VMEM((count, FEAT, 256), BF),
+            pltpu.VMEM((count, 224, FEAT), BF),
+            pltpu.VMEM((count, 256, FEAT), BF),
+            pltpu.VMEM((TOK, 768), F32),
+            pltpu.VMEM((TOK, 1), F32),
+            pltpu.SemaphoreType.DMA((count, 5)),
+            pltpu.SemaphoreType.DMA((2,)),
+        ],
+        compiler_params=ROOM,
+        cost_estimate=cost(2 * count * TOK * FEAT * 736, 16_000_000),
+        name="project",
+    )(jnp.stack(index), *chunks, *grad_chunks, *projections)
 
     asked = exchange(wanted, "dp")
     part = exchange(part, Z).transpose(1, 0, 2).reshape(144, HALF)
-    kv_weights = lax.all_gather(part[:112], "dp", axis=0, tiled=True).reshape(16, 2, 112, HALF)
-    q_rows, _ = tie(part[112:], right)
-    q_weights = lax.all_gather(q_rows, "dp", axis=0, tiled=True).reshape(NDP, 2, 16, HALF)
+    weights = lax.all_gather(part, "dp", axis=0, tiled=True).reshape(16, 2, 144, HALF)
     returned = exchange(database[asked].reshape(NDP, NEIGH * NLEN // NZ, DE), "dp")
     fetched = exchange(returned[jnp.concatenate([owner, owner[:1]])], Z).reshape(KEYS, DE)
     enc_q = pl.pallas_call(
         encoder_queries,
         out_shape=jax.ShapeDtypeStruct((KEYS, DE), BF),
-        in_specs=[HBM, HBM],
-        out_specs=VMEM,
-        scratch_shapes=[like(fetched), like(encoder_query), pltpu.SemaphoreType.DMA((2,))],
+        in_specs=[ANY, ANY],
+        out_specs=ANY,
+        scratch_shapes=[
+            like(fetched), like(encoder_query), like(fetched), pltpu.SemaphoreType.DMA((3,))
+        ],
         compiler_params=PARAMS,
         cost_estimate=cost(2 * KEYS * DE * DE, 3_000_000),
         name="encoder_queries",
@@ -390,18 +380,23 @@
             jax.ShapeDtypeStruct((NZ, SEG, 768), BF),
             jax.ShapeDtypeStruct((TOK, 1), F32),
         ),
-        in_specs=[SMEM] + [ANY] * 2 + [VMEM] * 2 + [HBM] * 3,
-        out_specs=(VMEM, VMEM),
+        in_specs=[SMEM] + [ANY] * 7,
+        out_specs=(ANY, ANY),
         scratch_shapes=[
             pltpu.VMEM((TOK, FEAT), BF),
             pltpu.VMEM((TOK, FEAT), BF),
+            like(acc),
+            like(squares),
             pltpu.VMEM((FEAT, 256), BF),
             pltpu.VMEM((224, FEAT), BF),
             pltpu.VMEM((256, FEAT), BF),
-            pltpu.SemaphoreType.DMA((5,)),
+            pltpu.VMEM((NZ, SEG, 768), BF),
+            like(squares),
+            pltpu.SemaphoreType.DMA((7,)),
+            pltpu.SemaphoreType.DMA((2,)),
         ],
         compiler_params=PARAMS,
-        cost_estimate=cost(2 * TOK * FEAT * 736, 4_000_000),
+        cost_estimate=cost(KNOB, 4_000_000),
         name="project_last",
     )(
         jnp.stack([(me + 4) % NZ]), far[0], far[1], acc, squares, *projections
@@ -411,11 +406,11 @@
     grad_query = pl.pallas_call(
         attention,
         out_shape=jax.ShapeDtypeStruct((SEG, 2 * HALF + HEAD), BF),
-        in_specs=[HBM, ANY, HBM, HBM, HBM],
+        in_specs=[ANY] * 5,
         out_specs=VMEM,
         scratch_shapes=[like(x) for x in operands]
         + [
-            like(kv_weights.transpose(1, 0, 2, 3)),
+            pltpu.VMEM((2, 16, 112, HALF), BF),
             pltpu.VMEM((2, KEYS, HALF), BF),
             pltpu.VMEM((2, KEYS, HALF), BF),
             pltpu.VMEM((KEYS, DE), BF),
@@ -424,12 +419,12 @@
         compiler_params=PARAMS,
         cost_estimate=cost(4_000_000_000, 12_000_000),
         name="attention",
-    )(*operands, kv_weights)
+    )(*operands, weights)
 
     def finished(group, offsets, out):
         sources = jnp.stack([(me + offset) % NZ for offset in offsets])
         starts = (0, SEG // 2) if group[0].shape[0] < SEG else (0,) * len(group)
-        return finish_call(group, starts, sources, hidden, inverse, q_weights, out)
+        return finish_call(group, starts, sources, hidden, inverse, weights.reshape(NDP, 144, HALF), out)
 
     right = left = grad_query
     group, offsets, out = [grad_query], [0], None

time: 239 us -> 220 us (0.921)
  local copies, waits for them, and re-layouts: 44.9 us -> 8.71 us
  waiting for transfers between devices: 52.5 us -> 74.6 us
  starting transfers between devices: 65.6 us -> 53.6 us
  Pallas kernels: 42.5 us -> 47.1 us
  blocking collectives: 17.1 us -> 20.8 us
    unnamed x61 -> x43, local copies, waits for them, and re-layouts: 33.8 us -> 1.76 us
    ppermute x22, waiting for transfers between devices: 31.9 us -> 44.6 us  [shift(): return lax.ppermute(x, Z, [(i, (i + by) % NZ) for i in range(NZ)])]
    all_to_all x4, waiting for transfers between devices: 20.5 us -> 30 us  [exchange(): return lax.all_to_all(x, axis, split_axis=0, concat_axis=0, tiled=True)]
    all_to_all x4, starting transfers between devices: 26.7 us -> 20.3 us  [exchange(): return lax.all_to_all(x, axis, split_axis=0, concat_axis=0, tiled=True)]
    ppermute x22, starting transfers between devices: 38.9 us -> 33.2 us  [shift(): return lax.ppermute(x, Z, [(i, (i + by) % NZ) for i in range(NZ)])]
    pallas_call x5, Pallas kernels: 15.3 us -> 19.2 us  [finish_call(): pl.pallas_call(functools.partial(finish, starts, first), out_shape=jax.Sh...]
    all_to_all x1, blocking collectives: 17.1 us -> 20.8 us  [exchange(): return lax.all_to_all(x, axis, split_axis=0, concat_axis=0, tiled=True)]
    pallas_call x4 -> x1, Pallas kernels: 10.7 us -> 7.78 us  [shards(): pl.pallas_call(functools.partial(project, count), out_shape=(jax.ShapeDty...]
  transfers between devices with their start and end apart: 28 -> 27, of which waited for: 9 -> 12; matrix products, arithmetic and copies ran while one was open for 5% -> 2% of each run, Pallas kernels for 17% -> 14%
where the time goes in v2:
time: 220 us; the launch traced here: 219 us
  waiting for transfers between devices  74.6 us (34%)
  starting transfers between devices  53.6 us (24%)
  Pallas kernels  47.1 us (21%)
  blocking collectives  20.8 us (9%)
  between operations  13.7 us (6%)
  local copies, waits for them, and re-layouts  8.71 us (4%)
    ppermute x22, waiting for transfers between devices, shift(): return lax.ppermute(x, Z, [(i, (i + by) % NZ) for i in range(NZ)])  44.6 us
    ppermute x22, starting transfers between devices, shift(): return lax.ppermute(x, Z, [(i, (i + by) % NZ) for i in range(NZ)])  33.2 us
    all_to_all x4, waiting for transfers between devices, exchange(): return lax.all_to_all(x, axis, split_axis=0, concat_axis=0, tiled=True)  30 us
    all_to_all x1, blocking collectives, exchange(): return lax.all_to_all(x, axis, split_axis=0, concat_axis=0, tiled=True)  20.8 us
    all_to_all x4, starting transfers between devices, exchange(): return lax.all_to_all(x, axis, split_axis=0, concat_axis=0, tiled=True)  20.3 us
    pallas_call x5, Pallas kernels, finish_call(): pl.pallas_call(functools.partial(finish, starts, first), out_shape=jax.Sh...  19.2 us
    pallas_call x1, Pallas kernels, shards(): pl.pallas_call(attention, out_shape=jax.ShapeDtypeStruct((SEG, 2 * HALF +...  13.5 us
    pallas_call x1, Pallas kernels, shards(): pl.pallas_call(functools.partial(project, count), out_shape=(jax.ShapeDty...  7.78 us
  transfers between devices with their start and end apart: 27, of which 12 were waited for; matrix products, arithmetic and copies ran while one was open for 2% of the time, Pallas kernels for 14%

profile of v2, /device:TPU:2, one launch (start us, length us, event | category | flops | bytes accessed | tf_op | source)
XLA Modules:
  0.0 219.2 jit_solution(11574479419158656294)
XLA Ops:
  6.6 1.0 constant_dynamic-slice_fusion
  7.6 0.8 dynamic_slice.6
  8.5 20.8 %all_to_all.32 = bf16[8,144,128]{2,1,0:T(8,128)(2,1)S(1)} all-to-all(bf16[8,144,128]{2,1,0:T(8,128)(2,1)S(1)} %pad_maximum_fusion), channel_id=1, replica_groups=mesh['group'=2,'dp'=32,'tensor'=4] {'group','tensor'}, dimensions={0} | all-to-all | bytes 589824 | tf_op jit(solution)/shard_map/all_to_all | solution.py:56
  29.3 0.7 copy_bitcast_fusion
  30.1 0.1 copy.35
  30.3 0.1 multiply_reduce_fusion
  30.3 0.7 copy.36
  31.0 7.6 %all-to-all-start = ((s32[32,1,2]{2,1,0:T(1,128)}), s32[32,1,2]{2,1,0:T(1,128)S(1)}, u32[]{:S(2)}, u32[]{:S(2)}) async-start(s32[32,1,2]{2,1,0:T(1,128)} %copy.36), calls=%async_computation | async-start | bytes 32768 | tf_op jit(solution)/shard_map/all_to_all | solution.py:56
  38.7 0.6 collective-permute-start
  39.3 2.7 %collective-permute-start.4 = (bf16[448,512]{1,0:T(8,128)(2,1)S(1)}, bf16[448,512]{1,0:T(8,128)(2,1)}, u32[]{:S(2)}, u32[]{:S(2)}) collective-permute-start(bf16[448,512]{1,0:T(8,128)(2,1)S(1)} %copy-done.8), channel_id=1, source_target_pairs={{0,131},{1,0},{2,1},{3,2},{128,3},{129,128},{130,129},{131,130},{4... | collective-permute-start | bytes 1376264 | tf_op jit(solution)/shard_map/ppermute | solution.py:48
  42.0 2.7 %all-to-all-done = s32[32,1,2]{2,1,0:T(1,128)S(1)} async-done(((s32[32,1,2]{2,1,0:T(1,128)}), s32[32,1,2]{2,1,0:T(1,128)S(1)}, u32[]{:S(2)}, u32[]{:S(2)}) %all-to-all-start) | async-done | bytes 288 | tf_op jit(solution)/shard_map/all_to_all | solution.py:56
  44.7 0.1 copy.37
  44.8 0.1 copy.38
  44.9 0.1 reshape.154
  45.0 2.0 gather_fusion
  47.0 5.1 %all-to-all-start.1 = ((bf16[32,32,896]{2,1,0:T(8,128)(2,1)}), bf16[32,32,896]{2,1,0:T(8,128)(2,1)S(1)}, u32[]{:S(2)}, u32[]{:S(2)}) async-start(bf16[32,32,896]{2,1,0:T(8,128)(2,1)} %bitcast.4), calls=%async_computation.1 | async-start | bytes 3670016 | tf_op jit(solution)/shard_map/all_to_all | solution.py:56
  52.1 0.4 collective-permute-start.8
  52.5 1.7 collective-permute-start.11
  54.2 0.6 collective-permute-start.1
  54.8 2.7 %collective-permute-start.5 = (bf16[448,512]{1,0:T(8,128)(2,1)}, bf16[448,512]{1,0:T(8,128)(2,1)S(1)}, u32[]{:S(2)}, u32[]{:S(2)}) collective-permute-start(bf16[448,512]{1,0:T(8,128)(2,1)} %collective-permute-done.4.refs_9_), channel_id=1, source_target_pairs={{0,131},{1,0},{2,1},{3,2},{128,3},{129,128},{130,129},{131,130},{4... | collective-permute-start | bytes 1376264 | tf_op jit(solution)/shard_map/ppermute | solution.py:48
  57.5 8.1 %collective-permute-done.8.refs_2_ = bf16[448,512]{1,0:T(8,128)(2,1)S(1)} collective-permute-done((bf16[448,512]{1,0:T(8,128)(2,1)S(1)}, bf16[448,512]{1,0:T(8,128)(2,1)S(1)}, u32[]{:S(2)}, u32[]{:S(2)}) %collective-permute-start.8) | collective-permute-done | bytes 458784 | tf_op jit(solution)/shard_map/ppermute | solution.py:48
  65.6 1.6 collective-permute-start.9
  67.2 0.5 collective-permute-start.12
  67.7 9.3 %collective-permute-done.1.refs_3_ = bf16[448,512]{1,0:T(8,128)(2,1)S(1)} collective-permute-done((bf16[448,512]{1,0:T(8,128)(2,1)}, bf16[448,512]{1,0:T(8,128)(2,1)S(1)}, u32[]{:S(2)}, u32[]{:S(2)}) %collective-permute-start.1) | collective-permute-done | bytes 458784 | tf_op jit(solution)/shard_map/ppermute | solution.py:48
  77.0 0.5 collective-permute-start.2
  77.5 2.8 %collective-permute-start.6 = (bf16[448,512]{1,0:T(8,128)(2,1)S(1)}, bf16[448,512]{1,0:T(8,128)(2,1)S(1)}, u32[]{:S(2)}, u32[]{:S(2)}) collective-permute-start(bf16[448,512]{1,0:T(8,128)(2,1)S(1)} %collective-permute-done.5.refs_11_), channel_id=1, source_target_pairs={{0,131},{1,0},{2,1},{3,2},{128,3},{129,128},{130,129},{131,130},{4... | collective-permute-start | bytes 1376264 | tf_op jit(solution)/shard_map/ppermute | solution.py:48
  80.2 5.1 %collective-permute-done.9.refs_4_ = bf16[448,512]{1,0:T(8,128)(2,1)} collective-permute-done((bf16[448,512]{1,0:T(8,128)(2,1)S(1)}, bf16[448,512]{1,0:T(8,128)(2,1)}, u32[]{:S(2)}, u32[]{:S(2)}) %collective-permute-start.9) | collective-permute-done | bytes 458784 | tf_op jit(solution)/shard_map/ppermute | solution.py:48
  85.3 1.6 collective-permute-start.10
  86.9 0.5 collective-permute-start.13
  87.4 9.2 %collective-permute-done.2.refs_5_ = bf16[448,512]{1,0:T(8,128)(2,1)S(1)} collective-permute-done((bf16[448,512]{1,0:T(8,128)(2,1)S(1)}, bf16[448,512]{1,0:T(8,128)(2,1)S(1)}, u32[]{:S(2)}, u32[]{:S(2)}) %collective-permute-start.2) | collective-permute-done | bytes 458784 | tf_op jit(solution)/shard_map/ppermute | solution.py:48
  96.6 0.5 collective-permute-start.3
  97.1 2.8 %collective-permute-start.7 = (bf16[448,512]{1,0:T(8,128)(2,1)S(1)}, bf16[448,512]{1,0:T(8,128)(2,1)}, u32[]{:S(2)}, u32[]{:S(2)}) collective-permute-start(bf16[448,512]{1,0:T(8,128)(2,1)S(1)} %collective-permute-done.6.refs_13_), channel_id=1, source_target_pairs={{0,131},{1,0},{2,1},{3,2},{128,3},{129,128},{130,129},{131,130},{4... | collective-permute-start | bytes 1376264 | tf_op jit(solution)/shard_map/ppermute | solution.py:48
  99.9 0.1 stack.59.index_ref
  100.0 0.1 fusion.1
  100.1 4.9 %collective-permute-done.10.refs_6_ = bf16[448,512]{1,0:T(8,128)(2,1)} collective-permute-done((bf16[448,512]{1,0:T(8,128)(2,1)}, bf16[448,512]{1,0:T(8,128)(2,1)}, u32[]{:S(2)}, u32[]{:S(2)}) %collective-permute-start.10) | collective-permute-done | bytes 458784 | tf_op jit(solution)/shard_map/ppermute | solution.py:48
  105.0 1.6 collective-permute-done.13.refs_12_
  106.6 7.8 %project.1 = (f32[448,768]{1,0:T(8,128)}, f32[448,1]{1,0:T(8,128)S(1)}) custom-call(s32[7]{0:T(128)S(1)} %stack.59.index_ref, bf16[448,512]{1,0:T(8,128)(2,1)} %refs_3_.7, bf16[448,512]{1,0:T(8,128)(2,1)} %collective-permute-done.refs_1_, bf16[448,512]{1,0:T(8,128)(2,1)} %copy-done.9, bf16[448,512]{1,0:T(8,128)(2,1)} %copy-done.11, ...), custom_call_target="tpu_custom_call" | custom-call | flops 2363490304 | bytes 16000000 | tf_op jit(solution)/shard_map/project/pallas_call | solution.py:335
  114.4 0.7 copy-done.2
  115.1 1.4 gather_fusion.1
  116.4 4.1 %all-to-all-start.2 = ((bf16[8,32,896]{2,1,0:T(8,128)(2,1)}), bf16[8,32,896]{2,1,0:T(8,128)(2,1)S(1)}, u32[]{:S(2)}, u32[]{:S(2)}) async-start(bf16[8,32,896]{2,1,0:T(8,128)(2,1)} %gather_fusion.1), calls=%async_computation.2 | async-start | bytes 917504 | tf_op jit(solution)/shard_map/all_to_all | solution.py:56
  120.5 3.6 %project_last.1 = (bf16[8,64,768]{2,1,0:T(8,128)(2,1)}, f32[448,1]{1,0:T(8,128)}) custom-call(s32[1]{0:T(128)} %bitcast.index_ref, bf16[448,512]{1,0:T(8,128)(2,1)} %collective-permute-done.3.hidden_hbm, bf16[448,512]{1,0:T(8,128)(2,1)} %collective-permute-done.7.cot_hbm, f32[448,768]{1,0:T(8,128)} %get-tuple-element.18.acc_hbm, f32[448,1]{1,0:T(8,128)} %copy-done.2, ...), custom_call_target="tpu_custom_call" | custom-call | flops 20000000000 | bytes 4000000 | tf_op jit(solution)/shard_map/project_last/pallas_call | solution.py:377
  124.1 10.5 %all-to-all-done.2 = bf16[8,32,896]{2,1,0:T(8,128)(2,1)S(1)} async-done(((bf16[8,32,896]{2,1,0:T(8,128)(2,1)}), bf16[8,32,896]{2,1,0:T(8,128)(2,1)S(1)}, u32[]{:S(2)}, u32[]{:S(2)}) %all-to-all-start.2) | async-done | bytes 458784 | tf_op jit(solution)/shard_map/all_to_all | solution.py:56
  134.7 3.5 %all-to-all-start.3 = ((bf16[8,64,768]{2,1,0:T(8,128)(2,1)}), bf16[8,64,768]{2,1,0:T(8,128)(2,1)S(1)}, u32[]{:S(2)}, u32[]{:S(2)}) async-start(bf16[8,64,768]{2,1,0:T(8,128)(2,1)} %get-tuple-element.20), calls=%async_computation.3 | async-start | bytes 1572864 | tf_op jit(solution)/shard_map/all_to_all | solution.py:56
  138.2 3.1 %encoder_queries.1.enc_q_hbm = bf16[256,896]{1,0:T(8,128)(2,1)} custom-call(bf16[256,896]{1,0:T(8,128)(2,1)} %bitcast.42, bf16[896,896]{1,0:T(8,128)(2,1)} %weight_hbm.1), custom_call_target="tpu_custom_call" | custom-call | flops 411041792 | bytes 3000000 | tf_op jit(solution)/shard_map/encoder_queries/pallas_call | solution.py:364
  141.3 16.7 %all-to-all-done.3.got_hbm = bf16[8,64,768]{2,1,0:T(8,128)(2,1)S(1)} async-done(((bf16[8,64,768]{2,1,0:T(8,128)(2,1)}), bf16[8,64,768]{2,1,0:T(8,128)(2,1)S(1)}, u32[]{:S(2)}, u32[]{:S(2)}) %all-to-all-start.3) | async-done | bytes 786464 | tf_op jit(solution)/shard_map/all_to_all | solution.py:56
  158.0 0.9 copy-done.5
  158.9 13.5 %attention.1.refs_1_ = bf16[64,2176]{1,0:T(8,128)(2,1)} custom-call(bf16[256,896]{1,0:T(8,128)(2,1)} %bitcast.43, bf16[256,896]{1,0:T(8,128)(2,1)} %encoder_queries.1.enc_q_hbm, bf16[8,64,768]{2,1,0:T(8,128)(2,1)} %copy-done.5, bf16[896,896]{1,0:T(8,128)(2,1)} %enc_out_hbm.1, bf16[16,2,144,1024]{3,2,1,0:T(8,128)(2,1)} %bitcast.33), custom_call_target="tpu_custom_call" | custom-call | flops 4000000000 | bytes 12000000 | tf_op jit(solution)/shard_map/attention/pallas_call | solution.py:406
  172.4 0.8 collective-permute-start.14
  173.2 2.7 %collective-permute-start.15 = (bf16[64,2176]{1,0:T(8,128)(2,1)}, bf16[64,2176]{1,0:T(8,128)(2,1)S(1)}, u32[]{:S(2)}, u32[]{:S(2)}) collective-permute-start(bf16[64,2176]{1,0:T(8,128)(2,1)} %attention.1.refs_1_), channel_id=1, source_target_pairs={{0,131},{1,0},{2,1},{3,2},{128,3},{129,128},{130,129},{131,130},{4... | collective-permute-start | bytes 835592 | tf_op jit(solution)/shard_map/ppermute | solution.py:48
  176.0 3.3 %finish.5.refs_6_ = bf16[448,512]{1,0:T(8,128)(2,1)} custom-call(s32[1]{0:T(128)} %bitcast.21.refs_0_, bf16[64,2176]{1,0:T(8,128)(2,1)} %attention.1.refs_1_, bf16[448,512]{1,0:T(8,128)(2,1)} %refs_3_.7, f32[448,1]{1,0:T(8,128)S(1)} %copy-done.1, bf16[32,144,1024]{2,1,0:T(8,128)(2,1)} %bitcast.34), custom_call_target="tpu_custom_call" | custom-call | flops 134217728 | bytes 4000000 | tf_op jit(solution)/shard_map/finish/pallas_call | solution.py:273
  179.3 2.2 %collective-permute-done.14.refs_1_ = bf16[64,2176]{1,0:T(8,128)(2,1)S(1)} collective-permute-done((bf16[64,2176]{1,0:T(8,128)(2,1)}, bf16[64,2176]{1,0:T(8,128)(2,1)S(1)}, u32[]{:S(2)}, u32[]{:S(2)}) %collective-permute-start.14) | collective-permute-done | bytes 278560 | tf_op jit(solution)/shard_map/ppermute | solution.py:48
  181.5 0.1 collective-permute-start.16
  181.6 3.4 %collective-permute-start.17 = (bf16[64,2176]{1,0:T(8,128)(2,1)S(1)}, bf16[64,2176]{1,0:T(8,128)(2,1)S(1)}, u32[]{:S(2)}, u32[]{:S(2)}) collective-permute-start(bf16[64,2176]{1,0:T(8,128)(2,1)S(1)} %collective-permute-done.15.refs_2_), channel_id=1, source_target_pairs={{0,131},{1,0},{2,1},{3,2},{128,3},{129,128},{130,129},{131,130},{4... | collective-permute-start | bytes 835592 | tf_op jit(solution)/shard_map/ppermute | solution.py:48
  185.0 0.1 pad_add_fusion.1.refs_0_
  185.1 4.1 %finish.6.refs_6_ = bf16[448,512]{1,0:T(8,128)(2,1)} custom-call(s32[2]{0:T(128)S(1)} %pad_add_fusion.1.refs_0_, bf16[64,2176]{1,0:T(8,128)(2,1)} %copy-done.15, bf16[64,2176]{1,0:T(8,128)(2,1)} %copy-done.16, bf16[448,512]{1,0:T(8,128)(2,1)} %refs_3_.7, f32[448,1]{1,0:T(8,128)S(1)} %copy-done.1, ...), custom_call_target="tpu_custom_call", output_to_operand_aliasing={{}: (6, {})} | custom-call | flops 268435456 | bytes 4000000 | tf_op jit(solution)/shard_map/finish/pallas_call | solution.py:273
  189.2 2.3 %collective-permute-done.16.refs_1_ = bf16[64,2176]{1,0:T(8,128)(2,1)S(1)} collective-permute-done((bf16[64,2176]{1,0:T(8,128)(2,1)S(1)}, bf16[64,2176]{1,0:T(8,128)(2,1)S(1)}, u32[]{:S(2)}, u32[]{:S(2)}) %collective-permute-start.16) | collective-permute-done | bytes 278560 | tf_op jit(solution)/shard_map/ppermute | solution.py:48
  191.5 0.1 collective-permute-start.18
  191.5 3.5 %collective-permute-start.19 = (bf16[64,2176]{1,0:T(8,128)(2,1)S(1)}, bf16[64,2176]{1,0:T(8,128)(2,1)S(1)}, u32[]{:S(2)}, u32[]{:S(2)}) collective-permute-start(bf16[64,2176]{1,0:T(8,128)(2,1)S(1)} %collective-permute-done.17.refs_2_), channel_id=1, source_target_pairs={{0,131},{1,0},{2,1},{3,2},{128,3},{129,128},{130,129},{131,130},{4... | collective-permute-start | bytes 835592 | tf_op jit(solution)/shard_map/ppermute | solution.py:48
  195.1 4.1 %finish.7.refs_6_ = bf16[448,512]{1,0:T(8,128)(2,1)} custom-call(s32[2]{0:T(128)S(1)} %pad_add_fusion.2.refs_0_, bf16[64,2176]{1,0:T(8,128)(2,1)} %copy-done.17, bf16[64,2176]{1,0:T(8,128)(2,1)} %copy-done.18, bf16[448,512]{1,0:T(8,128)(2,1)} %refs_3_.7, f32[448,1]{1,0:T(8,128)S(1)} %copy-done.1, ...), custom_call_target="tpu_custom_call", output_to_operand_aliasing={{}: (6, {})} | custom-call | flops 268435456 | bytes 4000000 | tf_op jit(solution)/shard_map/finish/pallas_call | solution.py:273
  199.2 1.8 collective-permute-done.18.refs_1_
  201.0 0.1 collective-permute-start.20
  201.1 3.3 %collective-permute-start.21 = (bf16[32,2176]{1,0:T(8,128)(2,1)S(1)}, bf16[32,2176]{1,0:T(8,128)(2,1)S(1)}, u32[]{:S(2)}, u32[]{:S(2)}) collective-permute-start(bf16[32,2176]{1,0:T(8,128)(2,1)S(1)} %slice.12), channel_id=1, source_target_pairs={{0,131},{1,0},{2,1},{3,2},{128,3},{129,128},{130,129},{131,130},{4... | collective-permute-start | bytes 417800 | tf_op jit(solution)/shard_map/ppermute | solution.py:48
  204.6 4.1 %finish.8.refs_6_ = bf16[448,512]{1,0:T(8,128)(2,1)} custom-call(s32[2]{0:T(128)S(1)} %pad_add_fusion.3.refs_0_, bf16[64,2176]{1,0:T(8,128)(2,1)} %copy-done.6, bf16[64,2176]{1,0:T(8,128)(2,1)} %copy-done.7, bf16[448,512]{1,0:T(8,128)(2,1)} %refs_3_.7, f32[448,1]{1,0:T(8,128)S(1)} %copy-done.1, ...), custom_call_target="tpu_custom_call", output_to_operand_aliasing={{}: (6, {})} | custom-call | flops 268435456 | bytes 4000000 | tf_op jit(solution)/shard_map/finish/pallas_call | solution.py:273
  208.7 3.7 %finish.9 = bf16[448,512]{1,0:T(8,128)(2,1)} custom-call(s32[2]{0:T(128)S(1)} %pad_add_fusion.refs_0_, bf16[32,2176]{1,0:T(8,128)(2,1)S(1)} %collective-permute-done.20.refs_1_, bf16[32,2176]{1,0:T(8,128)(2,1)S(1)} %collective-permute-done.21.refs_2_, bf16[448,512]{1,0:T(8,128)(2,1)} %refs_3_.7, ...), custom_call_target="tpu_custom_call", output_to_operand_aliasing={{}: (6, {})} | custom-call | flops 134217728 | bytes 4000000 | tf_op jit(solution)/shard_map/finish/pallas_call | solution.py:273
  (70 shorter events, 0.7 us)
Async XLA Ops:
  6.5 38.5 %copy-start = (bf16[16,16,896]{2,1,0:T(8,128)(2,1)S(1)}, bf16[16,16,896]{2,1,0:T(8,128)(2,1)}, u32[]{:S(2)}) copy-start(bf16[16,16,896]{2,1,0:T(8,128)(2,1)} %param.19) | copy-start | bytes 1376260
  6.5 23.5 %copy-start.19 = (s32[7,2]{0,1:T(2,128)S(1)}, s32[7,2]{0,1:T(2,128)}, u32[]{:S(2)}) copy-start(s32[7,2]{0,1:T(2,128)} %param.20) | copy-start | bytes 172
  6.5 23.6 %copy-start.20 = (s32[7,1]{0,1:T(1,128)S(1)}, s32[7,1]{0,1:T(1,128)}, u32[]{:S(2)}) copy-start(s32[7,1]{0,1:T(1,128)} %param.21) | copy-start | bytes 88
  6.5 32.1 %copy-start.3 = (bf16[448,512]{1,0:T(8,128)(2,1)S(1)}, bf16[448,512]{1,0:T(8,128)(2,1)}, u32[]{:S(2)}) copy-start(bf16[448,512]{1,0:T(8,128)(2,1)} %refs_3_.7) | copy-start | bytes 1376260
  6.5 32.8 %copy-start.8 = (bf16[448,512]{1,0:T(8,128)(2,1)S(1)}, bf16[448,512]{1,0:T(8,128)(2,1)}, u32[]{:S(2)}) copy-start(bf16[448,512]{1,0:T(8,128)(2,1)} %refs_7_.1) | copy-start | bytes 1376260
  6.6 151.4 %all-gather.2.cloned.1.call-start = ((), (), s32[]{:S(2)}) async-start(), calls=%async_computation.5 | async-start | bytes 9732096 | tf_op jit(solution)/shard_map/all_gather | solution.py:361
  31.0 13.7 %all-to-all-start = ((s32[32,1,2]{2,1,0:T(1,128)}), s32[32,1,2]{2,1,0:T(1,128)S(1)}, u32[]{:S(2)}, u32[]{:S(2)}) async-start(s32[32,1,2]{2,1,0:T(1,128)} %copy.36), calls=%async_computation | async-start | bytes 32768 | tf_op jit(solution)/shard_map/all_to_all | solution.py:56
  38.7 15.6 %collective-permute-start = (bf16[448,512]{1,0:T(8,128)(2,1)S(1)}, bf16[448,512]{1,0:T(8,128)(2,1)}, u32[]{:S(2)}, u32[]{:S(2)}) collective-permute-start(bf16[448,512]{1,0:T(8,128)(2,1)S(1)} %copy-done.3), channel_id=1, source_target_pairs={{0,1},{1,2},{2,3},{3,128},{128,129},{129,130},{130,131},{131,0},{4... | collective-permute-start | bytes 1376264 | tf_op jit(solution)/shard_map/ppermute | solution.py:48
  39.3 15.5 %collective-permute-start.4 = (bf16[448,512]{1,0:T(8,128)(2,1)S(1)}, bf16[448,512]{1,0:T(8,128)(2,1)}, u32[]{:S(2)}, u32[]{:S(2)}) collective-permute-start(bf16[448,512]{1,0:T(8,128)(2,1)S(1)} %copy-done.8), channel_id=1, source_target_pairs={{0,131},{1,0},{2,1},{3,2},{128,3},{129,128},{130,129},{131,130},{4... | collective-permute-start | bytes 1376264 | tf_op jit(solution)/shard_map/ppermute | solution.py:48
  47.0 68.0 %all-to-all-start.1 = ((bf16[32,32,896]{2,1,0:T(8,128)(2,1)}), bf16[32,32,896]{2,1,0:T(8,128)(2,1)S(1)}, u32[]{:S(2)}, u32[]{:S(2)}) async-start(bf16[32,32,896]{2,1,0:T(8,128)(2,1)} %bitcast.4), calls=%async_computation.1 | async-start | bytes 3670016 | tf_op jit(solution)/shard_map/all_to_all | solution.py:56
  52.1 13.4 %collective-permute-start.8 = (bf16[448,512]{1,0:T(8,128)(2,1)S(1)}, bf16[448,512]{1,0:T(8,128)(2,1)S(1)}, u32[]{:S(2)}, u32[]{:S(2)}) collective-permute-start(bf16[448,512]{1,0:T(8,128)(2,1)S(1)} %copy-done.3), channel_id=1, source_target_pairs={{0,131},{1,0},{2,1},{3,2},{128,3},{129,128},{130,129},{131,130},{4... | collective-permute-start | bytes 1376264 | tf_op jit(solution)/shard_map/ppermute | solution.py:48
  52.5 14.6 %collective-permute-start.11 = (bf16[448,512]{1,0:T(8,128)(2,1)S(1)}, bf16[448,512]{1,0:T(8,128)(2,1)S(1)}, u32[]{:S(2)}, u32[]{:S(2)}) collective-permute-start(bf16[448,512]{1,0:T(8,128)(2,1)S(1)} %copy-done.8), channel_id=1, source_target_pairs={{0,1},{1,2},{2,3},{3,128},{128,129},{129,130},{130,131},{131,0},{4... | collective-permute-start | bytes 1376264 | tf_op jit(solution)/shard_map/ppermute | solution.py:48
  54.2 22.8 %collective-permute-start.1 = (bf16[448,512]{1,0:T(8,128)(2,1)}, bf16[448,512]{1,0:T(8,128)(2,1)S(1)}, u32[]{:S(2)}, u32[]{:S(2)}) collective-permute-start(bf16[448,512]{1,0:T(8,128)(2,1)} %collective-permute-done.refs_1_), channel_id=1, source_target_pairs={{0,1},{1,2},{2,3},{3,128},{128,129},{129,130},{130,131},{131,0},{4... | collective-permute-start | bytes 1376264 | tf_op jit(solution)/shard_map/ppermute | solution.py:48
  54.8 22.7 %collective-permute-start.5 = (bf16[448,512]{1,0:T(8,128)(2,1)}, bf16[448,512]{1,0:T(8,128)(2,1)S(1)}, u32[]{:S(2)}, u32[]{:S(2)}) collective-permute-start(bf16[448,512]{1,0:T(8,128)(2,1)} %collective-permute-done.4.refs_9_), channel_id=1, source_target_pairs={{0,131},{1,0},{2,1},{3,2},{128,3},{129,128},{130,129},{131,130},{4... | collective-permute-start | bytes 1376264 | tf_op jit(solution)/shard_map/ppermute | solution.py:48
  65.6 1.6 copy-start.9
  65.6 19.8 %collective-permute-start.9 = (bf16[448,512]{1,0:T(8,128)(2,1)S(1)}, bf16[448,512]{1,0:T(8,128)(2,1)}, u32[]{:S(2)}, u32[]{:S(2)}) collective-permute-start(bf16[448,512]{1,0:T(8,128)(2,1)S(1)} %collective-permute-done.8.refs_2_), channel_id=1, source_target_pairs={{0,131},{1,0},{2,1},{3,2},{128,3},{129,128},{130,129},{131,130},{4... | collective-permute-start | bytes 1376264 | tf_op jit(solution)/shard_map/ppermute | solution.py:48
  67.2 18.2 %copy-start.10 = (bf16[448,512]{1,0:T(8,128)(2,1)}, bf16[448,512]{1,0:T(8,128)(2,1)S(1)}, u32[]{:S(2)}) copy-start(bf16[448,512]{1,0:T(8,128)(2,1)S(1)} %collective-permute-done.11.refs_8_) | copy-start | bytes 1376260
  67.2 19.8 %collective-permute-start.12 = (bf16[448,512]{1,0:T(8,128)(2,1)S(1)}, bf16[448,512]{1,0:T(8,128)(2,1)}, u32[]{:S(2)}, u32[]{:S(2)}) collective-permute-start(bf16[448,512]{1,0:T(8,128)(2,1)S(1)} %collective-permute-done.11.refs_8_), channel_id=1, source_target_pairs={{0,1},{1,2},{2,3},{3,128},{128,129},{129,130},{130,131},{131,0},{4... | collective-permute-start | bytes 1376264 | tf_op jit(solution)/shard_map/ppermute | solution.py:48
  77.0 9.9 %copy-start.11 = (bf16[448,512]{1,0:T(8,128)(2,1)}, bf16[448,512]{1,0:T(8,128)(2,1)S(1)}, u32[]{:S(2)}) copy-start(bf16[448,512]{1,0:T(8,128)(2,1)S(1)} %collective-permute-done.1.refs_3_) | copy-start | bytes 1376260
  77.0 19.7 %collective-permute-start.2 = (bf16[448,512]{1,0:T(8,128)(2,1)S(1)}, bf16[448,512]{1,0:T(8,128)(2,1)S(1)}, u32[]{:S(2)}, u32[]{:S(2)}) collective-permute-start(bf16[448,512]{1,0:T(8,128)(2,1)S(1)} %collective-permute-done.1.refs_3_), channel_id=1, source_target_pairs={{0,1},{1,2},{2,3},{3,128},{128,129},{129,130},{130,131},{131,0},{4... | collective-permute-start | bytes 1376264 | tf_op jit(solution)/shard_map/ppermute | solution.py:48
  77.5 19.2 %copy-start.12 = (bf16[448,512]{1,0:T(8,128)(2,1)}, bf16[448,512]{1,0:T(8,128)(2,1)S(1)}, u32[]{:S(2)}) copy-start(bf16[448,512]{1,0:T(8,128)(2,1)S(1)} %collective-permute-done.5.refs_11_) | copy-start | bytes 1376260
  77.5 19.7 %collective-permute-start.6 = (bf16[448,512]{1,0:T(8,128)(2,1)S(1)}, bf16[448,512]{1,0:T(8,128)(2,1)S(1)}, u32[]{:S(2)}, u32[]{:S(2)}) collective-permute-start(bf16[448,512]{1,0:T(8,128)(2,1)S(1)} %collective-permute-done.5.refs_11_), channel_id=1, source_target_pairs={{0,131},{1,0},{2,1},{3,2},{128,3},{129,128},{130,129},{131,130},{4... | collective-permute-start | bytes 1376264 | tf_op jit(solution)/shard_map/ppermute | solution.py:48
  85.3 19.7 %collective-permute-start.10 = (bf16[448,512]{1,0:T(8,128)(2,1)}, bf16[448,512]{1,0:T(8,128)(2,1)}, u32[]{:S(2)}, u32[]{:S(2)}) collective-permute-start(bf16[448,512]{1,0:T(8,128)(2,1)} %collective-permute-done.9.refs_4_), channel_id=1, source_target_pairs={{0,131},{1,0},{2,1},{3,2},{128,3},{129,128},{130,129},{131,130},{4... | collective-permute-start | bytes 1376264 | tf_op jit(solution)/shard_map/ppermute | solution.py:48
  86.9 19.7 %collective-permute-start.13 = (bf16[448,512]{1,0:T(8,128)(2,1)}, bf16[448,512]{1,0:T(8,128)(2,1)}, u32[]{:S(2)}, u32[]{:S(2)}) collective-permute-start(bf16[448,512]{1,0:T(8,128)(2,1)} %collective-permute-done.12.refs_10_), channel_id=1, source_target_pairs={{0,1},{1,2},{2,3},{3,128},{128,129},{129,130},{130,131},{131,0},{4... | collective-permute-start | bytes 1376264 | tf_op jit(solution)/shard_map/ppermute | solution.py:48
  96.6 9.9 %copy-start.13 = (bf16[448,512]{1,0:T(8,128)(2,1)}, bf16[448,512]{1,0:T(8,128)(2,1)S(1)}, u32[]{:S(2)}) copy-start(bf16[448,512]{1,0:T(8,128)(2,1)S(1)} %collective-permute-done.2.refs_5_) | copy-start | bytes 1376260
  96.6 23.9 %collective-permute-start.3 = (bf16[448,512]{1,0:T(8,128)(2,1)S(1)}, bf16[448,512]{1,0:T(8,128)(2,1)}, u32[]{:S(2)}, u32[]{:S(2)}) collective-permute-start(bf16[448,512]{1,0:T(8,128)(2,1)S(1)} %collective-permute-done.2.refs_5_), channel_id=1, source_target_pairs={{0,1},{1,2},{2,3},{3,128},{128,129},{129,130},{130,131},{131,0},{4... | collective-permute-start | bytes 1376264 | tf_op jit(solution)/shard_map/ppermute | solution.py:48
  97.1 9.5 %copy-start.14 = (bf16[448,512]{1,0:T(8,128)(2,1)}, bf16[448,512]{1,0:T(8,128)(2,1)S(1)}, u32[]{:S(2)}) copy-start(bf16[448,512]{1,0:T(8,128)(2,1)S(1)} %collective-permute-done.6.refs_13_) | copy-start | bytes 1376260
  97.1 23.4 %collective-permute-start.7 = (bf16[448,512]{1,0:T(8,128)(2,1)S(1)}, bf16[448,512]{1,0:T(8,128)(2,1)}, u32[]{:S(2)}, u32[]{:S(2)}) collective-permute-start(bf16[448,512]{1,0:T(8,128)(2,1)S(1)} %collective-permute-done.6.refs_13_), channel_id=1, source_target_pairs={{0,131},{1,0},{2,1},{3,2},{128,3},{129,128},{130,129},{131,130},{4... | collective-permute-start | bytes 1376264 | tf_op jit(solution)/shard_map/ppermute | solution.py:48
  114.4 0.7 copy-start.2
  116.4 18.2 %all-to-all-start.2 = ((bf16[8,32,896]{2,1,0:T(8,128)(2,1)}), bf16[8,32,896]{2,1,0:T(8,128)(2,1)S(1)}, u32[]{:S(2)}, u32[]{:S(2)}) async-start(bf16[8,32,896]{2,1,0:T(8,128)(2,1)} %gather_fusion.1), calls=%async_computation.2 | async-start | bytes 917504 | tf_op jit(solution)/shard_map/all_to_all | solution.py:56
  134.7 3.6 %copy-start.4 = (bf16[8,32,896]{2,1,0:T(8,128)(2,1)}, bf16[8,32,896]{2,1,0:T(8,128)(2,1)S(1)}, u32[]{:S(2)}) copy-start(bf16[8,32,896]{2,1,0:T(8,128)(2,1)S(1)} %all-to-all-done.2) | copy-start | bytes 1376260
  134.7 23.3 %all-to-all-start.3 = ((bf16[8,64,768]{2,1,0:T(8,128)(2,1)}), bf16[8,64,768]{2,1,0:T(8,128)(2,1)S(1)}, u32[]{:S(2)}, u32[]{:S(2)}) async-start(bf16[8,64,768]{2,1,0:T(8,128)(2,1)} %get-tuple-element.20), calls=%async_computation.3 | async-start | bytes 1572864 | tf_op jit(solution)/shard_map/all_to_all | solution.py:56
  158.0 0.9 copy-start.5
  158.9 17.1 %copy-start.1 = (f32[448,1]{1,0:T(8,128)S(1)}, f32[448,1]{1,0:T(8,128)}, u32[]{:S(2)}) copy-start(f32[448,1]{1,0:T(8,128)} %get-tuple-element.21.refs_3_.refs_4_) | copy-start | bytes 5380
  172.4 9.1 %collective-permute-start.14 = (bf16[64,2176]{1,0:T(8,128)(2,1)}, bf16[64,2176]{1,0:T(8,128)(2,1)S(1)}, u32[]{:S(2)}, u32[]{:S(2)}) collective-permute-start(bf16[64,2176]{1,0:T(8,128)(2,1)} %attention.1.refs_1_), channel_id=1, source_target_pairs={{0,1},{1,2},{2,3},{3,128},{128,129},{129,130},{130,131},{131,0},{4... | collective-permute-start | bytes 835592 | tf_op jit(solution)/shard_map/ppermute | solution.py:48
  173.2 8.2 %collective-permute-start.15 = (bf16[64,2176]{1,0:T(8,128)(2,1)}, bf16[64,2176]{1,0:T(8,128)(2,1)S(1)}, u32[]{:S(2)}, u32[]{:S(2)}) collective-permute-start(bf16[64,2176]{1,0:T(8,128)(2,1)} %attention.1.refs_1_), channel_id=1, source_target_pairs={{0,131},{1,0},{2,1},{3,2},{128,3},{129,128},{130,129},{131,130},{4... | collective-permute-start | bytes 835592 | tf_op jit(solution)/shard_map/ppermute | solution.py:48
  181.5 3.6 %copy-start.15 = (bf16[64,2176]{1,0:T(8,128)(2,1)}, bf16[64,2176]{1,0:T(8,128)(2,1)S(1)}, u32[]{:S(2)}) copy-start(bf16[64,2176]{1,0:T(8,128)(2,1)S(1)} %collective-permute-done.14.refs_1_) | copy-start | bytes 835588
  181.5 3.6 %copy-start.16 = (bf16[64,2176]{1,0:T(8,128)(2,1)}, bf16[64,2176]{1,0:T(8,128)(2,1)S(1)}, u32[]{:S(2)}) copy-start(bf16[64,2176]{1,0:T(8,128)(2,1)S(1)} %collective-permute-done.15.refs_2_) | copy-start | bytes 835588
  181.5 10.0 %collective-permute-start.16 = (bf16[64,2176]{1,0:T(8,128)(2,1)S(1)}, bf16[64,2176]{1,0:T(8,128)(2,1)S(1)}, u32[]{:S(2)}, u32[]{:S(2)}) collective-permute-start(bf16[64,2176]{1,0:T(8,128)(2,1)S(1)} %collective-permute-done.14.refs_1_), channel_id=1, source_target_pairs={{0,1},{1,2},{2,3},{3,128},{128,129},{129,130},{130,131},{131,0},{4... | collective-permute-start | bytes 835592 | tf_op jit(solution)/shard_map/ppermute | solution.py:48
  181.6 9.9 %collective-permute-start.17 = (bf16[64,2176]{1,0:T(8,128)(2,1)S(1)}, bf16[64,2176]{1,0:T(8,128)(2,1)S(1)}, u32[]{:S(2)}, u32[]{:S(2)}) collective-permute-start(bf16[64,2176]{1,0:T(8,128)(2,1)S(1)} %collective-permute-done.15.refs_2_), channel_id=1, source_target_pairs={{0,131},{1,0},{2,1},{3,2},{128,3},{129,128},{130,129},{131,130},{4... | collective-permute-start | bytes 835592 | tf_op jit(solution)/shard_map/ppermute | solution.py:48
  191.5 3.6 %copy-start.17 = (bf16[64,2176]{1,0:T(8,128)(2,1)}, bf16[64,2176]{1,0:T(8,128)(2,1)S(1)}, u32[]{:S(2)}) copy-start(bf16[64,2176]{1,0:T(8,128)(2,1)S(1)} %collective-permute-done.16.refs_1_) | copy-start | bytes 835588
  191.5 3.6 %copy-start.18 = (bf16[64,2176]{1,0:T(8,128)(2,1)}, bf16[64,2176]{1,0:T(8,128)(2,1)S(1)}, u32[]{:S(2)}) copy-start(bf16[64,2176]{1,0:T(8,128)(2,1)S(1)} %collective-permute-done.17.refs_2_) | copy-start | bytes 835588
  191.5 9.5 %collective-permute-start.18 = (bf16[64,2176]{1,0:T(8,128)(2,1)S(1)}, bf16[64,2176]{1,0:T(8,128)(2,1)S(1)}, u32[]{:S(2)}, u32[]{:S(2)}) collective-permute-start(bf16[64,2176]{1,0:T(8,128)(2,1)S(1)} %collective-permute-done.16.refs_1_), channel_id=1, source_target_pairs={{0,1},{1,2},{2,3},{3,128},{128,129},{129,130},{130,131},{131,0},{4... | collective-permute-start | bytes 835592 | tf_op jit(solution)/shard_map/ppermute | solution.py:48
  191.5 9.4 %collective-permute-start.19 = (bf16[64,2176]{1,0:T(8,128)(2,1)S(1)}, bf16[64,2176]{1,0:T(8,128)(2,1)S(1)}, u32[]{:S(2)}, u32[]{:S(2)}) collective-permute-start(bf16[64,2176]{1,0:T(8,128)(2,1)S(1)} %collective-permute-done.17.refs_2_), channel_id=1, source_target_pairs={{0,131},{1,0},{2,1},{3,2},{128,3},{129,128},{130,129},{131,130},{4... | collective-permute-start | bytes 835592 | tf_op jit(solution)/shard_map/ppermute | solution.py:48
  201.0 3.6 %copy-start.6 = (bf16[64,2176]{1,0:T(8,128)(2,1)}, bf16[64,2176]{1,0:T(8,128)(2,1)S(1)}, u32[]{:S(2)}) copy-start(bf16[64,2176]{1,0:T(8,128)(2,1)S(1)} %collective-permute-done.18.refs_1_) | copy-start | bytes 835588
  201.0 3.6 %copy-start.7 = (bf16[64,2176]{1,0:T(8,128)(2,1)}, bf16[64,2176]{1,0:T(8,128)(2,1)S(1)}, u32[]{:S(2)}) copy-start(bf16[64,2176]{1,0:T(8,128)(2,1)S(1)} %collective-permute-done.19.refs_2_) | copy-start | bytes 835588
  201.0 7.6 %collective-permute-start.20 = (bf16[32,2176]{1,0:T(8,128)(2,1)S(1)}, bf16[32,2176]{1,0:T(8,128)(2,1)S(1)}, u32[]{:S(2)}, u32[]{:S(2)}) collective-permute-start(bf16[32,2176]{1,0:T(8,128)(2,1)S(1)} %slice.11), channel_id=1, source_target_pairs={{0,1},{1,2},{2,3},{3,128},{128,129},{129,130},{130,131},{131,0},{4... | collective-permute-start | bytes 417800 | tf_op jit(solution)/shard_map/ppermute | solution.py:48
  201.1 7.5 %collective-permute-start.21 = (bf16[32,2176]{1,0:T(8,128)(2,1)S(1)}, bf16[32,2176]{1,0:T(8,128)(2,1)S(1)}, u32[]{:S(2)}, u32[]{:S(2)}) collective-permute-start(bf16[32,2176]{1,0:T(8,128)(2,1)S(1)} %slice.12), channel_id=1, source_target_pairs={{0,131},{1,0},{2,1},{3,2},{128,3},{129,128},{130,129},{131,130},{4... | collective-permute-start | bytes 417800 | tf_op jit(solution)/shard_map/ppermute | solution.py:48
Sparse Core Ops, SparseCore 0:
  30.2 68.7 all-gather.1

commit v3 on v2

--- a/solution.py
+++ b/solution.py
@@ -29,6 +29,7 @@
 MIB = 1024 * 1024
 KNOB = 20_000_000_000
 PARAMS = pltpu.CompilerParams(vmem_limit_bytes=59 * MIB)
+SMALL = pltpu.CompilerParams(vmem_limit_bytes=24 * MIB)
 ROOM = pltpu.CompilerParams(vmem_limit_bytes=53 * MIB + MIB // 2)
 VMEM = pl.BlockSpec(memory_space=pltpu.VMEM)
 SMEM = pl.BlockSpec(memory_space=pltpu.SMEM)
@@ -119,37 +120,46 @@
     wait(start([(acc_ref, acc_hbm), (squares_ref, squares_hbm)], out_sem))
 
 
-def project_last(
-    index_ref, hidden_hbm, cot_hbm, acc_hbm, squares_hbm, query_hbm, cond_hbm, out_hbm,
-    sent_hbm, inverse_hbm,
-    hidden_ref, cot_ref, acc_ref, squares_ref, query_ref, cond_ref, out_weight_ref,
-    sent_ref, inverse_ref, sem, out_sem,
-):
-    at = pl.ds(pl.multiple_of(index_ref[0] * FEAT, FEAT), FEAT)
-    copies = start(
-        [
-            (hidden_hbm, hidden_ref), (squares_hbm, squares_ref), (acc_hbm, acc_ref),
-            (query_hbm.at[at], query_ref), (cond_hbm.at[:, at], cond_ref),
-            (cot_hbm, cot_ref), (out_hbm.at[:, at], out_weight_ref),
-        ], sem,
-    )
-    wait(copies)
-    chunk = hidden_ref[...]
-    squares = squares_ref[...] + jnp.sum(
-        jnp.square(chunk.astype(F32)), axis=-1, keepdims=True
-    )
-    inverse = lax.rsqrt(squares / D + epsilon)
+def project_last(count, index_ref, *refs):
+    hiddens_hbm, cots_hbm, refs = refs[:count], refs[count : 2 * count], refs[2 * count :]
+    acc_hbm, squares_hbm, query_hbm, cond_hbm, out_hbm, sent_hbm, inverse_hbm = refs[:7]
+    hidden_ref, cot_ref, acc_ref, squares_ref, query_ref, cond_ref, out_weight_ref = refs[7:14]
+    sent_ref, inverse_ref, sem, acc_sem, out_sem = refs[14:]
+    before = start([(acc_hbm, acc_ref), (squares_hbm, squares_ref)], acc_sem)
+    copies = []
+    for k in range(count):
+        at = pl.ds(pl.multiple_of(index_ref[k] * FEAT, FEAT), FEAT)
+        copies.append(
+            start(
+                [
+                    (hiddens_hbm[k], hidden_ref.at[k]), (query_hbm.at[at], query_ref.at[k]),
+                    (cond_hbm.at[:, at], cond_ref.at[k]), (cots_hbm[k], cot_ref.at[k]),
+                    (out_hbm.at[:, at], out_weight_ref.at[k]),
+                ], sem.at[k],
+            )
+        )
+    wait(before)
+    for k in range(count):
+        wait(copies[k])
+        chunk = hidden_ref[k]
+        squares_ref[...] += jnp.sum(jnp.square(chunk.astype(F32)), axis=-1, keepdims=True)
+        if k < count - 1:
+            acc_ref[:, 0:256] += dot(chunk, query_ref[k])
+            acc_ref[:, 256:512] += dot_nt(cot_ref[k], out_weight_ref[k])
+            acc_ref[:, 512:736] += dot_nt(chunk, cond_ref[k])
+    inverse = lax.rsqrt(squares_ref[...] / D + epsilon)
     inverse_ref[...] = inverse
-    queries = (acc_ref[:, :256] + dot(chunk, query_ref[...])) * inverse
-    grads = acc_ref[:, 256:512] + dot_nt(cot_ref[...], out_weight_ref[...])
-    condition = (acc_ref[:, 512:736] + dot_nt(chunk, cond_ref[...])) * inverse
-    for columns, part in (
-        (slice(0, 256), queries), (slice(256, 512), grads), (slice(512, 736), condition)
-    ):
-        sent_ref[:SEGS, :, columns] = part.astype(BF).reshape(SEGS, SEG, -1)
+    outs = start([(inverse_ref, inverse_hbm)], out_sem.at[pl.ds(0, 1)])
+    k = count - 1
+    queries = (acc_ref[:, :256] + dot(chunk, query_ref[k])) * inverse
+    sent_ref[:SEGS, :, 0:256] = queries.astype(BF).reshape(SEGS, SEG, -1)
+    grads = acc_ref[:, 256:512] + dot_nt(cot_ref[k], out_weight_ref[k])
+    sent_ref[:SEGS, :, 256:512] = grads.astype(BF).reshape(SEGS, SEG, -1)
+    condition = (acc_ref[:, 512:736] + dot_nt(chunk, cond_ref[k])) * inverse
+    sent_ref[:SEGS, :, 512:736] = condition.astype(BF).reshape(SEGS, SEG, -1)
     sent_ref[:, :, 736:] = jnp.zeros((NZ, SEG, 32), BF)
     sent_ref[SEGS, :, :736] = jnp.zeros((SEG, 736), BF)
-    wait(start([(sent_ref, sent_hbm), (inverse_ref, inverse_hbm)], out_sem))
+    wait(start([(sent_ref, sent_hbm)], out_sem.at[pl.ds(1, 1)]) + outs)
 
 
 def attention(
@@ -211,80 +221,70 @@
     ).astype(BF)
 
 
-def finish(starts, first, *refs):
-    count = len(starts)
-    source_ref, refs = refs[0], refs[1:]
-    chunks_hbm, refs = refs[:count], refs[count:]
-    hidden_hbm, inverse_hbm, weights_hbm = refs[:3]
-    refs = refs[3 if first else 4 :]
-    out_hbm, refs = refs[0], refs[1:]
-    chunk_refs, refs = refs[:count], refs[count:]
-    hidden_refs, refs = refs[:count], refs[count:]
-    out_refs, refs = refs[:count], refs[count:]
-    inverse_ref, weight_ref, sem, out_sem = refs
-    places = []
-    for k in range(count):
-        source = source_ref[k]
-        rows = chunk_refs[k].shape[0]
-        at = jnp.where(source < SEGS, source, 0) * SEG + starts[k]
-        places.append((source < SEGS, pl.ds(pl.multiple_of(at, 32), rows)))
-    loads = [(inverse_hbm, inverse_ref)]
-    loads += [
-        (weights_hbm.at[:, pl.ds(112 + 16 * j, 16), :], weight_ref.at[j]) for j in range(2)
-    ]
-    for k in range(count):
-        loads.append((chunks_hbm[k], chunk_refs[k]))
-        loads.append((hidden_hbm.at[places[k][1]], hidden_refs[k]))
-    wait(start(loads, sem))
+def finish_rows(chunk_refs, hidden_ref, inverse_ref, weight_ref, source_ref, starts, out_refs, out_hbm, sem):
     rows = [c.shape[0] for c in chunk_refs]
     chunks = jnp.concatenate([c[...] for c in chunk_refs], axis=0)
     grads = sum(
         dot_nt(chunks[:, j * HALF : (j + 1) * HALF], weight_ref[j].reshape(FEAT, HALF))
         for j in range(2)
     )
-    for k in range(count):
+    inside, copies = [], []
+    for k, chunk_ref in enumerate(chunk_refs):
+        source = source_ref[k]
+        at = jnp.where(source < SEGS, source, 0) * SEG + starts[k]
+        place = pl.ds(pl.multiple_of(at, 32), rows[k])
         grad = grads[sum(rows[:k]) : sum(rows[: k + 1])]
-        tail = chunk_refs[k][:, 2 * HALF :].astype(F32)
+        tail = chunk_ref[:, 2 * HALF :].astype(F32)
         stat = tail[:, 0:1] + tail[:, 1:2]
-        inverse = inverse_ref[places[k][1], :]
+        inverse = inverse_ref[place, :]
         out_refs[k][...] = (
-            inverse * grad - hidden_refs[k][...].astype(F32) * (inverse * inverse * stat)
+            inverse * grad - hidden_ref[place, :].astype(F32) * (inverse * inverse * stat)
         ).astype(BF)
-
-        @pl.when(places[k][0])
-        def _(k=k):
-            pltpu.make_async_copy(
-                out_refs[k], out_hbm.at[places[k][1]], out_sem.at[k]
-            ).start()
-
-    for k in range(count):
-
-        @pl.when(places[k][0])
-        def _(k=k):
-            pltpu.make_async_copy(
-                out_refs[k], out_hbm.at[places[k][1]], out_sem.at[k]
-            ).wait()
-
-
-def finish_call(chunks, starts, sources, hidden, inverse, weights, previous):
-    first = previous is None
-    operands = [sources, *chunks, hidden, inverse, weights] + ([] if first else [previous])
+        inside.append(source < SEGS)
+        copies.append(pltpu.make_async_copy(out_refs[k], out_hbm.at[place], sem.at[k]))
+        pl.when(inside[k])(copies[k].start)
+    for k, copy in enumerate(copies):
+        pl.when(inside[k])(copy.wait)
+
+
+def finish_first(
+    source_ref, chunk_ref, hidden_hbm, inverse_hbm, weights_hbm,
+    out_hbm, hidden_ref, inverse_ref, weight_ref, result_ref, sem, out_sem,
+):
+    loads = [(inverse_hbm, inverse_ref), (hidden_hbm, hidden_ref)]
+    loads += [
+        (weights_hbm.at[:, pl.ds(112 + 16 * j, 16), :], weight_ref.at[j]) for j in range(2)
+    ]
+    wait(start(loads, sem))
+    finish_rows(
+        [chunk_ref], hidden_ref, inverse_ref, weight_ref, source_ref, (0,), [result_ref],
+        out_hbm, out_sem,
+    )
+
+
+def finish(starts, source_ref, *refs):
+    count = len(starts)
+    chunk_refs, refs = refs[:count], refs[count:]
+    hidden_ref, inverse_ref, weight_ref, _, out_hbm = refs[:5]
+    result_refs, sem = refs[5 : 5 + count], refs[5 + count]
+    finish_rows(
+        chunk_refs, hidden_ref, inverse_ref, weight_ref, source_ref, starts, result_refs,
+        out_hbm, sem,
+    )
+
+
+def finish_call(chunks, starts, sources, held, previous):
     rows = [c.shape[0] for c in chunks]
+    operands = [sources, *chunks, *held, previous]
     return pl.pallas_call(
-        functools.partial(finish, starts, first),
+        functools.partial(finish, starts),
         out_shape=jax.ShapeDtypeStruct((TOK, FEAT), BF),
-        in_specs=[SMEM] + [ANY] * (len(operands) - 1),
+        in_specs=[SMEM] + [VMEM] * (len(chunks) + 3) + [ANY],
         out_specs=ANY,
-        scratch_shapes=[like(c) for c in chunks]
-        + [pltpu.VMEM((r, FEAT), BF) for r in rows] * 2
-        + [
-            like(inverse),
-            pltpu.VMEM((2, NDP, 16, HALF), BF),
-            pltpu.SemaphoreType.DMA((3 + 2 * len(chunks),)),
-            pltpu.SemaphoreType.DMA((len(chunks),)),
-        ],
-        input_output_aliases={} if first else {len(operands) - 1: 0},
-        compiler_params=ROOM,
+        scratch_shapes=[pltpu.VMEM((r, FEAT), BF) for r in rows]
+        + [pltpu.SemaphoreType.DMA((len(chunks),))],
+        input_output_aliases={len(operands) - 1: 0},
+        compiler_params=SMALL,
         cost_estimate=cost(2 * sum(rows) * FEAT * 2048, 4_000_000),
         name="finish",
     )(*operands)
@@ -320,6 +320,9 @@
     q_part = q_part.reshape(NZ, 16, 2, HEAD).transpose(0, 2, 1, 3).reshape(NZ, 32, HEAD)
     part = jnp.concatenate([jnp.broadcast_to(kv_part, (NZ, 112, HEAD)), q_part], axis=1)
 
+    asked = exchange(wanted, "dp")
+    part = exchange(part, Z)
+
     projections = (query_weight, condition_weight.T, out_weight)
     right = left = hidden
     grad_right = grad_left = cotangent
@@ -327,40 +330,46 @@
     for step in range(1, 4):
         right, left = shift(right, 1), shift(left, -1)
         grad_right, grad_left = shift(grad_right, 1), shift(grad_left, -1)
+        if step == 1:
+            part, right, left, grad_right, grad_left, asked = tie(
+                part, right, left, grad_right, grad_left, asked
+            )
         index += [(me - step) % NZ, (me + step) % NZ]
         chunks += [right, left]
         grad_chunks += [grad_right, grad_left]
-    far = (shift(right, 1), shift(grad_left, -1))
-    count = len(chunks)
+    part = part.transpose(1, 0, 2).reshape(144, HALF)
+    weights = lax.all_gather(part, "dp", axis=0, tiled=True).reshape(16, 2, 144, HALF)
+    returned = exchange(database[asked].reshape(NDP, NEIGH * NLEN // NZ, DE), "dp")
+    chosen = returned[jnp.concatenate([owner, owner[:1]])]
+    early = 5
     acc, squares = pl.pallas_call(
-        functools.partial(project, count),
+        functools.partial(project, early),
         out_shape=(
             jax.ShapeDtypeStruct((TOK, 768), F32),
             jax.ShapeDtypeStruct((TOK, 1), F32),
         ),
-        in_specs=[SMEM] + [ANY] * (2 * count + 3),
+        in_specs=[SMEM] + [ANY] * (2 * early + 3),
         out_specs=(ANY, ANY),
         scratch_shapes=[
-            pltpu.VMEM((count, TOK, FEAT), BF),
-            pltpu.VMEM((count, TOK, FEAT), BF),
-            pltpu.VMEM((count, FEAT, 256), BF),
-            pltpu.VMEM((count, 224, FEAT), BF),
-            pltpu.VMEM((count, 256, FEAT), BF),
+            pltpu.VMEM((early, TOK, FEAT), BF),
+            pltpu.VMEM((early, TOK, FEAT), BF),
+            pltpu.VMEM((early, FEAT, 256), BF),
+            pltpu.VMEM((early, 224, FEAT), BF),
+            pltpu.VMEM((early, 256, FEAT), BF),
             pltpu.VMEM((TOK, 768), F32),
             pltpu.VMEM((TOK, 1), F32),
-            pltpu.SemaphoreType.DMA((count, 5)),
+            pltpu.SemaphoreType.DMA((early, 5)),
             pltpu.SemaphoreType.DMA((2,)),
         ],
         compiler_params=ROOM,
-        cost_estimate=cost(2 * count * TOK * FEAT * 736, 16_000_000),
+        cost_estimate=cost(2 * early * TOK * FEAT * 736, 16_000_000),
         name="project",
-    )(jnp.stack(index), *chunks, *grad_chunks, *projections)
-
-    asked = exchange(wanted, "dp")
-    part = exchange(part, Z).transpose(1, 0, 2).reshape(144, HALF)
-    weights = lax.all_gather(part, "dp", axis=0, tiled=True).reshape(16, 2, 144, HALF)
-    returned = exchange(database[asked].reshape(NDP, NEIGH * NLEN // NZ, DE), "dp")
-    fetched = exchange(returned[jnp.concatenate([owner, owner[:1]])], Z).reshape(KEYS, DE)
+    )(jnp.stack(index[:early]), *chunks[:early], *grad_chunks[:early], *projections)
+
+    right, acc, chosen = tie(right, acc, chosen)
+    chunks[5] = right
+    fetched = exchange(chosen, Z).reshape(KEYS, DE)
+    far = (shift(right, 1), shift(grad_left, -1))
     enc_q = pl.pallas_call(
         encoder_queries,
         out_shape=jax.ShapeDtypeStruct((KEYS, DE), BF),
@@ -373,34 +382,34 @@
         cost_estimate=cost(2 * KEYS * DE * DE, 3_000_000),
         name="encoder_queries",
     )(fetched, encoder_query)
-
+    hiddens, cots = (*chunks[5:], far[0]), (*grad_chunks[5:], far[1])
+    index = index[5:] + [(me + 4) % NZ]
     sent, inverse = pl.pallas_call(
-        project_last,
+        functools.partial(project_last, len(hiddens)),
         out_shape=(
             jax.ShapeDtypeStruct((NZ, SEG, 768), BF),
             jax.ShapeDtypeStruct((TOK, 1), F32),
         ),
-        in_specs=[SMEM] + [ANY] * 7,
+        in_specs=[SMEM] + [ANY] * (2 * len(hiddens) + 5),
         out_specs=(ANY, ANY),
         scratch_shapes=[
-            pltpu.VMEM((TOK, FEAT), BF),
-            pltpu.VMEM((TOK, FEAT), BF),
+            pltpu.VMEM((len(hiddens), TOK, FEAT), BF),
+            pltpu.VMEM((len(hiddens), TOK, FEAT), BF),
             like(acc),
             like(squares),
-            pltpu.VMEM((FEAT, 256), BF),
-            pltpu.VMEM((224, FEAT), BF),
-            pltpu.VMEM((256, FEAT), BF),
+            pltpu.VMEM((len(hiddens), FEAT, 256), BF),
+            pltpu.VMEM((len(hiddens), 224, FEAT), BF),
+            pltpu.VMEM((len(hiddens), 256, FEAT), BF),
             pltpu.VMEM((NZ, SEG, 768), BF),
             like(squares),
-            pltpu.SemaphoreType.DMA((7,)),
+            pltpu.SemaphoreType.DMA((len(hiddens), 5)),
+            pltpu.SemaphoreType.DMA((2,)),
             pltpu.SemaphoreType.DMA((2,)),
         ],
-        compiler_params=PARAMS,
+        compiler_params=ROOM,
         cost_estimate=cost(KNOB, 4_000_000),
         name="project_last",
-    )(
-        jnp.stack([(me + 4) % NZ]), far[0], far[1], acc, squares, *projections
-    )
+    )(jnp.stack(index), *hiddens, *cots, acc, squares, *projections)
     got = exchange(sent, Z)
     operands = (fetched, enc_q, got, encoder_out)
     grad_query = pl.pallas_call(
@@ -421,21 +430,37 @@
         name="attention",
     )(*operands, weights)
 
-    def finished(group, offsets, out):
-        sources = jnp.stack([(me + offset) % NZ for offset in offsets])
-        starts = (0, SEG // 2) if group[0].shape[0] < SEG else (0,) * len(group)
-        return finish_call(group, starts, sources, hidden, inverse, weights.reshape(NDP, 144, HALF), out)
+    results = (
+        jax.ShapeDtypeStruct((TOK, FEAT), BF),
+        jax.ShapeDtypeStruct((TOK, FEAT), BF),
+        jax.ShapeDtypeStruct((TOK, 1), F32),
+        jax.ShapeDtypeStruct((2, NDP, 16, HALF), BF),
+    )
+    out, *held = pl.pallas_call(
+        finish_first,
+        out_shape=results,
+        in_specs=[SMEM, VMEM, ANY, ANY, ANY],
+        out_specs=(ANY, VMEM, VMEM, VMEM),
+        scratch_shapes=[
+            pltpu.VMEM((SEG, FEAT), BF),
+            pltpu.SemaphoreType.DMA((4,)),
+            pltpu.SemaphoreType.DMA((1,)),
+        ],
+        compiler_params=ROOM,
+        cost_estimate=cost(2 * SEG * FEAT * 2048, 4_000_000),
+        name="finish_first",
+    )(jnp.stack([me]), grad_query, hidden, inverse, weights.reshape(NDP, 144, HALF))
 
     right = left = grad_query
-    group, offsets, out = [grad_query], [0], None
     for step in range(1, 4):
         right, left = shift(right, 1), shift(left, -1)
-        out = finished(group, offsets, out)
-        group, offsets = [right, left], [-step, step]
+        if step > 1:
+            out = finish_call(*group, held, out)
         right, left, out = tie(right, left, out)
+        group = [right, left], (0, 0), jnp.stack([(me - step) % NZ, (me + step) % NZ])
     far = [shift(right[: SEG // 2], 1), shift(left[SEG // 2 :], -1)]
-    out = finished(group, offsets, out)
-    return finished(far, (4, 4), out)
+    out = finish_call(*group, held, out)
+    return finish_call(far, (0, SEG // 2), jnp.stack([(me + 4) % NZ] * 2), held, out)
 
 
 def solution(mesh):

time: 220 us -> 219 us (level)
  blocking collectives: 20.8 us -> 0 us
  starting transfers between devices: 53.6 us -> 67.4 us
  local copies, waits for them, and re-layouts: 8.71 us -> 13.5 us
  Pallas kernels: 47.1 us -> 43.5 us
  waiting for transfers between devices: 74.6 us -> 77.7 us
    all_to_all x1 -> x0, blocking collectives: 20.8 us -> none  [exchange(): return lax.all_to_all(x, axis, split_axis=0, concat_axis=0, tiled=True)]
    all_to_all x4 -> x5, starting transfers between devices: 20.3 us -> 34 us  [exchange(): return lax.all_to_all(x, axis, split_axis=0, concat_axis=0, tiled=True)]
    ppermute x22, waiting for transfers between devices: 44.6 us -> 58.1 us  [shift(): return lax.ppermute(x, Z, [(i, (i + by) % NZ) for i in range(NZ)])]
    all_to_all x4 -> x5, waiting for transfers between devices: 30 us -> 19.6 us  [exchange(): return lax.all_to_all(x, axis, split_axis=0, concat_axis=0, tiled=True)]
    unnamed x43 -> x33, local copies, waits for them, and re-layouts: 1.76 us -> 6.57 us
    pallas_call x7, Pallas kernels: 30.5 us -> 26.9 us  [the longest x4 7.96 us: finish_call(): pl.pallas_call(functools.partial(finish, starts), out_shape=jax.ShapeDtyp...]
  transfers between devices with their start and end apart: 27 -> 28, of which waited for: 12 -> 12; matrix products, arithmetic and copies ran while one was open for 2% -> 3% of each run, Pallas kernels for 14% -> 13%
where the time goes in v3:
time: 219 us; the launch traced here: 218 us
  waiting for transfers between devices  77.7 us (35%)
  starting transfers between devices  67.4 us (31%)
  Pallas kernels  43.5 us (20%)
  between operations  13.7 us (6%)
  local copies, waits for them, and re-layouts  13.5 us (6%)
    ppermute x22, waiting for transfers between devices, shift(): return lax.ppermute(x, Z, [(i, (i + by) % NZ) for i in range(NZ)])  58.1 us
    all_to_all x5, starting transfers between devices, exchange(): return lax.all_to_all(x, axis, split_axis=0, concat_axis=0, tiled=True)  34 us
    ppermute x22, starting transfers between devices, shift(): return lax.ppermute(x, Z, [(i, (i + by) % NZ) for i in range(NZ)])  33.4 us
    all_to_all x5, waiting for transfers between devices, exchange(): return lax.all_to_all(x, axis, split_axis=0, concat_axis=0, tiled=True)  19.6 us
    pallas_call x1, Pallas kernels, shards(): pl.pallas_call(attention, out_shape=jax.ShapeDtypeStruct((SEG, 2 * HALF +...  13.5 us
    pallas_call x4, Pallas kernels, finish_call(): pl.pallas_call(functools.partial(finish, starts), out_shape=jax.ShapeDtyp...  7.96 us
    pallas_call x1, Pallas kernels, shards(): pl.pallas_call(functools.partial(project_last, len(hiddens)), out_shape=(...  6.86 us
    unnamed x33, local copies, waits for them, and re-layouts  6.57 us
  transfers between devices with their start and end apart: 28, of which 12 were waited for; matrix products, arithmetic and copies ran while one was open for 3% of the time, Pallas kernels for 13%

profile of v3, /device:TPU:2, one launch (start us, length us, event | category | flops | bytes accessed | tf_op | source)
XLA Modules:
  0.0 217.8 jit_solution(13064751448003543103)
XLA Ops:
  6.5 0.9 copy.36
  7.4 0.7 fusion
  8.1 0.1 multiply_reduce_fusion
  8.2 0.7 copy.37
  8.9 7.6 %all-to-all-start.1 = ((s32[32,1,2]{2,1,0:T(1,128)}), s32[32,1,2]{2,1,0:T(1,128)S(1)}, u32[]{:S(2)}, u32[]{:S(2)}) async-start(s32[32,1,2]{2,1,0:T(1,128)} %copy.37), calls=%async_computation.1 | async-start | bytes 32768 | tf_op jit(solution)/shard_map/all_to_all | solution.py:57
  16.6 0.9 constant_dynamic-slice_fusion
  17.5 0.8 dynamic_slice.6
  18.3 0.7 pad_maximum_fusion
  19.0 3.6 %all-to-all-done.1 = s32[32,1,2]{2,1,0:T(1,128)S(1)} async-done(((s32[32,1,2]{2,1,0:T(1,128)}), s32[32,1,2]{2,1,0:T(1,128)S(1)}, u32[]{:S(2)}, u32[]{:S(2)}) %all-to-all-start.1) | async-done | bytes 288 | tf_op jit(solution)/shard_map/all_to_all | solution.py:57
  22.6 8.5 %all-to-all-start = ((bf16[8,144,128]{2,1,0:T(8,128)(2,1)}), bf16[8,144,128]{2,1,0:T(8,128)(2,1)S(1)}, u32[]{:S(2)}, u32[]{:S(2)}) async-start(bf16[8,144,128]{2,1,0:T(8,128)(2,1)} %pad_maximum_fusion), calls=%async_computation | async-start | bytes 589824 | tf_op jit(solution)/shard_map/all_to_all | solution.py:57
  31.1 2.1 collective-permute-start
  33.2 1.3 collective-permute-start.1
  34.5 0.7 collective-permute-start.2
  35.2 2.5 %collective-permute-start.3 = (bf16[448,512]{1,0:T(8,128)(2,1)S(1)}, bf16[448,512]{1,0:T(8,128)(2,1)S(1)}, u32[]{:S(2)}, u32[]{:S(2)}) collective-permute-start(bf16[448,512]{1,0:T(8,128)(2,1)S(1)} %copy-done.8), channel_id=1, source_target_pairs={{0,131},{1,0},{2,1},{3,2},{128,3},{129,128},{130,129},{131,130},{4... | collective-permute-start | bytes 1376264 | tf_op jit(solution)/shard_map/ppermute | solution.py:49
  37.8 14.2 %collective-permute-done.refs_1_ = bf16[448,512]{1,0:T(8,128)(2,1)} collective-permute-done((bf16[448,512]{1,0:T(8,128)(2,1)S(1)}, bf16[448,512]{1,0:T(8,128)(2,1)}, u32[]{:S(2)}, u32[]{:S(2)}) %collective-permute-start) | collective-permute-done | bytes 458784 | tf_op jit(solution)/shard_map/ppermute | solution.py:49
  52.0 8.7 %collective-permute-done.2.refs_6_ = bf16[448,512]{1,0:T(8,128)(2,1)S(1)} collective-permute-done((bf16[448,512]{1,0:T(8,128)(2,1)S(1)}, bf16[448,512]{1,0:T(8,128)(2,1)S(1)}, u32[]{:S(2)}, u32[]{:S(2)}) %collective-permute-start.2) | collective-permute-done | bytes 458784 | tf_op jit(solution)/shard_map/ppermute | solution.py:49
  60.7 0.8 copy_bitcast_fusion
  61.5 0.1 copy.39
  61.6 0.1 reshape.126
  61.7 2.0 gather_fusion
  63.7 5.1 %all-to-all-start.2 = ((bf16[32,32,896]{2,1,0:T(8,128)(2,1)}), bf16[32,32,896]{2,1,0:T(8,128)(2,1)S(1)}, u32[]{:S(2)}, u32[]{:S(2)}) async-start(bf16[32,32,896]{2,1,0:T(8,128)(2,1)} %bitcast.14), calls=%async_computation.2 | async-start | bytes 3670016 | tf_op jit(solution)/shard_map/all_to_all | solution.py:57
  68.8 1.5 collective-permute-start.8
  70.4 0.6 collective-permute-start.4
  70.9 0.4 collective-permute-start.7
  71.3 2.9 %collective-permute-start.6 = (bf16[448,512]{1,0:T(8,128)(2,1)}, bf16[448,512]{1,0:T(8,128)(2,1)S(1)}, u32[]{:S(2)}, u32[]{:S(2)}) collective-permute-start(bf16[448,512]{1,0:T(8,128)(2,1)} %copy-done.11), channel_id=1, source_target_pairs={{0,131},{1,0},{2,1},{3,2},{128,3},{129,128},{130,129},{131,130},{4... | collective-permute-start | bytes 1376264 | tf_op jit(solution)/shard_map/ppermute | solution.py:49
  74.2 8.4 %collective-permute-done.8.refs_9_ = bf16[448,512]{1,0:T(8,128)(2,1)} collective-permute-done((bf16[448,512]{1,0:T(8,128)(2,1)}, bf16[448,512]{1,0:T(8,128)(2,1)}, u32[]{:S(2)}, u32[]{:S(2)}) %collective-permute-start.8) | collective-permute-done | bytes 458784 | tf_op jit(solution)/shard_map/ppermute | solution.py:49
  82.6 2.7 %collective-permute-start.12 = (bf16[448,512]{1,0:T(8,128)(2,1)}, bf16[448,512]{1,0:T(8,128)(2,1)}, u32[]{:S(2)}, u32[]{:S(2)}) collective-permute-start(bf16[448,512]{1,0:T(8,128)(2,1)} %collective-permute-done.8.refs_9_), channel_id=1, source_target_pairs={{0,131},{1,0},{2,1},{3,2},{128,3},{129,128},{130,129},{131,130},{4... | collective-permute-start | bytes 1376264 | tf_op jit(solution)/shard_map/ppermute | solution.py:49
  85.4 0.1 fusion.1
  85.5 9.5 %collective-permute-done.7.refs_8_ = bf16[448,512]{1,0:T(8,128)(2,1)S(1)} collective-permute-done((bf16[448,512]{1,0:T(8,128)(2,1)}, bf16[448,512]{1,0:T(8,128)(2,1)S(1)}, u32[]{:S(2)}, u32[]{:S(2)}) %collective-permute-start.7) | collective-permute-done | bytes 458784 | tf_op jit(solution)/shard_map/ppermute | solution.py:49
  95.0 3.2 %collective-permute-start.9 = (bf16[448,512]{1,0:T(8,128)(2,1)S(1)}, bf16[448,512]{1,0:T(8,128)(2,1)}, u32[]{:S(2)}, u32[]{:S(2)}) collective-permute-start(bf16[448,512]{1,0:T(8,128)(2,1)S(1)} %collective-permute-done.6.refs_4_), channel_id=1, source_target_pairs={{0,131},{1,0},{2,1},{3,2},{128,3},{129,128},{130,129},{131,130},{4... | collective-permute-start | bytes 1376264 | tf_op jit(solution)/shard_map/ppermute | solution.py:49
  98.3 6.4 %project.1 = (f32[448,768]{1,0:T(8,128)}, f32[448,1]{1,0:T(8,128)S(1)}) custom-call(s32[5]{0:T(128)S(1)} %stack.58.index_ref, bf16[448,512]{1,0:T(8,128)(2,1)} %hidden_hbm.1, bf16[448,512]{1,0:T(8,128)(2,1)} %collective-permute-done.refs_1_, bf16[448,512]{1,0:T(8,128)(2,1)} %copy-done.11, bf16[448,512]{1,0:T(8,128)(2,1)} %collective-permute-done.4.refs_3_, ...), custom_call_target="tpu_custom_call" | custom-call | flops 1688207360 | bytes 16000000 | tf_op jit(solution)/shard_map/project/pallas_call | solution.py:345
  104.7 0.7 copy-done.4
  105.4 0.8 collective-permute-start.13
  106.2 1.4 gather_fusion.1
  107.5 1.2 collective-permute-start.10
  108.9 5.8 %all-to-all-start.3 = ((bf16[8,32,896]{2,1,0:T(8,128)(2,1)}), bf16[8,32,896]{2,1,0:T(8,128)(2,1)S(1)}, u32[]{:S(2)}, u32[]{:S(2)}) async-start(bf16[8,32,896]{2,1,0:T(8,128)(2,1)} %gather_fusion.1), calls=%async_computation.3 | async-start | bytes 917504 | tf_op jit(solution)/shard_map/all_to_all | solution.py:57
  114.6 0.2 collective-permute-done.11.refs_3_
  114.8 7.7 %collective-permute-done.13.refs_5_ = bf16[448,512]{1,0:T(8,128)(2,1)} collective-permute-done((bf16[448,512]{1,0:T(8,128)(2,1)}, bf16[448,512]{1,0:T(8,128)(2,1)}, u32[]{:S(2)}, u32[]{:S(2)}) %collective-permute-start.13) | collective-permute-done | bytes 458784 | tf_op jit(solution)/shard_map/ppermute | solution.py:49
  122.5 4.0 %collective-permute-done.10.refs_2_ = bf16[448,512]{1,0:T(8,128)(2,1)S(1)} collective-permute-done((bf16[448,512]{1,0:T(8,128)(2,1)}, bf16[448,512]{1,0:T(8,128)(2,1)S(1)}, u32[]{:S(2)}, u32[]{:S(2)}) %collective-permute-start.10) | collective-permute-done | bytes 458784 | tf_op jit(solution)/shard_map/ppermute | solution.py:49
  126.5 0.8 copy-done.15
  127.3 6.9 %project_last.1 = (bf16[8,64,768]{2,1,0:T(8,128)(2,1)}, f32[448,1]{1,0:T(8,128)S(1)}) custom-call(s32[3]{0:T(128)S(1)} %pad_add_fusion.1.index_ref, bf16[448,512]{1,0:T(8,128)(2,1)} %collective-permute-done.5.refs_0_, bf16[448,512]{1,0:T(8,128)(2,1)} %collective-permute-done.9.refs_1_, bf16[448,512]{1,0:T(8,128)(2,1)} %copy-done.15, ...), custom_call_target="tpu_custom_call" | custom-call | flops 20000000000 | bytes 4000000 | tf_op jit(solution)/shard_map/project_last/pallas_call | solution.py:387
  134.1 0.7 copy-done.3
  134.8 7.1 %all-to-all-start.4 = ((bf16[8,64,768]{2,1,0:T(8,128)(2,1)}), bf16[8,64,768]{2,1,0:T(8,128)(2,1)S(1)}, u32[]{:S(2)}, u32[]{:S(2)}) async-start(bf16[8,64,768]{2,1,0:T(8,128)(2,1)} %get-tuple-element.41), calls=%async_computation.4 | async-start | bytes 1572864 | tf_op jit(solution)/shard_map/all_to_all | solution.py:57
  141.9 3.1 %encoder_queries.1.enc_q_hbm = bf16[256,896]{1,0:T(8,128)(2,1)} custom-call(bf16[256,896]{1,0:T(8,128)(2,1)} %bitcast.32, bf16[896,896]{1,0:T(8,128)(2,1)} %weight_hbm.1), custom_call_target="tpu_custom_call" | custom-call | flops 411041792 | bytes 3000000 | tf_op jit(solution)/shard_map/encoder_queries/pallas_call | solution.py:373
  145.0 16.0 %all-to-all-done.4.got_hbm = bf16[8,64,768]{2,1,0:T(8,128)(2,1)S(1)} async-done(((bf16[8,64,768]{2,1,0:T(8,128)(2,1)}), bf16[8,64,768]{2,1,0:T(8,128)(2,1)S(1)}, u32[]{:S(2)}, u32[]{:S(2)}) %all-to-all-start.4) | async-done | bytes 786464 | tf_op jit(solution)/shard_map/all_to_all | solution.py:57
  161.0 0.9 copy-done.7
  161.9 13.5 %attention.1.chunk_ref = bf16[64,2176]{1,0:T(8,128)(2,1)} custom-call(bf16[256,896]{1,0:T(8,128)(2,1)} %bitcast.33, bf16[256,896]{1,0:T(8,128)(2,1)} %encoder_queries.1.enc_q_hbm, bf16[8,64,768]{2,1,0:T(8,128)(2,1)} %copy-done.7, bf16[896,896]{1,0:T(8,128)(2,1)} %enc_out_hbm.1, bf16[16,2,144,1024]{3,2,1,0:T(8,128)(2,1)} %bitcast.29), custom_call_target="tpu_custom_call" | custom-call | flops 4000000000 | bytes 12000000 | tf_op jit(solution)/shard_map/attention/pallas_call | solution.py:415
  175.4 0.6 collective-permute-start.14
  176.0 2.7 %collective-permute-start.15 = (bf16[64,2176]{1,0:T(8,128)(2,1)}, bf16[64,2176]{1,0:T(8,128)(2,1)S(1)}, u32[]{:S(2)}, u32[]{:S(2)}) collective-permute-start(bf16[64,2176]{1,0:T(8,128)(2,1)} %attention.1.chunk_ref), channel_id=1, source_target_pairs={{0,131},{1,0},{2,1},{3,2},{128,3},{129,128},{130,129},{131,130},{4... | collective-permute-start | bytes 835592 | tf_op jit(solution)/shard_map/ppermute | solution.py:49
  178.7 5.7 %finish_first.1 = (bf16[448,512]{1,0:T(8,128)(2,1)}, bf16[448,512]{1,0:T(8,128)(2,1)}, f32[448,1]{1,0:T(8,128)S(1)}, bf16[2,32,16,1024]{3,2,1,0:T(8,128)(2,1)}) custom-call(s32[1]{0:T(128)} %bitcast.8.source_ref, bf16[64,2176]{1,0:T(8,128)(2,1)} %attention.1.chunk_ref, bf16[448,512]{1,0:T(8,128)(2,1)} %hidden_hbm.1, f32[448,1]{1,0:T(8,128)} %copy-done.3, ...), custom_call_target="tpu_custom_call" | custom-call | flops 134217728 | bytes 4000000 | tf_op jit(solution)/shard_map/finish_first/pallas_call | solution.py:439
  184.4 0.1 collective-permute-start.16
  184.5 3.2 %collective-permute-start.17 = (bf16[64,2176]{1,0:T(8,128)(2,1)S(1)}, bf16[64,2176]{1,0:T(8,128)(2,1)S(1)}, u32[]{:S(2)}, u32[]{:S(2)}) collective-permute-start(bf16[64,2176]{1,0:T(8,128)(2,1)S(1)} %collective-permute-done.15.refs_1_), channel_id=1, source_target_pairs={{0,131},{1,0},{2,1},{3,2},{128,3},{129,128},{130,129},{131,130},{4... | collective-permute-start | bytes 835592 | tf_op jit(solution)/shard_map/ppermute | solution.py:49
  187.8 1.6 copy-done.1
  189.4 1.0 copy-done.2
  190.4 2.0 finish.4.refs_5_
  192.5 0.7 collective-permute-done.16.refs_0_
  193.1 3.5 %collective-permute-start.19 = (bf16[64,2176]{1,0:T(8,128)(2,1)S(1)}, bf16[64,2176]{1,0:T(8,128)(2,1)S(1)}, u32[]{:S(2)}, u32[]{:S(2)}) collective-permute-start(bf16[64,2176]{1,0:T(8,128)(2,1)S(1)} %collective-permute-done.17.refs_1_), channel_id=1, source_target_pairs={{0,131},{1,0},{2,1},{3,2},{128,3},{129,128},{130,129},{131,130},{4... | collective-permute-start | bytes 835592 | tf_op jit(solution)/shard_map/ppermute | solution.py:49
  196.7 2.0 finish.5.refs_5_
  198.8 3.9 %collective-permute-done.18.refs_0_ = bf16[64,2176]{1,0:T(8,128)(2,1)S(1)} collective-permute-done((bf16[64,2176]{1,0:T(8,128)(2,1)S(1)}, bf16[64,2176]{1,0:T(8,128)(2,1)S(1)}, u32[]{:S(2)}, u32[]{:S(2)}) %collective-permute-start.18) | collective-permute-done | bytes 278560 | tf_op jit(solution)/shard_map/ppermute | solution.py:49
  202.7 0.3 collective-permute-start.20
  203.0 3.1 %collective-permute-start.21 = (bf16[32,2176]{1,0:T(8,128)(2,1)S(1)}, bf16[32,2176]{1,0:T(8,128)(2,1)S(1)}, u32[]{:S(2)}, u32[]{:S(2)}) collective-permute-start(bf16[32,2176]{1,0:T(8,128)(2,1)S(1)} %slice.12), channel_id=1, source_target_pairs={{0,131},{1,0},{2,1},{3,2},{128,3},{129,128},{130,129},{131,130},{4... | collective-permute-start | bytes 417800 | tf_op jit(solution)/shard_map/ppermute | solution.py:49
  206.3 2.0 finish.6.refs_5_
  208.3 0.8 collective-permute-done.20.refs_0_
  209.0 1.9 finish.7
  (62 shorter events, 0.8 us)
Async XLA Ops:
  6.5 55.2 %copy-start = (bf16[16,16,896]{2,1,0:T(8,128)(2,1)S(1)}, bf16[16,16,896]{2,1,0:T(8,128)(2,1)}, u32[]{:S(2)}) copy-start(bf16[16,16,896]{2,1,0:T(8,128)(2,1)} %param.19) | copy-start | bytes 1376260
  6.5 24.6 %copy-start.6 = (bf16[448,512]{1,0:T(8,128)(2,1)S(1)}, bf16[448,512]{1,0:T(8,128)(2,1)}, u32[]{:S(2)}) copy-start(bf16[448,512]{1,0:T(8,128)(2,1)} %hidden_hbm.1) | copy-start | bytes 1376260
  6.5 28.0 %copy-start.8 = (bf16[448,512]{1,0:T(8,128)(2,1)S(1)}, bf16[448,512]{1,0:T(8,128)(2,1)}, u32[]{:S(2)}) copy-start(bf16[448,512]{1,0:T(8,128)(2,1)} %refs_5_.1) | copy-start | bytes 1376260
  8.9 13.7 %all-to-all-start.1 = ((s32[32,1,2]{2,1,0:T(1,128)}), s32[32,1,2]{2,1,0:T(1,128)S(1)}, u32[]{:S(2)}, u32[]{:S(2)}) async-start(s32[32,1,2]{2,1,0:T(1,128)} %copy.37), calls=%async_computation.1 | async-start | bytes 32768 | tf_op jit(solution)/shard_map/all_to_all | solution.py:57
  22.6 38.1 %all-to-all-start = ((bf16[8,144,128]{2,1,0:T(8,128)(2,1)}), bf16[8,144,128]{2,1,0:T(8,128)(2,1)S(1)}, u32[]{:S(2)}, u32[]{:S(2)}) async-start(bf16[8,144,128]{2,1,0:T(8,128)(2,1)} %pad_maximum_fusion), calls=%async_computation | async-start | bytes 589824 | tf_op jit(solution)/shard_map/all_to_all | solution.py:57
  31.1 129.9 %all-gather.2.cloned.1.call-start = ((), (), s32[]{:S(2)}) async-start(), calls=%async_computation.5 | async-start | bytes 9732096 | tf_op jit(solution)/shard_map/all_gather | solution.py:341
  31.1 20.8 %collective-permute-start = (bf16[448,512]{1,0:T(8,128)(2,1)S(1)}, bf16[448,512]{1,0:T(8,128)(2,1)}, u32[]{:S(2)}, u32[]{:S(2)}) collective-permute-start(bf16[448,512]{1,0:T(8,128)(2,1)S(1)} %copy-done.6), channel_id=1, source_target_pairs={{0,1},{1,2},{2,3},{3,128},{128,129},{129,130},{130,131},{131,0},{4... | collective-permute-start | bytes 1376264 | tf_op jit(solution)/shard_map/ppermute | solution.py:49
  33.2 18.8 %collective-permute-start.1 = (bf16[448,512]{1,0:T(8,128)(2,1)S(1)}, bf16[448,512]{1,0:T(8,128)(2,1)S(1)}, u32[]{:S(2)}, u32[]{:S(2)}) collective-permute-start(bf16[448,512]{1,0:T(8,128)(2,1)S(1)} %copy-done.6), channel_id=1, source_target_pairs={{0,131},{1,0},{2,1},{3,2},{128,3},{129,128},{130,129},{131,130},{4... | collective-permute-start | bytes 1376264 | tf_op jit(solution)/shard_map/ppermute | solution.py:49
  34.5 26.2 %collective-permute-start.2 = (bf16[448,512]{1,0:T(8,128)(2,1)S(1)}, bf16[448,512]{1,0:T(8,128)(2,1)S(1)}, u32[]{:S(2)}, u32[]{:S(2)}) collective-permute-start(bf16[448,512]{1,0:T(8,128)(2,1)S(1)} %copy-done.8), channel_id=1, source_target_pairs={{0,1},{1,2},{2,3},{3,128},{128,129},{129,130},{130,131},{131,0},{4... | collective-permute-start | bytes 1376264 | tf_op jit(solution)/shard_map/ppermute | solution.py:49
  35.2 25.4 %collective-permute-start.3 = (bf16[448,512]{1,0:T(8,128)(2,1)S(1)}, bf16[448,512]{1,0:T(8,128)(2,1)S(1)}, u32[]{:S(2)}, u32[]{:S(2)}) collective-permute-start(bf16[448,512]{1,0:T(8,128)(2,1)S(1)} %copy-done.8), channel_id=1, source_target_pairs={{0,131},{1,0},{2,1},{3,2},{128,3},{129,128},{130,129},{131,130},{4... | collective-permute-start | bytes 1376264 | tf_op jit(solution)/shard_map/ppermute | solution.py:49
  52.0 11.7 %copy-start.11 = (bf16[448,512]{1,0:T(8,128)(2,1)}, bf16[448,512]{1,0:T(8,128)(2,1)S(1)}, u32[]{:S(2)}) copy-start(bf16[448,512]{1,0:T(8,128)(2,1)S(1)} %collective-permute-done.1.refs_2_) | copy-start | bytes 1376260
  60.7 3.0 %copy-start.12 = (bf16[448,512]{1,0:T(8,128)(2,1)}, bf16[448,512]{1,0:T(8,128)(2,1)S(1)}, u32[]{:S(2)}) copy-start(bf16[448,512]{1,0:T(8,128)(2,1)S(1)} %collective-permute-done.2.refs_6_) | copy-start | bytes 1376260
  60.7 3.0 %copy-start.13 = (bf16[448,512]{1,0:T(8,128)(2,1)}, bf16[448,512]{1,0:T(8,128)(2,1)S(1)}, u32[]{:S(2)}) copy-start(bf16[448,512]{1,0:T(8,128)(2,1)S(1)} %collective-permute-done.3.refs_7_) | copy-start | bytes 1376260
  63.7 21.7 %copy-start.14 = (s32[7,1]{0,1:T(1,128)S(1)}, s32[7,1]{0,1:T(1,128)}, u32[]{:S(2)}) copy-start(s32[7,1]{0,1:T(1,128)} %param.21) | copy-start | bytes 88
  63.7 42.5 %all-to-all-start.2 = ((bf16[32,32,896]{2,1,0:T(8,128)(2,1)}), bf16[32,32,896]{2,1,0:T(8,128)(2,1)S(1)}, u32[]{:S(2)}, u32[]{:S(2)}) async-start(bf16[32,32,896]{2,1,0:T(8,128)(2,1)} %bitcast.14), calls=%async_computation.2 | async-start | bytes 3670016 | tf_op jit(solution)/shard_map/all_to_all | solution.py:57
  68.8 13.8 %collective-permute-start.8 = (bf16[448,512]{1,0:T(8,128)(2,1)}, bf16[448,512]{1,0:T(8,128)(2,1)}, u32[]{:S(2)}, u32[]{:S(2)}) collective-permute-start(bf16[448,512]{1,0:T(8,128)(2,1)} %copy-done.13), channel_id=1, source_target_pairs={{0,131},{1,0},{2,1},{3,2},{128,3},{129,128},{130,129},{131,130},{4... | collective-permute-start | bytes 1376264 | tf_op jit(solution)/shard_map/ppermute | solution.py:49
  70.4 14.9 %collective-permute-start.4 = (bf16[448,512]{1,0:T(8,128)(2,1)}, bf16[448,512]{1,0:T(8,128)(2,1)}, u32[]{:S(2)}, u32[]{:S(2)}) collective-permute-start(bf16[448,512]{1,0:T(8,128)(2,1)} %collective-permute-done.refs_1_), channel_id=1, source_target_pairs={{0,1},{1,2},{2,3},{3,128},{128,129},{129,130},{130,131},{131,0},{4... | collective-permute-start | bytes 1376264 | tf_op jit(solution)/shard_map/ppermute | solution.py:49
  70.9 24.1 %collective-permute-start.7 = (bf16[448,512]{1,0:T(8,128)(2,1)}, bf16[448,512]{1,0:T(8,128)(2,1)S(1)}, u32[]{:S(2)}, u32[]{:S(2)}) collective-permute-start(bf16[448,512]{1,0:T(8,128)(2,1)} %copy-done.12), channel_id=1, source_target_pairs={{0,1},{1,2},{2,3},{3,128},{128,129},{129,130},{130,131},{131,0},{4... | collective-permute-start | bytes 1376264 | tf_op jit(solution)/shard_map/ppermute | solution.py:49
  71.3 23.7 %collective-permute-start.6 = (bf16[448,512]{1,0:T(8,128)(2,1)}, bf16[448,512]{1,0:T(8,128)(2,1)S(1)}, u32[]{:S(2)}, u32[]{:S(2)}) collective-permute-start(bf16[448,512]{1,0:T(8,128)(2,1)} %copy-done.11), channel_id=1, source_target_pairs={{0,131},{1,0},{2,1},{3,2},{128,3},{129,128},{130,129},{131,130},{4... | collective-permute-start | bytes 1376264 | tf_op jit(solution)/shard_map/ppermute | solution.py:49
  82.6 22.8 %collective-permute-start.12 = (bf16[448,512]{1,0:T(8,128)(2,1)}, bf16[448,512]{1,0:T(8,128)(2,1)}, u32[]{:S(2)}, u32[]{:S(2)}) collective-permute-start(bf16[448,512]{1,0:T(8,128)(2,1)} %collective-permute-done.8.refs_9_), channel_id=1, source_target_pairs={{0,131},{1,0},{2,1},{3,2},{128,3},{129,128},{130,129},{131,130},{4... | collective-permute-start | bytes 1376264 | tf_op jit(solution)/shard_map/ppermute | solution.py:49
  85.3 22.2 %collective-permute-start.5 = (bf16[448,512]{1,0:T(8,128)(2,1)}, bf16[448,512]{1,0:T(8,128)(2,1)}, u32[]{:S(2)}, u32[]{:S(2)}) collective-permute-start(bf16[448,512]{1,0:T(8,128)(2,1)} %collective-permute-done.4.refs_3_), channel_id=1, source_target_pairs={{0,1},{1,2},{2,3},{3,128},{128,129},{129,130},{130,131},{131,0},{4... | collective-permute-start | bytes 1376264 | tf_op jit(solution)/shard_map/ppermute | solution.py:49
  95.0 3.2 %copy-start.9 = (bf16[448,512]{1,0:T(8,128)(2,1)}, bf16[448,512]{1,0:T(8,128)(2,1)S(1)}, u32[]{:S(2)}) copy-start(bf16[448,512]{1,0:T(8,128)(2,1)S(1)} %collective-permute-done.7.refs_8_) | copy-start | bytes 1376260
  95.0 19.8 %collective-permute-start.11 = (bf16[448,512]{1,0:T(8,128)(2,1)S(1)}, bf16[448,512]{1,0:T(8,128)(2,1)}, u32[]{:S(2)}, u32[]{:S(2)}) collective-permute-start(bf16[448,512]{1,0:T(8,128)(2,1)S(1)} %collective-permute-done.7.refs_8_), channel_id=1, source_target_pairs={{0,1},{1,2},{2,3},{3,128},{128,129},{129,130},{130,131},{131,0},{4... | collective-permute-start | bytes 1376264 | tf_op jit(solution)/shard_map/ppermute | solution.py:49
  95.0 3.2 %copy-start.10 = (bf16[448,512]{1,0:T(8,128)(2,1)}, bf16[448,512]{1,0:T(8,128)(2,1)S(1)}, u32[]{:S(2)}) copy-start(bf16[448,512]{1,0:T(8,128)(2,1)S(1)} %collective-permute-done.6.refs_4_) | copy-start | bytes 1376260
  95.0 19.7 %collective-permute-start.9 = (bf16[448,512]{1,0:T(8,128)(2,1)S(1)}, bf16[448,512]{1,0:T(8,128)(2,1)}, u32[]{:S(2)}, u32[]{:S(2)}) collective-permute-start(bf16[448,512]{1,0:T(8,128)(2,1)S(1)} %collective-permute-done.6.refs_4_), channel_id=1, source_target_pairs={{0,131},{1,0},{2,1},{3,2},{128,3},{129,128},{130,129},{131,130},{4... | collective-permute-start | bytes 1376264 | tf_op jit(solution)/shard_map/ppermute | solution.py:49
  104.7 0.7 copy-start.4
  105.4 17.1 %collective-permute-start.13 = (bf16[448,512]{1,0:T(8,128)(2,1)}, bf16[448,512]{1,0:T(8,128)(2,1)}, u32[]{:S(2)}, u32[]{:S(2)}) collective-permute-start(bf16[448,512]{1,0:T(8,128)(2,1)} %collective-permute-done.12.refs_4_), channel_id=1, source_target_pairs={{0,131},{1,0},{2,1},{3,2},{128,3},{129,128},{130,129},{131,130},{4... | collective-permute-start | bytes 1376264 | tf_op jit(solution)/shard_map/ppermute | solution.py:49
  107.5 18.9 %collective-permute-start.10 = (bf16[448,512]{1,0:T(8,128)(2,1)}, bf16[448,512]{1,0:T(8,128)(2,1)S(1)}, u32[]{:S(2)}, u32[]{:S(2)}) collective-permute-start(bf16[448,512]{1,0:T(8,128)(2,1)} %collective-permute-done.5.refs_0_), channel_id=1, source_target_pairs={{0,1},{1,2},{2,3},{3,128},{128,129},{129,130},{130,131},{131,0},{4... | collective-permute-start | bytes 1376264 | tf_op jit(solution)/shard_map/ppermute | solution.py:49
  108.9 26.0 %all-to-all-start.3 = ((bf16[8,32,896]{2,1,0:T(8,128)(2,1)}), bf16[8,32,896]{2,1,0:T(8,128)(2,1)S(1)}, u32[]{:S(2)}, u32[]{:S(2)}) async-start(bf16[8,32,896]{2,1,0:T(8,128)(2,1)} %gather_fusion.1), calls=%async_computation.3 | async-start | bytes 917504 | tf_op jit(solution)/shard_map/all_to_all | solution.py:57
  126.5 0.8 copy-start.15
  134.1 0.7 copy-start.3
  134.8 7.1 %copy-start.5 = (bf16[8,32,896]{2,1,0:T(8,128)(2,1)}, bf16[8,32,896]{2,1,0:T(8,128)(2,1)S(1)}, u32[]{:S(2)}) copy-start(bf16[8,32,896]{2,1,0:T(8,128)(2,1)S(1)} %all-to-all-done.3) | copy-start | bytes 1376260
  134.8 26.2 %all-to-all-start.4 = ((bf16[8,64,768]{2,1,0:T(8,128)(2,1)}), bf16[8,64,768]{2,1,0:T(8,128)(2,1)S(1)}, u32[]{:S(2)}, u32[]{:S(2)}) async-start(bf16[8,64,768]{2,1,0:T(8,128)(2,1)} %get-tuple-element.41), calls=%async_computation.4 | async-start | bytes 1572864 | tf_op jit(solution)/shard_map/all_to_all | solution.py:57
  161.0 0.9 copy-start.7
  175.4 9.0 %collective-permute-start.14 = (bf16[64,2176]{1,0:T(8,128)(2,1)}, bf16[64,2176]{1,0:T(8,128)(2,1)S(1)}, u32[]{:S(2)}, u32[]{:S(2)}) collective-permute-start(bf16[64,2176]{1,0:T(8,128)(2,1)} %attention.1.chunk_ref), channel_id=1, source_target_pairs={{0,1},{1,2},{2,3},{3,128},{128,129},{129,130},{130,131},{131,0},{4... | collective-permute-start | bytes 835592 | tf_op jit(solution)/shard_map/ppermute | solution.py:49
  176.0 8.4 %collective-permute-start.15 = (bf16[64,2176]{1,0:T(8,128)(2,1)}, bf16[64,2176]{1,0:T(8,128)(2,1)S(1)}, u32[]{:S(2)}, u32[]{:S(2)}) collective-permute-start(bf16[64,2176]{1,0:T(8,128)(2,1)} %attention.1.chunk_ref), channel_id=1, source_target_pairs={{0,131},{1,0},{2,1},{3,2},{128,3},{129,128},{130,129},{131,130},{4... | collective-permute-start | bytes 835592 | tf_op jit(solution)/shard_map/ppermute | solution.py:49
  184.4 8.7 %collective-permute-start.16 = (bf16[64,2176]{1,0:T(8,128)(2,1)S(1)}, bf16[64,2176]{1,0:T(8,128)(2,1)S(1)}, u32[]{:S(2)}, u32[]{:S(2)}) collective-permute-start(bf16[64,2176]{1,0:T(8,128)(2,1)S(1)} %collective-permute-done.14.refs_0_), channel_id=1, source_target_pairs={{0,1},{1,2},{2,3},{3,128},{128,129},{129,130},{130,131},{131,0},{4... | collective-permute-start | bytes 835592 | tf_op jit(solution)/shard_map/ppermute | solution.py:49
  184.5 8.6 %collective-permute-start.17 = (bf16[64,2176]{1,0:T(8,128)(2,1)S(1)}, bf16[64,2176]{1,0:T(8,128)(2,1)S(1)}, u32[]{:S(2)}, u32[]{:S(2)}) collective-permute-start(bf16[64,2176]{1,0:T(8,128)(2,1)S(1)} %collective-permute-done.15.refs_1_), channel_id=1, source_target_pairs={{0,131},{1,0},{2,1},{3,2},{128,3},{129,128},{130,129},{131,130},{4... | collective-permute-start | bytes 835592 | tf_op jit(solution)/shard_map/ppermute | solution.py:49
  187.8 1.6 copy-start.1
  189.4 1.0 copy-start.2
  193.1 9.5 %collective-permute-start.18 = (bf16[64,2176]{1,0:T(8,128)(2,1)S(1)}, bf16[64,2176]{1,0:T(8,128)(2,1)S(1)}, u32[]{:S(2)}, u32[]{:S(2)}) collective-permute-start(bf16[64,2176]{1,0:T(8,128)(2,1)S(1)} %collective-permute-done.16.refs_0_), channel_id=1, source_target_pairs={{0,1},{1,2},{2,3},{3,128},{128,129},{129,130},{130,131},{131,0},{4... | collective-permute-start | bytes 835592 | tf_op jit(solution)/shard_map/ppermute | solution.py:49
  193.1 9.5 %collective-permute-start.19 = (bf16[64,2176]{1,0:T(8,128)(2,1)S(1)}, bf16[64,2176]{1,0:T(8,128)(2,1)S(1)}, u32[]{:S(2)}, u32[]{:S(2)}) collective-permute-start(bf16[64,2176]{1,0:T(8,128)(2,1)S(1)} %collective-permute-done.17.refs_1_), channel_id=1, source_target_pairs={{0,131},{1,0},{2,1},{3,2},{128,3},{129,128},{130,129},{131,130},{4... | collective-permute-start | bytes 835592 | tf_op jit(solution)/shard_map/ppermute | solution.py:49
  202.7 6.3 %collective-permute-start.20 = (bf16[32,2176]{1,0:T(8,128)(2,1)S(1)}, bf16[32,2176]{1,0:T(8,128)(2,1)S(1)}, u32[]{:S(2)}, u32[]{:S(2)}) collective-permute-start(bf16[32,2176]{1,0:T(8,128)(2,1)S(1)} %slice.11), channel_id=1, source_target_pairs={{0,1},{1,2},{2,3},{3,128},{128,129},{129,130},{130,131},{131,0},{4... | collective-permute-start | bytes 417800 | tf_op jit(solution)/shard_map/ppermute | solution.py:49
  203.0 6.1 %collective-permute-start.21 = (bf16[32,2176]{1,0:T(8,128)(2,1)S(1)}, bf16[32,2176]{1,0:T(8,128)(2,1)S(1)}, u32[]{:S(2)}, u32[]{:S(2)}) collective-permute-start(bf16[32,2176]{1,0:T(8,128)(2,1)S(1)} %slice.12), channel_id=1, source_target_pairs={{0,131},{1,0},{2,1},{3,2},{128,3},{129,128},{130,129},{131,130},{4... | collective-permute-start | bytes 417800 | tf_op jit(solution)/shard_map/ppermute | solution.py:49
Sparse Core Ops, SparseCore 0:
  61.6 68.9 all-gather.1

commit v4 on v3

--- a/solution.py
+++ b/solution.py
@@ -331,8 +331,8 @@
         right, left = shift(right, 1), shift(left, -1)
         grad_right, grad_left = shift(grad_right, 1), shift(grad_left, -1)
         if step == 1:
-            part, right, left, grad_right, grad_left, asked = tie(
-                part, right, left, grad_right, grad_left, asked
+            right, left, asked = tie(
+                right, left, asked
             )
         index += [(me - step) % NZ, (me + step) % NZ]
         chunks += [right, left]
@@ -366,7 +366,7 @@
         name="project",
     )(jnp.stack(index[:early]), *chunks[:early], *grad_chunks[:early], *projections)
 
-    right, acc, chosen = tie(right, acc, chosen)
+    right, acc = tie(right, acc)
     chunks[5] = right
     fetched = exchange(chosen, Z).reshape(KEYS, DE)
     far = (shift(right, 1), shift(grad_left, -1))

time: 219 us -> 211 us (0.963)
  blocking collectives: 0 us -> 20.8 us
  starting transfers between devices: 67.4 us -> 48.6 us
  waiting for transfers between devices: 77.7 us -> 70.7 us
    all_to_all x0 -> x1, blocking collectives: none -> 20.8 us  [exchange(): return lax.all_to_all(x, axis, split_axis=0, concat_axis=0, tiled=True)]
    all_to_all x5 -> x4, starting transfers between devices: 34 us -> 19.7 us  [exchange(): return lax.all_to_all(x, axis, split_axis=0, concat_axis=0, tiled=True)]
    ppermute x22, waiting for transfers between devices: 58.1 us -> 47.4 us  [shift(): return lax.ppermute(x, Z, [(i, (i + by) % NZ) for i in range(NZ)])]
    ppermute x22, starting transfers between devices: 33.4 us -> 28.9 us  [shift(): return lax.ppermute(x, Z, [(i, (i + by) % NZ) for i in range(NZ)])]
    all_to_all x5 -> x4, waiting for transfers between devices: 19.6 us -> 23.2 us  [exchange(): return lax.all_to_all(x, axis, split_axis=0, concat_axis=0, tiled=True)]
    unnamed x33 -> x29, local copies, waits for them, and re-layouts: 6.57 us -> 5.79 us
  transfers between devices with their start and end apart: 28 -> 27, of which waited for: 12 -> 11; matrix products, arithmetic and copies ran while one was open for 3% -> 2% of each run, Pallas kernels for 13% -> 13%
where the time goes in v4:
time: 211 us
  waiting for transfers between devices  70.7 us (34%)
  starting transfers between devices  48.6 us (23%)
  Pallas kernels  43.5 us (21%)
  blocking collectives  20.8 us (10%)
  between operations  13.8 us (7%)
  local copies, waits for them, and re-layouts  12.7 us (6%)
    ppermute x22, waiting for transfers between devices, shift(): return lax.ppermute(x, Z, [(i, (i + by) % NZ) for i in range(NZ)])  47.4 us
    ppermute x22, starting transfers between devices, shift(): return lax.ppermute(x, Z, [(i, (i + by) % NZ) for i in range(NZ)])  28.9 us
    all_to_all x4, waiting for transfers between devices, exchange(): return lax.all_to_all(x, axis, split_axis=0, concat_axis=0, tiled=True)  23.2 us
    all_to_all x1, blocking collectives, exchange(): return lax.all_to_all(x, axis, split_axis=0, concat_axis=0, tiled=True)  20.8 us
    all_to_all x4, starting transfers between devices, exchange(): return lax.all_to_all(x, axis, split_axis=0, concat_axis=0, tiled=True)  19.7 us
    pallas_call x1, Pallas kernels, shards(): pl.pallas_call(attention, out_shape=jax.ShapeDtypeStruct((SEG, 2 * HALF +...  13.5 us
    pallas_call x4, Pallas kernels, finish_call(): pl.pallas_call(functools.partial(finish, starts), out_shape=jax.ShapeDtyp...  7.96 us
    pallas_call x1, Pallas kernels, shards(): pl.pallas_call(functools.partial(project_last, len(hiddens)), out_shape=(...  6.71 us
  transfers between devices with their start and end apart: 27, of which 11 were waited for; matrix products, arithmetic and copies ran while one was open for 2% of the time, Pallas kernels for 13%

profile of v4, /device:TPU:2, one launch (start us, length us, event | category | flops | bytes accessed | tf_op | source)
XLA Modules:
  0.0 210.8 jit_solution(13491705496993956131)
XLA Ops:
  6.6 0.9 constant_dynamic-slice_fusion
  7.6 0.8 dynamic_slice.6
  8.5 20.8 %all_to_all.32 = bf16[8,144,128]{2,1,0:T(8,128)(2,1)S(1)} all-to-all(bf16[8,144,128]{2,1,0:T(8,128)(2,1)S(1)} %pad_maximum_fusion), channel_id=1, replica_groups=mesh['group'=2,'dp'=32,'tensor'=4] {'group','tensor'}, dimensions={0} | all-to-all | bytes 589824 | tf_op jit(solution)/shard_map/all_to_all | solution.py:57
  29.3 0.7 copy_bitcast_fusion
  30.1 0.6 collective-permute-start
  30.7 2.7 %collective-permute-start.1 = (bf16[448,512]{1,0:T(8,128)(2,1)S(1)}, bf16[448,512]{1,0:T(8,128)(2,1)S(1)}, u32[]{:S(2)}, u32[]{:S(2)}) collective-permute-start(bf16[448,512]{1,0:T(8,128)(2,1)S(1)} %copy-done.6), channel_id=1, source_target_pairs={{0,131},{1,0},{2,1},{3,2},{128,3},{129,128},{130,129},{131,130},{4... | collective-permute-start | bytes 1376264 | tf_op jit(solution)/shard_map/ppermute | solution.py:49
  33.4 0.1 copy.35
  33.6 0.1 multiply_reduce_fusion
  33.6 0.7 copy.36
  34.3 7.6 %all-to-all-start = ((s32[32,1,2]{2,1,0:T(1,128)}), s32[32,1,2]{2,1,0:T(1,128)S(1)}, u32[]{:S(2)}, u32[]{:S(2)}) async-start(s32[32,1,2]{2,1,0:T(1,128)} %copy.36), calls=%async_computation | async-start | bytes 32768 | tf_op jit(solution)/shard_map/all_to_all | solution.py:57
  42.0 0.1 collective-permute-start.6
  42.1 6.0 %all-to-all-done = s32[32,1,2]{2,1,0:T(1,128)S(1)} async-done(((s32[32,1,2]{2,1,0:T(1,128)}), s32[32,1,2]{2,1,0:T(1,128)S(1)}, u32[]{:S(2)}, u32[]{:S(2)}) %all-to-all-start) | async-done | bytes 288 | tf_op jit(solution)/shard_map/all_to_all | solution.py:57
  48.0 0.1 copy.37
  48.1 0.1 copy.38
  48.2 0.1 reshape.126
  48.4 2.0 gather_fusion
  50.3 5.1 %all-to-all-start.1 = ((bf16[32,32,896]{2,1,0:T(8,128)(2,1)}), bf16[32,32,896]{2,1,0:T(8,128)(2,1)S(1)}, u32[]{:S(2)}, u32[]{:S(2)}) async-start(bf16[32,32,896]{2,1,0:T(8,128)(2,1)} %bitcast.4), calls=%async_computation.1 | async-start | bytes 3670016 | tf_op jit(solution)/shard_map/all_to_all | solution.py:57
  55.4 0.1 collective-permute-start.5
  55.5 0.1 collective-permute-start.2
  55.6 3.2 %collective-permute-start.8 = (bf16[448,512]{1,0:T(8,128)(2,1)}, bf16[448,512]{1,0:T(8,128)(2,1)}, u32[]{:S(2)}, u32[]{:S(2)}) collective-permute-start(bf16[448,512]{1,0:T(8,128)(2,1)} %collective-permute-done.6.refs_7_), channel_id=1, source_target_pairs={{0,131},{1,0},{2,1},{3,2},{128,3},{129,128},{130,129},{131,130},{4... | collective-permute-start | bytes 1376264 | tf_op jit(solution)/shard_map/ppermute | solution.py:49
  58.8 1.9 collective-permute-start.4
  60.8 9.4 %collective-permute-done.5.refs_6_ = bf16[448,512]{1,0:T(8,128)(2,1)} collective-permute-done((bf16[448,512]{1,0:T(8,128)(2,1)S(1)}, bf16[448,512]{1,0:T(8,128)(2,1)}, u32[]{:S(2)}, u32[]{:S(2)}) %collective-permute-start.5) | collective-permute-done | bytes 458784 | tf_op jit(solution)/shard_map/ppermute | solution.py:49
  70.2 9.8 %collective-permute-done.2.refs_3_ = bf16[448,512]{1,0:T(8,128)(2,1)} collective-permute-done((bf16[448,512]{1,0:T(8,128)(2,1)}, bf16[448,512]{1,0:T(8,128)(2,1)}, u32[]{:S(2)}, u32[]{:S(2)}) %collective-permute-start.2) | collective-permute-done | bytes 458784 | tf_op jit(solution)/shard_map/ppermute | solution.py:49
  80.0 3.2 %collective-permute-start.12 = (bf16[448,512]{1,0:T(8,128)(2,1)}, bf16[448,512]{1,0:T(8,128)(2,1)}, u32[]{:S(2)}, u32[]{:S(2)}) collective-permute-start(bf16[448,512]{1,0:T(8,128)(2,1)} %collective-permute-done.8.refs_9_), channel_id=1, source_target_pairs={{0,131},{1,0},{2,1},{3,2},{128,3},{129,128},{130,129},{131,130},{4... | collective-permute-start | bytes 1376264 | tf_op jit(solution)/shard_map/ppermute | solution.py:49
  83.3 0.1 stack.61.index_ref
  83.4 0.1 collective-permute-start.9
  83.4 6.3 %collective-permute-done.7.refs_8_ = bf16[448,512]{1,0:T(8,128)(2,1)S(1)} collective-permute-done((bf16[448,512]{1,0:T(8,128)(2,1)}, bf16[448,512]{1,0:T(8,128)(2,1)S(1)}, u32[]{:S(2)}, u32[]{:S(2)}) %collective-permute-start.7) | collective-permute-done | bytes 458784 | tf_op jit(solution)/shard_map/ppermute | solution.py:49
  89.8 0.8 copy-done.10
  90.5 6.6 %project.1 = (f32[448,768]{1,0:T(8,128)}, f32[448,1]{1,0:T(8,128)S(1)}) custom-call(s32[5]{0:T(128)S(1)} %stack.61.index_ref, bf16[448,512]{1,0:T(8,128)(2,1)} %hidden_hbm.1, bf16[448,512]{1,0:T(8,128)(2,1)} %collective-permute-done.refs_1_, bf16[448,512]{1,0:T(8,128)(2,1)} %copy-done.11, bf16[448,512]{1,0:T(8,128)(2,1)} %collective-permute-done.2.refs_3_, ...), custom_call_target="tpu_custom_call" | custom-call | flops 1688207360 | bytes 16000000 | tf_op jit(solution)/shard_map/project/pallas_call | solution.py:345
  97.1 0.7 copy-done.4
  97.8 1.9 collective-permute-done.3.refs_0_
  99.7 3.2 %collective-permute-start.13 = (bf16[448,512]{1,0:T(8,128)(2,1)}, bf16[448,512]{1,0:T(8,128)(2,1)}, u32[]{:S(2)}, u32[]{:S(2)}) collective-permute-start(bf16[448,512]{1,0:T(8,128)(2,1)} %collective-permute-done.12.refs_4_), channel_id=1, source_target_pairs={{0,131},{1,0},{2,1},{3,2},{128,3},{129,128},{130,129},{131,130},{4... | collective-permute-start | bytes 1376264 | tf_op jit(solution)/shard_map/ppermute | solution.py:49
  102.9 0.1 fusion.1
  103.0 0.1 pad_add_fusion.1.index_ref
  103.1 1.4 gather_fusion.1
  104.5 3.5 %all-to-all-start.2 = ((bf16[8,32,896]{2,1,0:T(8,128)(2,1)}), bf16[8,32,896]{2,1,0:T(8,128)(2,1)S(1)}, u32[]{:S(2)}, u32[]{:S(2)}) async-start(bf16[8,32,896]{2,1,0:T(8,128)(2,1)} %gather_fusion.1), calls=%async_computation.2 | async-start | bytes 917504 | tf_op jit(solution)/shard_map/all_to_all | solution.py:57
  108.0 1.5 collective-permute-done.11.refs_3_
  109.5 13.6 %collective-permute-done.10.refs_2_ = bf16[448,512]{1,0:T(8,128)(2,1)} collective-permute-done((bf16[448,512]{1,0:T(8,128)(2,1)}, bf16[448,512]{1,0:T(8,128)(2,1)}, u32[]{:S(2)}, u32[]{:S(2)}) %collective-permute-start.10) | collective-permute-done | bytes 458784 | tf_op jit(solution)/shard_map/ppermute | solution.py:49
  123.1 6.7 %project_last.1 = (bf16[8,64,768]{2,1,0:T(8,128)(2,1)}, f32[448,1]{1,0:T(8,128)S(1)}) custom-call(s32[3]{0:T(128)S(1)} %pad_add_fusion.1.index_ref, bf16[448,512]{1,0:T(8,128)(2,1)} %collective-permute-done.3.refs_0_, bf16[448,512]{1,0:T(8,128)(2,1)} %collective-permute-done.9.refs_1_, bf16[448,512]{1,0:T(8,128)(2,1)} %collective-permute-done.10.refs_2_, ...), custom_call_target="tpu_custom_call" | custom-call | flops 20000000000 | bytes 4000000 | tf_op jit(solution)/shard_map/project_last/pallas_call | solution.py:387
  129.8 0.7 copy-done.3
  130.5 3.5 %all-to-all-start.3 = ((bf16[8,64,768]{2,1,0:T(8,128)(2,1)}), bf16[8,64,768]{2,1,0:T(8,128)(2,1)S(1)}, u32[]{:S(2)}, u32[]{:S(2)}) async-start(bf16[8,64,768]{2,1,0:T(8,128)(2,1)} %get-tuple-element.34), calls=%async_computation.3 | async-start | bytes 1572864 | tf_op jit(solution)/shard_map/all_to_all | solution.py:57
  134.1 3.1 %encoder_queries.1.enc_q_hbm = bf16[256,896]{1,0:T(8,128)(2,1)} custom-call(bf16[256,896]{1,0:T(8,128)(2,1)} %bitcast.32, bf16[896,896]{1,0:T(8,128)(2,1)} %weight_hbm.1), custom_call_target="tpu_custom_call" | custom-call | flops 411041792 | bytes 3000000 | tf_op jit(solution)/shard_map/encoder_queries/pallas_call | solution.py:373
  137.1 17.2 %all-to-all-done.3.got_hbm = bf16[8,64,768]{2,1,0:T(8,128)(2,1)S(1)} async-done(((bf16[8,64,768]{2,1,0:T(8,128)(2,1)}), bf16[8,64,768]{2,1,0:T(8,128)(2,1)S(1)}, u32[]{:S(2)}, u32[]{:S(2)}) %all-to-all-start.3) | async-done | bytes 786464 | tf_op jit(solution)/shard_map/all_to_all | solution.py:57
  154.4 0.9 copy-done.7
  155.3 13.5 %attention.1.chunk_ref = bf16[64,2176]{1,0:T(8,128)(2,1)} custom-call(bf16[256,896]{1,0:T(8,128)(2,1)} %bitcast.33, bf16[256,896]{1,0:T(8,128)(2,1)} %encoder_queries.1.enc_q_hbm, bf16[8,64,768]{2,1,0:T(8,128)(2,1)} %copy-done.7, bf16[896,896]{1,0:T(8,128)(2,1)} %enc_out_hbm.1, bf16[16,2,144,1024]{3,2,1,0:T(8,128)(2,1)} %bitcast.29), custom_call_target="tpu_custom_call" | custom-call | flops 4000000000 | bytes 12000000 | tf_op jit(solution)/shard_map/attention/pallas_call | solution.py:415
  168.8 0.6 collective-permute-start.14
  169.4 2.7 %collective-permute-start.15 = (bf16[64,2176]{1,0:T(8,128)(2,1)}, bf16[64,2176]{1,0:T(8,128)(2,1)S(1)}, u32[]{:S(2)}, u32[]{:S(2)}) collective-permute-start(bf16[64,2176]{1,0:T(8,128)(2,1)} %attention.1.chunk_ref), channel_id=1, source_target_pairs={{0,131},{1,0},{2,1},{3,2},{128,3},{129,128},{130,129},{131,130},{4... | collective-permute-start | bytes 835592 | tf_op jit(solution)/shard_map/ppermute | solution.py:49
  172.1 5.7 %finish_first.1 = (bf16[448,512]{1,0:T(8,128)(2,1)}, bf16[448,512]{1,0:T(8,128)(2,1)}, f32[448,1]{1,0:T(8,128)S(1)}, bf16[2,32,16,1024]{3,2,1,0:T(8,128)(2,1)}) custom-call(s32[1]{0:T(128)} %bitcast.9.source_ref, bf16[64,2176]{1,0:T(8,128)(2,1)} %attention.1.chunk_ref, bf16[448,512]{1,0:T(8,128)(2,1)} %hidden_hbm.1, f32[448,1]{1,0:T(8,128)} %copy-done.3, ...), custom_call_target="tpu_custom_call" | custom-call | flops 134217728 | bytes 4000000 | tf_op jit(solution)/shard_map/finish_first/pallas_call | solution.py:439
  177.8 0.1 collective-permute-start.16
  177.9 3.2 %collective-permute-start.17 = (bf16[64,2176]{1,0:T(8,128)(2,1)S(1)}, bf16[64,2176]{1,0:T(8,128)(2,1)S(1)}, u32[]{:S(2)}, u32[]{:S(2)}) collective-permute-start(bf16[64,2176]{1,0:T(8,128)(2,1)S(1)} %collective-permute-done.15.refs_1_), channel_id=1, source_target_pairs={{0,131},{1,0},{2,1},{3,2},{128,3},{129,128},{130,129},{131,130},{4... | collective-permute-start | bytes 835592 | tf_op jit(solution)/shard_map/ppermute | solution.py:49
  181.1 0.1 pad_add_fusion.2.source_ref
  181.2 1.6 copy-done.1
  182.8 1.0 copy-done.2
  183.8 2.0 finish.4.refs_5_
  185.8 0.3 collective-permute-done.16.refs_0_
  186.1 3.5 %collective-permute-start.19 = (bf16[64,2176]{1,0:T(8,128)(2,1)S(1)}, bf16[64,2176]{1,0:T(8,128)(2,1)S(1)}, u32[]{:S(2)}, u32[]{:S(2)}) collective-permute-start(bf16[64,2176]{1,0:T(8,128)(2,1)S(1)} %collective-permute-done.17.refs_1_), channel_id=1, source_target_pairs={{0,131},{1,0},{2,1},{3,2},{128,3},{129,128},{130,129},{131,130},{4... | collective-permute-start | bytes 835592 | tf_op jit(solution)/shard_map/ppermute | solution.py:49
  189.6 0.1 pad_add_fusion.3.source_ref
  189.7 2.0 finish.5.refs_5_
  191.7 3.9 %collective-permute-done.18.refs_0_ = bf16[64,2176]{1,0:T(8,128)(2,1)S(1)} collective-permute-done((bf16[64,2176]{1,0:T(8,128)(2,1)S(1)}, bf16[64,2176]{1,0:T(8,128)(2,1)S(1)}, u32[]{:S(2)}, u32[]{:S(2)}) %collective-permute-start.18) | collective-permute-done | bytes 278560 | tf_op jit(solution)/shard_map/ppermute | solution.py:49
  195.6 0.1 collective-permute-start.20
  195.7 3.4 %collective-permute-start.21 = (bf16[32,2176]{1,0:T(8,128)(2,1)S(1)}, bf16[32,2176]{1,0:T(8,128)(2,1)S(1)}, u32[]{:S(2)}, u32[]{:S(2)}) collective-permute-start(bf16[32,2176]{1,0:T(8,128)(2,1)S(1)} %slice.12), channel_id=1, source_target_pairs={{0,131},{1,0},{2,1},{3,2},{128,3},{129,128},{130,129},{131,130},{4... | collective-permute-start | bytes 417800 | tf_op jit(solution)/shard_map/ppermute | solution.py:49
  199.2 2.0 finish.6.refs_5_
  201.2 0.8 collective-permute-done.20.refs_0_
  202.0 1.9 finish.7
  (57 shorter events, 0.5 us)
Async XLA Ops:
  6.5 41.8 %copy-start = (bf16[16,16,896]{2,1,0:T(8,128)(2,1)S(1)}, bf16[16,16,896]{2,1,0:T(8,128)(2,1)}, u32[]{:S(2)}) copy-start(bf16[16,16,896]{2,1,0:T(8,128)(2,1)} %param.19) | copy-start | bytes 1376260
  6.5 23.5 %copy-start.6 = (bf16[448,512]{1,0:T(8,128)(2,1)S(1)}, bf16[448,512]{1,0:T(8,128)(2,1)}, u32[]{:S(2)}) copy-start(bf16[448,512]{1,0:T(8,128)(2,1)} %hidden_hbm.1) | copy-start | bytes 1376260
  6.5 26.8 %copy-start.12 = (s32[7,2]{0,1:T(2,128)S(1)}, s32[7,2]{0,1:T(2,128)}, u32[]{:S(2)}) copy-start(s32[7,2]{0,1:T(2,128)} %param.20) | copy-start | bytes 172
  6.5 26.9 %copy-start.13 = (s32[7,1]{0,1:T(1,128)S(1)}, s32[7,1]{0,1:T(1,128)}, u32[]{:S(2)}) copy-start(s32[7,1]{0,1:T(1,128)} %param.21) | copy-start | bytes 88
  6.5 35.4 %copy-start.8 = (bf16[448,512]{1,0:T(8,128)(2,1)S(1)}, bf16[448,512]{1,0:T(8,128)(2,1)}, u32[]{:S(2)}) copy-start(bf16[448,512]{1,0:T(8,128)(2,1)} %refs_5_.1) | copy-start | bytes 1376260
  6.6 147.8 %all-gather.2.cloned.1.call-start = ((), (), s32[]{:S(2)}) async-start(), calls=%async_computation.5 | async-start | bytes 9732096 | tf_op jit(solution)/shard_map/all_gather | solution.py:341
  30.1 18.0 %collective-permute-start = (bf16[448,512]{1,0:T(8,128)(2,1)S(1)}, bf16[448,512]{1,0:T(8,128)(2,1)}, u32[]{:S(2)}, u32[]{:S(2)}) collective-permute-start(bf16[448,512]{1,0:T(8,128)(2,1)S(1)} %copy-done.6), channel_id=1, source_target_pairs={{0,1},{1,2},{2,3},{3,128},{128,129},{129,130},{130,131},{131,0},{4... | collective-permute-start | bytes 1376264 | tf_op jit(solution)/shard_map/ppermute | solution.py:49
  30.7 17.4 %collective-permute-start.1 = (bf16[448,512]{1,0:T(8,128)(2,1)S(1)}, bf16[448,512]{1,0:T(8,128)(2,1)S(1)}, u32[]{:S(2)}, u32[]{:S(2)}) collective-permute-start(bf16[448,512]{1,0:T(8,128)(2,1)S(1)} %copy-done.6), channel_id=1, source_target_pairs={{0,131},{1,0},{2,1},{3,2},{128,3},{129,128},{130,129},{131,130},{4... | collective-permute-start | bytes 1376264 | tf_op jit(solution)/shard_map/ppermute | solution.py:49
  34.3 13.7 %all-to-all-start = ((s32[32,1,2]{2,1,0:T(1,128)}), s32[32,1,2]{2,1,0:T(1,128)S(1)}, u32[]{:S(2)}, u32[]{:S(2)}) async-start(s32[32,1,2]{2,1,0:T(1,128)} %copy.36), calls=%async_computation | async-start | bytes 32768 | tf_op jit(solution)/shard_map/all_to_all | solution.py:57
  42.0 13.7 %collective-permute-start.6 = (bf16[448,512]{1,0:T(8,128)(2,1)S(1)}, bf16[448,512]{1,0:T(8,128)(2,1)}, u32[]{:S(2)}, u32[]{:S(2)}) collective-permute-start(bf16[448,512]{1,0:T(8,128)(2,1)S(1)} %copy-done.8), channel_id=1, source_target_pairs={{0,131},{1,0},{2,1},{3,2},{128,3},{129,128},{130,129},{131,130},{4... | collective-permute-start | bytes 1376264 | tf_op jit(solution)/shard_map/ppermute | solution.py:49
  48.1 2.2 %copy-start.11 = (bf16[448,512]{1,0:T(8,128)(2,1)}, bf16[448,512]{1,0:T(8,128)(2,1)S(1)}, u32[]{:S(2)}) copy-start(bf16[448,512]{1,0:T(8,128)(2,1)S(1)} %collective-permute-done.1.refs_2_) | copy-start | bytes 1376260
  50.3 52.8 %all-to-all-start.1 = ((bf16[32,32,896]{2,1,0:T(8,128)(2,1)}), bf16[32,32,896]{2,1,0:T(8,128)(2,1)S(1)}, u32[]{:S(2)}, u32[]{:S(2)}) async-start(bf16[32,32,896]{2,1,0:T(8,128)(2,1)} %bitcast.4), calls=%async_computation.1 | async-start | bytes 3670016 | tf_op jit(solution)/shard_map/all_to_all | solution.py:57
  55.4 14.8 %collective-permute-start.5 = (bf16[448,512]{1,0:T(8,128)(2,1)S(1)}, bf16[448,512]{1,0:T(8,128)(2,1)}, u32[]{:S(2)}, u32[]{:S(2)}) collective-permute-start(bf16[448,512]{1,0:T(8,128)(2,1)S(1)} %copy-done.8), channel_id=1, source_target_pairs={{0,1},{1,2},{2,3},{3,128},{128,129},{129,130},{130,131},{131,0},{4... | collective-permute-start | bytes 1376264 | tf_op jit(solution)/shard_map/ppermute | solution.py:49
  55.5 24.5 %collective-permute-start.2 = (bf16[448,512]{1,0:T(8,128)(2,1)}, bf16[448,512]{1,0:T(8,128)(2,1)}, u32[]{:S(2)}, u32[]{:S(2)}) collective-permute-start(bf16[448,512]{1,0:T(8,128)(2,1)} %collective-permute-done.refs_1_), channel_id=1, source_target_pairs={{0,1},{1,2},{2,3},{3,128},{128,129},{129,130},{130,131},{131,0},{4... | collective-permute-start | bytes 1376264 | tf_op jit(solution)/shard_map/ppermute | solution.py:49
  55.6 24.4 %collective-permute-start.8 = (bf16[448,512]{1,0:T(8,128)(2,1)}, bf16[448,512]{1,0:T(8,128)(2,1)}, u32[]{:S(2)}, u32[]{:S(2)}) collective-permute-start(bf16[448,512]{1,0:T(8,128)(2,1)} %collective-permute-done.6.refs_7_), channel_id=1, source_target_pairs={{0,131},{1,0},{2,1},{3,2},{128,3},{129,128},{130,129},{131,130},{4... | collective-permute-start | bytes 1376264 | tf_op jit(solution)/shard_map/ppermute | solution.py:49
  58.8 24.5 %collective-permute-start.4 = (bf16[448,512]{1,0:T(8,128)(2,1)}, bf16[448,512]{1,0:T(8,128)(2,1)S(1)}, u32[]{:S(2)}, u32[]{:S(2)}) collective-permute-start(bf16[448,512]{1,0:T(8,128)(2,1)} %copy-done.11), channel_id=1, source_target_pairs={{0,131},{1,0},{2,1},{3,2},{128,3},{129,128},{130,129},{131,130},{4... | collective-permute-start | bytes 1376264 | tf_op jit(solution)/shard_map/ppermute | solution.py:49
  70.2 19.6 %collective-permute-start.7 = (bf16[448,512]{1,0:T(8,128)(2,1)}, bf16[448,512]{1,0:T(8,128)(2,1)S(1)}, u32[]{:S(2)}, u32[]{:S(2)}) collective-permute-start(bf16[448,512]{1,0:T(8,128)(2,1)} %collective-permute-done.5.refs_6_), channel_id=1, source_target_pairs={{0,1},{1,2},{2,3},{3,128},{128,129},{129,130},{130,131},{131,0},{4... | collective-permute-start | bytes 1376264 | tf_op jit(solution)/shard_map/ppermute | solution.py:49
  80.0 19.7 %collective-permute-start.3 = (bf16[448,512]{1,0:T(8,128)(2,1)}, bf16[448,512]{1,0:T(8,128)(2,1)}, u32[]{:S(2)}, u32[]{:S(2)}) collective-permute-start(bf16[448,512]{1,0:T(8,128)(2,1)} %collective-permute-done.2.refs_3_), channel_id=1, source_target_pairs={{0,1},{1,2},{2,3},{3,128},{128,129},{129,130},{130,131},{131,0},{4... | collective-permute-start | bytes 1376264 | tf_op jit(solution)/shard_map/ppermute | solution.py:49
  80.0 19.7 %collective-permute-start.12 = (bf16[448,512]{1,0:T(8,128)(2,1)}, bf16[448,512]{1,0:T(8,128)(2,1)}, u32[]{:S(2)}, u32[]{:S(2)}) collective-permute-start(bf16[448,512]{1,0:T(8,128)(2,1)} %collective-permute-done.8.refs_9_), channel_id=1, source_target_pairs={{0,131},{1,0},{2,1},{3,2},{128,3},{129,128},{130,129},{131,130},{4... | collective-permute-start | bytes 1376264 | tf_op jit(solution)/shard_map/ppermute | solution.py:49
  83.4 6.4 %copy-start.9 = (bf16[448,512]{1,0:T(8,128)(2,1)}, bf16[448,512]{1,0:T(8,128)(2,1)S(1)}, u32[]{:S(2)}) copy-start(bf16[448,512]{1,0:T(8,128)(2,1)S(1)} %collective-permute-done.4.refs_4_) | copy-start | bytes 1376260
  83.4 24.6 %collective-permute-start.9 = (bf16[448,512]{1,0:T(8,128)(2,1)S(1)}, bf16[448,512]{1,0:T(8,128)(2,1)}, u32[]{:S(2)}, u32[]{:S(2)}) collective-permute-start(bf16[448,512]{1,0:T(8,128)(2,1)S(1)} %collective-permute-done.4.refs_4_), channel_id=1, source_target_pairs={{0,131},{1,0},{2,1},{3,2},{128,3},{129,128},{130,129},{131,130},{4... | collective-permute-start | bytes 1376264 | tf_op jit(solution)/shard_map/ppermute | solution.py:49
  89.8 0.8 copy-start.10
  89.8 19.8 %collective-permute-start.11 = (bf16[448,512]{1,0:T(8,128)(2,1)S(1)}, bf16[448,512]{1,0:T(8,128)(2,1)}, u32[]{:S(2)}, u32[]{:S(2)}) collective-permute-start(bf16[448,512]{1,0:T(8,128)(2,1)S(1)} %collective-permute-done.7.refs_8_), channel_id=1, source_target_pairs={{0,1},{1,2},{2,3},{3,128},{128,129},{129,130},{130,131},{131,0},{4... | collective-permute-start | bytes 1376264 | tf_op jit(solution)/shard_map/ppermute | solution.py:49
  97.1 0.7 copy-start.4
  99.7 23.4 %collective-permute-start.10 = (bf16[448,512]{1,0:T(8,128)(2,1)}, bf16[448,512]{1,0:T(8,128)(2,1)}, u32[]{:S(2)}, u32[]{:S(2)}) collective-permute-start(bf16[448,512]{1,0:T(8,128)(2,1)} %collective-permute-done.3.refs_0_), channel_id=1, source_target_pairs={{0,1},{1,2},{2,3},{3,128},{128,129},{129,130},{130,131},{131,0},{4... | collective-permute-start | bytes 1376264 | tf_op jit(solution)/shard_map/ppermute | solution.py:49
  99.7 23.4 %collective-permute-start.13 = (bf16[448,512]{1,0:T(8,128)(2,1)}, bf16[448,512]{1,0:T(8,128)(2,1)}, u32[]{:S(2)}, u32[]{:S(2)}) collective-permute-start(bf16[448,512]{1,0:T(8,128)(2,1)} %collective-permute-done.12.refs_4_), channel_id=1, source_target_pairs={{0,131},{1,0},{2,1},{3,2},{128,3},{129,128},{130,129},{131,130},{4... | collective-permute-start | bytes 1376264 | tf_op jit(solution)/shard_map/ppermute | solution.py:49
  104.5 26.0 %all-to-all-start.2 = ((bf16[8,32,896]{2,1,0:T(8,128)(2,1)}), bf16[8,32,896]{2,1,0:T(8,128)(2,1)S(1)}, u32[]{:S(2)}, u32[]{:S(2)}) async-start(bf16[8,32,896]{2,1,0:T(8,128)(2,1)} %gather_fusion.1), calls=%async_computation.2 | async-start | bytes 917504 | tf_op jit(solution)/shard_map/all_to_all | solution.py:57
  129.8 0.7 copy-start.3
  130.5 3.6 %copy-start.5 = (bf16[8,32,896]{2,1,0:T(8,128)(2,1)}, bf16[8,32,896]{2,1,0:T(8,128)(2,1)S(1)}, u32[]{:S(2)}) copy-start(bf16[8,32,896]{2,1,0:T(8,128)(2,1)S(1)} %all-to-all-done.2) | copy-start | bytes 1376260
  130.5 23.9 %all-to-all-start.3 = ((bf16[8,64,768]{2,1,0:T(8,128)(2,1)}), bf16[8,64,768]{2,1,0:T(8,128)(2,1)S(1)}, u32[]{:S(2)}, u32[]{:S(2)}) async-start(bf16[8,64,768]{2,1,0:T(8,128)(2,1)} %get-tuple-element.34), calls=%async_computation.3 | async-start | bytes 1572864 | tf_op jit(solution)/shard_map/all_to_all | solution.py:57
  154.4 0.9 copy-start.7
  168.8 9.0 %collective-permute-start.14 = (bf16[64,2176]{1,0:T(8,128)(2,1)}, bf16[64,2176]{1,0:T(8,128)(2,1)S(1)}, u32[]{:S(2)}, u32[]{:S(2)}) collective-permute-start(bf16[64,2176]{1,0:T(8,128)(2,1)} %attention.1.chunk_ref), channel_id=1, source_target_pairs={{0,1},{1,2},{2,3},{3,128},{128,129},{129,130},{130,131},{131,0},{4... | collective-permute-start | bytes 835592 | tf_op jit(solution)/shard_map/ppermute | solution.py:49
  169.4 8.4 %collective-permute-start.15 = (bf16[64,2176]{1,0:T(8,128)(2,1)}, bf16[64,2176]{1,0:T(8,128)(2,1)S(1)}, u32[]{:S(2)}, u32[]{:S(2)}) collective-permute-start(bf16[64,2176]{1,0:T(8,128)(2,1)} %attention.1.chunk_ref), channel_id=1, source_target_pairs={{0,131},{1,0},{2,1},{3,2},{128,3},{129,128},{130,129},{131,130},{4... | collective-permute-start | bytes 835592 | tf_op jit(solution)/shard_map/ppermute | solution.py:49
  177.8 8.3 %collective-permute-start.16 = (bf16[64,2176]{1,0:T(8,128)(2,1)S(1)}, bf16[64,2176]{1,0:T(8,128)(2,1)S(1)}, u32[]{:S(2)}, u32[]{:S(2)}) collective-permute-start(bf16[64,2176]{1,0:T(8,128)(2,1)S(1)} %collective-permute-done.14.refs_0_), channel_id=1, source_target_pairs={{0,1},{1,2},{2,3},{3,128},{128,129},{129,130},{130,131},{131,0},{4... | collective-permute-start | bytes 835592 | tf_op jit(solution)/shard_map/ppermute | solution.py:49
  177.9 8.2 %collective-permute-start.17 = (bf16[64,2176]{1,0:T(8,128)(2,1)S(1)}, bf16[64,2176]{1,0:T(8,128)(2,1)S(1)}, u32[]{:S(2)}, u32[]{:S(2)}) collective-permute-start(bf16[64,2176]{1,0:T(8,128)(2,1)S(1)} %collective-permute-done.15.refs_1_), channel_id=1, source_target_pairs={{0,131},{1,0},{2,1},{3,2},{128,3},{129,128},{130,129},{131,130},{4... | collective-permute-start | bytes 835592 | tf_op jit(solution)/shard_map/ppermute | solution.py:49
  181.2 1.6 copy-start.1
  182.8 1.0 copy-start.2
  186.1 9.5 %collective-permute-start.18 = (bf16[64,2176]{1,0:T(8,128)(2,1)S(1)}, bf16[64,2176]{1,0:T(8,128)(2,1)S(1)}, u32[]{:S(2)}, u32[]{:S(2)}) collective-permute-start(bf16[64,2176]{1,0:T(8,128)(2,1)S(1)} %collective-permute-done.16.refs_0_), channel_id=1, source_target_pairs={{0,1},{1,2},{2,3},{3,128},{128,129},{129,130},{130,131},{131,0},{4... | collective-permute-start | bytes 835592 | tf_op jit(solution)/shard_map/ppermute | solution.py:49
  186.1 9.5 %collective-permute-start.19 = (bf16[64,2176]{1,0:T(8,128)(2,1)S(1)}, bf16[64,2176]{1,0:T(8,128)(2,1)S(1)}, u32[]{:S(2)}, u32[]{:S(2)}) collective-permute-start(bf16[64,2176]{1,0:T(8,128)(2,1)S(1)} %collective-permute-done.17.refs_1_), channel_id=1, source_target_pairs={{0,131},{1,0},{2,1},{3,2},{128,3},{129,128},{130,129},{131,130},{4... | collective-permute-start | bytes 835592 | tf_op jit(solution)/shard_map/ppermute | solution.py:49
  195.6 6.4 %collective-permute-start.20 = (bf16[32,2176]{1,0:T(8,128)(2,1)S(1)}, bf16[32,2176]{1,0:T(8,128)(2,1)S(1)}, u32[]{:S(2)}, u32[]{:S(2)}) collective-permute-start(bf16[32,2176]{1,0:T(8,128)(2,1)S(1)} %slice.11), channel_id=1, source_target_pairs={{0,1},{1,2},{2,3},{3,128},{128,129},{129,130},{130,131},{131,0},{4... | collective-permute-start | bytes 417800 | tf_op jit(solution)/shard_map/ppermute | solution.py:49
  195.7 6.3 %collective-permute-start.21 = (bf16[32,2176]{1,0:T(8,128)(2,1)S(1)}, bf16[32,2176]{1,0:T(8,128)(2,1)S(1)}, u32[]{:S(2)}, u32[]{:S(2)}) collective-permute-start(bf16[32,2176]{1,0:T(8,128)(2,1)S(1)} %slice.12), channel_id=1, source_target_pairs={{0,131},{1,0},{2,1},{3,2},{128,3},{129,128},{130,129},{131,130},{4... | collective-permute-start | bytes 417800 | tf_op jit(solution)/shard_map/ppermute | solution.py:49
Sparse Core Ops, SparseCore 0:
  30.2 69.6 all-gather.1

commit v5 on v4

--- a/solution.py
+++ b/solution.py
@@ -185,33 +185,39 @@
         jnp.concatenate([got_ref[z, :, 512:736] for z in range(n, n + 4)], axis=1)
         for n in (0, 4)
     )
-    for h in range(EHEADS):
-        columns = slice(h * HEAD, (h + 1) * HEAD)
-        exponent = jnp.exp(dot_nt(enc_q_ref[:, columns], cond_keys[:, columns]) * SCALE)
-        weights = (exponent / jnp.sum(exponent, axis=-1, keepdims=True)).astype(BF)
-        mixed_ref[:, columns] = dot(weights, cond_values[:, columns]).astype(BF)
+    parts = [slice(h * HEAD, (h + 1) * HEAD) for h in range(EHEADS)]
+    exponents = [
+        jnp.exp(dot_nt(enc_q_ref[:, columns], cond_keys[:, columns]) * SCALE) for columns in parts
+    ]
+    weights = [(e / jnp.sum(e, axis=-1, keepdims=True)).astype(BF) for e in exponents]
+    for columns, weight in zip(parts, weights):
+        mixed_ref[:, columns] = dot(weight, cond_values[:, columns]).astype(BF)
     encoded = (fetched_ref[...].astype(F32) + dot(mixed_ref[...], enc_out_ref[...])).astype(BF)
     total = jnp.zeros((SEG, HEAD), F32)
     for j in range(2):
         large[j].wait()
         key_ref[j] = dot(encoded, kv_ref[j, 0:8].reshape(DE, HALF)).astype(BF)
         value_ref[j] = dot(encoded, kv_ref[j, 8:16].reshape(DE, HALF)).astype(BF)
-        for z in range(NZ):
-            columns = slice(z * HEAD, (z + 1) * HEAD)
-            query = got_ref[z, :, j * HEAD : (j + 1) * HEAD]
-            grad_att = got_ref[z, :, (2 + j) * HEAD : (3 + j) * HEAD]
-            key, value = key_ref[j, :, columns], value_ref[j, :, columns]
-            exponent = jnp.exp(dot_nt(query, key) * SCALE)
-            probs = exponent / jnp.sum(exponent, axis=-1, keepdims=True)
-            attended = dot(probs.astype(BF), value).astype(BF)
-            delta = jnp.sum(
-                grad_att.astype(F32) * attended.astype(F32), axis=-1, keepdims=True
-            )
-            grad_probs = dot_nt(grad_att, value)
-            grad_scores = (probs * (grad_probs - delta) * SCALE).astype(BF)
-            grad_query = dot(grad_scores, key).astype(BF)
-            out_ref[:, j * HALF + z * HEAD : j * HALF + (z + 1) * HEAD] = grad_query
-            total = total + grad_query.astype(F32) * query.astype(F32)
+        for group in (range(0, 4), range(4, 8)):
+            queries = [got_ref[z, :, j * HEAD : (j + 1) * HEAD] for z in group]
+            grads = [got_ref[z, :, (2 + j) * HEAD : (3 + j) * HEAD] for z in group]
+            keys = [key_ref[j, :, z * HEAD : (z + 1) * HEAD] for z in group]
+            values = [value_ref[j, :, z * HEAD : (z + 1) * HEAD] for z in group]
+            exponents = [jnp.exp(dot_nt(q, k) * SCALE) for q, k in zip(queries, keys)]
+            grad_probs = [dot_nt(g, v) for g, v in zip(grads, values)]
+            probs = [e / jnp.sum(e, axis=-1, keepdims=True) for e in exponents]
+            attended = [dot(p.astype(BF), v).astype(BF) for p, v in zip(probs, values)]
+            deltas = [
+                jnp.sum(g.astype(F32) * x.astype(F32), axis=-1, keepdims=True)
+                for g, x in zip(grads, attended)
+            ]
+            grad_scores = [
+                (p * (g - d) * SCALE).astype(BF) for p, g, d in zip(probs, grad_probs, deltas)
+            ]
+            for z, score, key, query in zip(group, grad_scores, keys, queries):
+                grad_query = dot(score, key).astype(BF)
+                out_ref[:, j * HALF + z * HEAD : j * HALF + (z + 1) * HEAD] = grad_query
+                total = total + grad_query.astype(F32) * query.astype(F32)
     stat = jnp.sum(total, axis=-1, keepdims=True) / D
     high = stat.astype(BF)
     low = (stat - high.astype(F32)).astype(BF)
@@ -329,11 +335,11 @@
     index, chunks, grad_chunks = [me], [hidden], [cotangent]
     for step in range(1, 4):
         right, left = shift(right, 1), shift(left, -1)
+        if step == 1:
+            part, right, left = tie(part, right, left)
         grad_right, grad_left = shift(grad_right, 1), shift(grad_left, -1)
-        if step == 1:
-            right, left, asked = tie(
-                right, left, asked
-            )
+        if step == 2:
+            asked, right, left = tie(asked, right, left)
         index += [(me - step) % NZ, (me + step) % NZ]
         chunks += [right, left]
         grad_chunks += [grad_right, grad_left]

time: 211 us -> 206 us (0.976)
  blocking collectives: 20.8 us -> 0 us
  starting transfers between devices: 48.6 us -> 61.5 us
  waiting for transfers between devices: 70.7 us -> 78.3 us
  Pallas kernels: 43.5 us -> 38.5 us
    all_to_all x1 -> x0, blocking collectives: 20.8 us -> none  [exchange(): return lax.all_to_all(x, axis, split_axis=0, concat_axis=0, tiled=True)]
    ppermute x22, waiting for transfers between devices: 47.4 us -> 59.2 us  [shift(): return lax.ppermute(x, Z, [(i, (i + by) % NZ) for i in range(NZ)])]
    all_to_all x4 -> x5, starting transfers between devices: 19.7 us -> 29.3 us  [exchange(): return lax.all_to_all(x, axis, split_axis=0, concat_axis=0, tiled=True)]
    pallas_call x1, Pallas kernels: 13.5 us -> 8.65 us  [shards(): pl.pallas_call(attention, out_shape=jax.ShapeDtypeStruct((SEG, 2 * HALF +...]
    all_to_all x4 -> x5, waiting for transfers between devices: 23.2 us -> 19.1 us  [exchange(): return lax.all_to_all(x, axis, split_axis=0, concat_axis=0, tiled=True)]
    ppermute x22, starting transfers between devices: 28.9 us -> 32.2 us  [shift(): return lax.ppermute(x, Z, [(i, (i + by) % NZ) for i in range(NZ)])]
    unnamed x29 -> x33, local copies, waits for them, and re-layouts: 5.79 us -> 5.01 us
  transfers between devices with their start and end apart: 27 -> 28, of which waited for: 11 -> 12; matrix products, arithmetic and copies ran while one was open for 2% -> 3% of each run, Pallas kernels for 13% -> 14%
where the time goes in v5:
time: 206 us; the launch traced here: 205 us
  waiting for transfers between devices  78.3 us (38%)
  starting transfers between devices  61.5 us (30%)
  Pallas kernels  38.5 us (19%)
  between operations  13.7 us (7%)
  local copies, waits for them, and re-layouts  12 us (6%)
    ppermute x22, waiting for transfers between devices, shift(): return lax.ppermute(x, Z, [(i, (i + by) % NZ) for i in range(NZ)])  59.2 us
    ppermute x22, starting transfers between devices, shift(): return lax.ppermute(x, Z, [(i, (i + by) % NZ) for i in range(NZ)])  32.2 us
    all_to_all x5, starting transfers between devices, exchange(): return lax.all_to_all(x, axis, split_axis=0, concat_axis=0, tiled=True)  29.3 us
    all_to_all x5, waiting for transfers between devices, exchange(): return lax.all_to_all(x, axis, split_axis=0, concat_axis=0, tiled=True)  19.1 us
    pallas_call x1, Pallas kernels, shards(): pl.pallas_call(attention, out_shape=jax.ShapeDtypeStruct((SEG, 2 * HALF +...  8.65 us
    pallas_call x4, Pallas kernels, finish_call(): pl.pallas_call(functools.partial(finish, starts), out_shape=jax.ShapeDtyp...  7.96 us
    pallas_call x1, Pallas kernels, shards(): pl.pallas_call(functools.partial(project_last, len(hiddens)), out_shape=(...  6.69 us
    pallas_call x1, Pallas kernels, shards(): pl.pallas_call(functools.partial(project, early), out_shape=(jax.ShapeDty...  6.47 us
  transfers between devices with their start and end apart: 28, of which 12 were waited for; matrix products, arithmetic and copies ran while one was open for 3% of the time, Pallas kernels for 14%

profile of v5, /device:TPU:2, one launch (start us, length us, event | category | flops | bytes accessed | tf_op | source)
XLA Modules:
  0.0 205.5 jit_solution(15659648707631805815)
XLA Ops:
  6.6 1.0 constant_dynamic-slice_fusion
  7.6 0.8 dynamic_slice.6
  8.4 0.7 pad_maximum_fusion
  9.1 8.5 %all-to-all-start.1 = ((bf16[8,144,128]{2,1,0:T(8,128)(2,1)}), bf16[8,144,128]{2,1,0:T(8,128)(2,1)S(1)}, u32[]{:S(2)}, u32[]{:S(2)}) async-start(bf16[8,144,128]{2,1,0:T(8,128)(2,1)} %pad_maximum_fusion), calls=%async_computation.1 | async-start | bytes 589824 | tf_op jit(solution)/shard_map/all_to_all | solution.py:57
  17.6 2.1 collective-permute-start
  19.7 1.3 collective-permute-start.1
  21.0 16.3 %collective-permute-done.refs_1_ = bf16[448,512]{1,0:T(8,128)(2,1)S(1)} collective-permute-done((bf16[448,512]{1,0:T(8,128)(2,1)S(1)}, bf16[448,512]{1,0:T(8,128)(2,1)S(1)}, u32[]{:S(2)}, u32[]{:S(2)}) %collective-permute-start) | collective-permute-done | bytes 458784 | tf_op jit(solution)/shard_map/ppermute | solution.py:49
  37.3 0.8 copy_bitcast_fusion
  38.1 0.4 collective-permute-start.2
  38.6 2.9 %collective-permute-start.3 = (bf16[448,512]{1,0:T(8,128)(2,1)S(1)}, bf16[448,512]{1,0:T(8,128)(2,1)S(1)}, u32[]{:S(2)}, u32[]{:S(2)}) collective-permute-start(bf16[448,512]{1,0:T(8,128)(2,1)S(1)} %collective-permute-done.1.refs_2_), channel_id=1, source_target_pairs={{0,131},{1,0},{2,1},{3,2},{128,3},{129,128},{130,129},{131,130},{4... | collective-permute-start | bytes 1376264 | tf_op jit(solution)/shard_map/ppermute | solution.py:49
  41.4 0.1 copy.35
  41.6 0.1 multiply_reduce_fusion
  41.7 0.7 copy.36
  42.4 7.6 %all-to-all-start = ((s32[32,1,2]{2,1,0:T(1,128)}), s32[32,1,2]{2,1,0:T(1,128)S(1)}, u32[]{:S(2)}, u32[]{:S(2)}) async-start(s32[32,1,2]{2,1,0:T(1,128)} %copy.36), calls=%async_computation | async-start | bytes 32768 | tf_op jit(solution)/shard_map/all_to_all | solution.py:57
  50.0 0.3 collective-permute-start.6
  50.4 5.7 %all-to-all-done = s32[32,1,2]{2,1,0:T(1,128)S(1)} async-done(((s32[32,1,2]{2,1,0:T(1,128)}), s32[32,1,2]{2,1,0:T(1,128)S(1)}, u32[]{:S(2)}, u32[]{:S(2)}) %all-to-all-start) | async-done | bytes 288 | tf_op jit(solution)/shard_map/all_to_all | solution.py:57
  56.1 0.1 copy.37
  56.2 0.1 copy.39
  56.3 0.1 reshape.126
  56.4 2.0 gather_fusion
  58.4 5.1 %all-to-all-start.2 = ((bf16[32,32,896]{2,1,0:T(8,128)(2,1)}), bf16[32,32,896]{2,1,0:T(8,128)(2,1)S(1)}, u32[]{:S(2)}, u32[]{:S(2)}) async-start(bf16[32,32,896]{2,1,0:T(8,128)(2,1)} %bitcast.8), calls=%async_computation.2 | async-start | bytes 3670016 | tf_op jit(solution)/shard_map/all_to_all | solution.py:57
  63.5 0.1 collective-permute-start.5
  63.6 3.2 %collective-permute-start.8 = (bf16[448,512]{1,0:T(8,128)(2,1)}, bf16[448,512]{1,0:T(8,128)(2,1)}, u32[]{:S(2)}, u32[]{:S(2)}) collective-permute-start(bf16[448,512]{1,0:T(8,128)(2,1)} %collective-permute-done.6.refs_7_), channel_id=1, source_target_pairs={{0,131},{1,0},{2,1},{3,2},{128,3},{129,128},{130,129},{131,130},{4... | collective-permute-start | bytes 1376264 | tf_op jit(solution)/shard_map/ppermute | solution.py:49
  66.8 10.6 %collective-permute-done.5.refs_6_ = bf16[448,512]{1,0:T(8,128)(2,1)} collective-permute-done((bf16[448,512]{1,0:T(8,128)(2,1)S(1)}, bf16[448,512]{1,0:T(8,128)(2,1)}, u32[]{:S(2)}, u32[]{:S(2)}) %collective-permute-start.5) | collective-permute-done | bytes 458784 | tf_op jit(solution)/shard_map/ppermute | solution.py:49
  77.5 3.2 %collective-permute-start.12 = (bf16[448,512]{1,0:T(8,128)(2,1)}, bf16[448,512]{1,0:T(8,128)(2,1)}, u32[]{:S(2)}, u32[]{:S(2)}) collective-permute-start(bf16[448,512]{1,0:T(8,128)(2,1)} %collective-permute-done.8.refs_9_), channel_id=1, source_target_pairs={{0,131},{1,0},{2,1},{3,2},{128,3},{129,128},{130,129},{131,130},{4... | collective-permute-start | bytes 1376264 | tf_op jit(solution)/shard_map/ppermute | solution.py:49
  80.7 0.1 stack.61.index_ref
  80.8 11.5 %collective-permute-done.7.refs_8_ = bf16[448,512]{1,0:T(8,128)(2,1)S(1)} collective-permute-done((bf16[448,512]{1,0:T(8,128)(2,1)}, bf16[448,512]{1,0:T(8,128)(2,1)S(1)}, u32[]{:S(2)}, u32[]{:S(2)}) %collective-permute-start.7) | collective-permute-done | bytes 458784 | tf_op jit(solution)/shard_map/ppermute | solution.py:49
  92.4 3.2 %collective-permute-start.9 = (bf16[448,512]{1,0:T(8,128)(2,1)S(1)}, bf16[448,512]{1,0:T(8,128)(2,1)}, u32[]{:S(2)}, u32[]{:S(2)}) collective-permute-start(bf16[448,512]{1,0:T(8,128)(2,1)S(1)} %collective-permute-done.3.refs_4_), channel_id=1, source_target_pairs={{0,131},{1,0},{2,1},{3,2},{128,3},{129,128},{130,129},{131,130},{4... | collective-permute-start | bytes 1376264 | tf_op jit(solution)/shard_map/ppermute | solution.py:49
  95.6 6.5 %project.1 = (f32[448,768]{1,0:T(8,128)}, f32[448,1]{1,0:T(8,128)S(1)}) custom-call(s32[5]{0:T(128)S(1)} %stack.61.index_ref, bf16[448,512]{1,0:T(8,128)(2,1)} %hidden_hbm.1, bf16[448,512]{1,0:T(8,128)(2,1)} %copy-done.11, bf16[448,512]{1,0:T(8,128)(2,1)} %copy-done.12, bf16[448,512]{1,0:T(8,128)(2,1)} %copy-done.13, bf16[448,512]{1,0:T(8,128)(2,1)} %copy-done.9, ...), custom_call_target="tpu_custom_call" | custom-call | flops 1688207360 | bytes 16000000 | tf_op jit(solution)/shard_map/project/pallas_call | solution.py:351
  102.1 0.7 copy-done.4
  102.8 2.0 collective-permute-start.10
  104.8 0.1 fusion.1
  104.9 0.1 pad_add_fusion.1.index_ref
  105.0 1.4 gather_fusion.1
  106.4 4.6 %all-to-all-start.3 = ((bf16[8,32,896]{2,1,0:T(8,128)(2,1)}), bf16[8,32,896]{2,1,0:T(8,128)(2,1)S(1)}, u32[]{:S(2)}, u32[]{:S(2)}) async-start(bf16[8,32,896]{2,1,0:T(8,128)(2,1)} %gather_fusion.1), calls=%async_computation.3 | async-start | bytes 917504 | tf_op jit(solution)/shard_map/all_to_all | solution.py:57
  111.0 1.2 collective-permute-done.11.refs_3_
  112.1 5.4 %collective-permute-done.13.refs_5_ = bf16[448,512]{1,0:T(8,128)(2,1)} collective-permute-done((bf16[448,512]{1,0:T(8,128)(2,1)}, bf16[448,512]{1,0:T(8,128)(2,1)}, u32[]{:S(2)}, u32[]{:S(2)}) %collective-permute-start.13) | collective-permute-done | bytes 458784 | tf_op jit(solution)/shard_map/ppermute | solution.py:49
  117.6 10.6 %collective-permute-done.10.refs_2_ = bf16[448,512]{1,0:T(8,128)(2,1)} collective-permute-done((bf16[448,512]{1,0:T(8,128)(2,1)}, bf16[448,512]{1,0:T(8,128)(2,1)}, u32[]{:S(2)}, u32[]{:S(2)}) %collective-permute-start.10) | collective-permute-done | bytes 458784 | tf_op jit(solution)/shard_map/ppermute | solution.py:49
  128.1 6.7 %project_last.1 = (bf16[8,64,768]{2,1,0:T(8,128)(2,1)}, f32[448,1]{1,0:T(8,128)S(1)}) custom-call(s32[3]{0:T(128)S(1)} %pad_add_fusion.1.index_ref, bf16[448,512]{1,0:T(8,128)(2,1)} %collective-permute-done.4.refs_0_, bf16[448,512]{1,0:T(8,128)(2,1)} %collective-permute-done.9.refs_1_, bf16[448,512]{1,0:T(8,128)(2,1)} %collective-permute-done.10.refs_2_, ...), custom_call_target="tpu_custom_call" | custom-call | flops 20000000000 | bytes 4000000 | tf_op jit(solution)/shard_map/project_last/pallas_call | solution.py:393
  134.8 0.7 copy-done.3
  135.5 3.5 %all-to-all-start.4 = ((bf16[8,64,768]{2,1,0:T(8,128)(2,1)}), bf16[8,64,768]{2,1,0:T(8,128)(2,1)S(1)}, u32[]{:S(2)}, u32[]{:S(2)}) async-start(bf16[8,64,768]{2,1,0:T(8,128)(2,1)} %get-tuple-element.39), calls=%async_computation.4 | async-start | bytes 1572864 | tf_op jit(solution)/shard_map/all_to_all | solution.py:57
  139.1 3.1 %encoder_queries.1.enc_q_hbm = bf16[256,896]{1,0:T(8,128)(2,1)} custom-call(bf16[256,896]{1,0:T(8,128)(2,1)} %bitcast.32, bf16[896,896]{1,0:T(8,128)(2,1)} %weight_hbm.1), custom_call_target="tpu_custom_call" | custom-call | flops 411041792 | bytes 3000000 | tf_op jit(solution)/shard_map/encoder_queries/pallas_call | solution.py:379
  142.2 13.3 %all-to-all-done.4.got_hbm = bf16[8,64,768]{2,1,0:T(8,128)(2,1)S(1)} async-done(((bf16[8,64,768]{2,1,0:T(8,128)(2,1)}), bf16[8,64,768]{2,1,0:T(8,128)(2,1)S(1)}, u32[]{:S(2)}, u32[]{:S(2)}) %all-to-all-start.4) | async-done | bytes 786464 | tf_op jit(solution)/shard_map/all_to_all | solution.py:57
  155.5 0.9 copy-done.7
  156.4 8.7 %attention.1.chunk_ref = bf16[64,2176]{1,0:T(8,128)(2,1)} custom-call(bf16[256,896]{1,0:T(8,128)(2,1)} %bitcast.33, bf16[256,896]{1,0:T(8,128)(2,1)} %encoder_queries.1.enc_q_hbm, bf16[8,64,768]{2,1,0:T(8,128)(2,1)} %copy-done.7, bf16[896,896]{1,0:T(8,128)(2,1)} %enc_out_hbm.1, bf16[16,2,144,1024]{3,2,1,0:T(8,128)(2,1)} %bitcast.29), custom_call_target="tpu_custom_call" | custom-call | flops 4000000000 | bytes 12000000 | tf_op jit(solution)/shard_map/attention/pallas_call | solution.py:421
  165.0 0.3 collective-permute-start.14
  165.4 3.2 %collective-permute-start.15 = (bf16[64,2176]{1,0:T(8,128)(2,1)}, bf16[64,2176]{1,0:T(8,128)(2,1)S(1)}, u32[]{:S(2)}, u32[]{:S(2)}) collective-permute-start(bf16[64,2176]{1,0:T(8,128)(2,1)} %attention.1.chunk_ref), channel_id=1, source_target_pairs={{0,131},{1,0},{2,1},{3,2},{128,3},{129,128},{130,129},{131,130},{4... | collective-permute-start | bytes 835592 | tf_op jit(solution)/shard_map/ppermute | solution.py:49
  168.6 5.7 %finish_first.1 = (bf16[448,512]{1,0:T(8,128)(2,1)}, bf16[448,512]{1,0:T(8,128)(2,1)}, f32[448,1]{1,0:T(8,128)S(1)}, bf16[2,32,16,1024]{3,2,1,0:T(8,128)(2,1)}) custom-call(s32[1]{0:T(128)} %bitcast.13.source_ref, bf16[64,2176]{1,0:T(8,128)(2,1)} %attention.1.chunk_ref, bf16[448,512]{1,0:T(8,128)(2,1)} %hidden_hbm.1, f32[448,1]{1,0:T(8,128)} %copy-done.3, ...), custom_call_target="tpu_custom_call" | custom-call | flops 134217728 | bytes 4000000 | tf_op jit(solution)/shard_map/finish_first/pallas_call | solution.py:445
  174.2 0.3 collective-permute-done.14.refs_0_
  174.5 3.2 %collective-permute-start.17 = (bf16[64,2176]{1,0:T(8,128)(2,1)S(1)}, bf16[64,2176]{1,0:T(8,128)(2,1)S(1)}, u32[]{:S(2)}, u32[]{:S(2)}) collective-permute-start(bf16[64,2176]{1,0:T(8,128)(2,1)S(1)} %collective-permute-done.15.refs_1_), channel_id=1, source_target_pairs={{0,131},{1,0},{2,1},{3,2},{128,3},{129,128},{130,129},{131,130},{4... | collective-permute-start | bytes 835592 | tf_op jit(solution)/shard_map/ppermute | solution.py:49
  177.8 0.1 pad_add_fusion.2.source_ref
  177.8 1.6 copy-done.1
  179.4 1.0 copy-done.2
  180.4 2.0 finish.4.refs_5_
  182.5 0.1 collective-permute-done.16.refs_0_
  182.6 3.2 %collective-permute-start.19 = (bf16[64,2176]{1,0:T(8,128)(2,1)S(1)}, bf16[64,2176]{1,0:T(8,128)(2,1)S(1)}, u32[]{:S(2)}, u32[]{:S(2)}) collective-permute-start(bf16[64,2176]{1,0:T(8,128)(2,1)S(1)} %collective-permute-done.17.refs_1_), channel_id=1, source_target_pairs={{0,131},{1,0},{2,1},{3,2},{128,3},{129,128},{130,129},{131,130},{4... | collective-permute-start | bytes 835592 | tf_op jit(solution)/shard_map/ppermute | solution.py:49
  185.9 2.0 finish.5.refs_5_
  187.9 2.4 %collective-permute-done.18.refs_0_ = bf16[64,2176]{1,0:T(8,128)(2,1)S(1)} collective-permute-done((bf16[64,2176]{1,0:T(8,128)(2,1)S(1)}, bf16[64,2176]{1,0:T(8,128)(2,1)S(1)}, u32[]{:S(2)}, u32[]{:S(2)}) %collective-permute-start.18) | collective-permute-done | bytes 278560 | tf_op jit(solution)/shard_map/ppermute | solution.py:49
  190.3 0.1 collective-permute-start.20
  190.5 3.3 %collective-permute-start.21 = (bf16[32,2176]{1,0:T(8,128)(2,1)S(1)}, bf16[32,2176]{1,0:T(8,128)(2,1)S(1)}, u32[]{:S(2)}, u32[]{:S(2)}) collective-permute-start(bf16[32,2176]{1,0:T(8,128)(2,1)S(1)} %slice.12), channel_id=1, source_target_pairs={{0,131},{1,0},{2,1},{3,2},{128,3},{129,128},{130,129},{131,130},{4... | collective-permute-start | bytes 417800 | tf_op jit(solution)/shard_map/ppermute | solution.py:49
  193.8 0.1 pad_add_fusion.4.source_ref
  193.9 2.0 finish.6.refs_5_
  195.9 0.8 collective-permute-done.20.refs_0_
  196.7 1.9 finish.7
  (62 shorter events, 0.5 us)
Async XLA Ops:
  6.5 49.9 %copy-start = (bf16[16,16,896]{2,1,0:T(8,128)(2,1)S(1)}, bf16[16,16,896]{2,1,0:T(8,128)(2,1)}, u32[]{:S(2)}) copy-start(bf16[16,16,896]{2,1,0:T(8,128)(2,1)} %param.19) | copy-start | bytes 1376260
  6.5 11.1 %copy-start.6 = (bf16[448,512]{1,0:T(8,128)(2,1)S(1)}, bf16[448,512]{1,0:T(8,128)(2,1)}, u32[]{:S(2)}) copy-start(bf16[448,512]{1,0:T(8,128)(2,1)} %hidden_hbm.1) | copy-start | bytes 1376260
  6.5 34.9 %copy-start.14 = (s32[7,2]{0,1:T(2,128)S(1)}, s32[7,2]{0,1:T(2,128)}, u32[]{:S(2)}) copy-start(s32[7,2]{0,1:T(2,128)} %param.20) | copy-start | bytes 172
  6.5 35.0 %copy-start.15 = (s32[7,1]{0,1:T(1,128)S(1)}, s32[7,1]{0,1:T(1,128)}, u32[]{:S(2)}) copy-start(s32[7,1]{0,1:T(1,128)} %param.21) | copy-start | bytes 88
  6.5 43.5 %copy-start.8 = (bf16[448,512]{1,0:T(8,128)(2,1)S(1)}, bf16[448,512]{1,0:T(8,128)(2,1)}, u32[]{:S(2)}) copy-start(bf16[448,512]{1,0:T(8,128)(2,1)} %refs_5_.1) | copy-start | bytes 1376260
  9.1 28.2 %all-to-all-start.1 = ((bf16[8,144,128]{2,1,0:T(8,128)(2,1)}), bf16[8,144,128]{2,1,0:T(8,128)(2,1)S(1)}, u32[]{:S(2)}, u32[]{:S(2)}) async-start(bf16[8,144,128]{2,1,0:T(8,128)(2,1)} %pad_maximum_fusion), calls=%async_computation.1 | async-start | bytes 589824 | tf_op jit(solution)/shard_map/all_to_all | solution.py:57
  17.6 137.9 %all-gather.2.cloned.1.call-start = ((), (), s32[]{:S(2)}) async-start(), calls=%async_computation.5 | async-start | bytes 9732096 | tf_op jit(solution)/shard_map/all_gather | solution.py:347
  17.6 19.7 %collective-permute-start = (bf16[448,512]{1,0:T(8,128)(2,1)S(1)}, bf16[448,512]{1,0:T(8,128)(2,1)S(1)}, u32[]{:S(2)}, u32[]{:S(2)}) collective-permute-start(bf16[448,512]{1,0:T(8,128)(2,1)S(1)} %copy-done.6), channel_id=1, source_target_pairs={{0,1},{1,2},{2,3},{3,128},{128,129},{129,130},{130,131},{131,0},{4... | collective-permute-start | bytes 1376264 | tf_op jit(solution)/shard_map/ppermute | solution.py:49
  19.7 17.6 %collective-permute-start.1 = (bf16[448,512]{1,0:T(8,128)(2,1)S(1)}, bf16[448,512]{1,0:T(8,128)(2,1)S(1)}, u32[]{:S(2)}, u32[]{:S(2)}) collective-permute-start(bf16[448,512]{1,0:T(8,128)(2,1)S(1)} %copy-done.6), channel_id=1, source_target_pairs={{0,131},{1,0},{2,1},{3,2},{128,3},{129,128},{130,129},{131,130},{4... | collective-permute-start | bytes 1376264 | tf_op jit(solution)/shard_map/ppermute | solution.py:49
  37.3 21.1 %copy-start.11 = (bf16[448,512]{1,0:T(8,128)(2,1)}, bf16[448,512]{1,0:T(8,128)(2,1)S(1)}, u32[]{:S(2)}) copy-start(bf16[448,512]{1,0:T(8,128)(2,1)S(1)} %collective-permute-done.refs_1_) | copy-start | bytes 1376260
  37.3 21.1 %copy-start.12 = (bf16[448,512]{1,0:T(8,128)(2,1)}, bf16[448,512]{1,0:T(8,128)(2,1)S(1)}, u32[]{:S(2)}) copy-start(bf16[448,512]{1,0:T(8,128)(2,1)S(1)} %collective-permute-done.1.refs_2_) | copy-start | bytes 1376260
  38.1 18.1 %collective-permute-start.2 = (bf16[448,512]{1,0:T(8,128)(2,1)S(1)}, bf16[448,512]{1,0:T(8,128)(2,1)S(1)}, u32[]{:S(2)}, u32[]{:S(2)}) collective-permute-start(bf16[448,512]{1,0:T(8,128)(2,1)S(1)} %collective-permute-done.refs_1_), channel_id=1, source_target_pairs={{0,1},{1,2},{2,3},{3,128},{128,129},{129,130},{130,131},{131,0},{4... | collective-permute-start | bytes 1376264 | tf_op jit(solution)/shard_map/ppermute | solution.py:49
  38.6 17.6 %collective-permute-start.3 = (bf16[448,512]{1,0:T(8,128)(2,1)S(1)}, bf16[448,512]{1,0:T(8,128)(2,1)S(1)}, u32[]{:S(2)}, u32[]{:S(2)}) collective-permute-start(bf16[448,512]{1,0:T(8,128)(2,1)S(1)} %collective-permute-done.1.refs_2_), channel_id=1, source_target_pairs={{0,131},{1,0},{2,1},{3,2},{128,3},{129,128},{130,129},{131,130},{4... | collective-permute-start | bytes 1376264 | tf_op jit(solution)/shard_map/ppermute | solution.py:49
  42.4 13.7 %all-to-all-start = ((s32[32,1,2]{2,1,0:T(1,128)}), s32[32,1,2]{2,1,0:T(1,128)S(1)}, u32[]{:S(2)}, u32[]{:S(2)}) async-start(s32[32,1,2]{2,1,0:T(1,128)} %copy.36), calls=%async_computation | async-start | bytes 32768 | tf_op jit(solution)/shard_map/all_to_all | solution.py:57
  50.0 13.6 %collective-permute-start.6 = (bf16[448,512]{1,0:T(8,128)(2,1)S(1)}, bf16[448,512]{1,0:T(8,128)(2,1)}, u32[]{:S(2)}, u32[]{:S(2)}) collective-permute-start(bf16[448,512]{1,0:T(8,128)(2,1)S(1)} %copy-done.8), channel_id=1, source_target_pairs={{0,131},{1,0},{2,1},{3,2},{128,3},{129,128},{130,129},{131,130},{4... | collective-permute-start | bytes 1376264 | tf_op jit(solution)/shard_map/ppermute | solution.py:49
  56.2 2.2 %copy-start.13 = (bf16[448,512]{1,0:T(8,128)(2,1)}, bf16[448,512]{1,0:T(8,128)(2,1)S(1)}, u32[]{:S(2)}) copy-start(bf16[448,512]{1,0:T(8,128)(2,1)S(1)} %collective-permute-done.2.refs_3_) | copy-start | bytes 1376260
  56.2 36.2 %copy-start.9 = (bf16[448,512]{1,0:T(8,128)(2,1)}, bf16[448,512]{1,0:T(8,128)(2,1)S(1)}, u32[]{:S(2)}) copy-start(bf16[448,512]{1,0:T(8,128)(2,1)S(1)} %collective-permute-done.3.refs_4_) | copy-start | bytes 1376260
  58.4 46.6 %all-to-all-start.2 = ((bf16[32,32,896]{2,1,0:T(8,128)(2,1)}), bf16[32,32,896]{2,1,0:T(8,128)(2,1)S(1)}, u32[]{:S(2)}, u32[]{:S(2)}) async-start(bf16[32,32,896]{2,1,0:T(8,128)(2,1)} %bitcast.8), calls=%async_computation.2 | async-start | bytes 3670016 | tf_op jit(solution)/shard_map/all_to_all | solution.py:57
  63.5 14.0 %collective-permute-start.5 = (bf16[448,512]{1,0:T(8,128)(2,1)S(1)}, bf16[448,512]{1,0:T(8,128)(2,1)}, u32[]{:S(2)}, u32[]{:S(2)}) collective-permute-start(bf16[448,512]{1,0:T(8,128)(2,1)S(1)} %copy-done.8), channel_id=1, source_target_pairs={{0,1},{1,2},{2,3},{3,128},{128,129},{129,130},{130,131},{131,0},{4... | collective-permute-start | bytes 1376264 | tf_op jit(solution)/shard_map/ppermute | solution.py:49
  63.6 13.9 %collective-permute-start.8 = (bf16[448,512]{1,0:T(8,128)(2,1)}, bf16[448,512]{1,0:T(8,128)(2,1)}, u32[]{:S(2)}, u32[]{:S(2)}) collective-permute-start(bf16[448,512]{1,0:T(8,128)(2,1)} %collective-permute-done.6.refs_7_), channel_id=1, source_target_pairs={{0,131},{1,0},{2,1},{3,2},{128,3},{129,128},{130,129},{131,130},{4... | collective-permute-start | bytes 1376264 | tf_op jit(solution)/shard_map/ppermute | solution.py:49
  77.5 14.9 %collective-permute-start.7 = (bf16[448,512]{1,0:T(8,128)(2,1)}, bf16[448,512]{1,0:T(8,128)(2,1)S(1)}, u32[]{:S(2)}, u32[]{:S(2)}) collective-permute-start(bf16[448,512]{1,0:T(8,128)(2,1)} %collective-permute-done.5.refs_6_), channel_id=1, source_target_pairs={{0,1},{1,2},{2,3},{3,128},{128,129},{129,130},{130,131},{131,0},{4... | collective-permute-start | bytes 1376264 | tf_op jit(solution)/shard_map/ppermute | solution.py:49
  77.5 25.3 %collective-permute-start.12 = (bf16[448,512]{1,0:T(8,128)(2,1)}, bf16[448,512]{1,0:T(8,128)(2,1)}, u32[]{:S(2)}, u32[]{:S(2)}) collective-permute-start(bf16[448,512]{1,0:T(8,128)(2,1)} %collective-permute-done.8.refs_9_), channel_id=1, source_target_pairs={{0,131},{1,0},{2,1},{3,2},{128,3},{129,128},{130,129},{131,130},{4... | collective-permute-start | bytes 1376264 | tf_op jit(solution)/shard_map/ppermute | solution.py:49
  80.7 22.1 %collective-permute-start.4 = (bf16[448,512]{1,0:T(8,128)(2,1)}, bf16[448,512]{1,0:T(8,128)(2,1)}, u32[]{:S(2)}, u32[]{:S(2)}) collective-permute-start(bf16[448,512]{1,0:T(8,128)(2,1)} %copy-done.13), channel_id=1, source_target_pairs={{0,1},{1,2},{2,3},{3,128},{128,129},{129,130},{130,131},{131,0},{4... | collective-permute-start | bytes 1376264 | tf_op jit(solution)/shard_map/ppermute | solution.py:49
  92.4 3.2 %copy-start.10 = (bf16[448,512]{1,0:T(8,128)(2,1)}, bf16[448,512]{1,0:T(8,128)(2,1)S(1)}, u32[]{:S(2)}) copy-start(bf16[448,512]{1,0:T(8,128)(2,1)S(1)} %collective-permute-done.7.refs_8_) | copy-start | bytes 1376260
  92.4 19.8 %collective-permute-start.11 = (bf16[448,512]{1,0:T(8,128)(2,1)S(1)}, bf16[448,512]{1,0:T(8,128)(2,1)}, u32[]{:S(2)}, u32[]{:S(2)}) collective-permute-start(bf16[448,512]{1,0:T(8,128)(2,1)S(1)} %collective-permute-done.7.refs_8_), channel_id=1, source_target_pairs={{0,1},{1,2},{2,3},{3,128},{128,129},{129,130},{130,131},{131,0},{4... | collective-permute-start | bytes 1376264 | tf_op jit(solution)/shard_map/ppermute | solution.py:49
  92.4 19.8 %collective-permute-start.9 = (bf16[448,512]{1,0:T(8,128)(2,1)S(1)}, bf16[448,512]{1,0:T(8,128)(2,1)}, u32[]{:S(2)}, u32[]{:S(2)}) collective-permute-start(bf16[448,512]{1,0:T(8,128)(2,1)S(1)} %collective-permute-done.3.refs_4_), channel_id=1, source_target_pairs={{0,131},{1,0},{2,1},{3,2},{128,3},{129,128},{130,129},{131,130},{4... | collective-permute-start | bytes 1376264 | tf_op jit(solution)/shard_map/ppermute | solution.py:49
  102.1 0.7 copy-start.4
  102.8 14.8 %collective-permute-start.13 = (bf16[448,512]{1,0:T(8,128)(2,1)}, bf16[448,512]{1,0:T(8,128)(2,1)}, u32[]{:S(2)}, u32[]{:S(2)}) collective-permute-start(bf16[448,512]{1,0:T(8,128)(2,1)} %collective-permute-done.12.refs_4_), channel_id=1, source_target_pairs={{0,131},{1,0},{2,1},{3,2},{128,3},{129,128},{130,129},{131,130},{4... | collective-permute-start | bytes 1376264 | tf_op jit(solution)/shard_map/ppermute | solution.py:49
  102.8 25.3 %collective-permute-start.10 = (bf16[448,512]{1,0:T(8,128)(2,1)}, bf16[448,512]{1,0:T(8,128)(2,1)}, u32[]{:S(2)}, u32[]{:S(2)}) collective-permute-start(bf16[448,512]{1,0:T(8,128)(2,1)} %collective-permute-done.4.refs_0_), channel_id=1, source_target_pairs={{0,1},{1,2},{2,3},{3,128},{128,129},{129,130},{130,131},{131,0},{4... | collective-permute-start | bytes 1376264 | tf_op jit(solution)/shard_map/ppermute | solution.py:49
  106.4 29.1 %all-to-all-start.3 = ((bf16[8,32,896]{2,1,0:T(8,128)(2,1)}), bf16[8,32,896]{2,1,0:T(8,128)(2,1)S(1)}, u32[]{:S(2)}, u32[]{:S(2)}) async-start(bf16[8,32,896]{2,1,0:T(8,128)(2,1)} %gather_fusion.1), calls=%async_computation.3 | async-start | bytes 917504 | tf_op jit(solution)/shard_map/all_to_all | solution.py:57
  134.8 0.7 copy-start.3
  135.5 3.6 %copy-start.5 = (bf16[8,32,896]{2,1,0:T(8,128)(2,1)}, bf16[8,32,896]{2,1,0:T(8,128)(2,1)S(1)}, u32[]{:S(2)}) copy-start(bf16[8,32,896]{2,1,0:T(8,128)(2,1)S(1)} %all-to-all-done.3) | copy-start | bytes 1376260
  135.5 20.0 %all-to-all-start.4 = ((bf16[8,64,768]{2,1,0:T(8,128)(2,1)}), bf16[8,64,768]{2,1,0:T(8,128)(2,1)S(1)}, u32[]{:S(2)}, u32[]{:S(2)}) async-start(bf16[8,64,768]{2,1,0:T(8,128)(2,1)} %get-tuple-element.39), calls=%async_computation.4 | async-start | bytes 1572864 | tf_op jit(solution)/shard_map/all_to_all | solution.py:57
  155.5 0.9 copy-start.7
  165.0 9.5 %collective-permute-start.14 = (bf16[64,2176]{1,0:T(8,128)(2,1)}, bf16[64,2176]{1,0:T(8,128)(2,1)S(1)}, u32[]{:S(2)}, u32[]{:S(2)}) collective-permute-start(bf16[64,2176]{1,0:T(8,128)(2,1)} %attention.1.chunk_ref), channel_id=1, source_target_pairs={{0,1},{1,2},{2,3},{3,128},{128,129},{129,130},{130,131},{131,0},{4... | collective-permute-start | bytes 835592 | tf_op jit(solution)/shard_map/ppermute | solution.py:49
  165.4 9.2 %collective-permute-start.15 = (bf16[64,2176]{1,0:T(8,128)(2,1)}, bf16[64,2176]{1,0:T(8,128)(2,1)S(1)}, u32[]{:S(2)}, u32[]{:S(2)}) collective-permute-start(bf16[64,2176]{1,0:T(8,128)(2,1)} %attention.1.chunk_ref), channel_id=1, source_target_pairs={{0,131},{1,0},{2,1},{3,2},{128,3},{129,128},{130,129},{131,130},{4... | collective-permute-start | bytes 835592 | tf_op jit(solution)/shard_map/ppermute | solution.py:49
  174.5 8.0 %collective-permute-start.16 = (bf16[64,2176]{1,0:T(8,128)(2,1)S(1)}, bf16[64,2176]{1,0:T(8,128)(2,1)S(1)}, u32[]{:S(2)}, u32[]{:S(2)}) collective-permute-start(bf16[64,2176]{1,0:T(8,128)(2,1)S(1)} %collective-permute-done.14.refs_0_), channel_id=1, source_target_pairs={{0,1},{1,2},{2,3},{3,128},{128,129},{129,130},{130,131},{131,0},{4... | collective-permute-start | bytes 835592 | tf_op jit(solution)/shard_map/ppermute | solution.py:49
  174.5 8.0 %collective-permute-start.17 = (bf16[64,2176]{1,0:T(8,128)(2,1)S(1)}, bf16[64,2176]{1,0:T(8,128)(2,1)S(1)}, u32[]{:S(2)}, u32[]{:S(2)}) collective-permute-start(bf16[64,2176]{1,0:T(8,128)(2,1)S(1)} %collective-permute-done.15.refs_1_), channel_id=1, source_target_pairs={{0,131},{1,0},{2,1},{3,2},{128,3},{129,128},{130,129},{131,130},{4... | collective-permute-start | bytes 835592 | tf_op jit(solution)/shard_map/ppermute | solution.py:49
  177.8 1.6 copy-start.1
  179.4 1.0 copy-start.2
  182.6 7.8 %collective-permute-start.18 = (bf16[64,2176]{1,0:T(8,128)(2,1)S(1)}, bf16[64,2176]{1,0:T(8,128)(2,1)S(1)}, u32[]{:S(2)}, u32[]{:S(2)}) collective-permute-start(bf16[64,2176]{1,0:T(8,128)(2,1)S(1)} %collective-permute-done.16.refs_0_), channel_id=1, source_target_pairs={{0,1},{1,2},{2,3},{3,128},{128,129},{129,130},{130,131},{131,0},{4... | collective-permute-start | bytes 835592 | tf_op jit(solution)/shard_map/ppermute | solution.py:49
  182.6 7.8 %collective-permute-start.19 = (bf16[64,2176]{1,0:T(8,128)(2,1)S(1)}, bf16[64,2176]{1,0:T(8,128)(2,1)S(1)}, u32[]{:S(2)}, u32[]{:S(2)}) collective-permute-start(bf16[64,2176]{1,0:T(8,128)(2,1)S(1)} %collective-permute-done.17.refs_1_), channel_id=1, source_target_pairs={{0,131},{1,0},{2,1},{3,2},{128,3},{129,128},{130,129},{131,130},{4... | collective-permute-start | bytes 835592 | tf_op jit(solution)/shard_map/ppermute | solution.py:49
  190.3 6.3 %collective-permute-start.20 = (bf16[32,2176]{1,0:T(8,128)(2,1)S(1)}, bf16[32,2176]{1,0:T(8,128)(2,1)S(1)}, u32[]{:S(2)}, u32[]{:S(2)}) collective-permute-start(bf16[32,2176]{1,0:T(8,128)(2,1)S(1)} %slice.11), channel_id=1, source_target_pairs={{0,1},{1,2},{2,3},{3,128},{128,129},{129,130},{130,131},{131,0},{4... | collective-permute-start | bytes 417800 | tf_op jit(solution)/shard_map/ppermute | solution.py:49
  190.5 6.2 %collective-permute-start.21 = (bf16[32,2176]{1,0:T(8,128)(2,1)S(1)}, bf16[32,2176]{1,0:T(8,128)(2,1)S(1)}, u32[]{:S(2)}, u32[]{:S(2)}) collective-permute-start(bf16[32,2176]{1,0:T(8,128)(2,1)S(1)} %slice.12), channel_id=1, source_target_pairs={{0,131},{1,0},{2,1},{3,2},{128,3},{129,128},{130,129},{131,130},{4... | collective-permute-start | bytes 417800 | tf_op jit(solution)/shard_map/ppermute | solution.py:49
Sparse Core Ops, SparseCore 0:
  38.3 69.7 all-gather.1

commit v6 on v5

--- a/solution.py
+++ b/solution.py
@@ -334,15 +334,21 @@
     grad_right = grad_left = cotangent
     index, chunks, grad_chunks = [me], [hidden], [cotangent]
     for step in range(1, 4):
-        right, left = shift(right, 1), shift(left, -1)
         if step == 1:
+            right, left = shift(right, 1), shift(left, -1)
             part, right, left = tie(part, right, left)
+            chunks += [right, left]
+        if step < 3:
+            right, left = shift(right, 1), shift(left, -1)
         grad_right, grad_left = shift(grad_right, 1), shift(grad_left, -1)
-        if step == 2:
-            asked, right, left = tie(asked, right, left)
+        if step == 1:
+            asked, right, left, grad_right, grad_left = tie(
+                asked, right, left, grad_right, grad_left
+            )
+        if step < 3:
+            chunks += [right, left]
+        grad_chunks += [grad_right, grad_left]
         index += [(me - step) % NZ, (me + step) % NZ]
-        chunks += [right, left]
-        grad_chunks += [grad_right, grad_left]
     part = part.transpose(1, 0, 2).reshape(144, HALF)
     weights = lax.all_gather(part, "dp", axis=0, tiled=True).reshape(16, 2, 144, HALF)
     returned = exchange(database[asked].reshape(NDP, NEIGH * NLEN // NZ, DE), "dp")
@@ -452,7 +458,7 @@
             pltpu.SemaphoreType.DMA((4,)),
             pltpu.SemaphoreType.DMA((1,)),
         ],
-        compiler_params=ROOM,
+        compiler_params=pltpu.CompilerParams(vmem_limit_bytes=50 * MIB),
         cost_estimate=cost(2 * SEG * FEAT * 2048, 4_000_000),
         name="finish_first",
     )(jnp.stack([me]), grad_query, hidden, inverse, weights.reshape(NDP, 144, HALF))

time: 206 us -> 213 us (1.034)
  blocking collectives: 0 us -> 13.6 us
  Pallas kernels: 38.5 us -> 36.3 us
    ppermute x22, waiting for transfers between devices: 59.2 us -> 41 us  [shift(): return lax.ppermute(x, Z, [(i, (i + by) % NZ) for i in range(NZ)])]
    all_to_all x5 -> x4, waiting for transfers between devices: 19.1 us -> 35.8 us  [exchange(): return lax.all_to_all(x, axis, split_axis=0, concat_axis=0, tiled=True)]
    all_to_all x0 -> x1, blocking collectives: none -> 13.6 us  [exchange(): return lax.all_to_all(x, axis, split_axis=0, concat_axis=0, tiled=True)]
    all_to_all x5 -> x4, starting transfers between devices: 29.3 us -> 25.9 us  [exchange(): return lax.all_to_all(x, axis, split_axis=0, concat_axis=0, tiled=True)]
    ppermute x22, starting transfers between devices: 32.2 us -> 34.8 us  [shift(): return lax.ppermute(x, Z, [(i, (i + by) % NZ) for i in range(NZ)])]
    pallas_call x1, Pallas kernels: 5.66 us -> 3.5 us  [shards(): pl.pallas_call(finish_first, out_shape=results, in_specs=[SMEM, VMEM, ANY...]
    unnamed x33 -> x35, local copies, waits for them, and re-layouts: 5.01 us -> 3.52 us
  transfers between devices with their start and end apart: 28 -> 27, of which waited for: 12 -> 14; matrix products, arithmetic and copies ran while one was open for 3% -> 2% of each run, Pallas kernels for 14% -> 12%
where the time goes in v6:
time: 213 us; the launch traced here: 212 us
  waiting for transfers between devices  76.7 us (36%)
  starting transfers between devices  60.7 us (28%)
  Pallas kernels  36.3 us (17%)
  between operations  13.7 us (6%)
  blocking collectives  13.6 us (6%)
  local copies, waits for them, and re-layouts  9.95 us (5%)
    ppermute x22, waiting for transfers between devices, shift(): return lax.ppermute(x, Z, [(i, (i + by) % NZ) for i in range(NZ)])  41 us
    all_to_all x4, waiting for transfers between devices, exchange(): return lax.all_to_all(x, axis, split_axis=0, concat_axis=0, tiled=True)  35.8 us
    ppermute x22, starting transfers between devices, shift(): return lax.ppermute(x, Z, [(i, (i + by) % NZ) for i in range(NZ)])  34.8 us
    all_to_all x4, starting transfers between devices, exchange(): return lax.all_to_all(x, axis, split_axis=0, concat_axis=0, tiled=True)  25.9 us
    all_to_all x1, blocking collectives, exchange(): return lax.all_to_all(x, axis, split_axis=0, concat_axis=0, tiled=True)  13.6 us
    pallas_call x1, Pallas kernels, shards(): pl.pallas_call(attention, out_shape=jax.ShapeDtypeStruct((SEG, 2 * HALF +...  8.68 us
    pallas_call x4, Pallas kernels, finish_call(): pl.pallas_call(functools.partial(finish, starts), out_shape=jax.ShapeDtyp...  7.97 us
    pallas_call x1, Pallas kernels, shards(): pl.pallas_call(functools.partial(project_last, len(hiddens)), out_shape=(...  6.69 us
  transfers between devices with their start and end apart: 27, of which 14 were waited for; matrix products, arithmetic and copies ran while one was open for 2% of the time, Pallas kernels for 12%

profile of v6, /device:TPU:2, one launch (start us, length us, event | category | flops | bytes accessed | tf_op | source)
XLA Modules:
  0.0 212.4 jit_solution(16780173392610897704)
XLA Ops:
  6.6 1.0 constant_dynamic-slice_fusion
  7.6 0.8 dynamic_slice.6
  8.4 0.7 pad_maximum_fusion
  9.1 8.5 %all-to-all-start.1 = ((bf16[8,144,128]{2,1,0:T(8,128)(2,1)}), bf16[8,144,128]{2,1,0:T(8,128)(2,1)S(1)}, u32[]{:S(2)}, u32[]{:S(2)}) async-start(bf16[8,144,128]{2,1,0:T(8,128)(2,1)} %pad_maximum_fusion), calls=%async_computation.1 | async-start | bytes 589824 | tf_op jit(solution)/shard_map/all_to_all | solution.py:57
  17.6 2.1 collective-permute-start
  19.7 1.3 collective-permute-start.1
  21.0 16.3 %collective-permute-done.refs_1_ = bf16[448,512]{1,0:T(8,128)(2,1)S(1)} collective-permute-done((bf16[448,512]{1,0:T(8,128)(2,1)S(1)}, bf16[448,512]{1,0:T(8,128)(2,1)S(1)}, u32[]{:S(2)}, u32[]{:S(2)}) %collective-permute-start) | collective-permute-done | bytes 458784 | tf_op jit(solution)/shard_map/ppermute | solution.py:49
  37.3 0.8 copy_bitcast_fusion
  38.2 0.4 collective-permute-start.4
  38.6 2.9 %collective-permute-start.5 = (bf16[448,512]{1,0:T(8,128)(2,1)S(1)}, bf16[448,512]{1,0:T(8,128)(2,1)}, u32[]{:S(2)}, u32[]{:S(2)}) collective-permute-start(bf16[448,512]{1,0:T(8,128)(2,1)S(1)} %copy-done.7), channel_id=1, source_target_pairs={{0,131},{1,0},{2,1},{3,2},{128,3},{129,128},{130,129},{131,130},{4... | collective-permute-start | bytes 1376264 | tf_op jit(solution)/shard_map/ppermute | solution.py:49
  41.5 3.2 %collective-permute-start.3 = (bf16[448,512]{1,0:T(8,128)(2,1)S(1)}, bf16[448,512]{1,0:T(8,128)(2,1)S(1)}, u32[]{:S(2)}, u32[]{:S(2)}) collective-permute-start(bf16[448,512]{1,0:T(8,128)(2,1)S(1)} %collective-permute-done.1.refs_2_), channel_id=1, source_target_pairs={{0,131},{1,0},{2,1},{3,2},{128,3},{129,128},{130,129},{131,130},{4... | collective-permute-start | bytes 1376264 | tf_op jit(solution)/shard_map/ppermute | solution.py:49
  44.7 0.1 copy.35
  44.9 0.1 multiply_reduce_fusion
  45.0 0.1 copy.36
  45.1 13.6 %all_to_all.32 = s32[32,1,2]{2,1,0:T(1,128)S(1)} all-to-all(s32[32,1,2]{2,1,0:T(1,128)S(1)} %copy.36), channel_id=1, replica_groups=mesh['group'=2,'dp'=32,'tensor'=4] {'dp'}, dimensions={0} | all-to-all | bytes 512 | tf_op jit(solution)/shard_map/all_to_all | solution.py:57
  58.6 0.1 copy.37
  58.7 2.0 collective-permute-done.2.refs_3_
  60.8 0.1 copy.39
  60.9 0.1 reshape.126
  61.0 2.0 gather_fusion
  63.0 7.6 %all-to-all-start.2 = ((bf16[32,32,896]{2,1,0:T(8,128)(2,1)}), bf16[32,32,896]{2,1,0:T(8,128)(2,1)S(1)}, u32[]{:S(2)}, u32[]{:S(2)}) async-start(bf16[32,32,896]{2,1,0:T(8,128)(2,1)} %bitcast.8), calls=%async_computation.2 | async-start | bytes 3670016 | tf_op jit(solution)/shard_map/all_to_all | solution.py:57
  70.7 3.0 %collective-permute-start.8 = (bf16[448,512]{1,0:T(8,128)(2,1)}, bf16[448,512]{1,0:T(8,128)(2,1)}, u32[]{:S(2)}, u32[]{:S(2)}) collective-permute-start(bf16[448,512]{1,0:T(8,128)(2,1)} %collective-permute-done.5.refs_7_), channel_id=1, source_target_pairs={{0,131},{1,0},{2,1},{3,2},{128,3},{129,128},{130,129},{131,130},{4... | collective-permute-start | bytes 1376264 | tf_op jit(solution)/shard_map/ppermute | solution.py:49
  73.7 0.4 collective-permute-start.6
  74.1 10.0 %collective-permute-done.8.refs_9_ = bf16[448,512]{1,0:T(8,128)(2,1)} collective-permute-done((bf16[448,512]{1,0:T(8,128)(2,1)}, bf16[448,512]{1,0:T(8,128)(2,1)}, u32[]{:S(2)}, u32[]{:S(2)}) %collective-permute-start.8) | collective-permute-done | bytes 458784 | tf_op jit(solution)/shard_map/ppermute | solution.py:49
  84.1 3.7 %collective-permute-start.12 = (bf16[448,512]{1,0:T(8,128)(2,1)}, bf16[448,512]{1,0:T(8,128)(2,1)}, u32[]{:S(2)}, u32[]{:S(2)}) collective-permute-start(bf16[448,512]{1,0:T(8,128)(2,1)} %collective-permute-done.8.refs_9_), channel_id=1, source_target_pairs={{0,131},{1,0},{2,1},{3,2},{128,3},{129,128},{130,129},{131,130},{4... | collective-permute-start | bytes 1376264 | tf_op jit(solution)/shard_map/ppermute | solution.py:49
  87.8 0.1 stack.61.index_ref
  87.9 0.2 collective-permute-start.9
  88.1 0.4 collective-permute-done.7.refs_8_
  88.5 0.8 copy-done.9
  89.3 6.4 %project.1 = (f32[448,768]{1,0:T(8,128)}, f32[448,1]{1,0:T(8,128)S(1)}) custom-call(s32[5]{0:T(128)S(1)} %stack.61.index_ref, bf16[448,512]{1,0:T(8,128)(2,1)} %hidden_hbm.1, bf16[448,512]{1,0:T(8,128)(2,1)} %copy-done.10, bf16[448,512]{1,0:T(8,128)(2,1)} %copy-done.11, bf16[448,512]{1,0:T(8,128)(2,1)} %copy-done.13, bf16[448,512]{1,0:T(8,128)(2,1)} %copy-done.8, ...), custom_call_target="tpu_custom_call" | custom-call | flops 1688207360 | bytes 16000000 | tf_op jit(solution)/shard_map/project/pallas_call | solution.py:357
  95.7 0.7 copy-done.4
  96.4 0.9 collective-permute-done.6.refs_0_
  97.3 0.7 collective-permute-start.10
  98.0 1.0 collective-permute-done.12.refs_4_
  99.1 3.7 %collective-permute-start.13 = (bf16[448,512]{1,0:T(8,128)(2,1)}, bf16[448,512]{1,0:T(8,128)(2,1)}, u32[]{:S(2)}, u32[]{:S(2)}) collective-permute-start(bf16[448,512]{1,0:T(8,128)(2,1)} %collective-permute-done.12.refs_4_), channel_id=1, source_target_pairs={{0,131},{1,0},{2,1},{3,2},{128,3},{129,128},{130,129},{131,130},{4... | collective-permute-start | bytes 1376264 | tf_op jit(solution)/shard_map/ppermute | solution.py:49
  102.8 0.1 fusion.1
  103.0 8.7 %all-to-all-done.2 = bf16[32,32,896]{2,1,0:T(8,128)(2,1)S(1)} async-done(((bf16[32,32,896]{2,1,0:T(8,128)(2,1)}), bf16[32,32,896]{2,1,0:T(8,128)(2,1)S(1)}, u32[]{:S(2)}, u32[]{:S(2)}) %all-to-all-start.2) | async-done | bytes 1835040 | tf_op jit(solution)/shard_map/all_to_all | solution.py:57
  111.7 1.4 gather_fusion.1
  113.1 6.0 %all-to-all-start.3 = ((bf16[8,32,896]{2,1,0:T(8,128)(2,1)}), bf16[8,32,896]{2,1,0:T(8,128)(2,1)S(1)}, u32[]{:S(2)}, u32[]{:S(2)}) async-start(bf16[8,32,896]{2,1,0:T(8,128)(2,1)} %gather_fusion.1), calls=%async_computation.3 | async-start | bytes 917504 | tf_op jit(solution)/shard_map/all_to_all | solution.py:57
  119.1 1.0 collective-permute-done.11.refs_3_
  120.1 6.7 %project_last.1 = (bf16[8,64,768]{2,1,0:T(8,128)(2,1)}, f32[448,1]{1,0:T(8,128)S(1)}) custom-call(s32[3]{0:T(128)S(1)} %pad_add_fusion.1.index_ref, bf16[448,512]{1,0:T(8,128)(2,1)} %collective-permute-done.6.refs_0_, bf16[448,512]{1,0:T(8,128)(2,1)} %collective-permute-done.9.refs_1_, bf16[448,512]{1,0:T(8,128)(2,1)} %copy-done.16, ...), custom_call_target="tpu_custom_call" | custom-call | flops 20000000000 | bytes 4000000 | tf_op jit(solution)/shard_map/project_last/pallas_call | solution.py:399
  126.8 8.6 %all-to-all-done.3 = bf16[8,32,896]{2,1,0:T(8,128)(2,1)S(1)} async-done(((bf16[8,32,896]{2,1,0:T(8,128)(2,1)}), bf16[8,32,896]{2,1,0:T(8,128)(2,1)S(1)}, u32[]{:S(2)}, u32[]{:S(2)}) %all-to-all-start.3) | async-done | bytes 458784 | tf_op jit(solution)/shard_map/all_to_all | solution.py:57
  135.4 3.8 %all-to-all-start.4 = ((bf16[8,64,768]{2,1,0:T(8,128)(2,1)}), bf16[8,64,768]{2,1,0:T(8,128)(2,1)S(1)}, u32[]{:S(2)}, u32[]{:S(2)}) async-start(bf16[8,64,768]{2,1,0:T(8,128)(2,1)} %get-tuple-element.43), calls=%async_computation.4 | async-start | bytes 1572864 | tf_op jit(solution)/shard_map/all_to_all | solution.py:57
  139.2 3.1 %encoder_queries.1.enc_q_hbm = bf16[256,896]{1,0:T(8,128)(2,1)} custom-call(bf16[256,896]{1,0:T(8,128)(2,1)} %bitcast.32, bf16[896,896]{1,0:T(8,128)(2,1)} %weight_hbm.1), custom_call_target="tpu_custom_call" | custom-call | flops 411041792 | bytes 3000000 | tf_op jit(solution)/shard_map/encoder_queries/pallas_call | solution.py:385
  142.3 18.4 %all-to-all-done.4.got_hbm = bf16[8,64,768]{2,1,0:T(8,128)(2,1)S(1)} async-done(((bf16[8,64,768]{2,1,0:T(8,128)(2,1)}), bf16[8,64,768]{2,1,0:T(8,128)(2,1)S(1)}, u32[]{:S(2)}, u32[]{:S(2)}) %all-to-all-start.4) | async-done | bytes 786464 | tf_op jit(solution)/shard_map/all_to_all | solution.py:57
  160.7 0.9 copy-done.6
  161.6 8.7 %attention.1.chunk_ref = bf16[64,2176]{1,0:T(8,128)(2,1)} custom-call(bf16[256,896]{1,0:T(8,128)(2,1)} %bitcast.33, bf16[256,896]{1,0:T(8,128)(2,1)} %encoder_queries.1.enc_q_hbm, bf16[8,64,768]{2,1,0:T(8,128)(2,1)} %copy-done.6, bf16[896,896]{1,0:T(8,128)(2,1)} %enc_out_hbm.1, bf16[16,2,144,1024]{3,2,1,0:T(8,128)(2,1)} %bitcast.29), custom_call_target="tpu_custom_call" | custom-call | flops 4000000000 | bytes 12000000 | tf_op jit(solution)/shard_map/attention/pallas_call | solution.py:427
  170.3 2.4 %collective-permute-start.14 = (bf16[64,2176]{1,0:T(8,128)(2,1)}, bf16[64,2176]{1,0:T(8,128)(2,1)S(1)}, u32[]{:S(2)}, u32[]{:S(2)}) collective-permute-start(bf16[64,2176]{1,0:T(8,128)(2,1)} %attention.1.chunk_ref), channel_id=1, source_target_pairs={{0,1},{1,2},{2,3},{3,128},{128,129},{129,130},{130,131},{131,0},{4... | collective-permute-start | bytes 835592 | tf_op jit(solution)/shard_map/ppermute | solution.py:49
  172.7 0.9 collective-permute-start.15
  173.6 1.0 copy-done.3
  174.6 3.5 %finish_first.1 = (bf16[448,512]{1,0:T(8,128)(2,1)}, bf16[448,512]{1,0:T(8,128)(2,1)S(1)}, f32[448,1]{1,0:T(8,128)S(1)}, bf16[2,32,16,1024]{3,2,1,0:T(8,128)(2,1)S(1)}) custom-call(s32[1]{0:T(128)} %bitcast.13.source_ref, bf16[64,2176]{1,0:T(8,128)(2,1)S(1)} %copy-done.3, bf16[448,512]{1,0:T(8,128)(2,1)S(1)} %copy-done.2, ...), custom_call_target="tpu_custom_call" | custom-call | flops 134217728 | bytes 4000000 | tf_op jit(solution)/shard_map/finish_first/pallas_call | solution.py:451
  178.1 2.2 %collective-permute-done.14.refs_0_ = bf16[64,2176]{1,0:T(8,128)(2,1)S(1)} collective-permute-done((bf16[64,2176]{1,0:T(8,128)(2,1)}, bf16[64,2176]{1,0:T(8,128)(2,1)S(1)}, u32[]{:S(2)}, u32[]{:S(2)}) %collective-permute-start.14) | collective-permute-done | bytes 278560 | tf_op jit(solution)/shard_map/ppermute | solution.py:49
  180.4 0.4 collective-permute-start.16
  180.8 2.9 %collective-permute-start.17 = (bf16[64,2176]{1,0:T(8,128)(2,1)S(1)}, bf16[64,2176]{1,0:T(8,128)(2,1)S(1)}, u32[]{:S(2)}, u32[]{:S(2)}) collective-permute-start(bf16[64,2176]{1,0:T(8,128)(2,1)S(1)} %collective-permute-done.15.refs_1_), channel_id=1, source_target_pairs={{0,131},{1,0},{2,1},{3,2},{128,3},{129,128},{130,129},{131,130},{4... | collective-permute-start | bytes 835592 | tf_op jit(solution)/shard_map/ppermute | solution.py:49
  183.7 2.0 finish.4.refs_5_
  185.7 3.5 %collective-permute-done.16.refs_0_ = bf16[64,2176]{1,0:T(8,128)(2,1)S(1)} collective-permute-done((bf16[64,2176]{1,0:T(8,128)(2,1)S(1)}, bf16[64,2176]{1,0:T(8,128)(2,1)S(1)}, u32[]{:S(2)}, u32[]{:S(2)}) %collective-permute-start.16) | collective-permute-done | bytes 278560 | tf_op jit(solution)/shard_map/ppermute | solution.py:49
  189.3 3.2 %collective-permute-start.19 = (bf16[64,2176]{1,0:T(8,128)(2,1)S(1)}, bf16[64,2176]{1,0:T(8,128)(2,1)S(1)}, u32[]{:S(2)}, u32[]{:S(2)}) collective-permute-start(bf16[64,2176]{1,0:T(8,128)(2,1)S(1)} %collective-permute-done.17.refs_1_), channel_id=1, source_target_pairs={{0,131},{1,0},{2,1},{3,2},{128,3},{129,128},{130,129},{131,130},{4... | collective-permute-start | bytes 835592 | tf_op jit(solution)/shard_map/ppermute | solution.py:49
  192.6 2.0 finish.5.refs_5_
  194.6 2.6 %collective-permute-done.18.refs_0_ = bf16[64,2176]{1,0:T(8,128)(2,1)S(1)} collective-permute-done((bf16[64,2176]{1,0:T(8,128)(2,1)S(1)}, bf16[64,2176]{1,0:T(8,128)(2,1)S(1)}, u32[]{:S(2)}, u32[]{:S(2)}) %collective-permute-start.18) | collective-permute-done | bytes 278560 | tf_op jit(solution)/shard_map/ppermute | solution.py:49
  197.3 0.1 collective-permute-start.20
  197.4 3.3 %collective-permute-start.21 = (bf16[32,2176]{1,0:T(8,128)(2,1)S(1)}, bf16[32,2176]{1,0:T(8,128)(2,1)S(1)}, u32[]{:S(2)}, u32[]{:S(2)}) collective-permute-start(bf16[32,2176]{1,0:T(8,128)(2,1)S(1)} %slice.12), channel_id=1, source_target_pairs={{0,131},{1,0},{2,1},{3,2},{128,3},{129,128},{130,129},{131,130},{4... | collective-permute-start | bytes 417800 | tf_op jit(solution)/shard_map/ppermute | solution.py:49
  200.8 2.0 finish.6.refs_5_
  202.8 0.8 collective-permute-done.20.refs_0_
  203.6 1.9 finish.7
  (63 shorter events, 0.8 us)
Async XLA Ops:
  6.5 54.5 %copy-start = (bf16[16,16,896]{2,1,0:T(8,128)(2,1)S(1)}, bf16[16,16,896]{2,1,0:T(8,128)(2,1)}, u32[]{:S(2)}) copy-start(bf16[16,16,896]{2,1,0:T(8,128)(2,1)} %param.19) | copy-start | bytes 1376260
  6.5 11.1 %copy-start.1 = (bf16[448,512]{1,0:T(8,128)(2,1)S(1)}, bf16[448,512]{1,0:T(8,128)(2,1)}, u32[]{:S(2)}) copy-start(bf16[448,512]{1,0:T(8,128)(2,1)} %hidden_hbm.1) | copy-start | bytes 1376260
  6.5 31.6 %copy-start.7 = (bf16[448,512]{1,0:T(8,128)(2,1)S(1)}, bf16[448,512]{1,0:T(8,128)(2,1)}, u32[]{:S(2)}) copy-start(bf16[448,512]{1,0:T(8,128)(2,1)} %refs_5_.1) | copy-start | bytes 1376260
  6.5 38.2 %copy-start.14 = (s32[7,2]{0,1:T(2,128)S(1)}, s32[7,2]{0,1:T(2,128)}, u32[]{:S(2)}) copy-start(s32[7,2]{0,1:T(2,128)} %param.20) | copy-start | bytes 172
  6.5 38.3 %copy-start.15 = (s32[7,1]{0,1:T(1,128)S(1)}, s32[7,1]{0,1:T(1,128)}, u32[]{:S(2)}) copy-start(s32[7,1]{0,1:T(1,128)} %param.21) | copy-start | bytes 88
  9.1 28.2 %all-to-all-start.1 = ((bf16[8,144,128]{2,1,0:T(8,128)(2,1)}), bf16[8,144,128]{2,1,0:T(8,128)(2,1)S(1)}, u32[]{:S(2)}, u32[]{:S(2)}) async-start(bf16[8,144,128]{2,1,0:T(8,128)(2,1)} %pad_maximum_fusion), calls=%async_computation.1 | async-start | bytes 589824 | tf_op jit(solution)/shard_map/all_to_all | solution.py:57
  17.6 143.1 %all-gather.2.cloned.1.call-start = ((), (), s32[]{:S(2)}) async-start(), calls=%async_computation.5 | async-start | bytes 9732096 | tf_op jit(solution)/shard_map/all_gather | solution.py:353
  17.6 19.7 %collective-permute-start = (bf16[448,512]{1,0:T(8,128)(2,1)S(1)}, bf16[448,512]{1,0:T(8,128)(2,1)S(1)}, u32[]{:S(2)}, u32[]{:S(2)}) collective-permute-start(bf16[448,512]{1,0:T(8,128)(2,1)S(1)} %copy-done.1), channel_id=1, source_target_pairs={{0,1},{1,2},{2,3},{3,128},{128,129},{129,130},{130,131},{131,0},{4... | collective-permute-start | bytes 1376264 | tf_op jit(solution)/shard_map/ppermute | solution.py:49
  19.7 17.6 %collective-permute-start.1 = (bf16[448,512]{1,0:T(8,128)(2,1)S(1)}, bf16[448,512]{1,0:T(8,128)(2,1)S(1)}, u32[]{:S(2)}, u32[]{:S(2)}) collective-permute-start(bf16[448,512]{1,0:T(8,128)(2,1)S(1)} %copy-done.1), channel_id=1, source_target_pairs={{0,131},{1,0},{2,1},{3,2},{128,3},{129,128},{130,129},{131,130},{4... | collective-permute-start | bytes 1376264 | tf_op jit(solution)/shard_map/ppermute | solution.py:49
  37.3 25.7 %copy-start.10 = (bf16[448,512]{1,0:T(8,128)(2,1)}, bf16[448,512]{1,0:T(8,128)(2,1)S(1)}, u32[]{:S(2)}) copy-start(bf16[448,512]{1,0:T(8,128)(2,1)S(1)} %collective-permute-done.refs_1_) | copy-start | bytes 1376260
  37.3 25.7 %copy-start.11 = (bf16[448,512]{1,0:T(8,128)(2,1)}, bf16[448,512]{1,0:T(8,128)(2,1)S(1)}, u32[]{:S(2)}) copy-start(bf16[448,512]{1,0:T(8,128)(2,1)S(1)} %collective-permute-done.1.refs_2_) | copy-start | bytes 1376260
  38.2 20.5 %collective-permute-start.4 = (bf16[448,512]{1,0:T(8,128)(2,1)S(1)}, bf16[448,512]{1,0:T(8,128)(2,1)S(1)}, u32[]{:S(2)}, u32[]{:S(2)}) collective-permute-start(bf16[448,512]{1,0:T(8,128)(2,1)S(1)} %copy-done.7), channel_id=1, source_target_pairs={{0,1},{1,2},{2,3},{3,128},{128,129},{129,130},{130,131},{131,0},{4... | collective-permute-start | bytes 1376264 | tf_op jit(solution)/shard_map/ppermute | solution.py:49
  38.6 20.1 %collective-permute-start.5 = (bf16[448,512]{1,0:T(8,128)(2,1)S(1)}, bf16[448,512]{1,0:T(8,128)(2,1)}, u32[]{:S(2)}, u32[]{:S(2)}) collective-permute-start(bf16[448,512]{1,0:T(8,128)(2,1)S(1)} %copy-done.7), channel_id=1, source_target_pairs={{0,131},{1,0},{2,1},{3,2},{128,3},{129,128},{130,129},{131,130},{4... | collective-permute-start | bytes 1376264 | tf_op jit(solution)/shard_map/ppermute | solution.py:49
  41.5 19.3 %collective-permute-start.2 = (bf16[448,512]{1,0:T(8,128)(2,1)S(1)}, bf16[448,512]{1,0:T(8,128)(2,1)S(1)}, u32[]{:S(2)}, u32[]{:S(2)}) collective-permute-start(bf16[448,512]{1,0:T(8,128)(2,1)S(1)} %collective-permute-done.refs_1_), channel_id=1, source_target_pairs={{0,1},{1,2},{2,3},{3,128},{128,129},{129,130},{130,131},{131,0},{4... | collective-permute-start | bytes 1376264 | tf_op jit(solution)/shard_map/ppermute | solution.py:49
  41.5 19.3 %collective-permute-start.3 = (bf16[448,512]{1,0:T(8,128)(2,1)S(1)}, bf16[448,512]{1,0:T(8,128)(2,1)S(1)}, u32[]{:S(2)}, u32[]{:S(2)}) collective-permute-start(bf16[448,512]{1,0:T(8,128)(2,1)S(1)} %collective-permute-done.1.refs_2_), channel_id=1, source_target_pairs={{0,131},{1,0},{2,1},{3,2},{128,3},{129,128},{130,129},{131,130},{4... | collective-permute-start | bytes 1376264 | tf_op jit(solution)/shard_map/ppermute | solution.py:49
  58.7 4.3 %copy-start.12 = (bf16[448,512]{1,0:T(8,128)(2,1)}, bf16[448,512]{1,0:T(8,128)(2,1)S(1)}, u32[]{:S(2)}) copy-start(bf16[448,512]{1,0:T(8,128)(2,1)S(1)} %collective-permute-done.4.refs_6_) | copy-start | bytes 1376260
  60.8 2.2 %copy-start.13 = (bf16[448,512]{1,0:T(8,128)(2,1)}, bf16[448,512]{1,0:T(8,128)(2,1)S(1)}, u32[]{:S(2)}) copy-start(bf16[448,512]{1,0:T(8,128)(2,1)S(1)} %collective-permute-done.2.refs_3_) | copy-start | bytes 1376260
  60.8 27.1 %copy-start.8 = (bf16[448,512]{1,0:T(8,128)(2,1)}, bf16[448,512]{1,0:T(8,128)(2,1)S(1)}, u32[]{:S(2)}) copy-start(bf16[448,512]{1,0:T(8,128)(2,1)S(1)} %collective-permute-done.3.refs_4_) | copy-start | bytes 1376260
  63.0 48.7 %all-to-all-start.2 = ((bf16[32,32,896]{2,1,0:T(8,128)(2,1)}), bf16[32,32,896]{2,1,0:T(8,128)(2,1)S(1)}, u32[]{:S(2)}, u32[]{:S(2)}) async-start(bf16[32,32,896]{2,1,0:T(8,128)(2,1)} %bitcast.8), calls=%async_computation.2 | async-start | bytes 3670016 | tf_op jit(solution)/shard_map/all_to_all | solution.py:57
  70.7 13.4 %collective-permute-start.8 = (bf16[448,512]{1,0:T(8,128)(2,1)}, bf16[448,512]{1,0:T(8,128)(2,1)}, u32[]{:S(2)}, u32[]{:S(2)}) collective-permute-start(bf16[448,512]{1,0:T(8,128)(2,1)} %collective-permute-done.5.refs_7_), channel_id=1, source_target_pairs={{0,131},{1,0},{2,1},{3,2},{128,3},{129,128},{130,129},{131,130},{4... | collective-permute-start | bytes 1376264 | tf_op jit(solution)/shard_map/ppermute | solution.py:49
  73.7 14.8 %collective-permute-start.7 = (bf16[448,512]{1,0:T(8,128)(2,1)}, bf16[448,512]{1,0:T(8,128)(2,1)S(1)}, u32[]{:S(2)}, u32[]{:S(2)}) collective-permute-start(bf16[448,512]{1,0:T(8,128)(2,1)} %copy-done.12), channel_id=1, source_target_pairs={{0,1},{1,2},{2,3},{3,128},{128,129},{129,130},{130,131},{131,0},{4... | collective-permute-start | bytes 1376264 | tf_op jit(solution)/shard_map/ppermute | solution.py:49
  73.7 23.6 %collective-permute-start.6 = (bf16[448,512]{1,0:T(8,128)(2,1)}, bf16[448,512]{1,0:T(8,128)(2,1)}, u32[]{:S(2)}, u32[]{:S(2)}) collective-permute-start(bf16[448,512]{1,0:T(8,128)(2,1)} %copy-done.13), channel_id=1, source_target_pairs={{0,1},{1,2},{2,3},{3,128},{128,129},{129,130},{130,131},{131,0},{4... | collective-permute-start | bytes 1376264 | tf_op jit(solution)/shard_map/ppermute | solution.py:49
  84.1 15.0 %collective-permute-start.12 = (bf16[448,512]{1,0:T(8,128)(2,1)}, bf16[448,512]{1,0:T(8,128)(2,1)}, u32[]{:S(2)}, u32[]{:S(2)}) collective-permute-start(bf16[448,512]{1,0:T(8,128)(2,1)} %collective-permute-done.8.refs_9_), channel_id=1, source_target_pairs={{0,131},{1,0},{2,1},{3,2},{128,3},{129,128},{130,129},{131,130},{4... | collective-permute-start | bytes 1376264 | tf_op jit(solution)/shard_map/ppermute | solution.py:49
  87.9 31.2 %collective-permute-start.9 = (bf16[448,512]{1,0:T(8,128)(2,1)S(1)}, bf16[448,512]{1,0:T(8,128)(2,1)}, u32[]{:S(2)}, u32[]{:S(2)}) collective-permute-start(bf16[448,512]{1,0:T(8,128)(2,1)S(1)} %collective-permute-done.3.refs_4_), channel_id=1, source_target_pairs={{0,131},{1,0},{2,1},{3,2},{128,3},{129,128},{130,129},{131,130},{4... | collective-permute-start | bytes 1376264 | tf_op jit(solution)/shard_map/ppermute | solution.py:49
  88.5 0.8 copy-start.9
  95.7 0.7 copy-start.4
  97.3 21.8 %collective-permute-start.10 = (bf16[448,512]{1,0:T(8,128)(2,1)}, bf16[448,512]{1,0:T(8,128)(2,1)S(1)}, u32[]{:S(2)}, u32[]{:S(2)}) collective-permute-start(bf16[448,512]{1,0:T(8,128)(2,1)} %collective-permute-done.6.refs_0_), channel_id=1, source_target_pairs={{0,1},{1,2},{2,3},{3,128},{128,129},{129,130},{130,131},{131,0},{4... | collective-permute-start | bytes 1376264 | tf_op jit(solution)/shard_map/ppermute | solution.py:49
  98.0 22.1 %collective-permute-start.11 = (bf16[448,512]{1,0:T(8,128)(2,1)}, bf16[448,512]{1,0:T(8,128)(2,1)}, u32[]{:S(2)}, u32[]{:S(2)}) collective-permute-start(bf16[448,512]{1,0:T(8,128)(2,1)} %copy-done.9), channel_id=1, source_target_pairs={{0,1},{1,2},{2,3},{3,128},{128,129},{129,130},{130,131},{131,0},{4... | collective-permute-start | bytes 1376264 | tf_op jit(solution)/shard_map/ppermute | solution.py:49
  99.1 21.0 %collective-permute-start.13 = (bf16[448,512]{1,0:T(8,128)(2,1)}, bf16[448,512]{1,0:T(8,128)(2,1)}, u32[]{:S(2)}, u32[]{:S(2)}) collective-permute-start(bf16[448,512]{1,0:T(8,128)(2,1)} %collective-permute-done.12.refs_4_), channel_id=1, source_target_pairs={{0,131},{1,0},{2,1},{3,2},{128,3},{129,128},{130,129},{131,130},{4... | collective-permute-start | bytes 1376264 | tf_op jit(solution)/shard_map/ppermute | solution.py:49
  113.1 22.4 %all-to-all-start.3 = ((bf16[8,32,896]{2,1,0:T(8,128)(2,1)}), bf16[8,32,896]{2,1,0:T(8,128)(2,1)S(1)}, u32[]{:S(2)}, u32[]{:S(2)}) async-start(bf16[8,32,896]{2,1,0:T(8,128)(2,1)} %gather_fusion.1), calls=%async_computation.3 | async-start | bytes 917504 | tf_op jit(solution)/shard_map/all_to_all | solution.py:57
  119.1 1.0 copy-start.16
  135.4 3.8 %copy-start.5 = (bf16[8,32,896]{2,1,0:T(8,128)(2,1)}, bf16[8,32,896]{2,1,0:T(8,128)(2,1)S(1)}, u32[]{:S(2)}) copy-start(bf16[8,32,896]{2,1,0:T(8,128)(2,1)S(1)} %all-to-all-done.3) | copy-start | bytes 1376260
  135.4 25.3 %all-to-all-start.4 = ((bf16[8,64,768]{2,1,0:T(8,128)(2,1)}), bf16[8,64,768]{2,1,0:T(8,128)(2,1)S(1)}, u32[]{:S(2)}, u32[]{:S(2)}) async-start(bf16[8,64,768]{2,1,0:T(8,128)(2,1)} %get-tuple-element.43), calls=%async_computation.4 | async-start | bytes 1572864 | tf_op jit(solution)/shard_map/all_to_all | solution.py:57
  160.7 0.9 copy-start.6
  161.6 12.0 %copy-start.2 = (bf16[448,512]{1,0:T(8,128)(2,1)S(1)}, bf16[448,512]{1,0:T(8,128)(2,1)}, u32[]{:S(2)}) copy-start(bf16[448,512]{1,0:T(8,128)(2,1)} %hidden_hbm.1) | copy-start | bytes 1376260
  170.3 10.0 %collective-permute-start.14 = (bf16[64,2176]{1,0:T(8,128)(2,1)}, bf16[64,2176]{1,0:T(8,128)(2,1)S(1)}, u32[]{:S(2)}, u32[]{:S(2)}) collective-permute-start(bf16[64,2176]{1,0:T(8,128)(2,1)} %attention.1.chunk_ref), channel_id=1, source_target_pairs={{0,1},{1,2},{2,3},{3,128},{128,129},{129,130},{130,131},{131,0},{4... | collective-permute-start | bytes 835592 | tf_op jit(solution)/shard_map/ppermute | solution.py:49
  172.7 7.7 %collective-permute-start.15 = (bf16[64,2176]{1,0:T(8,128)(2,1)}, bf16[64,2176]{1,0:T(8,128)(2,1)S(1)}, u32[]{:S(2)}, u32[]{:S(2)}) collective-permute-start(bf16[64,2176]{1,0:T(8,128)(2,1)} %attention.1.chunk_ref), channel_id=1, source_target_pairs={{0,131},{1,0},{2,1},{3,2},{128,3},{129,128},{130,129},{131,130},{4... | collective-permute-start | bytes 835592 | tf_op jit(solution)/shard_map/ppermute | solution.py:49
  173.6 1.0 copy-start.3
  180.4 8.9 %collective-permute-start.16 = (bf16[64,2176]{1,0:T(8,128)(2,1)S(1)}, bf16[64,2176]{1,0:T(8,128)(2,1)S(1)}, u32[]{:S(2)}, u32[]{:S(2)}) collective-permute-start(bf16[64,2176]{1,0:T(8,128)(2,1)S(1)} %collective-permute-done.14.refs_0_), channel_id=1, source_target_pairs={{0,1},{1,2},{2,3},{3,128},{128,129},{129,130},{130,131},{131,0},{4... | collective-permute-start | bytes 835592 | tf_op jit(solution)/shard_map/ppermute | solution.py:49
  180.8 8.5 %collective-permute-start.17 = (bf16[64,2176]{1,0:T(8,128)(2,1)S(1)}, bf16[64,2176]{1,0:T(8,128)(2,1)S(1)}, u32[]{:S(2)}, u32[]{:S(2)}) collective-permute-start(bf16[64,2176]{1,0:T(8,128)(2,1)S(1)} %collective-permute-done.15.refs_1_), channel_id=1, source_target_pairs={{0,131},{1,0},{2,1},{3,2},{128,3},{129,128},{130,129},{131,130},{4... | collective-permute-start | bytes 835592 | tf_op jit(solution)/shard_map/ppermute | solution.py:49
  189.3 8.0 %collective-permute-start.18 = (bf16[64,2176]{1,0:T(8,128)(2,1)S(1)}, bf16[64,2176]{1,0:T(8,128)(2,1)S(1)}, u32[]{:S(2)}, u32[]{:S(2)}) collective-permute-start(bf16[64,2176]{1,0:T(8,128)(2,1)S(1)} %collective-permute-done.16.refs_0_), channel_id=1, source_target_pairs={{0,1},{1,2},{2,3},{3,128},{128,129},{129,130},{130,131},{131,0},{4... | collective-permute-start | bytes 835592 | tf_op jit(solution)/shard_map/ppermute | solution.py:49
  189.3 8.0 %collective-permute-start.19 = (bf16[64,2176]{1,0:T(8,128)(2,1)S(1)}, bf16[64,2176]{1,0:T(8,128)(2,1)S(1)}, u32[]{:S(2)}, u32[]{:S(2)}) collective-permute-start(bf16[64,2176]{1,0:T(8,128)(2,1)S(1)} %collective-permute-done.17.refs_1_), channel_id=1, source_target_pairs={{0,131},{1,0},{2,1},{3,2},{128,3},{129,128},{130,129},{131,130},{4... | collective-permute-start | bytes 835592 | tf_op jit(solution)/shard_map/ppermute | solution.py:49
  197.3 6.3 %collective-permute-start.20 = (bf16[32,2176]{1,0:T(8,128)(2,1)S(1)}, bf16[32,2176]{1,0:T(8,128)(2,1)S(1)}, u32[]{:S(2)}, u32[]{:S(2)}) collective-permute-start(bf16[32,2176]{1,0:T(8,128)(2,1)S(1)} %slice.11), channel_id=1, source_target_pairs={{0,1},{1,2},{2,3},{3,128},{128,129},{129,130},{130,131},{131,0},{4... | collective-permute-start | bytes 417800 | tf_op jit(solution)/shard_map/ppermute | solution.py:49
  197.4 6.2 %collective-permute-start.21 = (bf16[32,2176]{1,0:T(8,128)(2,1)S(1)}, bf16[32,2176]{1,0:T(8,128)(2,1)S(1)}, u32[]{:S(2)}, u32[]{:S(2)}) collective-permute-start(bf16[32,2176]{1,0:T(8,128)(2,1)S(1)} %slice.12), channel_id=1, source_target_pairs={{0,131},{1,0},{2,1},{3,2},{128,3},{129,128},{130,129},{131,130},{4... | collective-permute-start | bytes 417800 | tf_op jit(solution)/shard_map/ppermute | solution.py:49
Sparse Core Ops, SparseCore 0:
  38.3 76.6 all-gather.1

commit v7 on v6

--- a/solution.py
+++ b/solution.py
@@ -330,20 +330,18 @@
     part = exchange(part, Z)
 
     projections = (query_weight, condition_weight.T, out_weight)
-    right = left = hidden
+    right, left = shift(hidden, 1), shift(hidden, -1)
+    asked, right, left = tie(asked, right, left)
+    returned = exchange(database[asked].reshape(NDP, NEIGH * NLEN // NZ, DE), "dp")
+    index, chunks, grad_chunks = [me], [hidden, right, left], [cotangent]
     grad_right = grad_left = cotangent
-    index, chunks, grad_chunks = [me], [hidden], [cotangent]
     for step in range(1, 4):
-        if step == 1:
-            right, left = shift(right, 1), shift(left, -1)
-            part, right, left = tie(part, right, left)
-            chunks += [right, left]
         if step < 3:
             right, left = shift(right, 1), shift(left, -1)
         grad_right, grad_left = shift(grad_right, 1), shift(grad_left, -1)
-        if step == 1:
-            asked, right, left, grad_right, grad_left = tie(
-                asked, right, left, grad_right, grad_left
+        if step == 2:
+            part, returned, right, left, grad_right, grad_left = tie(
+                part, returned, right, left, grad_right, grad_left
             )
         if step < 3:
             chunks += [right, left]
@@ -351,7 +349,6 @@
         index += [(me - step) % NZ, (me + step) % NZ]
     part = part.transpose(1, 0, 2).reshape(144, HALF)
     weights = lax.all_gather(part, "dp", axis=0, tiled=True).reshape(16, 2, 144, HALF)
-    returned = exchange(database[asked].reshape(NDP, NEIGH * NLEN // NZ, DE), "dp")
     chosen = returned[jnp.concatenate([owner, owner[:1]])]
     early = 5
     acc, squares = pl.pallas_call(

time: 213 us -> 212 us (level)
  blocking collectives: 13.6 us -> 0 us
  starting transfers between devices: 60.7 us -> 66.2 us
  waiting for transfers between devices: 76.7 us -> 79.5 us
    all_to_all x1 -> x0, blocking collectives: 13.6 us -> none  [exchange(): return lax.all_to_all(x, axis, split_axis=0, concat_axis=0, tiled=True)]
    ppermute x22, waiting for transfers between devices: 41 us -> 52.8 us  [shift(): return lax.ppermute(x, Z, [(i, (i + by) % NZ) for i in range(NZ)])]
    all_to_all x4 -> x5, waiting for transfers between devices: 35.8 us -> 26.7 us  [exchange(): return lax.all_to_all(x, axis, split_axis=0, concat_axis=0, tiled=True)]
    ppermute x22, starting transfers between devices: 34.8 us -> 39.3 us  [shift(): return lax.ppermute(x, Z, [(i, (i + by) % NZ) for i in range(NZ)])]
    all_to_all x4 -> x5, starting transfers between devices: 25.9 us -> 26.8 us  [exchange(): return lax.all_to_all(x, axis, split_axis=0, concat_axis=0, tiled=True)]
  transfers between devices with their start and end apart: 27 -> 28, of which waited for: 14 -> 16; matrix products, arithmetic and copies ran while one was open for 2% -> 4% of each run, Pallas kernels for 12% -> 13%
where the time goes in v7:
time: 212 us; the launch traced here: 210 us
  waiting for transfers between devices  79.5 us (38%)
  starting transfers between devices  66.2 us (31%)
  Pallas kernels  37.2 us (18%)
  between operations  13.8 us (7%)
  local copies, waits for them, and re-layouts  11.1 us (5%)
    ppermute x22, waiting for transfers between devices, shift(): return lax.ppermute(x, Z, [(i, (i + by) % NZ) for i in range(NZ)])  52.8 us
    ppermute x22, starting transfers between devices, shift(): return lax.ppermute(x, Z, [(i, (i + by) % NZ) for i in range(NZ)])  39.3 us
    all_to_all x5, starting transfers between devices, exchange(): return lax.all_to_all(x, axis, split_axis=0, concat_axis=0, tiled=True)  26.8 us
    all_to_all x5, waiting for transfers between devices, exchange(): return lax.all_to_all(x, axis, split_axis=0, concat_axis=0, tiled=True)  26.7 us
    pallas_call x1, Pallas kernels, shards(): pl.pallas_call(attention, out_shape=jax.ShapeDtypeStruct((SEG, 2 * HALF +...  8.7 us
    pallas_call x4, Pallas kernels, finish_call(): pl.pallas_call(functools.partial(finish, starts), out_shape=jax.ShapeDtyp...  7.98 us
    pallas_call x1, Pallas kernels, shards(): pl.pallas_call(functools.partial(project_last, len(hiddens)), out_shape=(...  7.47 us
    pallas_call x1, Pallas kernels, shards(): pl.pallas_call(functools.partial(project, early), out_shape=(jax.ShapeDty...  6.36 us
  transfers between devices with their start and end apart: 28, of which 16 were waited for; matrix products, arithmetic and copies ran while one was open for 4% of the time, Pallas kernels for 13%

profile of v7, /device:TPU:2, one launch (start us, length us, event | category | flops | bytes accessed | tf_op | source)
XLA Modules:
  0.0 209.9 jit_solution(13460516763051410443)
XLA Ops:
  6.5 1.9 collective-permute-start
  8.5 3.9 %collective-permute-start.1 = (bf16[448,512]{1,0:T(8,128)(2,1)}, bf16[448,512]{1,0:T(8,128)(2,1)S(1)}, u32[]{:S(2)}, u32[]{:S(2)}) collective-permute-start(bf16[448,512]{1,0:T(8,128)(2,1)} %hidden_hbm.1), channel_id=1, source_target_pairs={{0,131},{1,0},{2,1},{3,2},{128,3},{129,128},{130,129},{131,130},{4... | collective-permute-start | bytes 1376264 | tf_op jit(solution)/shard_map/ppermute | solution.py:49
  12.4 0.8 copy.36
  13.2 0.7 fusion
  14.0 0.7 copy.37
  14.7 7.6 %all-to-all-start.1 = ((s32[32,1,2]{2,1,0:T(1,128)}), s32[32,1,2]{2,1,0:T(1,128)S(1)}, u32[]{:S(2)}, u32[]{:S(2)}) async-start(s32[32,1,2]{2,1,0:T(1,128)} %copy.37), calls=%async_computation.1 | async-start | bytes 32768 | tf_op jit(solution)/shard_map/all_to_all | solution.py:57
  22.3 0.9 constant_dynamic-slice_fusion
  23.2 0.8 dynamic_slice.6
  24.0 0.7 pad_maximum_fusion
  24.8 3.6 %all-to-all-done.1 = s32[32,1,2]{2,1,0:T(1,128)S(1)} async-done(((s32[32,1,2]{2,1,0:T(1,128)}), s32[32,1,2]{2,1,0:T(1,128)S(1)}, u32[]{:S(2)}, u32[]{:S(2)}) %all-to-all-start.1) | async-done | bytes 288 | tf_op jit(solution)/shard_map/all_to_all | solution.py:57
  28.4 5.8 %all-to-all-start = ((bf16[8,144,128]{2,1,0:T(8,128)(2,1)}), bf16[8,144,128]{2,1,0:T(8,128)(2,1)S(1)}, u32[]{:S(2)}, u32[]{:S(2)}) async-start(bf16[8,144,128]{2,1,0:T(8,128)(2,1)} %pad_maximum_fusion), calls=%async_computation | async-start | bytes 589824 | tf_op jit(solution)/shard_map/all_to_all | solution.py:57
  34.3 0.1 copy.39
  34.4 0.1 reshape.126
  34.5 2.0 gather_fusion
  36.6 10.3 %all-to-all-done = bf16[8,144,128]{2,1,0:T(8,128)(2,1)S(1)} async-done(((bf16[8,144,128]{2,1,0:T(8,128)(2,1)}), bf16[8,144,128]{2,1,0:T(8,128)(2,1)S(1)}, u32[]{:S(2)}, u32[]{:S(2)}) %all-to-all-start) | async-done | bytes 294944 | tf_op jit(solution)/shard_map/all_to_all | solution.py:57
  46.8 5.2 %all-to-all-start.2 = ((bf16[32,32,896]{2,1,0:T(8,128)(2,1)}), bf16[32,32,896]{2,1,0:T(8,128)(2,1)S(1)}, u32[]{:S(2)}, u32[]{:S(2)}) async-start(bf16[32,32,896]{2,1,0:T(8,128)(2,1)} %bitcast.8), calls=%async_computation.2 | async-start | bytes 3670016 | tf_op jit(solution)/shard_map/all_to_all | solution.py:57
  52.1 0.6 collective-permute-start.6
  52.7 2.7 %collective-permute-start.8 = (bf16[448,512]{1,0:T(8,128)(2,1)S(1)}, bf16[448,512]{1,0:T(8,128)(2,1)S(1)}, u32[]{:S(2)}, u32[]{:S(2)}) collective-permute-start(bf16[448,512]{1,0:T(8,128)(2,1)S(1)} %copy-done.6), channel_id=1, source_target_pairs={{0,131},{1,0},{2,1},{3,2},{128,3},{129,128},{130,129},{131,130},{4... | collective-permute-start | bytes 1376264 | tf_op jit(solution)/shard_map/ppermute | solution.py:49
  55.4 3.2 %collective-permute-start.4 = (bf16[448,512]{1,0:T(8,128)(2,1)}, bf16[448,512]{1,0:T(8,128)(2,1)S(1)}, u32[]{:S(2)}, u32[]{:S(2)}) collective-permute-start(bf16[448,512]{1,0:T(8,128)(2,1)} %copy-done.8), channel_id=1, source_target_pairs={{0,131},{1,0},{2,1},{3,2},{128,3},{129,128},{130,129},{131,130},{4... | collective-permute-start | bytes 1376264 | tf_op jit(solution)/shard_map/ppermute | solution.py:49
  58.7 8.1 %collective-permute-done.6.refs_6_ = bf16[448,512]{1,0:T(8,128)(2,1)S(1)} collective-permute-done((bf16[448,512]{1,0:T(8,128)(2,1)S(1)}, bf16[448,512]{1,0:T(8,128)(2,1)S(1)}, u32[]{:S(2)}, u32[]{:S(2)}) %collective-permute-start.6) | collective-permute-done | bytes 458784 | tf_op jit(solution)/shard_map/ppermute | solution.py:49
  66.8 3.3 %collective-permute-start.9 = (bf16[448,512]{1,0:T(8,128)(2,1)S(1)}, bf16[448,512]{1,0:T(8,128)(2,1)S(1)}, u32[]{:S(2)}, u32[]{:S(2)}) collective-permute-start(bf16[448,512]{1,0:T(8,128)(2,1)S(1)} %collective-permute-done.8.refs_7_), channel_id=1, source_target_pairs={{0,131},{1,0},{2,1},{3,2},{128,3},{129,128},{130,129},{131,130},{4... | collective-permute-start | bytes 1376264 | tf_op jit(solution)/shard_map/ppermute | solution.py:49
  70.0 6.6 %collective-permute-done.2.refs_3_ = bf16[448,512]{1,0:T(8,128)(2,1)S(1)} collective-permute-done((bf16[448,512]{1,0:T(8,128)(2,1)S(1)}, bf16[448,512]{1,0:T(8,128)(2,1)S(1)}, u32[]{:S(2)}, u32[]{:S(2)}) %collective-permute-start.2) | collective-permute-done | bytes 458784 | tf_op jit(solution)/shard_map/ppermute | solution.py:49
  76.6 3.3 %collective-permute-start.5 = (bf16[448,512]{1,0:T(8,128)(2,1)S(1)}, bf16[448,512]{1,0:T(8,128)(2,1)}, u32[]{:S(2)}, u32[]{:S(2)}) collective-permute-start(bf16[448,512]{1,0:T(8,128)(2,1)S(1)} %collective-permute-done.4.refs_4_), channel_id=1, source_target_pairs={{0,131},{1,0},{2,1},{3,2},{128,3},{129,128},{130,129},{131,130},{4... | collective-permute-start | bytes 1376264 | tf_op jit(solution)/shard_map/ppermute | solution.py:49
  79.9 6.6 %collective-permute-done.7.refs_8_ = bf16[448,512]{1,0:T(8,128)(2,1)S(1)} collective-permute-done((bf16[448,512]{1,0:T(8,128)(2,1)S(1)}, bf16[448,512]{1,0:T(8,128)(2,1)S(1)}, u32[]{:S(2)}, u32[]{:S(2)}) %collective-permute-start.7) | collective-permute-done | bytes 458784 | tf_op jit(solution)/shard_map/ppermute | solution.py:49
  86.4 9.0 %collective-permute-done.3.refs_0_ = bf16[448,512]{1,0:T(8,128)(2,1)S(1)} collective-permute-done((bf16[448,512]{1,0:T(8,128)(2,1)S(1)}, bf16[448,512]{1,0:T(8,128)(2,1)S(1)}, u32[]{:S(2)}, u32[]{:S(2)}) %collective-permute-start.3) | collective-permute-done | bytes 458784 | tf_op jit(solution)/shard_map/ppermute | solution.py:49
  95.5 0.8 copy_bitcast_fusion
  96.4 3.0 %collective-permute-start.12 = (bf16[448,512]{1,0:T(8,128)(2,1)S(1)}, bf16[448,512]{1,0:T(8,128)(2,1)}, u32[]{:S(2)}, u32[]{:S(2)}) collective-permute-start(bf16[448,512]{1,0:T(8,128)(2,1)S(1)} %collective-permute-done.9.refs_9_), channel_id=1, source_target_pairs={{0,131},{1,0},{2,1},{3,2},{128,3},{129,128},{130,129},{131,130},{4... | collective-permute-start | bytes 1376264 | tf_op jit(solution)/shard_map/ppermute | solution.py:49
  99.5 0.2 collective-permute-start.11
  99.7 6.4 %project.1 = (f32[448,768]{1,0:T(8,128)}, f32[448,1]{1,0:T(8,128)S(1)}) custom-call(s32[5]{0:T(128)S(1)} %stack.61.index_ref, bf16[448,512]{1,0:T(8,128)(2,1)} %hidden_hbm.1, bf16[448,512]{1,0:T(8,128)(2,1)} %copy-done.7, bf16[448,512]{1,0:T(8,128)(2,1)} %copy-done.8, bf16[448,512]{1,0:T(8,128)(2,1)} %copy-done.12, bf16[448,512]{1,0:T(8,128)(2,1)} %copy-done.13, ...), custom_call_target="tpu_custom_call" | custom-call | flops 1688207360 | bytes 16000000 | tf_op jit(solution)/shard_map/project/pallas_call | solution.py:354
  106.1 0.7 copy-done.3
  106.8 1.6 collective-permute-done.12.refs_4_
  108.3 3.8 %collective-permute-start.13 = (bf16[448,512]{1,0:T(8,128)(2,1)}, bf16[448,512]{1,0:T(8,128)(2,1)S(1)}, u32[]{:S(2)}, u32[]{:S(2)}) collective-permute-start(bf16[448,512]{1,0:T(8,128)(2,1)} %collective-permute-done.12.refs_4_), channel_id=1, source_target_pairs={{0,131},{1,0},{2,1},{3,2},{128,3},{129,128},{130,129},{131,130},{4... | collective-permute-start | bytes 1376264 | tf_op jit(solution)/shard_map/ppermute | solution.py:49
  112.1 0.1 fusion.1
  112.3 1.4 gather_fusion.1
  113.7 3.5 %all-to-all-start.3 = ((bf16[8,32,896]{2,1,0:T(8,128)(2,1)}), bf16[8,32,896]{2,1,0:T(8,128)(2,1)S(1)}, u32[]{:S(2)}, u32[]{:S(2)}) async-start(bf16[8,32,896]{2,1,0:T(8,128)(2,1)} %gather_fusion.1), calls=%async_computation.3 | async-start | bytes 917504 | tf_op jit(solution)/shard_map/all_to_all | solution.py:57
  117.2 11.5 %collective-permute-done.10.refs_2_ = bf16[448,512]{1,0:T(8,128)(2,1)} collective-permute-done((bf16[448,512]{1,0:T(8,128)(2,1)S(1)}, bf16[448,512]{1,0:T(8,128)(2,1)}, u32[]{:S(2)}, u32[]{:S(2)}) %collective-permute-start.10) | collective-permute-done | bytes 458784 | tf_op jit(solution)/shard_map/ppermute | solution.py:49
  128.7 0.8 copy-done.18
  129.4 7.5 %project_last.1 = (bf16[8,64,768]{2,1,0:T(8,128)(2,1)}, f32[448,1]{1,0:T(8,128)S(1)}) custom-call(s32[3]{0:T(128)S(1)} %pad_add_fusion.1.index_ref, bf16[448,512]{1,0:T(8,128)(2,1)} %copy-done.16, bf16[448,512]{1,0:T(8,128)(2,1)} %collective-permute-done.5.refs_1_, bf16[448,512]{1,0:T(8,128)(2,1)} %collective-permute-done.10.refs_2_, ...), custom_call_target="tpu_custom_call" | custom-call | flops 20000000000 | bytes 4000000 | tf_op jit(solution)/shard_map/project_last/pallas_call | solution.py:396
  136.9 4.7 %all-to-all-start.4 = ((bf16[8,64,768]{2,1,0:T(8,128)(2,1)}), bf16[8,64,768]{2,1,0:T(8,128)(2,1)S(1)}, u32[]{:S(2)}, u32[]{:S(2)}) async-start(bf16[8,64,768]{2,1,0:T(8,128)(2,1)} %get-tuple-element.45), calls=%async_computation.4 | async-start | bytes 1572864 | tf_op jit(solution)/shard_map/all_to_all | solution.py:57
  141.6 3.2 %encoder_queries.1.enc_q_hbm = bf16[256,896]{1,0:T(8,128)(2,1)} custom-call(bf16[256,896]{1,0:T(8,128)(2,1)} %bitcast.32, bf16[896,896]{1,0:T(8,128)(2,1)} %weight_hbm.1), custom_call_target="tpu_custom_call" | custom-call | flops 411041792 | bytes 3000000 | tf_op jit(solution)/shard_map/encoder_queries/pallas_call | solution.py:382
  144.8 12.9 %all-to-all-done.4.got_hbm = bf16[8,64,768]{2,1,0:T(8,128)(2,1)S(1)} async-done(((bf16[8,64,768]{2,1,0:T(8,128)(2,1)}), bf16[8,64,768]{2,1,0:T(8,128)(2,1)S(1)}, u32[]{:S(2)}, u32[]{:S(2)}) %all-to-all-start.4) | async-done | bytes 786464 | tf_op jit(solution)/shard_map/all_to_all | solution.py:57
  157.7 0.9 copy-done.5
  158.6 8.7 %attention.1.chunk_ref = bf16[64,2176]{1,0:T(8,128)(2,1)} custom-call(bf16[256,896]{1,0:T(8,128)(2,1)} %bitcast.33, bf16[256,896]{1,0:T(8,128)(2,1)} %encoder_queries.1.enc_q_hbm, bf16[8,64,768]{2,1,0:T(8,128)(2,1)} %copy-done.5, bf16[896,896]{1,0:T(8,128)(2,1)} %enc_out_hbm.1, bf16[16,2,144,1024]{3,2,1,0:T(8,128)(2,1)} %bitcast.29), custom_call_target="tpu_custom_call" | custom-call | flops 4000000000 | bytes 12000000 | tf_op jit(solution)/shard_map/attention/pallas_call | solution.py:424
  167.3 0.9 collective-permute-start.14
  168.1 2.7 %collective-permute-start.15 = (bf16[64,2176]{1,0:T(8,128)(2,1)}, bf16[64,2176]{1,0:T(8,128)(2,1)S(1)}, u32[]{:S(2)}, u32[]{:S(2)}) collective-permute-start(bf16[64,2176]{1,0:T(8,128)(2,1)} %attention.1.chunk_ref), channel_id=1, source_target_pairs={{0,131},{1,0},{2,1},{3,2},{128,3},{129,128},{130,129},{131,130},{4... | collective-permute-start | bytes 835592 | tf_op jit(solution)/shard_map/ppermute | solution.py:49
  170.8 1.0 copy-done.2
  171.8 3.5 %finish_first.1 = (bf16[448,512]{1,0:T(8,128)(2,1)}, bf16[448,512]{1,0:T(8,128)(2,1)S(1)}, f32[448,1]{1,0:T(8,128)S(1)}, bf16[2,32,16,1024]{3,2,1,0:T(8,128)(2,1)S(1)}) custom-call(s32[1]{0:T(128)} %bitcast.13.source_ref, bf16[64,2176]{1,0:T(8,128)(2,1)S(1)} %copy-done.2, bf16[448,512]{1,0:T(8,128)(2,1)S(1)} %copy-done.1, ...), custom_call_target="tpu_custom_call" | custom-call | flops 134217728 | bytes 4000000 | tf_op jit(solution)/shard_map/finish_first/pallas_call | solution.py:448
  175.3 0.2 collective-permute-done.14.refs_0_
  175.6 0.8 collective-permute-start.16
  176.3 2.5 %collective-permute-start.17 = (bf16[64,2176]{1,0:T(8,128)(2,1)S(1)}, bf16[64,2176]{1,0:T(8,128)(2,1)S(1)}, u32[]{:S(2)}, u32[]{:S(2)}) collective-permute-start(bf16[64,2176]{1,0:T(8,128)(2,1)S(1)} %collective-permute-done.15.refs_1_), channel_id=1, source_target_pairs={{0,131},{1,0},{2,1},{3,2},{128,3},{129,128},{130,129},{131,130},{4... | collective-permute-start | bytes 835592 | tf_op jit(solution)/shard_map/ppermute | solution.py:49
  178.9 2.0 finish.4.refs_5_
  180.9 2.4 %collective-permute-done.16.refs_0_ = bf16[64,2176]{1,0:T(8,128)(2,1)S(1)} collective-permute-done((bf16[64,2176]{1,0:T(8,128)(2,1)S(1)}, bf16[64,2176]{1,0:T(8,128)(2,1)S(1)}, u32[]{:S(2)}, u32[]{:S(2)}) %collective-permute-start.16) | collective-permute-done | bytes 278560 | tf_op jit(solution)/shard_map/ppermute | solution.py:49
  183.3 1.6 collective-permute-done.17.refs_1_
  184.9 2.6 %collective-permute-start.18 = (bf16[64,2176]{1,0:T(8,128)(2,1)S(1)}, bf16[64,2176]{1,0:T(8,128)(2,1)S(1)}, u32[]{:S(2)}, u32[]{:S(2)}) collective-permute-start(bf16[64,2176]{1,0:T(8,128)(2,1)S(1)} %collective-permute-done.16.refs_0_), channel_id=1, source_target_pairs={{0,1},{1,2},{2,3},{3,128},{128,129},{129,130},{130,131},{131,0},{4... | collective-permute-start | bytes 835592 | tf_op jit(solution)/shard_map/ppermute | solution.py:49
  187.5 0.6 collective-permute-start.19
  188.2 2.0 finish.5.refs_5_
  190.3 3.0 %collective-permute-done.18.refs_0_ = bf16[64,2176]{1,0:T(8,128)(2,1)S(1)} collective-permute-done((bf16[64,2176]{1,0:T(8,128)(2,1)S(1)}, bf16[64,2176]{1,0:T(8,128)(2,1)S(1)}, u32[]{:S(2)}, u32[]{:S(2)}) %collective-permute-start.18) | collective-permute-done | bytes 278560 | tf_op jit(solution)/shard_map/ppermute | solution.py:49
  193.2 0.8 collective-permute-done.19.refs_1_
  194.1 1.9 collective-permute-start.20
  196.0 1.5 collective-permute-start.21
  197.6 2.0 finish.6.refs_5_
  199.7 0.8 collective-permute-done.20.refs_0_
  200.4 0.7 collective-permute-done.21.refs_1_
  201.1 1.9 finish.7
  (68 shorter events, 0.9 us)
Async XLA Ops:
  6.5 28.0 %copy-start = (bf16[16,16,896]{2,1,0:T(8,128)(2,1)S(1)}, bf16[16,16,896]{2,1,0:T(8,128)(2,1)}, u32[]{:S(2)}) copy-start(bf16[16,16,896]{2,1,0:T(8,128)(2,1)} %param.19) | copy-start | bytes 1376260
  6.5 27.8 %collective-permute-start = (bf16[448,512]{1,0:T(8,128)(2,1)}, bf16[448,512]{1,0:T(8,128)(2,1)S(1)}, u32[]{:S(2)}, u32[]{:S(2)}) collective-permute-start(bf16[448,512]{1,0:T(8,128)(2,1)} %hidden_hbm.1), channel_id=1, source_target_pairs={{0,1},{1,2},{2,3},{3,128},{128,129},{129,130},{130,131},{131,0},{4... | collective-permute-start | bytes 1376264 | tf_op jit(solution)/shard_map/ppermute | solution.py:49
  8.5 25.8 %collective-permute-start.1 = (bf16[448,512]{1,0:T(8,128)(2,1)}, bf16[448,512]{1,0:T(8,128)(2,1)S(1)}, u32[]{:S(2)}, u32[]{:S(2)}) collective-permute-start(bf16[448,512]{1,0:T(8,128)(2,1)} %hidden_hbm.1), channel_id=1, source_target_pairs={{0,131},{1,0},{2,1},{3,2},{128,3},{129,128},{130,129},{131,130},{4... | collective-permute-start | bytes 1376264 | tf_op jit(solution)/shard_map/ppermute | solution.py:49
  14.7 13.7 %all-to-all-start.1 = ((s32[32,1,2]{2,1,0:T(1,128)}), s32[32,1,2]{2,1,0:T(1,128)S(1)}, u32[]{:S(2)}, u32[]{:S(2)}) async-start(s32[32,1,2]{2,1,0:T(1,128)} %copy.37), calls=%async_computation.1 | async-start | bytes 32768 | tf_op jit(solution)/shard_map/all_to_all | solution.py:57
  28.4 18.5 %all-to-all-start = ((bf16[8,144,128]{2,1,0:T(8,128)(2,1)}), bf16[8,144,128]{2,1,0:T(8,128)(2,1)S(1)}, u32[]{:S(2)}, u32[]{:S(2)}) async-start(bf16[8,144,128]{2,1,0:T(8,128)(2,1)} %pad_maximum_fusion), calls=%async_computation | async-start | bytes 589824 | tf_op jit(solution)/shard_map/all_to_all | solution.py:57
  34.3 21.1 %copy-start.7 = (bf16[448,512]{1,0:T(8,128)(2,1)}, bf16[448,512]{1,0:T(8,128)(2,1)S(1)}, u32[]{:S(2)}) copy-start(bf16[448,512]{1,0:T(8,128)(2,1)S(1)} %collective-permute-done.refs_1_) | copy-start | bytes 1376260
  34.3 2.3 %copy-start.8 = (bf16[448,512]{1,0:T(8,128)(2,1)}, bf16[448,512]{1,0:T(8,128)(2,1)S(1)}, u32[]{:S(2)}) copy-start(bf16[448,512]{1,0:T(8,128)(2,1)S(1)} %collective-permute-done.1.refs_2_) | copy-start | bytes 1376260
  46.8 5.3 %copy-start.6 = (bf16[448,512]{1,0:T(8,128)(2,1)S(1)}, bf16[448,512]{1,0:T(8,128)(2,1)}, u32[]{:S(2)}) copy-start(bf16[448,512]{1,0:T(8,128)(2,1)} %refs_5_.1) | copy-start | bytes 1376260
  46.8 48.7 %all-to-all-start.2 = ((bf16[32,32,896]{2,1,0:T(8,128)(2,1)}), bf16[32,32,896]{2,1,0:T(8,128)(2,1)S(1)}, u32[]{:S(2)}, u32[]{:S(2)}) async-start(bf16[32,32,896]{2,1,0:T(8,128)(2,1)} %bitcast.8), calls=%async_computation.2 | async-start | bytes 3670016 | tf_op jit(solution)/shard_map/all_to_all | solution.py:57
  52.0 105.7 %all-gather.2.cloned.1.call-start = ((), (), s32[]{:S(2)}) async-start(), calls=%async_computation.5 | async-start | bytes 9732096 | tf_op jit(solution)/shard_map/all_gather | solution.py:351
  52.1 14.7 %collective-permute-start.6 = (bf16[448,512]{1,0:T(8,128)(2,1)S(1)}, bf16[448,512]{1,0:T(8,128)(2,1)S(1)}, u32[]{:S(2)}, u32[]{:S(2)}) collective-permute-start(bf16[448,512]{1,0:T(8,128)(2,1)S(1)} %copy-done.6), channel_id=1, source_target_pairs={{0,1},{1,2},{2,3},{3,128},{128,129},{129,130},{130,131},{131,0},{4... | collective-permute-start | bytes 1376264 | tf_op jit(solution)/shard_map/ppermute | solution.py:49
  52.7 14.0 %collective-permute-start.8 = (bf16[448,512]{1,0:T(8,128)(2,1)S(1)}, bf16[448,512]{1,0:T(8,128)(2,1)S(1)}, u32[]{:S(2)}, u32[]{:S(2)}) collective-permute-start(bf16[448,512]{1,0:T(8,128)(2,1)S(1)} %copy-done.6), channel_id=1, source_target_pairs={{0,131},{1,0},{2,1},{3,2},{128,3},{129,128},{130,129},{131,130},{4... | collective-permute-start | bytes 1376264 | tf_op jit(solution)/shard_map/ppermute | solution.py:49
  55.4 21.2 %collective-permute-start.2 = (bf16[448,512]{1,0:T(8,128)(2,1)S(1)}, bf16[448,512]{1,0:T(8,128)(2,1)S(1)}, u32[]{:S(2)}, u32[]{:S(2)}) collective-permute-start(bf16[448,512]{1,0:T(8,128)(2,1)S(1)} %collective-permute-done.refs_1_), channel_id=1, source_target_pairs={{0,1},{1,2},{2,3},{3,128},{128,129},{129,130},{130,131},{131,0},{4... | collective-permute-start | bytes 1376264 | tf_op jit(solution)/shard_map/ppermute | solution.py:49
  55.4 21.2 %collective-permute-start.4 = (bf16[448,512]{1,0:T(8,128)(2,1)}, bf16[448,512]{1,0:T(8,128)(2,1)S(1)}, u32[]{:S(2)}, u32[]{:S(2)}) collective-permute-start(bf16[448,512]{1,0:T(8,128)(2,1)} %copy-done.8), channel_id=1, source_target_pairs={{0,131},{1,0},{2,1},{3,2},{128,3},{129,128},{130,129},{131,130},{4... | collective-permute-start | bytes 1376264 | tf_op jit(solution)/shard_map/ppermute | solution.py:49
  66.8 28.7 %copy-start.10 = (bf16[448,512]{1,0:T(8,128)(2,1)}, bf16[448,512]{1,0:T(8,128)(2,1)S(1)}, u32[]{:S(2)}) copy-start(bf16[448,512]{1,0:T(8,128)(2,1)S(1)} %collective-permute-done.6.refs_6_) | copy-start | bytes 1376260
  66.8 19.7 %collective-permute-start.7 = (bf16[448,512]{1,0:T(8,128)(2,1)S(1)}, bf16[448,512]{1,0:T(8,128)(2,1)S(1)}, u32[]{:S(2)}, u32[]{:S(2)}) collective-permute-start(bf16[448,512]{1,0:T(8,128)(2,1)S(1)} %collective-permute-done.6.refs_6_), channel_id=1, source_target_pairs={{0,1},{1,2},{2,3},{3,128},{128,129},{129,130},{130,131},{131,0},{4... | collective-permute-start | bytes 1376264 | tf_op jit(solution)/shard_map/ppermute | solution.py:49
  66.8 28.7 %copy-start.11 = (bf16[448,512]{1,0:T(8,128)(2,1)}, bf16[448,512]{1,0:T(8,128)(2,1)S(1)}, u32[]{:S(2)}) copy-start(bf16[448,512]{1,0:T(8,128)(2,1)S(1)} %collective-permute-done.8.refs_7_) | copy-start | bytes 1376260
  66.8 19.6 %collective-permute-start.9 = (bf16[448,512]{1,0:T(8,128)(2,1)S(1)}, bf16[448,512]{1,0:T(8,128)(2,1)S(1)}, u32[]{:S(2)}, u32[]{:S(2)}) collective-permute-start(bf16[448,512]{1,0:T(8,128)(2,1)S(1)} %collective-permute-done.8.refs_7_), channel_id=1, source_target_pairs={{0,131},{1,0},{2,1},{3,2},{128,3},{129,128},{130,129},{131,130},{4... | collective-permute-start | bytes 1376264 | tf_op jit(solution)/shard_map/ppermute | solution.py:49
  76.6 18.9 %copy-start.12 = (bf16[448,512]{1,0:T(8,128)(2,1)}, bf16[448,512]{1,0:T(8,128)(2,1)S(1)}, u32[]{:S(2)}) copy-start(bf16[448,512]{1,0:T(8,128)(2,1)S(1)} %collective-permute-done.2.refs_3_) | copy-start | bytes 1376260
  76.6 18.9 %collective-permute-start.3 = (bf16[448,512]{1,0:T(8,128)(2,1)S(1)}, bf16[448,512]{1,0:T(8,128)(2,1)S(1)}, u32[]{:S(2)}, u32[]{:S(2)}) collective-permute-start(bf16[448,512]{1,0:T(8,128)(2,1)S(1)} %collective-permute-done.2.refs_3_), channel_id=1, source_target_pairs={{0,1},{1,2},{2,3},{3,128},{128,129},{129,130},{130,131},{131,0},{4... | collective-permute-start | bytes 1376264 | tf_op jit(solution)/shard_map/ppermute | solution.py:49
  76.6 18.9 %copy-start.13 = (bf16[448,512]{1,0:T(8,128)(2,1)}, bf16[448,512]{1,0:T(8,128)(2,1)S(1)}, u32[]{:S(2)}) copy-start(bf16[448,512]{1,0:T(8,128)(2,1)S(1)} %collective-permute-done.4.refs_4_) | copy-start | bytes 1376260
  76.6 18.9 %collective-permute-start.5 = (bf16[448,512]{1,0:T(8,128)(2,1)S(1)}, bf16[448,512]{1,0:T(8,128)(2,1)}, u32[]{:S(2)}, u32[]{:S(2)}) collective-permute-start(bf16[448,512]{1,0:T(8,128)(2,1)S(1)} %collective-permute-done.4.refs_4_), channel_id=1, source_target_pairs={{0,131},{1,0},{2,1},{3,2},{128,3},{129,128},{130,129},{131,130},{4... | collective-permute-start | bytes 1376264 | tf_op jit(solution)/shard_map/ppermute | solution.py:49
  86.4 9.1 %copy-start.9 = (bf16[448,512]{1,0:T(8,128)(2,1)}, bf16[448,512]{1,0:T(8,128)(2,1)S(1)}, u32[]{:S(2)}) copy-start(bf16[448,512]{1,0:T(8,128)(2,1)S(1)} %collective-permute-done.7.refs_8_) | copy-start | bytes 1376260
  86.4 13.3 %copy-start.14 = (bf16[448,512]{1,0:T(8,128)(2,1)}, bf16[448,512]{1,0:T(8,128)(2,1)S(1)}, u32[]{:S(2)}) copy-start(bf16[448,512]{1,0:T(8,128)(2,1)S(1)} %collective-permute-done.9.refs_9_) | copy-start | bytes 1376260
  95.5 3.9 %copy-start.16 = (bf16[448,512]{1,0:T(8,128)(2,1)}, bf16[448,512]{1,0:T(8,128)(2,1)S(1)}, u32[]{:S(2)}) copy-start(bf16[448,512]{1,0:T(8,128)(2,1)S(1)} %collective-permute-done.3.refs_0_) | copy-start | bytes 1376260
  96.4 12.0 %collective-permute-start.12 = (bf16[448,512]{1,0:T(8,128)(2,1)S(1)}, bf16[448,512]{1,0:T(8,128)(2,1)}, u32[]{:S(2)}, u32[]{:S(2)}) collective-permute-start(bf16[448,512]{1,0:T(8,128)(2,1)S(1)} %collective-permute-done.9.refs_9_), channel_id=1, source_target_pairs={{0,131},{1,0},{2,1},{3,2},{128,3},{129,128},{130,129},{131,130},{4... | collective-permute-start | bytes 1376264 | tf_op jit(solution)/shard_map/ppermute | solution.py:49
  99.5 29.2 %collective-permute-start.11 = (bf16[448,512]{1,0:T(8,128)(2,1)}, bf16[448,512]{1,0:T(8,128)(2,1)}, u32[]{:S(2)}, u32[]{:S(2)}) collective-permute-start(bf16[448,512]{1,0:T(8,128)(2,1)} %copy-done.9), channel_id=1, source_target_pairs={{0,1},{1,2},{2,3},{3,128},{128,129},{129,130},{130,131},{131,0},{4... | collective-permute-start | bytes 1376264 | tf_op jit(solution)/shard_map/ppermute | solution.py:49
  99.7 7.1 %copy-start.17 = (bf16[448,512]{1,0:T(8,128)(2,1)S(1)}, bf16[448,512]{1,0:T(8,128)(2,1)}, u32[]{:S(2)}) copy-start(bf16[448,512]{1,0:T(8,128)(2,1)} %copy-done.16) | copy-start | bytes 1376260
  99.7 12.4 %copy-start.15 = (s32[7,1]{0,1:T(1,128)S(1)}, s32[7,1]{0,1:T(1,128)}, u32[]{:S(2)}) copy-start(s32[7,1]{0,1:T(1,128)} %param.21) | copy-start | bytes 88
  106.1 0.7 copy-start.3
  106.8 21.9 %collective-permute-start.10 = (bf16[448,512]{1,0:T(8,128)(2,1)S(1)}, bf16[448,512]{1,0:T(8,128)(2,1)}, u32[]{:S(2)}, u32[]{:S(2)}) collective-permute-start(bf16[448,512]{1,0:T(8,128)(2,1)S(1)} %copy-done.17), channel_id=1, source_target_pairs={{0,1},{1,2},{2,3},{3,128},{128,129},{129,130},{130,131},{131,0},{4... | collective-permute-start | bytes 1376264 | tf_op jit(solution)/shard_map/ppermute | solution.py:49
  108.3 20.3 %collective-permute-start.13 = (bf16[448,512]{1,0:T(8,128)(2,1)}, bf16[448,512]{1,0:T(8,128)(2,1)S(1)}, u32[]{:S(2)}, u32[]{:S(2)}) collective-permute-start(bf16[448,512]{1,0:T(8,128)(2,1)} %collective-permute-done.12.refs_4_), channel_id=1, source_target_pairs={{0,131},{1,0},{2,1},{3,2},{128,3},{129,128},{130,129},{131,130},{4... | collective-permute-start | bytes 1376264 | tf_op jit(solution)/shard_map/ppermute | solution.py:49
  113.7 23.2 %all-to-all-start.3 = ((bf16[8,32,896]{2,1,0:T(8,128)(2,1)}), bf16[8,32,896]{2,1,0:T(8,128)(2,1)S(1)}, u32[]{:S(2)}, u32[]{:S(2)}) async-start(bf16[8,32,896]{2,1,0:T(8,128)(2,1)} %gather_fusion.1), calls=%async_computation.3 | async-start | bytes 917504 | tf_op jit(solution)/shard_map/all_to_all | solution.py:57
  128.7 0.8 copy-start.18
  136.9 4.7 %copy-start.4 = (bf16[8,32,896]{2,1,0:T(8,128)(2,1)}, bf16[8,32,896]{2,1,0:T(8,128)(2,1)S(1)}, u32[]{:S(2)}) copy-start(bf16[8,32,896]{2,1,0:T(8,128)(2,1)S(1)} %all-to-all-done.3) | copy-start | bytes 1376260
  136.9 20.8 %all-to-all-start.4 = ((bf16[8,64,768]{2,1,0:T(8,128)(2,1)}), bf16[8,64,768]{2,1,0:T(8,128)(2,1)S(1)}, u32[]{:S(2)}, u32[]{:S(2)}) async-start(bf16[8,64,768]{2,1,0:T(8,128)(2,1)} %get-tuple-element.45), calls=%async_computation.4 | async-start | bytes 1572864 | tf_op jit(solution)/shard_map/all_to_all | solution.py:57
  157.7 0.9 copy-start.5
  158.6 12.3 %copy-start.1 = (bf16[448,512]{1,0:T(8,128)(2,1)S(1)}, bf16[448,512]{1,0:T(8,128)(2,1)}, u32[]{:S(2)}) copy-start(bf16[448,512]{1,0:T(8,128)(2,1)} %hidden_hbm.1) | copy-start | bytes 1376260
  167.3 8.3 %collective-permute-start.14 = (bf16[64,2176]{1,0:T(8,128)(2,1)}, bf16[64,2176]{1,0:T(8,128)(2,1)S(1)}, u32[]{:S(2)}, u32[]{:S(2)}) collective-permute-start(bf16[64,2176]{1,0:T(8,128)(2,1)} %attention.1.chunk_ref), channel_id=1, source_target_pairs={{0,1},{1,2},{2,3},{3,128},{128,129},{129,130},{130,131},{131,0},{4... | collective-permute-start | bytes 835592 | tf_op jit(solution)/shard_map/ppermute | solution.py:49
  168.1 7.4 %collective-permute-start.15 = (bf16[64,2176]{1,0:T(8,128)(2,1)}, bf16[64,2176]{1,0:T(8,128)(2,1)S(1)}, u32[]{:S(2)}, u32[]{:S(2)}) collective-permute-start(bf16[64,2176]{1,0:T(8,128)(2,1)} %attention.1.chunk_ref), channel_id=1, source_target_pairs={{0,131},{1,0},{2,1},{3,2},{128,3},{129,128},{130,129},{131,130},{4... | collective-permute-start | bytes 835592 | tf_op jit(solution)/shard_map/ppermute | solution.py:49
  170.8 1.0 copy-start.2
  175.6 7.8 %collective-permute-start.16 = (bf16[64,2176]{1,0:T(8,128)(2,1)S(1)}, bf16[64,2176]{1,0:T(8,128)(2,1)S(1)}, u32[]{:S(2)}, u32[]{:S(2)}) collective-permute-start(bf16[64,2176]{1,0:T(8,128)(2,1)S(1)} %collective-permute-done.14.refs_0_), channel_id=1, source_target_pairs={{0,1},{1,2},{2,3},{3,128},{128,129},{129,130},{130,131},{131,0},{4... | collective-permute-start | bytes 835592 | tf_op jit(solution)/shard_map/ppermute | solution.py:49
  176.3 8.6 %collective-permute-start.17 = (bf16[64,2176]{1,0:T(8,128)(2,1)S(1)}, bf16[64,2176]{1,0:T(8,128)(2,1)S(1)}, u32[]{:S(2)}, u32[]{:S(2)}) collective-permute-start(bf16[64,2176]{1,0:T(8,128)(2,1)S(1)} %collective-permute-done.15.refs_1_), channel_id=1, source_target_pairs={{0,131},{1,0},{2,1},{3,2},{128,3},{129,128},{130,129},{131,130},{4... | collective-permute-start | bytes 835592 | tf_op jit(solution)/shard_map/ppermute | solution.py:49
  184.9 8.3 %collective-permute-start.18 = (bf16[64,2176]{1,0:T(8,128)(2,1)S(1)}, bf16[64,2176]{1,0:T(8,128)(2,1)S(1)}, u32[]{:S(2)}, u32[]{:S(2)}) collective-permute-start(bf16[64,2176]{1,0:T(8,128)(2,1)S(1)} %collective-permute-done.16.refs_0_), channel_id=1, source_target_pairs={{0,1},{1,2},{2,3},{3,128},{128,129},{129,130},{130,131},{131,0},{4... | collective-permute-start | bytes 835592 | tf_op jit(solution)/shard_map/ppermute | solution.py:49
  187.5 6.5 %collective-permute-start.19 = (bf16[64,2176]{1,0:T(8,128)(2,1)S(1)}, bf16[64,2176]{1,0:T(8,128)(2,1)S(1)}, u32[]{:S(2)}, u32[]{:S(2)}) collective-permute-start(bf16[64,2176]{1,0:T(8,128)(2,1)S(1)} %collective-permute-done.17.refs_1_), channel_id=1, source_target_pairs={{0,131},{1,0},{2,1},{3,2},{128,3},{129,128},{130,129},{131,130},{4... | collective-permute-start | bytes 835592 | tf_op jit(solution)/shard_map/ppermute | solution.py:49
  194.1 6.3 %collective-permute-start.20 = (bf16[32,2176]{1,0:T(8,128)(2,1)S(1)}, bf16[32,2176]{1,0:T(8,128)(2,1)S(1)}, u32[]{:S(2)}, u32[]{:S(2)}) collective-permute-start(bf16[32,2176]{1,0:T(8,128)(2,1)S(1)} %slice.11), channel_id=1, source_target_pairs={{0,1},{1,2},{2,3},{3,128},{128,129},{129,130},{130,131},{131,0},{4... | collective-permute-start | bytes 417800 | tf_op jit(solution)/shard_map/ppermute | solution.py:49
  196.0 5.1 %collective-permute-start.21 = (bf16[32,2176]{1,0:T(8,128)(2,1)S(1)}, bf16[32,2176]{1,0:T(8,128)(2,1)S(1)}, u32[]{:S(2)}, u32[]{:S(2)}) collective-permute-start(bf16[32,2176]{1,0:T(8,128)(2,1)S(1)} %slice.12), channel_id=1, source_target_pairs={{0,131},{1,0},{2,1},{3,2},{128,3},{129,128},{130,129},{131,130},{4... | collective-permute-start | bytes 417800 | tf_op jit(solution)/shard_map/ppermute | solution.py:49
Sparse Core Ops, SparseCore 0:
  96.5 58.8 all-gather.1

commit v8 on v5

--- a/solution.py
+++ b/solution.py
@@ -338,8 +338,8 @@
         if step == 1:
             part, right, left = tie(part, right, left)
         grad_right, grad_left = shift(grad_right, 1), shift(grad_left, -1)
-        if step == 2:
-            asked, right, left = tie(asked, right, left)
+        if step == 1:
+            asked, grad_right, grad_left = tie(asked, grad_right, grad_left)
         index += [(me - step) % NZ, (me + step) % NZ]
         chunks += [right, left]
         grad_chunks += [grad_right, grad_left]

time: 206 us -> 207 us (level)
  blocking collectives: 0 us -> 13.6 us
  waiting for transfers between devices: 78.3 us -> 69.7 us
  starting transfers between devices: 61.5 us -> 57.7 us
    all_to_all x0 -> x1, blocking collectives: none -> 13.6 us  [exchange(): return lax.all_to_all(x, axis, split_axis=0, concat_axis=0, tiled=True)]
    ppermute x22, waiting for transfers between devices: 59.2 us -> 52.8 us  [shift(): return lax.ppermute(x, Z, [(i, (i + by) % NZ) for i in range(NZ)])]
    all_to_all x5 -> x4, starting transfers between devices: 29.3 us -> 24.4 us  [exchange(): return lax.all_to_all(x, axis, split_axis=0, concat_axis=0, tiled=True)]
    all_to_all x5 -> x4, waiting for transfers between devices: 19.1 us -> 16.9 us  [exchange(): return lax.all_to_all(x, axis, split_axis=0, concat_axis=0, tiled=True)]
    unnamed x33 -> x27, local copies, waits for them, and re-layouts: 5.01 us -> 5.03 us
  transfers between devices with their start and end apart: 28 -> 27, of which waited for: 12 -> 10; matrix products, arithmetic and copies ran while one was open for 3% -> 2% of each run, Pallas kernels for 14% -> 14%
where the time goes in v8:
time: 207 us; the launch traced here: 206 us
  waiting for transfers between devices  69.7 us (34%)
  starting transfers between devices  57.7 us (28%)
  Pallas kernels  38.6 us (19%)
  between operations  13.7 us (7%)
  blocking collectives  13.6 us (7%)
  local copies, waits for them, and re-layouts  11.4 us (6%)
    ppermute x22, waiting for transfers between devices, shift(): return lax.ppermute(x, Z, [(i, (i + by) % NZ) for i in range(NZ)])  52.8 us
    ppermute x22, starting transfers between devices, shift(): return lax.ppermute(x, Z, [(i, (i + by) % NZ) for i in range(NZ)])  33.3 us
    all_to_all x4, starting transfers between devices, exchange(): return lax.all_to_all(x, axis, split_axis=0, concat_axis=0, tiled=True)  24.4 us
    all_to_all x4, waiting for transfers between devices, exchange(): return lax.all_to_all(x, axis, split_axis=0, concat_axis=0, tiled=True)  16.9 us
    all_to_all x1, blocking collectives, exchange(): return lax.all_to_all(x, axis, split_axis=0, concat_axis=0, tiled=True)  13.6 us
    pallas_call x1, Pallas kernels, shards(): pl.pallas_call(attention, out_shape=jax.ShapeDtypeStruct((SEG, 2 * HALF +...  8.65 us
    pallas_call x4, Pallas kernels, finish_call(): pl.pallas_call(functools.partial(finish, starts), out_shape=jax.ShapeDtyp...  7.97 us
    pallas_call x1, Pallas kernels, shards(): pl.pallas_call(functools.partial(project_last, len(hiddens)), out_shape=(...  6.69 us
  transfers between devices with their start and end apart: 27, of which 10 were waited for; matrix products, arithmetic and copies ran while one was open for 2% of the time, Pallas kernels for 14%

profile of v8, /device:TPU:2, one launch (start us, length us, event | category | flops | bytes accessed | tf_op | source)
XLA Modules:
  0.0 206.0 jit_solution(12570434869203164379)
XLA Ops:
  6.6 1.0 constant_dynamic-slice_fusion
  7.6 0.8 dynamic_slice.6
  8.4 0.7 pad_maximum_fusion
  9.1 8.5 %all-to-all-start.3 = ((bf16[8,144,128]{2,1,0:T(8,128)(2,1)}), bf16[8,144,128]{2,1,0:T(8,128)(2,1)S(1)}, u32[]{:S(2)}, u32[]{:S(2)}) async-start(bf16[8,144,128]{2,1,0:T(8,128)(2,1)} %pad_maximum_fusion), calls=%async_computation.3 | async-start | bytes 589824 | tf_op jit(solution)/shard_map/all_to_all | solution.py:57
  17.6 2.1 collective-permute-start.2
  19.7 1.3 collective-permute-start.3
  21.0 16.4 %collective-permute-done.2.refs_1_ = bf16[448,512]{1,0:T(8,128)(2,1)} collective-permute-done((bf16[448,512]{1,0:T(8,128)(2,1)S(1)}, bf16[448,512]{1,0:T(8,128)(2,1)}, u32[]{:S(2)}, u32[]{:S(2)}) %collective-permute-start.2) | collective-permute-done | bytes 458784 | tf_op jit(solution)/shard_map/ppermute | solution.py:49
  37.4 0.7 copy_bitcast_fusion
  38.2 0.4 collective-permute-start
  38.6 2.9 %collective-permute-start.1 = (bf16[448,512]{1,0:T(8,128)(2,1)S(1)}, bf16[448,512]{1,0:T(8,128)(2,1)}, u32[]{:S(2)}, u32[]{:S(2)}) collective-permute-start(bf16[448,512]{1,0:T(8,128)(2,1)S(1)} %copy-done.8), channel_id=1, source_target_pairs={{0,131},{1,0},{2,1},{3,2},{128,3},{129,128},{130,129},{131,130},{4... | collective-permute-start | bytes 1376264 | tf_op jit(solution)/shard_map/ppermute | solution.py:49
  41.5 0.1 copy.35
  41.7 0.1 multiply_reduce_fusion
  41.8 0.1 copy.36
  41.9 13.6 %all_to_all.32 = s32[32,1,2]{2,1,0:T(1,128)S(1)} all-to-all(s32[32,1,2]{2,1,0:T(1,128)S(1)} %copy.36), channel_id=1, replica_groups=mesh['group'=2,'dp'=32,'tensor'=4] {'dp'}, dimensions={0} | all-to-all | bytes 512 | tf_op jit(solution)/shard_map/all_to_all | solution.py:57
  55.4 0.1 copy.37
  55.5 0.1 copy.38
  55.6 0.1 reshape.126
  55.7 2.0 gather_fusion
  57.7 5.1 %all-to-all-start.1 = ((bf16[32,32,896]{2,1,0:T(8,128)(2,1)}), bf16[32,32,896]{2,1,0:T(8,128)(2,1)S(1)}, u32[]{:S(2)}, u32[]{:S(2)}) async-start(bf16[32,32,896]{2,1,0:T(8,128)(2,1)} %bitcast.4), calls=%async_computation.1 | async-start | bytes 3670016 | tf_op jit(solution)/shard_map/all_to_all | solution.py:57
  62.8 1.1 collective-permute-start.8
  63.9 1.0 collective-permute-start.4
  65.0 3.2 %collective-permute-start.6 = (bf16[448,512]{1,0:T(8,128)(2,1)}, bf16[448,512]{1,0:T(8,128)(2,1)S(1)}, u32[]{:S(2)}, u32[]{:S(2)}) collective-permute-start(bf16[448,512]{1,0:T(8,128)(2,1)} %collective-permute-done.3.refs_2_), channel_id=1, source_target_pairs={{0,131},{1,0},{2,1},{3,2},{128,3},{129,128},{130,129},{131,130},{4... | collective-permute-start | bytes 1376264 | tf_op jit(solution)/shard_map/ppermute | solution.py:49
  68.2 8.4 %collective-permute-done.8.refs_9_ = bf16[448,512]{1,0:T(8,128)(2,1)} collective-permute-done((bf16[448,512]{1,0:T(8,128)(2,1)}, bf16[448,512]{1,0:T(8,128)(2,1)}, u32[]{:S(2)}, u32[]{:S(2)}) %collective-permute-start.8) | collective-permute-done | bytes 458784 | tf_op jit(solution)/shard_map/ppermute | solution.py:49
  76.6 2.3 %collective-permute-start.12 = (bf16[448,512]{1,0:T(8,128)(2,1)}, bf16[448,512]{1,0:T(8,128)(2,1)}, u32[]{:S(2)}, u32[]{:S(2)}) collective-permute-start(bf16[448,512]{1,0:T(8,128)(2,1)} %collective-permute-done.8.refs_9_), channel_id=1, source_target_pairs={{0,131},{1,0},{2,1},{3,2},{128,3},{129,128},{130,129},{131,130},{4... | collective-permute-start | bytes 1376264 | tf_op jit(solution)/shard_map/ppermute | solution.py:49
  78.9 0.1 stack.61.index_ref
  79.0 9.6 %collective-permute-done.7.refs_8_ = bf16[448,512]{1,0:T(8,128)(2,1)S(1)} collective-permute-done((bf16[448,512]{1,0:T(8,128)(2,1)}, bf16[448,512]{1,0:T(8,128)(2,1)S(1)}, u32[]{:S(2)}, u32[]{:S(2)}) %collective-permute-start.7) | collective-permute-done | bytes 458784 | tf_op jit(solution)/shard_map/ppermute | solution.py:49
  88.6 3.2 %collective-permute-start.9 = (bf16[448,512]{1,0:T(8,128)(2,1)S(1)}, bf16[448,512]{1,0:T(8,128)(2,1)}, u32[]{:S(2)}, u32[]{:S(2)}) collective-permute-start(bf16[448,512]{1,0:T(8,128)(2,1)S(1)} %collective-permute-done.6.refs_4_), channel_id=1, source_target_pairs={{0,131},{1,0},{2,1},{3,2},{128,3},{129,128},{130,129},{131,130},{4... | collective-permute-start | bytes 1376264 | tf_op jit(solution)/shard_map/ppermute | solution.py:49
  91.9 6.5 %project.1 = (f32[448,768]{1,0:T(8,128)}, f32[448,1]{1,0:T(8,128)S(1)}) custom-call(s32[5]{0:T(128)S(1)} %stack.61.index_ref, bf16[448,512]{1,0:T(8,128)(2,1)} %hidden_hbm.1, bf16[448,512]{1,0:T(8,128)(2,1)} %collective-permute-done.2.refs_1_, bf16[448,512]{1,0:T(8,128)(2,1)} %collective-permute-done.3.refs_2_, ...), custom_call_target="tpu_custom_call" | custom-call | flops 1688207360 | bytes 16000000 | tf_op jit(solution)/shard_map/project/pallas_call | solution.py:351
  98.4 0.7 copy-done.4
  99.1 0.7 collective-permute-start.13
  99.8 1.3 collective-permute-start.10
  101.1 0.1 fusion.1
  101.2 0.1 pad_add_fusion.1.index_ref
  101.3 1.4 gather_fusion.1
  102.6 5.2 %all-to-all-start.2 = ((bf16[8,32,896]{2,1,0:T(8,128)(2,1)}), bf16[8,32,896]{2,1,0:T(8,128)(2,1)S(1)}, u32[]{:S(2)}, u32[]{:S(2)}) async-start(bf16[8,32,896]{2,1,0:T(8,128)(2,1)} %gather_fusion.1), calls=%async_computation.2 | async-start | bytes 917504 | tf_op jit(solution)/shard_map/all_to_all | solution.py:57
  107.9 0.5 collective-permute-done.11.refs_3_
  108.4 9.2 %collective-permute-done.13.refs_5_ = bf16[448,512]{1,0:T(8,128)(2,1)} collective-permute-done((bf16[448,512]{1,0:T(8,128)(2,1)}, bf16[448,512]{1,0:T(8,128)(2,1)}, u32[]{:S(2)}, u32[]{:S(2)}) %collective-permute-start.13) | collective-permute-done | bytes 458784 | tf_op jit(solution)/shard_map/ppermute | solution.py:49
  117.6 3.4 %collective-permute-done.10.refs_2_ = bf16[448,512]{1,0:T(8,128)(2,1)} collective-permute-done((bf16[448,512]{1,0:T(8,128)(2,1)}, bf16[448,512]{1,0:T(8,128)(2,1)}, u32[]{:S(2)}, u32[]{:S(2)}) %collective-permute-start.10) | collective-permute-done | bytes 458784 | tf_op jit(solution)/shard_map/ppermute | solution.py:49
  121.1 6.7 %project_last.1 = (bf16[8,64,768]{2,1,0:T(8,128)(2,1)}, f32[448,1]{1,0:T(8,128)S(1)}) custom-call(s32[3]{0:T(128)S(1)} %pad_add_fusion.1.index_ref, bf16[448,512]{1,0:T(8,128)(2,1)} %collective-permute-done.5.refs_0_, bf16[448,512]{1,0:T(8,128)(2,1)} %collective-permute-done.9.refs_1_, bf16[448,512]{1,0:T(8,128)(2,1)} %collective-permute-done.10.refs_2_, ...), custom_call_target="tpu_custom_call" | custom-call | flops 20000000000 | bytes 4000000 | tf_op jit(solution)/shard_map/project_last/pallas_call | solution.py:393
  127.8 0.7 copy-done.3
  128.5 5.6 %all-to-all-start.4 = ((bf16[8,64,768]{2,1,0:T(8,128)(2,1)}), bf16[8,64,768]{2,1,0:T(8,128)(2,1)S(1)}, u32[]{:S(2)}, u32[]{:S(2)}) async-start(bf16[8,64,768]{2,1,0:T(8,128)(2,1)} %get-tuple-element.39), calls=%async_computation.4 | async-start | bytes 1572864 | tf_op jit(solution)/shard_map/all_to_all | solution.py:57
  134.0 3.1 %encoder_queries.1.enc_q_hbm = bf16[256,896]{1,0:T(8,128)(2,1)} custom-call(bf16[256,896]{1,0:T(8,128)(2,1)} %bitcast.32, bf16[896,896]{1,0:T(8,128)(2,1)} %weight_hbm.1), custom_call_target="tpu_custom_call" | custom-call | flops 411041792 | bytes 3000000 | tf_op jit(solution)/shard_map/encoder_queries/pallas_call | solution.py:379
  137.1 16.9 %all-to-all-done.4.got_hbm = bf16[8,64,768]{2,1,0:T(8,128)(2,1)S(1)} async-done(((bf16[8,64,768]{2,1,0:T(8,128)(2,1)}), bf16[8,64,768]{2,1,0:T(8,128)(2,1)S(1)}, u32[]{:S(2)}, u32[]{:S(2)}) %all-to-all-start.4) | async-done | bytes 786464 | tf_op jit(solution)/shard_map/all_to_all | solution.py:57
  154.0 0.9 copy-done.7
  154.9 8.6 %attention.1.chunk_ref = bf16[64,2176]{1,0:T(8,128)(2,1)} custom-call(bf16[256,896]{1,0:T(8,128)(2,1)} %bitcast.33, bf16[256,896]{1,0:T(8,128)(2,1)} %encoder_queries.1.enc_q_hbm, bf16[8,64,768]{2,1,0:T(8,128)(2,1)} %copy-done.7, bf16[896,896]{1,0:T(8,128)(2,1)} %enc_out_hbm.1, bf16[16,2,144,1024]{3,2,1,0:T(8,128)(2,1)} %bitcast.29), custom_call_target="tpu_custom_call" | custom-call | flops 4000000000 | bytes 12000000 | tf_op jit(solution)/shard_map/attention/pallas_call | solution.py:421
  163.6 0.8 collective-permute-start.14
  164.4 2.7 %collective-permute-start.15 = (bf16[64,2176]{1,0:T(8,128)(2,1)}, bf16[64,2176]{1,0:T(8,128)(2,1)S(1)}, u32[]{:S(2)}, u32[]{:S(2)}) collective-permute-start(bf16[64,2176]{1,0:T(8,128)(2,1)} %attention.1.chunk_ref), channel_id=1, source_target_pairs={{0,131},{1,0},{2,1},{3,2},{128,3},{129,128},{130,129},{131,130},{4... | collective-permute-start | bytes 835592 | tf_op jit(solution)/shard_map/ppermute | solution.py:49
  167.1 5.7 %finish_first.1 = (bf16[448,512]{1,0:T(8,128)(2,1)}, bf16[448,512]{1,0:T(8,128)(2,1)}, f32[448,1]{1,0:T(8,128)S(1)}, bf16[2,32,16,1024]{3,2,1,0:T(8,128)(2,1)}) custom-call(s32[1]{0:T(128)} %bitcast.13.source_ref, bf16[64,2176]{1,0:T(8,128)(2,1)} %attention.1.chunk_ref, bf16[448,512]{1,0:T(8,128)(2,1)} %hidden_hbm.1, f32[448,1]{1,0:T(8,128)} %copy-done.3, ...), custom_call_target="tpu_custom_call" | custom-call | flops 134217728 | bytes 4000000 | tf_op jit(solution)/shard_map/finish_first/pallas_call | solution.py:445
  172.8 0.1 collective-permute-start.16
  172.9 3.2 %collective-permute-start.17 = (bf16[64,2176]{1,0:T(8,128)(2,1)S(1)}, bf16[64,2176]{1,0:T(8,128)(2,1)S(1)}, u32[]{:S(2)}, u32[]{:S(2)}) collective-permute-start(bf16[64,2176]{1,0:T(8,128)(2,1)S(1)} %collective-permute-done.15.refs_1_), channel_id=1, source_target_pairs={{0,131},{1,0},{2,1},{3,2},{128,3},{129,128},{130,129},{131,130},{4... | collective-permute-start | bytes 835592 | tf_op jit(solution)/shard_map/ppermute | solution.py:49
  176.1 0.1 pad_add_fusion.2.source_ref
  176.2 1.6 copy-done.1
  177.8 1.0 copy-done.2
  178.8 2.0 finish.4.refs_5_
  180.8 0.4 collective-permute-done.16.refs_0_
  181.3 3.5 %collective-permute-start.19 = (bf16[64,2176]{1,0:T(8,128)(2,1)S(1)}, bf16[64,2176]{1,0:T(8,128)(2,1)S(1)}, u32[]{:S(2)}, u32[]{:S(2)}) collective-permute-start(bf16[64,2176]{1,0:T(8,128)(2,1)S(1)} %collective-permute-done.17.refs_1_), channel_id=1, source_target_pairs={{0,131},{1,0},{2,1},{3,2},{128,3},{129,128},{130,129},{131,130},{4... | collective-permute-start | bytes 835592 | tf_op jit(solution)/shard_map/ppermute | solution.py:49
  184.8 0.1 pad_add_fusion.3.source_ref
  184.9 2.0 finish.5.refs_5_
  186.9 3.9 %collective-permute-done.18.refs_0_ = bf16[64,2176]{1,0:T(8,128)(2,1)S(1)} collective-permute-done((bf16[64,2176]{1,0:T(8,128)(2,1)S(1)}, bf16[64,2176]{1,0:T(8,128)(2,1)S(1)}, u32[]{:S(2)}, u32[]{:S(2)}) %collective-permute-start.18) | collective-permute-done | bytes 278560 | tf_op jit(solution)/shard_map/ppermute | solution.py:49
  190.8 0.1 collective-permute-start.20
  190.9 3.3 %collective-permute-start.21 = (bf16[32,2176]{1,0:T(8,128)(2,1)S(1)}, bf16[32,2176]{1,0:T(8,128)(2,1)S(1)}, u32[]{:S(2)}, u32[]{:S(2)}) collective-permute-start(bf16[32,2176]{1,0:T(8,128)(2,1)S(1)} %slice.12), channel_id=1, source_target_pairs={{0,131},{1,0},{2,1},{3,2},{128,3},{129,128},{130,129},{131,130},{4... | collective-permute-start | bytes 417800 | tf_op jit(solution)/shard_map/ppermute | solution.py:49
  194.4 2.0 finish.6.refs_5_
  196.4 0.8 collective-permute-done.20.refs_0_
  197.2 1.9 finish.7
  (55 shorter events, 0.5 us)
Async XLA Ops:
  6.5 49.2 %copy-start = (bf16[16,16,896]{2,1,0:T(8,128)(2,1)S(1)}, bf16[16,16,896]{2,1,0:T(8,128)(2,1)}, u32[]{:S(2)}) copy-start(bf16[16,16,896]{2,1,0:T(8,128)(2,1)} %param.19) | copy-start | bytes 1376260
  6.5 11.1 %copy-start.6 = (bf16[448,512]{1,0:T(8,128)(2,1)S(1)}, bf16[448,512]{1,0:T(8,128)(2,1)}, u32[]{:S(2)}) copy-start(bf16[448,512]{1,0:T(8,128)(2,1)} %hidden_hbm.1) | copy-start | bytes 1376260
  6.5 31.6 %copy-start.8 = (bf16[448,512]{1,0:T(8,128)(2,1)S(1)}, bf16[448,512]{1,0:T(8,128)(2,1)}, u32[]{:S(2)}) copy-start(bf16[448,512]{1,0:T(8,128)(2,1)} %refs_5_.1) | copy-start | bytes 1376260
  6.5 35.0 %copy-start.11 = (s32[7,2]{0,1:T(2,128)S(1)}, s32[7,2]{0,1:T(2,128)}, u32[]{:S(2)}) copy-start(s32[7,2]{0,1:T(2,128)} %param.20) | copy-start | bytes 172
  6.5 35.1 %copy-start.12 = (s32[7,1]{0,1:T(1,128)S(1)}, s32[7,1]{0,1:T(1,128)}, u32[]{:S(2)}) copy-start(s32[7,1]{0,1:T(1,128)} %param.21) | copy-start | bytes 88
  9.1 28.3 %all-to-all-start.3 = ((bf16[8,144,128]{2,1,0:T(8,128)(2,1)}), bf16[8,144,128]{2,1,0:T(8,128)(2,1)S(1)}, u32[]{:S(2)}, u32[]{:S(2)}) async-start(bf16[8,144,128]{2,1,0:T(8,128)(2,1)} %pad_maximum_fusion), calls=%async_computation.3 | async-start | bytes 589824 | tf_op jit(solution)/shard_map/all_to_all | solution.py:57
  17.6 136.4 %all-gather.2.cloned.1.call-start = ((), (), s32[]{:S(2)}) async-start(), calls=%async_computation.5 | async-start | bytes 9732096 | tf_op jit(solution)/shard_map/all_gather | solution.py:347
  17.6 19.8 %collective-permute-start.2 = (bf16[448,512]{1,0:T(8,128)(2,1)S(1)}, bf16[448,512]{1,0:T(8,128)(2,1)}, u32[]{:S(2)}, u32[]{:S(2)}) collective-permute-start(bf16[448,512]{1,0:T(8,128)(2,1)S(1)} %copy-done.6), channel_id=1, source_target_pairs={{0,1},{1,2},{2,3},{3,128},{128,129},{129,130},{130,131},{131,0},{4... | collective-permute-start | bytes 1376264 | tf_op jit(solution)/shard_map/ppermute | solution.py:49
  19.7 17.7 %collective-permute-start.3 = (bf16[448,512]{1,0:T(8,128)(2,1)S(1)}, bf16[448,512]{1,0:T(8,128)(2,1)}, u32[]{:S(2)}, u32[]{:S(2)}) collective-permute-start(bf16[448,512]{1,0:T(8,128)(2,1)S(1)} %copy-done.6), channel_id=1, source_target_pairs={{0,131},{1,0},{2,1},{3,2},{128,3},{129,128},{130,129},{131,130},{4... | collective-permute-start | bytes 1376264 | tf_op jit(solution)/shard_map/ppermute | solution.py:49
  38.2 17.3 %collective-permute-start = (bf16[448,512]{1,0:T(8,128)(2,1)S(1)}, bf16[448,512]{1,0:T(8,128)(2,1)}, u32[]{:S(2)}, u32[]{:S(2)}) collective-permute-start(bf16[448,512]{1,0:T(8,128)(2,1)S(1)} %copy-done.8), channel_id=1, source_target_pairs={{0,1},{1,2},{2,3},{3,128},{128,129},{129,130},{130,131},{131,0},{4... | collective-permute-start | bytes 1376264 | tf_op jit(solution)/shard_map/ppermute | solution.py:49
  38.6 16.9 %collective-permute-start.1 = (bf16[448,512]{1,0:T(8,128)(2,1)S(1)}, bf16[448,512]{1,0:T(8,128)(2,1)}, u32[]{:S(2)}, u32[]{:S(2)}) collective-permute-start(bf16[448,512]{1,0:T(8,128)(2,1)S(1)} %copy-done.8), channel_id=1, source_target_pairs={{0,131},{1,0},{2,1},{3,2},{128,3},{129,128},{130,129},{131,130},{4... | collective-permute-start | bytes 1376264 | tf_op jit(solution)/shard_map/ppermute | solution.py:49
  57.7 43.6 %all-to-all-start.1 = ((bf16[32,32,896]{2,1,0:T(8,128)(2,1)}), bf16[32,32,896]{2,1,0:T(8,128)(2,1)S(1)}, u32[]{:S(2)}, u32[]{:S(2)}) async-start(bf16[32,32,896]{2,1,0:T(8,128)(2,1)} %bitcast.4), calls=%async_computation.1 | async-start | bytes 3670016 | tf_op jit(solution)/shard_map/all_to_all | solution.py:57
  62.8 13.8 %collective-permute-start.8 = (bf16[448,512]{1,0:T(8,128)(2,1)}, bf16[448,512]{1,0:T(8,128)(2,1)}, u32[]{:S(2)}, u32[]{:S(2)}) collective-permute-start(bf16[448,512]{1,0:T(8,128)(2,1)} %collective-permute-done.1.refs_7_), channel_id=1, source_target_pairs={{0,131},{1,0},{2,1},{3,2},{128,3},{129,128},{130,129},{131,130},{4... | collective-permute-start | bytes 1376264 | tf_op jit(solution)/shard_map/ppermute | solution.py:49
  63.9 14.9 %collective-permute-start.4 = (bf16[448,512]{1,0:T(8,128)(2,1)}, bf16[448,512]{1,0:T(8,128)(2,1)}, u32[]{:S(2)}, u32[]{:S(2)}) collective-permute-start(bf16[448,512]{1,0:T(8,128)(2,1)} %collective-permute-done.2.refs_1_), channel_id=1, source_target_pairs={{0,1},{1,2},{2,3},{3,128},{128,129},{129,130},{130,131},{131,0},{4... | collective-permute-start | bytes 1376264 | tf_op jit(solution)/shard_map/ppermute | solution.py:49
  64.9 23.7 %collective-permute-start.7 = (bf16[448,512]{1,0:T(8,128)(2,1)}, bf16[448,512]{1,0:T(8,128)(2,1)S(1)}, u32[]{:S(2)}, u32[]{:S(2)}) collective-permute-start(bf16[448,512]{1,0:T(8,128)(2,1)} %collective-permute-done.refs_6_), channel_id=1, source_target_pairs={{0,1},{1,2},{2,3},{3,128},{128,129},{129,130},{130,131},{131,0},{4... | collective-permute-start | bytes 1376264 | tf_op jit(solution)/shard_map/ppermute | solution.py:49
  65.0 23.7 %collective-permute-start.6 = (bf16[448,512]{1,0:T(8,128)(2,1)}, bf16[448,512]{1,0:T(8,128)(2,1)S(1)}, u32[]{:S(2)}, u32[]{:S(2)}) collective-permute-start(bf16[448,512]{1,0:T(8,128)(2,1)} %collective-permute-done.3.refs_2_), channel_id=1, source_target_pairs={{0,131},{1,0},{2,1},{3,2},{128,3},{129,128},{130,129},{131,130},{4... | collective-permute-start | bytes 1376264 | tf_op jit(solution)/shard_map/ppermute | solution.py:49
  76.6 22.5 %collective-permute-start.12 = (bf16[448,512]{1,0:T(8,128)(2,1)}, bf16[448,512]{1,0:T(8,128)(2,1)}, u32[]{:S(2)}, u32[]{:S(2)}) collective-permute-start(bf16[448,512]{1,0:T(8,128)(2,1)} %collective-permute-done.8.refs_9_), channel_id=1, source_target_pairs={{0,131},{1,0},{2,1},{3,2},{128,3},{129,128},{130,129},{131,130},{4... | collective-permute-start | bytes 1376264 | tf_op jit(solution)/shard_map/ppermute | solution.py:49
  78.9 20.9 %collective-permute-start.5 = (bf16[448,512]{1,0:T(8,128)(2,1)}, bf16[448,512]{1,0:T(8,128)(2,1)}, u32[]{:S(2)}, u32[]{:S(2)}) collective-permute-start(bf16[448,512]{1,0:T(8,128)(2,1)} %collective-permute-done.4.refs_3_), channel_id=1, source_target_pairs={{0,1},{1,2},{2,3},{3,128},{128,129},{129,130},{130,131},{131,0},{4... | collective-permute-start | bytes 1376264 | tf_op jit(solution)/shard_map/ppermute | solution.py:49
  88.6 3.2 %copy-start.9 = (bf16[448,512]{1,0:T(8,128)(2,1)}, bf16[448,512]{1,0:T(8,128)(2,1)S(1)}, u32[]{:S(2)}) copy-start(bf16[448,512]{1,0:T(8,128)(2,1)S(1)} %collective-permute-done.7.refs_8_) | copy-start | bytes 1376260
  88.6 19.8 %collective-permute-start.11 = (bf16[448,512]{1,0:T(8,128)(2,1)S(1)}, bf16[448,512]{1,0:T(8,128)(2,1)}, u32[]{:S(2)}, u32[]{:S(2)}) collective-permute-start(bf16[448,512]{1,0:T(8,128)(2,1)S(1)} %collective-permute-done.7.refs_8_), channel_id=1, source_target_pairs={{0,1},{1,2},{2,3},{3,128},{128,129},{129,130},{130,131},{131,0},{4... | collective-permute-start | bytes 1376264 | tf_op jit(solution)/shard_map/ppermute | solution.py:49
  88.6 3.2 %copy-start.10 = (bf16[448,512]{1,0:T(8,128)(2,1)}, bf16[448,512]{1,0:T(8,128)(2,1)S(1)}, u32[]{:S(2)}) copy-start(bf16[448,512]{1,0:T(8,128)(2,1)S(1)} %collective-permute-done.6.refs_4_) | copy-start | bytes 1376260
  88.6 19.7 %collective-permute-start.9 = (bf16[448,512]{1,0:T(8,128)(2,1)S(1)}, bf16[448,512]{1,0:T(8,128)(2,1)}, u32[]{:S(2)}, u32[]{:S(2)}) collective-permute-start(bf16[448,512]{1,0:T(8,128)(2,1)S(1)} %collective-permute-done.6.refs_4_), channel_id=1, source_target_pairs={{0,131},{1,0},{2,1},{3,2},{128,3},{129,128},{130,129},{131,130},{4... | collective-permute-start | bytes 1376264 | tf_op jit(solution)/shard_map/ppermute | solution.py:49
  98.3 0.7 copy-start.4
  99.1 18.6 %collective-permute-start.13 = (bf16[448,512]{1,0:T(8,128)(2,1)}, bf16[448,512]{1,0:T(8,128)(2,1)}, u32[]{:S(2)}, u32[]{:S(2)}) collective-permute-start(bf16[448,512]{1,0:T(8,128)(2,1)} %collective-permute-done.12.refs_4_), channel_id=1, source_target_pairs={{0,131},{1,0},{2,1},{3,2},{128,3},{129,128},{130,129},{131,130},{4... | collective-permute-start | bytes 1376264 | tf_op jit(solution)/shard_map/ppermute | solution.py:49
  99.8 21.3 %collective-permute-start.10 = (bf16[448,512]{1,0:T(8,128)(2,1)}, bf16[448,512]{1,0:T(8,128)(2,1)}, u32[]{:S(2)}, u32[]{:S(2)}) collective-permute-start(bf16[448,512]{1,0:T(8,128)(2,1)} %collective-permute-done.5.refs_0_), channel_id=1, source_target_pairs={{0,1},{1,2},{2,3},{3,128},{128,129},{129,130},{130,131},{131,0},{4... | collective-permute-start | bytes 1376264 | tf_op jit(solution)/shard_map/ppermute | solution.py:49
  102.6 25.8 %all-to-all-start.2 = ((bf16[8,32,896]{2,1,0:T(8,128)(2,1)}), bf16[8,32,896]{2,1,0:T(8,128)(2,1)S(1)}, u32[]{:S(2)}, u32[]{:S(2)}) async-start(bf16[8,32,896]{2,1,0:T(8,128)(2,1)} %gather_fusion.1), calls=%async_computation.2 | async-start | bytes 917504 | tf_op jit(solution)/shard_map/all_to_all | solution.py:57
  127.8 0.7 copy-start.3
  128.5 5.6 %copy-start.5 = (bf16[8,32,896]{2,1,0:T(8,128)(2,1)}, bf16[8,32,896]{2,1,0:T(8,128)(2,1)S(1)}, u32[]{:S(2)}) copy-start(bf16[8,32,896]{2,1,0:T(8,128)(2,1)S(1)} %all-to-all-done.2) | copy-start | bytes 1376260
  128.5 25.5 %all-to-all-start.4 = ((bf16[8,64,768]{2,1,0:T(8,128)(2,1)}), bf16[8,64,768]{2,1,0:T(8,128)(2,1)S(1)}, u32[]{:S(2)}, u32[]{:S(2)}) async-start(bf16[8,64,768]{2,1,0:T(8,128)(2,1)} %get-tuple-element.39), calls=%async_computation.4 | async-start | bytes 1572864 | tf_op jit(solution)/shard_map/all_to_all | solution.py:57
  154.0 0.9 copy-start.7
  163.6 9.2 %collective-permute-start.14 = (bf16[64,2176]{1,0:T(8,128)(2,1)}, bf16[64,2176]{1,0:T(8,128)(2,1)S(1)}, u32[]{:S(2)}, u32[]{:S(2)}) collective-permute-start(bf16[64,2176]{1,0:T(8,128)(2,1)} %attention.1.chunk_ref), channel_id=1, source_target_pairs={{0,1},{1,2},{2,3},{3,128},{128,129},{129,130},{130,131},{131,0},{4... | collective-permute-start | bytes 835592 | tf_op jit(solution)/shard_map/ppermute | solution.py:49
  164.4 8.4 %collective-permute-start.15 = (bf16[64,2176]{1,0:T(8,128)(2,1)}, bf16[64,2176]{1,0:T(8,128)(2,1)S(1)}, u32[]{:S(2)}, u32[]{:S(2)}) collective-permute-start(bf16[64,2176]{1,0:T(8,128)(2,1)} %attention.1.chunk_ref), channel_id=1, source_target_pairs={{0,131},{1,0},{2,1},{3,2},{128,3},{129,128},{130,129},{131,130},{4... | collective-permute-start | bytes 835592 | tf_op jit(solution)/shard_map/ppermute | solution.py:49
  172.8 8.5 %collective-permute-start.16 = (bf16[64,2176]{1,0:T(8,128)(2,1)S(1)}, bf16[64,2176]{1,0:T(8,128)(2,1)S(1)}, u32[]{:S(2)}, u32[]{:S(2)}) collective-permute-start(bf16[64,2176]{1,0:T(8,128)(2,1)S(1)} %collective-permute-done.14.refs_0_), channel_id=1, source_target_pairs={{0,1},{1,2},{2,3},{3,128},{128,129},{129,130},{130,131},{131,0},{4... | collective-permute-start | bytes 835592 | tf_op jit(solution)/shard_map/ppermute | solution.py:49
  172.9 8.4 %collective-permute-start.17 = (bf16[64,2176]{1,0:T(8,128)(2,1)S(1)}, bf16[64,2176]{1,0:T(8,128)(2,1)S(1)}, u32[]{:S(2)}, u32[]{:S(2)}) collective-permute-start(bf16[64,2176]{1,0:T(8,128)(2,1)S(1)} %collective-permute-done.15.refs_1_), channel_id=1, source_target_pairs={{0,131},{1,0},{2,1},{3,2},{128,3},{129,128},{130,129},{131,130},{4... | collective-permute-start | bytes 835592 | tf_op jit(solution)/shard_map/ppermute | solution.py:49
  176.2 1.6 copy-start.1
  177.8 1.0 copy-start.2
  181.3 9.5 %collective-permute-start.18 = (bf16[64,2176]{1,0:T(8,128)(2,1)S(1)}, bf16[64,2176]{1,0:T(8,128)(2,1)S(1)}, u32[]{:S(2)}, u32[]{:S(2)}) collective-permute-start(bf16[64,2176]{1,0:T(8,128)(2,1)S(1)} %collective-permute-done.16.refs_0_), channel_id=1, source_target_pairs={{0,1},{1,2},{2,3},{3,128},{128,129},{129,130},{130,131},{131,0},{4... | collective-permute-start | bytes 835592 | tf_op jit(solution)/shard_map/ppermute | solution.py:49
  181.3 9.5 %collective-permute-start.19 = (bf16[64,2176]{1,0:T(8,128)(2,1)S(1)}, bf16[64,2176]{1,0:T(8,128)(2,1)S(1)}, u32[]{:S(2)}, u32[]{:S(2)}) collective-permute-start(bf16[64,2176]{1,0:T(8,128)(2,1)S(1)} %collective-permute-done.17.refs_1_), channel_id=1, source_target_pairs={{0,131},{1,0},{2,1},{3,2},{128,3},{129,128},{130,129},{131,130},{4... | collective-permute-start | bytes 835592 | tf_op jit(solution)/shard_map/ppermute | solution.py:49
  190.8 6.3 %collective-permute-start.20 = (bf16[32,2176]{1,0:T(8,128)(2,1)S(1)}, bf16[32,2176]{1,0:T(8,128)(2,1)S(1)}, u32[]{:S(2)}, u32[]{:S(2)}) collective-permute-start(bf16[32,2176]{1,0:T(8,128)(2,1)S(1)} %slice.11), channel_id=1, source_target_pairs={{0,1},{1,2},{2,3},{3,128},{128,129},{129,130},{130,131},{131,0},{4... | collective-permute-start | bytes 417800 | tf_op jit(solution)/shard_map/ppermute | solution.py:49
  190.9 6.2 %collective-permute-start.21 = (bf16[32,2176]{1,0:T(8,128)(2,1)S(1)}, bf16[32,2176]{1,0:T(8,128)(2,1)S(1)}, u32[]{:S(2)}, u32[]{:S(2)}) collective-permute-start(bf16[32,2176]{1,0:T(8,128)(2,1)S(1)} %slice.12), channel_id=1, source_target_pairs={{0,131},{1,0},{2,1},{3,2},{128,3},{129,128},{130,129},{131,130},{4... | collective-permute-start | bytes 417800 | tf_op jit(solution)/shard_map/ppermute | solution.py:49
Sparse Core Ops, SparseCore 0:
  38.3 68.9 all-gather.1
